TPU v7x, 32 devices: a whole 2x2x4 slice. The times are simulated.
32 devices in a mesh: ckpt: 4 (over x, core), space: 8 (over z, y).
Axes of the slice: x: 2, y: 2, z: 4, core: 2. Of those that a mesh axis runs over, the one named last changes fastest.
Arguments:
- checkpoint: float32 [8, 6, 16, 16, 128], P('space', None, 'ckpt'), may hold values from -5 to 5
- seeds: float32 [4, 8, 6, 16, 16, 128], P('ckpt', 'space'), may hold values from -6 to 6
- cell_rate: float32 [8, 16, 16, 128], P('space'), may hold values from 0.5 to 2
- flux_mats: float32 [3, 6, 6], replicated, may hold values from -1.25 to 1.25
- owner: int32 [8], replicated, may hold values from 0 to 7, each once
- neighbours: int32 [8, 6], replicated, may hold values from 0 to 7, as said below
- orientation: int32 [8, 6], replicated, may hold values from 0 to 3, as said below
Outputs:
- adjoint: float32 [4, 8, 6, 16, 16, 128], P('ckpt', 'space')
- final_state: float32 [8, 6, 16, 16, 128], P('space')
Inputs may be any that keep to these rules, and one draw needn't show every extreme that they name: owner lists each space index once. The block across the -x face of neighbours[b, 0] is b, across the +x face of neighbours[b, 1] is b, and likewise for y and z; a block may be its own neighbour. orientation[b, f] equals the code of the same face seen from the block across it.
All inputs are finite; a program needn't handle non-finite values.
Results may differ from a plain program's by a relative error of at most 0.0001.
Values sent between devices are 32-bit elements; how exact they have to be, the bound alone decides.
No kernel may reach another device: no remote copies, remote signals or barrier semaphores. Data moves between devices by JAX's collectives and lax.ppermute only.
A program may use at most 128 MiB of HBM per device.

v0:
```python
import jax
import jax.numpy as jnp
from jax import lax
from jax.sharding import PartitionSpec as P

STEPS = 2


time_step = 0.05
damping = 0.015


def boundary(field, side):
    layer_axis = field.ndim - 3 + side // 2
    location = field.shape[layer_axis] - 1 if side % 2 == 0 else 0
    return lax.index_in_dim(field, location, layer_axis, keepdims=False)


def reorient(face, flips):
    face = jnp.where(flips % 2 == 1, jnp.flip(face, -2), face)
    return jnp.where(flips // 2 % 2 == 1, jnp.flip(face, -1), face)


def pad_with(field, ghosts):
    padded = jnp.pad(field, [(0, 0)] + [(1, 1)] * 3)
    for side in range(6):
        layer_axis = side // 2
        location = padded.shape[layer_axis + 1] - 1 if side % 2 == 0 else 0
        if layer_axis == 0:
            padded = padded.at[:, location, 1:-1, 1:-1].set(ghosts[side])
        elif layer_axis == 1:
            padded = padded.at[:, 1:-1, location, 1:-1].set(ghosts[side])
        else:
            padded = padded.at[:, 1:-1, 1:-1, location].set(ghosts[side])
    return padded


def ghost_layer(padded, side):
    layer_axis = side // 2
    location = padded.shape[layer_axis + 1] - 1 if side % 2 == 0 else 0
    if layer_axis == 0:
        return padded[:, location, 1:-1, 1:-1]
    if layer_axis == 1:
        return padded[:, 1:-1, location, 1:-1]
    return padded[:, 1:-1, 1:-1, location]


def add_layer(field, side, layer):
    layer_axis = side // 2
    location = field.shape[layer_axis + 1] - 1 if side % 2 == 0 else 0
    if layer_axis == 0:
        return field.at[:, location].add(layer)
    if layer_axis == 1:
        return field.at[:, :, location].add(layer)
    return field.at[:, :, :, location].add(layer)


def advance(padded, rates, flux_mats):
    interior = padded[:, 1:-1, 1:-1, 1:-1]
    divergence = jnp.zeros_like(interior)
    for direction in range(3):
        if direction == 0:
            strip = padded[:, :, 1:-1, 1:-1]
        elif direction == 1:
            strip = padded[:, 1:-1, :, 1:-1]
        else:
            strip = padded[:, 1:-1, 1:-1, :]
        length = strip.shape[direction + 1]
        left_cells = lax.slice_in_dim(strip, 0, length - 1, axis=direction + 1)
        right_cells = lax.slice_in_dim(strip, 1, length, axis=direction + 1)
        average = 0.5 * (left_cells + right_cells)
        difference = right_cells - left_cells
        spread = jnp.sqrt(1.0 + average[0] * average[0])
        face_flux = (
            jnp.einsum(
                "ij,jxyz->ixyz", flux_mats[direction], average, precision=lax.Precision.HIGHEST
            )
            - 0.5 * spread * difference
        )
        count = face_flux.shape[direction + 1]
        divergence = (
            divergence
            + lax.slice_in_dim(face_flux, 1, count, axis=direction + 1)
            - lax.slice_in_dim(face_flux, 0, count - 1, axis=direction + 1)
        )
    return interior - time_step * rates * divergence - damping * jnp.tanh(interior)


def pick(pieces, sources):
    count = pieces[0].shape[0]
    positions = jnp.arange(count, dtype=jnp.int32)
    result = []
    for side in range(6):
        weight = (positions == sources[side]).astype(jnp.float32)
        piece = pieces[side // 2][:, 1 - side % 2]
        result.append(jnp.sum(weight.reshape((count, 1, 1, 1)) * piece, axis=0))
    return tuple(result)


def side_pairs(layers):
    return [jnp.stack([layers[2 * pair], layers[2 * pair + 1]])[None] for pair in range(3)]


def on_device(checkpoint, seeds, cell_rate, flux_mats, owner, neighbours, orientation):
    restored = lax.all_gather(checkpoint, "ckpt", axis=2, tiled=True)[0]
    rates = cell_rate[0]
    block_count = owner.shape[0]
    indices = jnp.arange(block_count, dtype=jnp.int32)
    position = lax.axis_index("space")
    own_block = jnp.sum(jnp.where(owner == position, indices, 0))
    chosen = (indices == own_block).astype(jnp.int32)[:, None]
    across = jnp.sum(chosen * neighbours, axis=0)
    flips = jnp.sum(chosen * orientation, axis=0)
    sources = jnp.sum(
        (indices[None, :] == across[:, None]).astype(jnp.int32) * owner[None, :], axis=1
    )

    def gather_step(pieces):
        return pick(pieces, sources)

    def fetch(field):
        layers = [boundary(field, side) for side in range(6)]
        x_faces, y_faces, z_faces = side_pairs(layers)
        whole = gather_step(
            (
                lax.all_gather(x_faces, "space", axis=0, tiled=True),
                lax.all_gather(y_faces, "space", axis=0, tiled=True),
                lax.all_gather(z_faces, "space", axis=0, tiled=True),
            )
        )
        return [reorient(whole[side], flips[side]) for side in range(6)]

    padded_states = []
    state = restored
    for section in range(STEPS):
        padded = pad_with(state, fetch(state))
        padded_states.append(padded)
        state = advance(padded, rates, flux_mats)
    adjoint_now = seeds[0, 0]
    for section in reversed(range(STEPS)):
        _, pullback = jax.vjp(lambda grid: advance(grid, rates, flux_mats), padded_states[section])
        cotangent = pullback(adjoint_now)[0]
        x_ghosts, y_ghosts, z_ghosts = side_pairs(
            [ghost_layer(cotangent, side) for side in range(6)]
        )
        incoming = gather_step(
            (
                lax.all_gather(x_ghosts, "space", axis=0, tiled=True),
                lax.all_gather(y_ghosts, "space", axis=0, tiled=True),
                lax.all_gather(z_ghosts, "space", axis=0, tiled=True),
            )
        )
        adjoint_now = cotangent[:, 1:-1, 1:-1, 1:-1]
        for side in range(6):
            adjoint_now = add_layer(adjoint_now, side, reorient(incoming[side], flips[side]))
    return (adjoint_now[None, None], state[None])


def solution(mesh):
    return jax.shard_map(
        on_device,
        mesh=mesh,
        in_specs=(
            P("space", None, "ckpt", None, None),
            P("ckpt", "space", None, None, None, None),
            P("space", None, None, None),
            P(),
            P(),
            P(),
            P(),
        ),
        out_specs=(P("ckpt", "space", None, None, None, None), P("space", None, None, None, None)),
        check_vma=False,
    )
```

profile of v0, /device:TPU:0, one launch (start us, length us, event | category | flops | bytes accessed | tf_op | source)
XLA Modules:
  0.0 824.3 jit_solution(12966047192478581815)
XLA Ops:
  11.4 10.0 %all_gather.39 = f32[1,6,16,16,128]{4,3,1,0,2:T(8,128)S(1)} all-gather(f32[1,6,4,16,128]{4,3,1,0,2:T(8,128)S(1)} %copy.1406), channel_id=1, replica_groups=mesh['ckpt'=4,'space'=8] {'ckpt'}, dimensions={2}, use_global_device_ids=true | all-gather | bytes 983040 | tf_op jit(solution)/shard_map/all_gather | solution.py:105
  23.0 32.2 %all-gather.2 = f32[16,6,16,16]{3,2,1,0:T(8,128)S(1)} all-gather(f32[2,6,16,16]{3,2,1,0:T(8,128)S(1)} %pad_maximum_fusion.2), channel_id=4, replica_groups=mesh['ckpt'=4,'space'=8] {'space'}, dimensions={0}, use_global_device_ids=true | all-gather | bytes 110592 | tf_op jit(solution)/shard_map/all_gather | solution.py:128
  62.9 32.0 %all-gather.1 = f32[16,6,16,128]{3,2,1,0:T(8,128)S(1)} all-gather(f32[2,6,16,128]{3,2,1,0:T(8,128)S(1)} %pad_maximum_fusion.1), channel_id=3, replica_groups=mesh['ckpt'=4,'space'=8] {'space'}, dimensions={0}, use_global_device_ids=true | all-gather | bytes 884736 | tf_op jit(solution)/shard_map/all_gather | solution.py:127
  104.3 32.0 %all-gather = f32[16,6,16,128]{3,2,1,0:T(8,128)S(1)} all-gather(f32[2,6,16,128]{3,2,1,0:T(8,128)S(1)} %pad_maximum_fusion), channel_id=2, replica_groups=mesh['ckpt'=4,'space'=8] {'space'}, dimensions={0}, use_global_device_ids=true | all-gather | bytes 884736 | tf_op jit(solution)/shard_map/all_gather | solution.py:126
  139.8 3.3 scatter.40
  143.1 3.2 scatter.41
  146.4 19.9 %scatter.44 = f32[6,18,18,130]{3,2,0,1:T(8,128)S(1)} dynamic-update-slice(f32[6,18,18,130]{3,2,0,1:T(8,128)S(1)} %scatter.41, f32[6,16,1,128]{3,2,0,1:T(1,128)S(1)} %copy.1412, s32[]{:T(128)} %constant.830.clone.1, s32[]{:T(128)} %constant.831.clone.1, s32[]{:T(128)} %constant.834.clone.1, s32[]{:T(128)} %constant.831.clone.1) | dynamic-update-slice | bytes 98308 | tf_op jit(solution)/shard_map/scatter | solution.py:32
  166.3 19.9 %scatter.45 = f32[6,18,18,130]{3,2,0,1:T(8,128)S(1)} dynamic-update-slice(f32[6,18,18,130]{3,2,0,1:T(8,128)S(1)} %scatter.44, f32[6,16,1,128]{3,2,0,1:T(1,128)S(1)} %copy.1414, s32[]{:T(128)} %constant.830.clone.1, s32[]{:T(128)} %constant.831.clone.1, s32[]{:T(128)} %constant.830.clone.1, s32[]{:T(128)} %constant.831.clone.1) | dynamic-update-slice | bytes 98308 | tf_op jit(solution)/shard_map/scatter | solution.py:32
  186.2 23.4 %scatter.46 = f32[6,18,18,130]{3,2,0,1:T(8,128)S(1)} dynamic-update-slice(f32[6,18,18,130]{3,2,0,1:T(8,128)S(1)} %scatter.45, f32[6,16,16,1]{3,2,0,1:T(8,128)} %copy.1417, s32[]{:T(128)} %constant.830.clone.1, s32[]{:T(128)} %constant.831.clone.1, s32[]{:T(128)} %constant.831.clone.1, s32[]{:T(128)} %constant.835.clone.1) | dynamic-update-slice | bytes 12292 | tf_op jit(solution)/shard_map/scatter | solution.py:34
  209.7 12.1 %scatter.49 = f32[6,18,18,130]{3,2,0,1:T(8,128)S(1)} dynamic-update-slice(f32[6,18,18,130]{3,2,0,1:T(8,128)S(1)} %scatter.46, f32[6,16,16,1]{3,2,0,1:T(8,128)S(1)} %copy-done.20, s32[]{:T(128)} %constant.830.clone.1, s32[]{:T(128)} %constant.831.clone.1, s32[]{:T(128)} %constant.831.clone.1, s32[]{:T(128)} %constant.830.clone.1) | dynamic-update-slice | bytes 12292 | tf_op jit(solution)/shard_map/scatter | solution.py:34
  227.7 2.8 fusion.6
  238.4 32.4 %all-gather.5 = f32[16,6,16,16]{3,2,1,0:T(8,128)S(1)} all-gather(f32[2,6,16,16]{3,2,1,0:T(8,128)S(1)} %pad_maximum_fusion.5), channel_id=7, replica_groups=mesh['ckpt'=4,'space'=8] {'space'}, dimensions={0}, use_global_device_ids=true | all-gather | bytes 110592 | tf_op jit(solution)/shard_map/all_gather | solution.py:128
  275.8 2.3 copy.1444
  283.8 32.1 %all-gather.4 = f32[16,6,16,128]{3,2,1,0:T(8,128)S(1)} all-gather(f32[2,6,16,128]{3,2,1,0:T(8,128)S(1)} %pad_maximum_fusion.4), channel_id=6, replica_groups=mesh['ckpt'=4,'space'=8] {'space'}, dimensions={0}, use_global_device_ids=true | all-gather | bytes 884736 | tf_op jit(solution)/shard_map/all_gather | solution.py:127
  325.3 31.6 %all-gather.3 = f32[16,6,16,128]{3,2,1,0:T(8,128)S(1)} all-gather(f32[2,6,16,128]{3,2,1,0:T(8,128)S(1)} %pad_maximum_fusion.3), channel_id=5, replica_groups=mesh['ckpt'=4,'space'=8] {'space'}, dimensions={0}, use_global_device_ids=true | all-gather | bytes 884736 | tf_op jit(solution)/shard_map/all_gather | solution.py:126
  364.1 3.3 pad.200
  367.4 3.7 scatter.50
  371.2 3.7 scatter.51
  374.9 18.6 %scatter.54 = f32[6,18,18,130]{3,2,0,1:T(8,128)} dynamic-update-slice(f32[6,18,18,130]{3,2,0,1:T(8,128)} %scatter.51, f32[6,16,1,128]{3,2,0,1:T(1,128)S(1)} %copy-done.43, s32[]{:T(128)} %constant.830.clone.1, s32[]{:T(128)} %constant.831.clone.1, s32[]{:T(128)} %constant.834.clone.1, s32[]{:T(128)} %constant.831.clone.1) | dynamic-update-slice | bytes 98308 | tf_op jit(solution)/shard_map/scatter | solution.py:32
  393.4 18.6 %scatter.55 = f32[6,18,18,130]{3,2,0,1:T(8,128)} dynamic-update-slice(f32[6,18,18,130]{3,2,0,1:T(8,128)} %scatter.54, f32[6,16,1,128]{3,2,0,1:T(1,128)S(1)} %copy-done.42, s32[]{:T(128)} %constant.830.clone.1, s32[]{:T(128)} %constant.831.clone.1, s32[]{:T(128)} %constant.830.clone.1, s32[]{:T(128)} %constant.831.clone.1) | dynamic-update-slice | bytes 98308 | tf_op jit(solution)/shard_map/scatter | solution.py:32
  412.0 18.2 %scatter.56 = f32[6,18,18,130]{3,2,0,1:T(8,128)} dynamic-update-slice(f32[6,18,18,130]{3,2,0,1:T(8,128)} %scatter.55, f32[6,16,16,1]{3,2,0,1:T(8,128)} %copy.1442, s32[]{:T(128)} %constant.830.clone.1, s32[]{:T(128)} %constant.831.clone.1, s32[]{:T(128)} %constant.831.clone.1, s32[]{:T(128)} %constant.835.clone.1) | dynamic-update-slice | bytes 12292 | tf_op jit(solution)/shard_map/scatter | solution.py:34
  430.2 5.9 scatter.59
  436.1 2.9 add_multiply_fusion
  439.0 2.8 fusion
  443.5 2.8 fusion.4
  461.4 2.4 copy.1468
  463.7 2.4 copy.1469
  466.9 32.0 %all-gather.8 = f32[16,6,16,16]{3,2,1,0:T(8,128)S(1)} all-gather(f32[2,6,16,16]{3,2,1,0:T(8,128)S(1)} %pad_maximum_fusion.8), channel_id=10, replica_groups=mesh['ckpt'=4,'space'=8] {'space'}, dimensions={0}, use_global_device_ids=true | all-gather | bytes 110592 | tf_op jit(solution)/shard_map/all_gather | solution.py:150
  506.2 2.3 copy.1473
  514.3 2.3 copy.1471
  517.8 32.0 %all-gather.7 = f32[16,6,16,128]{3,2,1,0:T(8,128)S(1)} all-gather(f32[2,6,16,128]{3,2,1,0:T(8,128)S(1)} %pad_maximum_fusion.7), channel_id=9, replica_groups=mesh['ckpt'=4,'space'=8] {'space'}, dimensions={0}, use_global_device_ids=true | all-gather | bytes 884736 | tf_op jit(solution)/shard_map/all_gather | solution.py:149
  562.2 31.6 %all-gather.6 = f32[16,6,16,128]{3,2,1,0:T(8,128)S(1)} all-gather(f32[2,6,16,128]{3,2,1,0:T(8,128)S(1)} %pad_maximum_fusion.6), channel_id=8, replica_groups=mesh['ckpt'=4,'space'=8] {'space'}, dimensions={0}, use_global_device_ids=true | all-gather | bytes 884736 | tf_op jit(solution)/shard_map/all_gather | solution.py:148
  603.3 4.1 pad_add_fusion.3
  612.4 2.7 scatter-add.44
  616.2 2.7 scatter-add.45
  618.9 2.6 slice_add_fusion.5
  621.5 9.4 %scatter-add.46 = f32[6,16,16,128]{3,2,0,1:T(8,128)} dynamic-update-slice(f32[6,16,16,128]{3,2,0,1:T(8,128)} %scatter-add.45, f32[6,16,16,1]{3,2,0,1:T(8,128)} %slice_add_fusion.5, s32[]{:T(128)} %constant.830.clone.1, s32[]{:T(128)} %constant.830.clone.1, s32[]{:T(128)} %constant.830.clone.1, s32[]{:T(128)} %constant.841.clone.1) | dynamic-update-slice | bytes 12292 | tf_op jit(solution)/shard_map/scatter-add | solution.py:55
  633.0 3.6 scatter-add.49
  646.8 2.8 fusion.2
  653.1 32.2 %all-gather.11 = f32[16,6,16,16]{3,2,1,0:T(8,128)S(1)} all-gather(f32[2,6,16,16]{3,2,1,0:T(8,128)S(1)} %pad_maximum_fusion.11), channel_id=13, replica_groups=mesh['ckpt'=4,'space'=8] {'space'}, dimensions={0}, use_global_device_ids=true | all-gather | bytes 110592 | tf_op jit(solution)/shard_map/all_gather | solution.py:150
  691.8 2.3 copy.1509
  702.3 31.6 %all-gather.10 = f32[16,6,16,128]{3,2,1,0:T(8,128)S(1)} all-gather(f32[2,6,16,128]{3,2,1,0:T(8,128)S(1)} %pad_maximum_fusion.10), channel_id=12, replica_groups=mesh['ckpt'=4,'space'=8] {'space'}, dimensions={0}, use_global_device_ids=true | all-gather | bytes 884736 | tf_op jit(solution)/shard_map/all_gather | solution.py:149
  747.1 31.6 %all-gather.9 = f32[16,6,16,128]{3,2,1,0:T(8,128)S(1)} all-gather(f32[2,6,16,128]{3,2,1,0:T(8,128)S(1)} %pad_maximum_fusion.9), channel_id=11, replica_groups=mesh['ckpt'=4,'space'=8] {'space'}, dimensions={0}, use_global_device_ids=true | all-gather | bytes 884736 | tf_op jit(solution)/shard_map/all_gather | solution.py:148
  788.1 3.3 pad_add_fusion
  794.4 2.7 scatter-add.54
  798.2 2.7 scatter-add.55
  802.7 12.2 %scatter-add.56 = f32[6,16,16,128]{3,2,0,1:T(8,128)S(1)} dynamic-update-slice(f32[6,16,16,128]{3,2,0,1:T(8,128)S(1)} %copy-done.14, f32[6,16,16,1]{3,2,0,1:T(8,128)S(1)} %slice_add_fusion.3, s32[]{:T(128)} %constant.830.clone.1, s32[]{:T(128)} %constant.830.clone.1, s32[]{:T(128)} %constant.830.clone.1, s32[]{:T(128)} %constant.841.clone.1) | dynamic-update-slice | bytes 12292 | tf_op jit(solution)/shard_map/scatter-add | solution.py:55
  816.3 5.8 scatter-add.59
  (350 shorter events, 179.7 us)
Async XLA Ops:
  9.8 45.5 %copy-start.52 = (f32[8]{0:T(128)}, f32[8]{0:T(128)S(1)}, u32[]{:S(2)}) copy-start(f32[8]{0:T(128)S(1)} %compare_convert_fusion) | copy-start | bytes 100
  10.5 44.8 %copy-start.54 = (f32[8]{0:T(128)}, f32[8]{0:T(128)S(1)}, u32[]{:S(2)}) copy-start(f32[8]{0:T(128)S(1)} %compare_convert_fusion.1) | copy-start | bytes 100
  103.6 35.5 %copy-start.56 = (f32[8]{0:T(128)}, f32[8]{0:T(128)S(1)}, u32[]{:S(2)}) copy-start(f32[8]{0:T(128)S(1)} %compare_convert_fusion.4) | copy-start | bytes 100
  104.3 34.9 %copy-start.59 = (f32[8]{0:T(128)}, f32[8]{0:T(128)S(1)}, u32[]{:S(2)}) copy-start(f32[8]{0:T(128)S(1)} %compare_convert_fusion.5) | copy-start | bytes 100
  139.8 69.8 %copy-start.20 = (f32[6,16,16,1]{3,2,0,1:T(8,128)S(1)}, f32[6,16,16,1]{3,2,0,1:T(8,128)}, u32[]{:S(2)}) copy-start(f32[6,16,16,1]{3,2,0,1:T(8,128)} %copy.1418) | copy-start | bytes 18436
  222.5 1.3 copy-start.17
  225.2 1.2 copy-start.16
  227.7 2.8 copy-start.15
  230.5 1.3 copy-start.18
  230.6 1.3 copy-start.48
  230.6 1.3 copy-start.23
  231.9 1.6 copy-start.26
  233.4 1.4 copy-start.12
  364.1 10.8 %copy-start.43 = (f32[6,16,1,128]{3,2,0,1:T(1,128)S(1)}, f32[6,16,1,128]{3,2,0,1:T(1,128)}, u32[]{:S(2)}) copy-start(f32[6,16,1,128]{3,2,0,1:T(1,128)} %copy.1436) | copy-start | bytes 147460
  364.1 29.4 %copy-start.42 = (f32[6,16,1,128]{3,2,0,1:T(1,128)S(1)}, f32[6,16,1,128]{3,2,0,1:T(1,128)}, u32[]{:S(2)}) copy-start(f32[6,16,1,128]{3,2,0,1:T(1,128)} %copy.1438) | copy-start | bytes 147460
  438.9 2.9 copy-start
  439.0 2.9 copy-start.11
  447.9 12.1 %copy-start.1 = (f32[6,16,16,130]{3,2,0,1:T(8,128)}, f32[6,16,16,130]{3,2,0,1:T(8,128)S(1)}, u32[]{:S(2)}) copy-start(f32[6,16,16,130]{3,2,0,1:T(8,128)S(1)} %pad_add_fusion.6) | copy-start | bytes 2396164
  453.0 6.9 copy-start.5
  457.2 1.1 copy-start.24
  459.9 1.4 copy-start.9
  516.6 33.3 %copy-start.50 = (f32[8]{0:T(128)S(1)}, f32[8]{0:T(128)}, u32[]{:S(2)}) copy-start(f32[8]{0:T(128)} %copy-done.49) | copy-start | bytes 100
  562.1 31.7 %copy-start.57 = (f32[8]{0:T(128)S(1)}, f32[8]{0:T(128)}, u32[]{:S(2)}) copy-start(f32[8]{0:T(128)} %copy-done.56) | copy-start | bytes 100
  562.1 31.7 %copy-start.60 = (f32[8]{0:T(128)S(1)}, f32[8]{0:T(128)}, u32[]{:S(2)}) copy-start(f32[8]{0:T(128)} %copy-done.59) | copy-start | bytes 100
  603.3 5.4 copy-start.6
  603.3 5.4 copy-start.10
  603.3 5.4 copy-start.33
  603.3 5.4 copy-start.41
  607.4 1.7 copy-start.2
  609.1 2.2 copy-start.47
  618.9 12.0 %copy-start.22 = (f32[6,16,16,1]{3,2,0,1:T(8,128)S(1)}, f32[6,16,16,1]{3,2,0,1:T(8,128)}, u32[]{:S(2)}) copy-start(f32[6,16,16,1]{3,2,0,1:T(8,128)} %copy.1473) | copy-start | bytes 18436
  638.7 2.3 copy-start.31
  641.4 10.9 %copy-start.7 = (f32[6,18,16,128]{3,2,0,1:T(8,128)}, f32[6,18,16,128]{3,2,0,1:T(8,128)S(1)}, u32[]{:S(2)}) copy-start(f32[6,18,16,128]{3,2,0,1:T(8,128)S(1)} %pad_add_fusion.12) | copy-start | bytes 2654212
  642.2 2.2 copy-start.29
  645.8 6.5 copy-start.3
  652.3 32.9 %copy-start.53 = (f32[8]{0:T(128)S(1)}, f32[8]{0:T(128)}, u32[]{:S(2)}) copy-start(f32[8]{0:T(128)} %copy-done.52) | copy-start | bytes 100
  652.4 32.9 %copy-start.55 = (f32[8]{0:T(128)S(1)}, f32[8]{0:T(128)}, u32[]{:S(2)}) copy-start(f32[8]{0:T(128)} %copy-done.54) | copy-start | bytes 100
  685.3 16.9 %copy-start.4 = (f32[6,16,18,128]{3,2,0,1:T(8,128)S(1)}, f32[6,16,18,128]{3,2,0,1:T(8,128)}, u32[]{:S(2)}) copy-start(f32[6,16,18,128]{3,2,0,1:T(8,128)} %copy-done.3) | copy-start | bytes 2654212
  702.2 31.7 %copy-start.51 = (f32[8]{0:T(128)S(1)}, f32[8]{0:T(128)}, u32[]{:S(2)}) copy-start(f32[8]{0:T(128)} %copy-done.49) | copy-start | bytes 100
  746.2 32.5 %copy-start.58 = (f32[8]{0:T(128)S(1)}, f32[8]{0:T(128)}, u32[]{:S(2)}) copy-start(f32[8]{0:T(128)} %copy-done.56) | copy-start | bytes 100
  746.2 32.5 %copy-start.61 = (f32[8]{0:T(128)S(1)}, f32[8]{0:T(128)}, u32[]{:S(2)}) copy-start(f32[8]{0:T(128)} %copy-done.59) | copy-start | bytes 100
  791.4 1.2 copy-start.8
  791.4 1.2 copy-start.32
  791.5 1.2 copy-start.40
  792.6 1.7 copy-start.46
  800.9 1.8 copy-start.14
  800.9 14.0 %copy-start.21 = (f32[6,16,16,1]{3,2,0,1:T(8,128)S(1)}, f32[6,16,16,1]{3,2,0,1:T(8,128)}, u32[]{:S(2)}) copy-start(f32[6,16,16,1]{3,2,0,1:T(8,128)} %copy.1509) | copy-start | bytes 18436
  816.2 6.8 copy-start.25
  (14 other events, 10.7 us)
where the time goes:
time: 837 us; the launch traced here: 824 us
  blocking collectives  393 us (47%)
  local copies, waits for them, and re-layouts  284 us (34%)
  other arithmetic  108 us (13%)
  matrix products  20.9 us (2%)
  between operations  17.3 us (2%)
    scatter x4, local copies, waits for them, and re-layouts, pad_with(): padded = padded.at[:, 1:-1, location, 1:-1].set(ghosts[side])  76.9 us
    all_gather x2, blocking collectives, fetch(): lax.all_gather(z_faces, 'space', axis=0, tiled=True)  64.7 us
    all_gather x2, blocking collectives, on_device(): lax.all_gather(z_ghosts, 'space', axis=0, tiled=True)  64.2 us
    all_gather x2, blocking collectives, fetch(): lax.all_gather(y_faces, 'space', axis=0, tiled=True)  64.1 us
    all_gather x2, blocking collectives, on_device(): lax.all_gather(y_ghosts, 'space', axis=0, tiled=True)  63.7 us
    all_gather x2, blocking collectives, fetch(): lax.all_gather(x_faces, 'space', axis=0, tiled=True)  63.6 us
    all_gather x2, blocking collectives, on_device(): lax.all_gather(x_ghosts, 'space', axis=0, tiled=True)  63.2 us
    scatter x4, local copies, waits for them, and re-layouts, pad_with(): padded = padded.at[:, 1:-1, 1:-1, location].set(ghosts[side])  59.6 us

commit v1 on v0

v1 whole, which is shorter than its diff:
```python
import functools

import jax
import jax.numpy as jnp
from jax import lax
from jax.experimental import pallas as pl
from jax.experimental.pallas import tpu as pltpu
from jax.sharding import PartitionSpec as P

STEPS = 2
time_step = 0.05
damping = 0.015

PAD = 8
VMEM = pl.BlockSpec(memory_space=pltpu.VMEM)
SMEM = pl.BlockSpec(memory_space=pltpu.SMEM)
VMEM_LIMIT = 32 * 1024 * 1024


class Geometry:
    def __init__(self, nvars, cx, cy, cz, count):
        self.v, self.x, self.y, self.z, self.n = nvars, cx, cy, cz, count
        self.rows = [nvars * cy] * 2 + [nvars * cx] * 2 + [cy] * 2
        self.runs = [-(-rows // count) for rows in self.rows]
        self.starts = [sum(self.runs[:side]) for side in range(6)]
        self.slot = -(-sum(self.runs) // 8) * 8
        self.face_rows = -(-max(run * count for run in self.runs) // 8) * 8
        self.block = (nvars, cx, cy, cz)
        self.padded = (nvars, cx + 2, cy + 2 * PAD, cz)
        self.buffer = (count, self.slot, cz)
        self.faces = (6, self.face_rows, cz)


def pack(geo, source, faces, buffer):
    v, x, y, z = geo.block
    lane = lax.broadcasted_iota(jnp.int32, (y, z), 1)
    faces[0, : v * y] = source[:, x - 1].reshape(v * y, z)
    faces[1, : v * y] = source[:, 0].reshape(v * y, z)
    for var in range(v):
        faces[2, var * x : (var + 1) * x] = source[var, :, y - 1, :]
        faces[3, var * x : (var + 1) * x] = source[var, :, 0, :]
    high = jnp.zeros((y, z), jnp.float32)
    low = jnp.zeros((y, z), jnp.float32)
    for var in range(v):
        for plane in range(x):
            place = var * x + plane
            tile = source[var, plane]
            here = lane == place
            high = jnp.where(here, pltpu.roll(tile, (place + 1) % z, 1), high)
            low = jnp.where(here, pltpu.roll(tile, place, 1) if place else tile, low)
    faces[4, :y] = high
    faces[5, :y] = low
    for side in range(6):
        run, start = geo.runs[side], geo.starts[side]
        for slot in range(geo.n):
            buffer[slot, start : start + run] = faces[side, slot * run : (slot + 1) * run]


def own_codes(geo, place, owner, orientation):
    block = jnp.int32(0)
    for index in range(geo.n):
        block = jnp.where(owner[index] == place[0], index, block)
    return [orientation[block * 6 + side] for side in range(6)]


def flip_rows(values, flag, length):
    rows, z = values.shape
    grouped = values.reshape(rows // length, length // 8, 8, z)
    index = lax.broadcasted_iota(jnp.int32, (8, z), 0)
    index = jnp.where(flag == 1, 7 - index, index)
    tiles = length // 8
    out = []
    for group in range(rows // length):
        for tile in range(tiles):
            picked = jnp.where(flag == 1, grouped[group, tiles - 1 - tile], grouped[group, tile])
            out.append(jnp.take_along_axis(picked, index, axis=0))
    return jnp.stack(out).reshape(rows, z)


def flip_lanes(values, flag, length):
    rows, z = values.shape
    lane = lax.broadcasted_iota(jnp.int32, (8, z), 1)
    within = lax.rem(lane, length)
    index = jnp.where(flag == 1, lane + (length - 1) - 2 * within, lane)
    index = jnp.minimum(index, z - 1)
    tiles = values.reshape(rows // 8, 8, z)
    return jnp.stack(
        [jnp.take_along_axis(tiles[tile], index, axis=1) for tile in range(rows // 8)]
    ).reshape(rows, z)


def unpack(geo, codes, buffer, faces, padded, zfaces):
    v, x, y, z = geo.block
    for side in range(6):
        run, start = geo.runs[side], geo.starts[side]
        for slot in range(geo.n):
            faces[side, slot * run : (slot + 1) * run] = buffer[slot, start : start + run]
    for side in range(6):
        first, second = codes[side] & 1, (codes[side] >> 1) & 1
        layer = faces[side, : geo.rows[side]]
        if side < 2:
            layer = flip_lanes(flip_rows(layer, first, y), second, z)
            where = x + 1 if side == 0 else 0
            padded[:, where, PAD : PAD + y, :] = layer.reshape(v, y, z)
        elif side < 4:
            layer = flip_lanes(flip_rows(layer, first, x), second, z)
            where = PAD + y if side == 2 else PAD - 1
            for var in range(v):
                padded[var, 1 : x + 1, where, :] = layer[var * x : (var + 1) * x]
        else:
            layer = flip_lanes(flip_rows(layer, second, y), first, x)
            zfaces[side - 4] = layer


def around(geo, padded, zfaces, plane):
    v, x, y, z = geo.block
    lane = lax.broadcasted_iota(jnp.int32, (y, z), 1)
    cells, low, high = [], [[], [], []], [[], [], []]
    for var in range(v):
        mid = padded[var, plane + 1, PAD : PAD + y]
        cells.append(mid)
        low[0].append(padded[var, plane, PAD : PAD + y])
        high[0].append(padded[var, plane + 2, PAD : PAD + y])
        low[1].append(padded[var, plane + 1, PAD - 1 : PAD - 1 + y])
        high[1].append(padded[var, plane + 1, PAD + 1 : PAD + 1 + y])
        place = var * x + plane
        ghost_high = pltpu.roll(zfaces[0], lax.rem(2 * z - 1 - place, z), 1)
        ghost_low = pltpu.roll(zfaces[1], lax.rem(z - place, z), 1)
        low[2].append(jnp.where(lane == 0, ghost_low, pltpu.roll(mid, 1, 1)))
        high[2].append(jnp.where(lane == z - 1, ghost_high, pltpu.roll(mid, z - 1, 1)))
    return cells, low, high


def flux_entry(geo, mats, direction, row, column):
    return mats[(direction * geo.v + row) * geo.v + column]


def step_plane(geo, mats, cells, low, high, rate):
    v = geo.v
    total = [None] * v
    for direction in range(3):
        lows, highs = low[direction], high[direction]
        mean_low = 0.5 * (lows[0] + cells[0])
        mean_high = 0.5 * (cells[0] + highs[0])
        square_low = 1.0 + mean_low * mean_low
        square_high = 1.0 + mean_high * mean_high
        spread_low = square_low * lax.rsqrt(square_low)
        spread_high = square_high * lax.rsqrt(square_high)
        slopes = [highs[var] - lows[var] for var in range(v)]
        for var in range(v):
            term = spread_low * (cells[var] - lows[var]) - spread_high * (highs[var] - cells[var])
            for column in range(v):
                term = term + flux_entry(geo, mats, direction, var, column) * slopes[column]
            total[var] = term if total[var] is None else total[var] + term
    scale = (0.5 * time_step) * rate
    return [cells[var] - scale * total[var] - damping * jnp.tanh(cells[var]) for var in range(v)]


def adjoint_plane(geo, mats, cells, low, high, grads, weight, weight_low, weight_high):
    v = geo.v
    total = [None] * v
    extra = None
    for direction in range(3):
        spreads, steps = [], []
        for lower, upper, lower_weight, upper_weight in (
            (low[direction], cells, weight_low[direction], weight),
            (cells, high[direction], weight, weight_high[direction]),
        ):
            mean = 0.5 * (lower[0] + upper[0])
            square = 1.0 + mean * mean
            inverse = lax.rsqrt(square)
            jump = [lower_weight[var] - upper_weight[var] for var in range(v)]
            product = jump[0] * (upper[0] - lower[0])
            for var in range(1, v):
                product = product + jump[var] * (upper[var] - lower[var])
            product = product * (mean * inverse)
            extra = product if extra is None else extra + product
            spreads.append(square * inverse)
            steps.append(jump)
        slopes = [steps[0][var] + steps[1][var] for var in range(v)]
        for var in range(v):
            term = spreads[1] * steps[1][var] - spreads[0] * steps[0][var]
            for row in range(v):
                term = term + flux_entry(geo, mats, direction, row, var) * slopes[row]
            total[var] = term if total[var] is None else total[var] + term
    total[0] = total[0] - 0.5 * extra
    out = []
    for var in range(v):
        bend = jnp.tanh(cells[var])
        slope = (1.0 - damping) + damping * (bend * bend)
        out.append(grads[var] * slope - (0.5 * time_step) * total[var])
    return out


def load_gathered(geo, gathered, padded):
    parts, depth = gathered.shape[0], gathered.shape[2]
    for part in range(parts):
        padded[:, 1 + part * depth : 1 + (part + 1) * depth, PAD : PAD + geo.y, :] = gathered[part]


def pack_state_kernel(geo, gathered, state, buffer, faces):
    parts, depth = gathered.shape[0], gathered.shape[2]
    for part in range(parts):
        state[:, part * depth : (part + 1) * depth] = gathered[part]
    pack(geo, state, faces, buffer)


def pack_weight_kernel(geo, grads, rate, buffer, weight, faces):
    def body(plane, carry):
        for var in range(geo.v):
            weight[var, plane] = rate[plane] * grads[var, plane]
        return carry

    lax.fori_loop(0, geo.x, body, 0)
    pack(geo, weight, faces, buffer)


def route_kernel(geo, owner, neighbours, arrived, leaving):
    for block in range(geo.n):
        target = owner[block]
        for side in range(6):
            source = owner[neighbours[block * 6 + side]]
            run, start, far = geo.runs[side], geo.starts[side], geo.starts[side ^ 1]
            leaving[target, start : start + run] = arrived[source, far : far + run]


def fill(geo, place, owner, orientation, block, buffer, faces, padded, zfaces):
    v, x, y, z = geo.block
    padded[:, 1 : x + 1, PAD : PAD + y, :] = block[...]
    unpack(geo, own_codes(geo, place, owner, orientation), buffer, faces, padded, zfaces)


def step_kernel(geo, packed, place, owner, orientation, mats, block, buffer, rate, *rest):
    if packed:
        result, sent, faces, padded, zfaces = rest
    else:
        result, faces, padded, zfaces = rest
    fill(geo, place, owner, orientation, block, buffer, faces, padded, zfaces)

    def body(plane, carry):
        cells, low, high = around(geo, padded, zfaces, plane)
        for var, value in enumerate(step_plane(geo, mats, cells, low, high, rate[plane])):
            result[var, plane] = value
        return carry

    lax.fori_loop(0, geo.x, body, 0)
    if packed:
        pack(geo, result, faces, sent)


def adjoint_kernel(geo, packed, place, owner, orientation, mats, block, buffer, grads, weight_buffer, rate, *rest):
    if packed:
        result, sent, faces, padded, zfaces, weights, weight_zfaces, weight_block = rest
    else:
        result, faces, padded, zfaces, weights, weight_zfaces = rest
    v, x, y, z = geo.block
    fill(geo, place, owner, orientation, block, buffer, faces, padded, zfaces)
    codes = own_codes(geo, place, owner, orientation)
    unpack(geo, codes, weight_buffer, faces, weights, weight_zfaces)

    def scale(plane, carry):
        for var in range(v):
            weights[var, plane + 1, PAD : PAD + y] = rate[plane] * grads[var, plane]
        return carry

    lax.fori_loop(0, x, scale, 0)

    def body(plane, carry):
        cells, low, high = around(geo, padded, zfaces, plane)
        weight, weight_low, weight_high = around(geo, weights, weight_zfaces, plane)
        here = [grads[var, plane] for var in range(v)]
        values = adjoint_plane(geo, mats, cells, low, high, here, weight, weight_low, weight_high)
        for var, value in enumerate(values):
            result[var, plane] = value
            if packed:
                weight_block[var, plane] = rate[plane] * value
        return carry

    lax.fori_loop(0, x, body, 0)
    if packed:
        pack(geo, weight_block, faces, sent)


def call(kernel, specs, outs, scratch, flops):
    return pl.pallas_call(
        kernel,
        in_specs=specs,
        out_specs=[VMEM] * len(outs),
        out_shape=[jax.ShapeDtypeStruct(shape, jnp.float32) for shape in outs],
        scratch_shapes=[pltpu.VMEM(shape, jnp.float32) for shape in scratch],
        compiler_params=pltpu.CompilerParams(vmem_limit_bytes=VMEM_LIMIT),
        cost_estimate=pl.CostEstimate(flops=flops, bytes_accessed=3 << 20, transcendentals=0),
    )


def on_device(count, checkpoint, seeds, cell_rate, flux_mats, owner, neighbours, orientation):
    nvars, cx, cy, cz = seeds.shape[2:]
    geo = Geometry(nvars, cx, cy, cz, count)
    rate = cell_rate[0]
    grads = seeds[0, 0]
    place = lax.axis_index("space").astype(jnp.int32).reshape(1)
    mats = flux_mats.reshape(-1)
    neighbours = neighbours.reshape(-1)
    orientation = orientation.reshape(-1)
    zfaces = (2, cy, cz)
    work = nvars * nvars * 3 * 4 * cx * cy * cz

    def exchange(buffer):
        arrived = lax.all_to_all(buffer, "space", 0, 0, tiled=True)
        leaving = call(
            functools.partial(route_kernel, geo), [SMEM, SMEM, VMEM], [geo.buffer], [], work // 16
        )(owner, neighbours, arrived)[0]
        return lax.all_to_all(leaving, "space", 0, 0, tiled=True)

    gathered = lax.all_gather(checkpoint, "ckpt", axis=0, tiled=True)
    (sent,) = call(
        functools.partial(pack_weight_kernel, geo), [VMEM, VMEM], [geo.buffer], [geo.block, geo.faces], work // 8
    )(grads, rate)
    weight_ghosts = exchange(sent)
    state, sent = call(
        functools.partial(pack_state_kernel, geo), [VMEM], [geo.block, geo.buffer], [geo.faces], work // 8
    )(gathered)
    ghosts = [exchange(sent)]
    states = [state]
    fixed = (place, owner, orientation, mats)
    step_specs = [SMEM] * 4 + [VMEM] * 3
    next_state, sent = call(
        functools.partial(step_kernel, geo, True),
        step_specs,
        [geo.block, geo.buffer],
        [geo.faces, geo.padded, zfaces],
        work,
    )(*fixed, states[0], ghosts[0], rate)
    states.append(next_state)
    ghosts.append(exchange(sent))
    adjoint_specs = [SMEM] * 4 + [VMEM] * 5
    pads = [geo.faces, geo.padded, zfaces, geo.padded, zfaces]
    grads_now, sent = call(
        functools.partial(adjoint_kernel, geo, True),
        adjoint_specs,
        [geo.block, geo.buffer],
        pads + [geo.block],
        2 * work,
    )(*fixed, states[1], ghosts[1], grads, weight_ghosts, rate)
    weight_ghosts = exchange(sent)
    (final,) = call(
        functools.partial(step_kernel, geo, False),
        step_specs,
        [geo.block],
        [geo.faces, geo.padded, zfaces],
        work,
    )(*fixed, states[1], ghosts[1], rate)
    (adjoint,) = call(
        functools.partial(adjoint_kernel, geo, False),
        adjoint_specs,
        [geo.block],
        pads,
        2 * work,
    )(*fixed, states[0], ghosts[0], grads_now, weight_ghosts, rate)
    return (adjoint[None, None], final[None])


def solution(mesh):
    return jax.shard_map(
        functools.partial(on_device, mesh.shape["space"]),
        mesh=mesh,
        in_specs=(
            P("space", None, "ckpt", None, None),
            P("ckpt", "space", None, None, None, None),
            P("space", None, None, None),
            P(),
            P(),
            P(),
            P(),
        ),
        out_specs=(P("ckpt", "space", None, None, None, None), P("space", None, None, None, None)),
        check_vma=False,
    )
```

time: 837 us -> 125 us (0.15); the launches traced: 824 us -> 124 us
  blocking collectives: 393 us -> 32.1 us
  local copies, waits for them, and re-layouts: 284 us -> 4.32 us
  other arithmetic: 108 us -> 0 us
  waiting for transfers between devices: 0 us -> 34.6 us
  Pallas kernels: 0 us -> 28.6 us
  starting transfers between devices: 0 us -> 23.6 us
  matrix products: 20.9 us -> 0 us
  between operations: 17.3 us -> 0.76 us
    all_gather x13 -> x1, blocking collectives: 393 us -> 10.3 us  [on_device(): gathered = lax.all_gather(checkpoint, 'ckpt', axis=0, tiled=True)]
    scatter x12 -> x0, local copies, waits for them, and re-layouts: 151 us -> none  [the longest x4 76.9 us: pad_with(): padded = padded.at[:, 1:-1, location, 1:-1].set(ghosts[side])]
    rev x48 -> x0, local copies, waits for them, and re-layouts: 42.7 us -> none  [the longest x24 21.9 us: reorient(): return jnp.where(flips // 2 % 2 == 1, jnp.flip(face, -1), face)]
    scatter-add x8 -> x0, local copies, waits for them, and re-layouts: 41.9 us -> none  [the longest x4 31 us: add_layer(): return field.at[:, :, :, location].add(layer)]
    all_to_all x0 -> x6, waiting for transfers between devices: none -> 34.6 us  [the longest x3 17.7 us: exchange(): arrived = lax.all_to_all(buffer, 'space', 0, 0, tiled=True)]
    pallas_call x0 -> x10, Pallas kernels: none -> 28.6 us  [the longest x1 6.42 us: on_device(): call(functools.partial(adjoint_kernel, geo, False), adjoint_specs, [geo.b...]
    all_to_all x0 -> x6, starting transfers between devices: none -> 23.6 us  [the longest x3 13.3 us: exchange(): arrived = lax.all_to_all(buffer, 'space', 0, 0, tiled=True)]
    select_n x22 -> x0, other arithmetic: 22 us -> none  [reorient(): face = jnp.where(flips % 2 == 1, jnp.flip(face, -2), face)]
  transfers between devices with their start and end apart: 0 -> 6, of which waited for: 0 -> 6; matrix products, arithmetic and copies ran while one was open for 0% -> 0% of each run, Pallas kernels for 0% -> 10%
where the time goes in v1:
time: 125 us; the launch traced here: 124 us
  waiting for transfers between devices  34.6 us (28%)
  blocking collectives  32.1 us (26%)
  Pallas kernels  28.6 us (23%)
  starting transfers between devices  23.6 us (19%)
  local copies, waits for them, and re-layouts  4.32 us (3%)
    all_to_all x3, waiting for transfers between devices, exchange(): arrived = lax.all_to_all(buffer, 'space', 0, 0, tiled=True)  17.7 us
    all_to_all x3, waiting for transfers between devices, exchange(): return lax.all_to_all(leaving, 'space', 0, 0, tiled=True)  16.9 us
    all_to_all x3, starting transfers between devices, exchange(): arrived = lax.all_to_all(buffer, 'space', 0, 0, tiled=True)  13.3 us
    all_to_all x1, blocking collectives, exchange(): return lax.all_to_all(leaving, 'space', 0, 0, tiled=True)  11.3 us
    all_to_all x1, blocking collectives, exchange(): arrived = lax.all_to_all(buffer, 'space', 0, 0, tiled=True)  10.5 us
    all_to_all x3, starting transfers between devices, exchange(): return lax.all_to_all(leaving, 'space', 0, 0, tiled=True)  10.3 us
    all_gather x1, blocking collectives, on_device(): gathered = lax.all_gather(checkpoint, 'ckpt', axis=0, tiled=True)  10.3 us
    pallas_call x1, Pallas kernels, on_device(): call(functools.partial(adjoint_kernel, geo, False), adjoint_specs, [geo.b...  6.42 us
  transfers between devices with their start and end apart: 6, of which 6 were waited for; matrix products, arithmetic and copies ran while one was open for 0% of the time, Pallas kernels for 10%

profile of v1, /device:TPU:0, one launch (start us, length us, event | category | flops | bytes accessed | tf_op | source)
XLA Modules:
  0.0 124.1 jit_solution(1899149218369025345)
XLA Ops:
  0.6 10.3 %all_gather.3.gathered = f32[4,6,4,16,128]{4,3,2,1,0:T(8,128)S(1)} all-gather(f32[1,6,4,16,128]{4,3,2,1,0:T(8,128)} %param.7), channel_id=1, replica_groups=mesh['ckpt'=4,'space'=8] {'ckpt'}, dimensions={0}, use_global_device_ids=true | all-gather | bytes 983040 | tf_op jit(solution)/shard_map/all_gather | solution.py:315
  10.9 0.0 copy-start.8
  10.9 0.0 copy-start.6
  10.9 1.2 shard_map.86
  12.1 0.0 copy-start.1
  12.1 6.0 %all-to-all-start = ((f32[8,56,128]{2,1,0:T(8,128)}), f32[8,56,128]{2,1,0:T(8,128)S(1)}, u32[]{:S(2)}, u32[]{:S(2)}) async-start(f32[8,56,128]{2,1,0:T(8,128)} %get-tuple-element.9), calls=%async_computation | async-start | bytes 458752 | tf_op jit(solution)/shard_map/all_to_all | solution.py:309
  18.1 0.0 copy-done.8
  18.1 0.1 reshape.19.neighbours
  18.2 8.9 %all-to-all-done.arrived = f32[8,56,128]{2,1,0:T(8,128)S(1)} async-done(((f32[8,56,128]{2,1,0:T(8,128)}), f32[8,56,128]{2,1,0:T(8,128)S(1)}, u32[]{:S(2)}, u32[]{:S(2)}) %all-to-all-start) | async-done | bytes 229408 | tf_op jit(solution)/shard_map/all_to_all | solution.py:309
  27.0 0.0 copy-done.6
  27.0 1.3 %shard_map.87 = f32[8,56,128]{2,1,0:T(8,128)} custom-call(s32[8]{0:T(128)S(1)} %copy-done.6, s32[48]{0:T(128)S(1)} %reshape.19.neighbours, f32[8,56,128]{2,1,0:T(8,128)S(1)} %all-to-all-done.arrived), custom_call_target="tpu_custom_call" | custom-call | flops 884736 | bytes 3145728 | tf_op jit(solution)/shard_map/pallas_call | solution.py:310
  28.3 0.0 copy-start
  28.3 3.5 %all-to-all-start.1 = ((f32[8,56,128]{2,1,0:T(8,128)}), f32[8,56,128]{2,1,0:T(8,128)S(1)}, u32[]{:S(2)}, u32[]{:S(2)}) async-start(f32[8,56,128]{2,1,0:T(8,128)} %shard_map.87), calls=%async_computation.1 | async-start | bytes 458752 | tf_op jit(solution)/shard_map/all_to_all | solution.py:313
  31.9 0.0 copy-done.1
  31.9 0.0 copy-done
  31.9 1.3 %shard_map.90 = f32[8,56,128]{2,1,0:T(8,128)} custom-call(f32[6,16,16,128]{3,2,1,0:T(8,128)S(1)} %bitcast.10, f32[16,16,128]{2,1,0:T(8,128)S(1)} %bitcast.5), custom_call_target="tpu_custom_call" | custom-call | flops 1769472 | bytes 3145728 | tf_op jit(solution)/shard_map/pallas_call | solution.py:316
  33.2 7.1 %all-to-all-done.1.buffer = f32[8,56,128]{2,1,0:T(8,128)S(1)} async-done(((f32[8,56,128]{2,1,0:T(8,128)}), f32[8,56,128]{2,1,0:T(8,128)S(1)}, u32[]{:S(2)}, u32[]{:S(2)}) %all-to-all-start.1) | async-done | bytes 229408 | tf_op jit(solution)/shard_map/all_to_all | solution.py:313
  40.3 0.0 copy-start.7
  40.3 3.5 %all-to-all-start.4 = ((f32[8,56,128]{2,1,0:T(8,128)}), f32[8,56,128]{2,1,0:T(8,128)S(1)}, u32[]{:S(2)}, u32[]{:S(2)}) async-start(f32[8,56,128]{2,1,0:T(8,128)} %shard_map.90), calls=%async_computation.4 | async-start | bytes 458752 | tf_op jit(solution)/shard_map/all_to_all | solution.py:309
  43.8 0.0 copy-start.9
  43.8 0.7 copy-done.9
  44.5 0.1 reshape.17.orientation
  44.6 0.0 copy-done.7
  44.6 0.1 reshape.18.mats
  44.7 5.1 %shard_map.88 = (f32[6,16,16,128]{3,2,1,0:T(8,128)S(1)}, f32[8,56,128]{2,1,0:T(8,128)}) custom-call(s32[1]{0:T(128)} %bitcast.place, s32[8]{0:T(128)S(1)} %copy-done.6, s32[48]{0:T(128)S(1)} %reshape.17.orientation, f32[108]{0:T(128)S(1)} %reshape.18.mats, f32[6,16,16,128]{3,2,1,0:T(8,128)S(1)} %get-tuple-element.8.block, ...), custom_call_target="tpu_custom_call" | custom-call | flops 14155776 | bytes 3145728 | tf_op jit(solution)/shard_map/pallas_call | solution.py:327
  49.7 2.2 %all-to-all-done.4.arrived = f32[8,56,128]{2,1,0:T(8,128)S(1)} async-done(((f32[8,56,128]{2,1,0:T(8,128)}), f32[8,56,128]{2,1,0:T(8,128)S(1)}, u32[]{:S(2)}, u32[]{:S(2)}) %all-to-all-start.4) | async-done | bytes 229408 | tf_op jit(solution)/shard_map/all_to_all | solution.py:309
  51.9 3.8 %all-to-all-start.2 = ((f32[8,56,128]{2,1,0:T(8,128)}), f32[8,56,128]{2,1,0:T(8,128)S(1)}, u32[]{:S(2)}, u32[]{:S(2)}) async-start(f32[8,56,128]{2,1,0:T(8,128)} %get-tuple-element.11), calls=%async_computation.2 | async-start | bytes 458752 | tf_op jit(solution)/shard_map/all_to_all | solution.py:309
  55.7 0.6 shard_map.91
  56.3 0.0 copy-start.2
  56.3 0.7 copy-done.2
  57.0 6.7 %all-to-all-done.2.arrived = f32[8,56,128]{2,1,0:T(8,128)S(1)} async-done(((f32[8,56,128]{2,1,0:T(8,128)}), f32[8,56,128]{2,1,0:T(8,128)S(1)}, u32[]{:S(2)}, u32[]{:S(2)}) %all-to-all-start.2) | async-done | bytes 229408 | tf_op jit(solution)/shard_map/all_to_all | solution.py:309
  63.7 3.4 %all-to-all-start.5 = ((f32[8,56,128]{2,1,0:T(8,128)}), f32[8,56,128]{2,1,0:T(8,128)S(1)}, u32[]{:S(2)}, u32[]{:S(2)}) async-start(f32[8,56,128]{2,1,0:T(8,128)} %copy-done.2), calls=%async_computation.5 | async-start | bytes 458752 | tf_op jit(solution)/shard_map/all_to_all | solution.py:313
  67.1 0.6 shard_map.89
  67.7 0.0 copy-start.3
  67.7 0.7 copy-done.3
  68.4 6.6 %all-to-all-done.5.weight_buffer = f32[8,56,128]{2,1,0:T(8,128)S(1)} async-done(((f32[8,56,128]{2,1,0:T(8,128)}), f32[8,56,128]{2,1,0:T(8,128)S(1)}, u32[]{:S(2)}, u32[]{:S(2)}) %all-to-all-start.5) | async-done | bytes 229408 | tf_op jit(solution)/shard_map/all_to_all | solution.py:313
  75.1 11.3 %all_to_all.40.buffer = f32[8,56,128]{2,1,0:T(8,128)S(1)} all-to-all(f32[8,56,128]{2,1,0:T(8,128)} %copy-done.3), channel_id=1, replica_groups=mesh['ckpt'=4,'space'=8] {'space'}, dimensions={0} | all-to-all | bytes 458752 | tf_op jit(solution)/shard_map/all_to_all | solution.py:313
  86.4 6.1 %shard_map.92 = (f32[6,16,16,128]{3,2,1,0:T(8,128)S(1)}, f32[8,56,128]{2,1,0:T(8,128)S(1)}) custom-call(s32[1]{0:T(128)} %bitcast.place, s32[8]{0:T(128)S(1)} %copy-done.6, s32[48]{0:T(128)S(1)} %reshape.17.orientation, f32[108]{0:T(128)S(1)} %reshape.18.mats, f32[6,16,16,128]{3,2,1,0:T(8,128)S(1)} %get-tuple-element.10.block, ...), custom_call_target="tpu_custom_call" | custom-call | flops 28311552 | bytes 3145728 | tf_op jit(solution)/shard_map/pallas_call | solution.py:338
  92.4 0.0 copy-start.4
  92.4 0.9 copy-done.4
  93.3 10.5 %all_to_all.41.arrived = f32[8,56,128]{2,1,0:T(8,128)S(1)} all-to-all(f32[8,56,128]{2,1,0:T(8,128)S(1)} %get-tuple-element.13), channel_id=1, replica_groups=mesh['ckpt'=4,'space'=8] {'space'}, dimensions={0} | all-to-all | bytes 458752 | tf_op jit(solution)/shard_map/all_to_all | solution.py:309
  103.8 1.3 %shard_map.93 = f32[8,56,128]{2,1,0:T(8,128)} custom-call(s32[8]{0:T(128)S(1)} %copy-done.6, s32[48]{0:T(128)S(1)} %reshape.19.neighbours, f32[8,56,128]{2,1,0:T(8,128)S(1)} %all_to_all.41.arrived), custom_call_target="tpu_custom_call" | custom-call | flops 884736 | bytes 3145728 | tf_op jit(solution)/shard_map/pallas_call | solution.py:310
  105.1 3.4 %all-to-all-start.7 = ((f32[8,56,128]{2,1,0:T(8,128)}), f32[8,56,128]{2,1,0:T(8,128)S(1)}, u32[]{:S(2)}, u32[]{:S(2)}) async-start(f32[8,56,128]{2,1,0:T(8,128)} %shard_map.93), calls=%async_computation.7 | async-start | bytes 458752 | tf_op jit(solution)/shard_map/all_to_all | solution.py:313
  108.6 4.8 %shard_map.95 = f32[6,16,16,128]{3,2,1,0:T(8,128)} custom-call(s32[1]{0:T(128)} %bitcast.place, s32[8]{0:T(128)S(1)} %copy-done.6, s32[48]{0:T(128)S(1)} %reshape.17.orientation, f32[108]{0:T(128)S(1)} %reshape.18.mats, f32[6,16,16,128]{3,2,1,0:T(8,128)S(1)} %get-tuple-element.10.block, f32[8,56,128]{2,1,0:T(8,128)S(1)} %all_to_all.40.buffer, ...), custom_call_target="tpu_custom_call" | custom-call | flops 14155776 | bytes 3145728 | tf_op jit(solution)/shard_map/pallas_call | solution.py:346
  113.3 3.2 %all-to-all-done.7.weight_buffer = f32[8,56,128]{2,1,0:T(8,128)S(1)} async-done(((f32[8,56,128]{2,1,0:T(8,128)}), f32[8,56,128]{2,1,0:T(8,128)S(1)}, u32[]{:S(2)}, u32[]{:S(2)}) %all-to-all-start.7) | async-done | bytes 229408 | tf_op jit(solution)/shard_map/all_to_all | solution.py:313
  116.5 0.0 copy-start.5
  116.5 1.1 copy-done.5
  117.6 6.4 %shard_map.94 = f32[6,16,16,128]{3,2,1,0:T(8,128)} custom-call(s32[1]{0:T(128)} %bitcast.place, s32[8]{0:T(128)S(1)} %copy-done.6, s32[48]{0:T(128)S(1)} %reshape.17.orientation, f32[108]{0:T(128)S(1)} %reshape.18.mats, f32[6,16,16,128]{3,2,1,0:T(8,128)S(1)} %get-tuple-element.8.block, f32[8,56,128]{2,1,0:T(8,128)S(1)} %all-to-all-done.1.buffer, ...), custom_call_target="tpu_custom_call" | custom-call | flops 28311552 | bytes 3145728 | tf_op jit(solution)/shard_map/pallas_call | solution.py:353
Async XLA Ops:
  10.9 7.2 %copy-start.8 = (s32[8,6]{1,0:T(8,128)S(1)}, s32[8,6]{1,0:T(8,128)}, u32[]{:S(2)}) copy-start(s32[8,6]{1,0:T(8,128)} %param.12) | copy-start | bytes 580
  10.9 16.2 %copy-start.6 = (s32[8]{0:T(128)S(1)}, s32[8]{0:T(128)}, u32[]{:S(2)}) copy-start(s32[8]{0:T(128)} %owner.15) | copy-start | bytes 100
  12.1 19.8 %copy-start.1 = (f32[1,1,6,16,16,128]{5,4,3,2,1,0:T(8,128)S(1)}, f32[1,1,6,16,16,128]{5,4,3,2,1,0:T(8,128)}, u32[]{:S(2)}) copy-start(f32[1,1,6,16,16,128]{5,4,3,2,1,0:T(8,128)} %param.8) | copy-start | bytes 2359300
  12.1 14.9 %all-to-all-start = ((f32[8,56,128]{2,1,0:T(8,128)}), f32[8,56,128]{2,1,0:T(8,128)S(1)}, u32[]{:S(2)}, u32[]{:S(2)}) async-start(f32[8,56,128]{2,1,0:T(8,128)} %get-tuple-element.9), calls=%async_computation | async-start | bytes 458752 | tf_op jit(solution)/shard_map/all_to_all | solution.py:309
  28.3 3.6 %copy-start = (f32[1,16,16,128]{3,2,1,0:T(8,128)S(1)}, f32[1,16,16,128]{3,2,1,0:T(8,128)}, u32[]{:S(2)}) copy-start(f32[1,16,16,128]{3,2,1,0:T(8,128)} %param.9) | copy-start | bytes 393220
  28.3 11.9 %all-to-all-start.1 = ((f32[8,56,128]{2,1,0:T(8,128)}), f32[8,56,128]{2,1,0:T(8,128)S(1)}, u32[]{:S(2)}, u32[]{:S(2)}) async-start(f32[8,56,128]{2,1,0:T(8,128)} %shard_map.87), calls=%async_computation.1 | async-start | bytes 458752 | tf_op jit(solution)/shard_map/all_to_all | solution.py:313
  40.3 4.3 %copy-start.7 = (f32[3,6,6]{2,1,0:T(8,128)S(1)}, f32[3,6,6]{2,1,0:T(8,128)}, u32[]{:S(2)}) copy-start(f32[3,6,6]{2,1,0:T(8,128)} %param.10) | copy-start | bytes 1300
  40.3 11.6 %all-to-all-start.4 = ((f32[8,56,128]{2,1,0:T(8,128)}), f32[8,56,128]{2,1,0:T(8,128)S(1)}, u32[]{:S(2)}, u32[]{:S(2)}) async-start(f32[8,56,128]{2,1,0:T(8,128)} %shard_map.90), calls=%async_computation.4 | async-start | bytes 458752 | tf_op jit(solution)/shard_map/all_to_all | solution.py:309
  43.8 0.7 copy-start.9
  51.9 11.8 %all-to-all-start.2 = ((f32[8,56,128]{2,1,0:T(8,128)}), f32[8,56,128]{2,1,0:T(8,128)S(1)}, u32[]{:S(2)}, u32[]{:S(2)}) async-start(f32[8,56,128]{2,1,0:T(8,128)} %get-tuple-element.11), calls=%async_computation.2 | async-start | bytes 458752 | tf_op jit(solution)/shard_map/all_to_all | solution.py:309
  56.3 0.7 copy-start.2
  63.7 11.3 %all-to-all-start.5 = ((f32[8,56,128]{2,1,0:T(8,128)}), f32[8,56,128]{2,1,0:T(8,128)S(1)}, u32[]{:S(2)}, u32[]{:S(2)}) async-start(f32[8,56,128]{2,1,0:T(8,128)} %copy-done.2), calls=%async_computation.5 | async-start | bytes 458752 | tf_op jit(solution)/shard_map/all_to_all | solution.py:313
  67.7 0.7 copy-start.3
  92.4 0.9 copy-start.4
  105.1 11.3 %all-to-all-start.7 = ((f32[8,56,128]{2,1,0:T(8,128)}), f32[8,56,128]{2,1,0:T(8,128)S(1)}, u32[]{:S(2)}, u32[]{:S(2)}) async-start(f32[8,56,128]{2,1,0:T(8,128)} %shard_map.93), calls=%async_computation.7 | async-start | bytes 458752 | tf_op jit(solution)/shard_map/all_to_all | solution.py:313
  116.5 1.1 copy-start.5

commit v2 on v1

--- a/solution.py
+++ b/solution.py
@@ -192,20 +192,34 @@
     return out
 
 
-def load_gathered(geo, gathered, padded):
-    parts, depth = gathered.shape[0], gathered.shape[2]
-    for part in range(parts):
-        padded[:, 1 + part * depth : 1 + (part + 1) * depth, PAD : PAD + geo.y, :] = gathered[part]
-
-
-def pack_state_kernel(geo, gathered, state, buffer, faces):
+def partner(count, place, distance):
+    if count & (count - 1) == 0:
+        return place ^ distance
+    return lax.rem(distance - place + 2 * count, count) if not isinstance(place, int) else (distance - place) % count
+
+
+def scatter_slots(geo, place, parts, buffer):
+    for distance in range(geo.n):
+        buffer[partner(geo.n, place[0], jnp.int32(distance))] = parts[distance][...]
+
+
+def collect_slots(geo, place, buffer, parts):
+    for distance in range(geo.n):
+        parts[distance][...] = buffer[partner(geo.n, place[0], jnp.int32(distance))]
+
+
+def pack_state_kernel(geo, place, gathered, state, *rest):
+    sent, (buffer, faces) = rest[: geo.n], rest[geo.n :]
     parts, depth = gathered.shape[0], gathered.shape[2]
     for part in range(parts):
         state[:, part * depth : (part + 1) * depth] = gathered[part]
     pack(geo, state, faces, buffer)
-
-
-def pack_weight_kernel(geo, grads, rate, buffer, weight, faces):
+    collect_slots(geo, place, buffer, sent)
+
+
+def pack_weight_kernel(geo, place, grads, rate, *rest):
+    sent, (buffer, weight, faces) = rest[: geo.n], rest[geo.n :]
+
     def body(plane, carry):
         for var in range(geo.v):
             weight[var, plane] = rate[plane] * grads[var, plane]
@@ -213,29 +227,34 @@
 
     lax.fori_loop(0, geo.x, body, 0)
     pack(geo, weight, faces, buffer)
-
-
-def route_kernel(geo, owner, neighbours, arrived, leaving):
+    collect_slots(geo, place, buffer, sent)
+
+
+def route_kernel(geo, place, owner, neighbours, *rest):
+    parts, sent, (arrived, leaving) = rest[: geo.n], rest[geo.n : 2 * geo.n], rest[2 * geo.n :]
+    scatter_slots(geo, place, parts, arrived)
     for block in range(geo.n):
         target = owner[block]
         for side in range(6):
             source = owner[neighbours[block * 6 + side]]
             run, start, far = geo.runs[side], geo.starts[side], geo.starts[side ^ 1]
             leaving[target, start : start + run] = arrived[source, far : far + run]
-
-
-def fill(geo, place, owner, orientation, block, buffer, faces, padded, zfaces):
+    collect_slots(geo, place, leaving, sent)
+
+
+def fill(geo, place, owner, orientation, block, parts, buffer, faces, padded, zfaces):
     v, x, y, z = geo.block
     padded[:, 1 : x + 1, PAD : PAD + y, :] = block[...]
+    scatter_slots(geo, place, parts, buffer)
     unpack(geo, own_codes(geo, place, owner, orientation), buffer, faces, padded, zfaces)
 
 
-def step_kernel(geo, packed, place, owner, orientation, mats, block, buffer, rate, *rest):
+def step_kernel(geo, packed, place, owner, orientation, mats, block, rate, *rest):
+    parts, result, rest = rest[: geo.n], rest[geo.n], rest[geo.n + 1 :]
     if packed:
-        result, sent, faces, padded, zfaces = rest
-    else:
-        result, faces, padded, zfaces = rest
-    fill(geo, place, owner, orientation, block, buffer, faces, padded, zfaces)
+        sent, rest = rest[: geo.n], rest[geo.n :]
+    buffer, faces, padded, zfaces = rest
+    fill(geo, place, owner, orientation, block, parts, buffer, faces, padded, zfaces)
 
     def body(plane, carry):
         cells, low, high = around(geo, padded, zfaces, plane)
@@ -245,18 +264,23 @@
 
     lax.fori_loop(0, geo.x, body, 0)
     if packed:
-        pack(geo, result, faces, sent)
-
-
-def adjoint_kernel(geo, packed, place, owner, orientation, mats, block, buffer, grads, weight_buffer, rate, *rest):
+        pack(geo, result, faces, buffer)
+        collect_slots(geo, place, buffer, sent)
+
+
+def adjoint_kernel(geo, packed, place, owner, orientation, mats, block, grads, rate, *rest):
+    v, x, y, z = geo.block
+    parts, weight_parts, result = rest[: geo.n], rest[geo.n : 2 * geo.n], rest[2 * geo.n]
+    rest = rest[2 * geo.n + 1 :]
     if packed:
-        result, sent, faces, padded, zfaces, weights, weight_zfaces, weight_block = rest
-    else:
-        result, faces, padded, zfaces, weights, weight_zfaces = rest
-    v, x, y, z = geo.block
-    fill(geo, place, owner, orientation, block, buffer, faces, padded, zfaces)
+        sent, rest = rest[: geo.n], rest[geo.n :]
+    buffer, faces, padded, zfaces, weights, weight_zfaces = rest[:6]
+    if packed:
+        weight_block = rest[6]
+    fill(geo, place, owner, orientation, block, parts, buffer, faces, padded, zfaces)
     codes = own_codes(geo, place, owner, orientation)
-    unpack(geo, codes, weight_buffer, faces, weights, weight_zfaces)
+    scatter_slots(geo, place, weight_parts, buffer)
+    unpack(geo, codes, buffer, faces, weights, weight_zfaces)
 
     def scale(plane, carry):
         for var in range(v):
@@ -278,7 +302,8 @@
 
     lax.fori_loop(0, x, body, 0)
     if packed:
-        pack(geo, weight_block, faces, sent)
+        pack(geo, weight_block, faces, buffer)
+        collect_slots(geo, place, buffer, sent)
 
 
 def call(kernel, specs, outs, scratch, flops):
@@ -305,58 +330,60 @@
     zfaces = (2, cy, cz)
     work = nvars * nvars * 3 * 4 * cx * cy * cz
 
-    def exchange(buffer):
-        arrived = lax.all_to_all(buffer, "space", 0, 0, tiled=True)
+    parts = [geo.buffer[1:]] * count
+
+    def swap(sent):
+        out = [sent[0]]
+        for distance in range(1, count):
+            pairs = [(index, partner(count, index, distance)) for index in range(count)]
+            out.append(lax.ppermute(sent[distance], "space", pairs))
+        return out
+
+    def exchange(sent):
         leaving = call(
-            functools.partial(route_kernel, geo), [SMEM, SMEM, VMEM], [geo.buffer], [], work // 16
-        )(owner, neighbours, arrived)[0]
-        return lax.all_to_all(leaving, "space", 0, 0, tiled=True)
+            functools.partial(route_kernel, geo), [SMEM] * 3 + [VMEM] * count, parts, [geo.buffer] * 2, work // 16
+        )(place, owner, neighbours, *swap(sent))
+        return swap(leaving)
 
     gathered = lax.all_gather(checkpoint, "ckpt", axis=0, tiled=True)
-    (sent,) = call(
-        functools.partial(pack_weight_kernel, geo), [VMEM, VMEM], [geo.buffer], [geo.block, geo.faces], work // 8
-    )(grads, rate)
+    sent = call(
+        functools.partial(pack_weight_kernel, geo),
+        [SMEM, VMEM, VMEM],
+        parts,
+        [geo.buffer, geo.block, geo.faces],
+        work // 8,
+    )(place, grads, rate)
     weight_ghosts = exchange(sent)
-    state, sent = call(
-        functools.partial(pack_state_kernel, geo), [VMEM], [geo.block, geo.buffer], [geo.faces], work // 8
-    )(gathered)
-    ghosts = [exchange(sent)]
-    states = [state]
+    state, *sent = call(
+        functools.partial(pack_state_kernel, geo),
+        [SMEM, VMEM],
+        [geo.block] + parts,
+        [geo.buffer, geo.faces],
+        work // 8,
+    )(place, gathered)
+    ghosts = exchange(sent)
     fixed = (place, owner, orientation, mats)
-    step_specs = [SMEM] * 4 + [VMEM] * 3
-    next_state, sent = call(
-        functools.partial(step_kernel, geo, True),
-        step_specs,
-        [geo.block, geo.buffer],
-        [geo.faces, geo.padded, zfaces],
-        work,
-    )(*fixed, states[0], ghosts[0], rate)
-    states.append(next_state)
-    ghosts.append(exchange(sent))
-    adjoint_specs = [SMEM] * 4 + [VMEM] * 5
-    pads = [geo.faces, geo.padded, zfaces, geo.padded, zfaces]
-    grads_now, sent = call(
+    step_specs = [SMEM] * 4 + [VMEM] * (2 + count)
+    pads = [geo.buffer, geo.faces, geo.padded, zfaces]
+    next_state, *sent = call(
+        functools.partial(step_kernel, geo, True), step_specs, [geo.block] + parts, pads, work
+    )(*fixed, state, rate, *ghosts)
+    next_ghosts = exchange(sent)
+    adjoint_specs = [SMEM] * 4 + [VMEM] * (3 + 2 * count)
+    grads_now, *sent = call(
         functools.partial(adjoint_kernel, geo, True),
         adjoint_specs,
-        [geo.block, geo.buffer],
-        pads + [geo.block],
+        [geo.block] + parts,
+        pads + [geo.padded, zfaces, geo.block],
         2 * work,
-    )(*fixed, states[1], ghosts[1], grads, weight_ghosts, rate)
+    )(*fixed, next_state, grads, rate, *next_ghosts, *weight_ghosts)
     weight_ghosts = exchange(sent)
-    (final,) = call(
-        functools.partial(step_kernel, geo, False),
-        step_specs,
-        [geo.block],
-        [geo.faces, geo.padded, zfaces],
-        work,
-    )(*fixed, states[1], ghosts[1], rate)
+    (final,) = call(functools.partial(step_kernel, geo, False), step_specs, [geo.block], pads, work)(
+        *fixed, next_state, rate, *next_ghosts
+    )
     (adjoint,) = call(
-        functools.partial(adjoint_kernel, geo, False),
-        adjoint_specs,
-        [geo.block],
-        pads,
-        2 * work,
-    )(*fixed, states[0], ghosts[0], grads_now, weight_ghosts, rate)
+        functools.partial(adjoint_kernel, geo, False), adjoint_specs, [geo.block], pads + [geo.padded, zfaces], 2 * work
+    )(*fixed, state, grads_now, rate, *ghosts, *weight_ghosts)
     return (adjoint[None, None], final[None])
 
 

time: 125 us -> 142 us (1.14)
  starting transfers between devices: 23.6 us -> 89.7 us
  blocking collectives: 32.1 us -> 10.4 us
  waiting for transfers between devices: 34.6 us -> 14.8 us
  local copies, waits for them, and re-layouts: 4.32 us -> 0.27 us
  Pallas kernels: 28.6 us -> 25.6 us
    ppermute x0 -> x56, starting transfers between devices: none -> 89.7 us  [swap(): out.append(lax.ppermute(sent[distance], 'space', pairs))]
    all_to_all x6 -> x0, waiting for transfers between devices: 34.6 us -> none  [the longest x3 17.7 us: exchange(): arrived = lax.all_to_all(buffer, 'space', 0, 0, tiled=True)]
    all_to_all x6 -> x0, starting transfers between devices: 23.6 us -> none  [the longest x3 13.3 us: exchange(): arrived = lax.all_to_all(buffer, 'space', 0, 0, tiled=True)]
    all_to_all x2 -> x0, blocking collectives: 21.8 us -> none  [the longest x1 11.3 us: exchange(): return lax.all_to_all(leaving, 'space', 0, 0, tiled=True)]
    ppermute x0 -> x56, waiting for transfers between devices: none -> 14.8 us  [swap(): out.append(lax.ppermute(sent[distance], 'space', pairs))]
    unnamed x20 -> x12, local copies, waits for them, and re-layouts: 4.07 us -> 0.03 us
    pallas_call x7, Pallas kernels: 11.4 us -> 8.14 us  [the longest x1 4.4 us: on_device(): call(functools.partial(step_kernel, geo, True), step_specs, [geo.block] +...]
  transfers between devices with their start and end apart: 6 -> 56, of which waited for: 6 -> 8; matrix products, arithmetic and copies ran while one was open for 0% -> 0% of each run, Pallas kernels for 10% -> 8%
where the time goes in v2:
time: 142 us
  starting transfers between devices  89.7 us (63%)
  Pallas kernels  25.6 us (18%)
  waiting for transfers between devices  14.8 us (10%)
  blocking collectives  10.4 us (7%)
    ppermute x56, starting transfers between devices, swap(): out.append(lax.ppermute(sent[distance], 'space', pairs))  89.7 us
    ppermute x56, waiting for transfers between devices, swap(): out.append(lax.ppermute(sent[distance], 'space', pairs))  14.8 us
    all_gather x1, blocking collectives, on_device(): gathered = lax.all_gather(checkpoint, 'ckpt', axis=0, tiled=True)  10.4 us
    pallas_call x1, Pallas kernels, on_device(): call(functools.partial(adjoint_kernel, geo, False), adjoint_specs, [geo.b...  6.49 us
    pallas_call x1, Pallas kernels, on_device(): call(functools.partial(adjoint_kernel, geo, True), adjoint_specs, [geo.bl...  6.16 us
    pallas_call x1, Pallas kernels, on_device(): call(functools.partial(step_kernel, geo, False), step_specs, [geo.block],...  4.77 us
    pallas_call x1, Pallas kernels, on_device(): call(functools.partial(step_kernel, geo, True), step_specs, [geo.block] +...  4.4 us
  transfers between devices with their start and end apart: 56, of which 8 were waited for; matrix products, arithmetic and copies ran while one was open for 0% of the time, Pallas kernels for 8%

profile of v2, /device:TPU:0, one launch (start us, length us, event | category | flops | bytes accessed | tf_op | source)
XLA Modules:
  0.0 141.6 jit_solution(8780948918080387628)
XLA Ops:
  0.6 10.4 %all_gather.3.gathered = f32[4,6,4,16,128]{4,3,2,1,0:T(8,128)S(1)} all-gather(f32[1,6,4,16,128]{4,3,2,1,0:T(8,128)} %param.7), channel_id=1, replica_groups=mesh['ckpt'=4,'space'=8] {'ckpt'}, dimensions={0}, use_global_device_ids=true | all-gather | bytes 983040 | tf_op jit(solution)/shard_map/all_gather | solution.py:348
  11.6 1.6 %collective-permute-start = (f32[56,128]{1,0:T(8,128)S(1)}, f32[56,128]{1,0:T(8,128)S(1)}, u32[]{:S(2)}, u32[]{:S(2)}) collective-permute-start(f32[56,128]{1,0:T(8,128)S(1)} %get-tuple-element.71), channel_id=1, source_target_pairs={{0,1},{1,0},{2,3},{3,2},{4,5},{5,4},{6,7},{7,6},{8,9},{9,8},{10,11... | collective-permute-start | bytes 86024 | tf_op jit(solution)/shard_map/ppermute | solution.py:339
  13.2 1.6 %collective-permute-start.1 = (f32[56,128]{1,0:T(8,128)S(1)}, f32[56,128]{1,0:T(8,128)S(1)}, u32[]{:S(2)}, u32[]{:S(2)}) collective-permute-start(f32[56,128]{1,0:T(8,128)S(1)} %get-tuple-element.72), channel_id=1, source_target_pairs={{0,2},{1,3},{2,0},{3,1},{4,6},{5,7},{6,4},{7,5},{8,10},{9,11},{10,... | collective-permute-start | bytes 86024 | tf_op jit(solution)/shard_map/ppermute | solution.py:339
  15.2 2.6 %collective-permute-start.3 = (f32[56,128]{1,0:T(8,128)S(1)}, f32[56,128]{1,0:T(8,128)S(1)}, u32[]{:S(2)}, u32[]{:S(2)}) collective-permute-start(f32[56,128]{1,0:T(8,128)S(1)} %get-tuple-element.74), channel_id=1, source_target_pairs={{0,4},{1,5},{2,6},{3,7},{4,0},{5,1},{6,2},{7,3},{8,12},{9,13},{10,... | collective-permute-start | bytes 86024 | tf_op jit(solution)/shard_map/ppermute | solution.py:339
  17.8 1.3 collective-permute-start.4
  19.1 3.6 %collective-permute-start.5 = (f32[56,128]{1,0:T(8,128)S(1)}, f32[56,128]{1,0:T(8,128)S(1)}, u32[]{:S(2)}, u32[]{:S(2)}) collective-permute-start(f32[56,128]{1,0:T(8,128)S(1)} %get-tuple-element.76), channel_id=1, source_target_pairs={{0,6},{1,7},{2,4},{3,5},{4,2},{5,3},{6,0},{7,1},{8,14},{9,15},{10,... | collective-permute-start | bytes 86024 | tf_op jit(solution)/shard_map/ppermute | solution.py:339
  23.4 1.4 collective-permute-done.5.rest_6_
  24.8 4.4 %collective-permute-done.6.rest_7_ = f32[56,128]{1,0:T(8,128)S(1)} collective-permute-done((f32[56,128]{1,0:T(8,128)S(1)}, f32[56,128]{1,0:T(8,128)S(1)}, u32[]{:S(2)}, u32[]{:S(2)}) %collective-permute-start.6) | collective-permute-done | bytes 28704 | tf_op jit(solution)/shard_map/ppermute | solution.py:339
  29.2 0.6 shard_map.87
  29.9 0.6 collective-permute-start.7
  30.5 3.0 %collective-permute-start.9 = (f32[56,128]{1,0:T(8,128)S(1)}, f32[56,128]{1,0:T(8,128)S(1)}, u32[]{:S(2)}, u32[]{:S(2)}) collective-permute-start(f32[56,128]{1,0:T(8,128)S(1)} %get-tuple-element.81), channel_id=1, source_target_pairs={{0,3},{1,2},{2,1},{3,0},{4,7},{5,6},{6,5},{7,4},{8,11},{9,10},{10,... | collective-permute-start | bytes 86024 | tf_op jit(solution)/shard_map/ppermute | solution.py:339
  33.4 2.9 %collective-permute-start.11 = (f32[56,128]{1,0:T(8,128)S(1)}, f32[56,128]{1,0:T(8,128)S(1)}, u32[]{:S(2)}, u32[]{:S(2)}) collective-permute-start(f32[56,128]{1,0:T(8,128)S(1)} %get-tuple-element.83), channel_id=1, source_target_pairs={{0,5},{1,4},{2,7},{3,6},{4,1},{5,0},{6,3},{7,2},{8,13},{9,12},{10,... | collective-permute-start | bytes 86024 | tf_op jit(solution)/shard_map/ppermute | solution.py:339
  36.7 4.4 %collective-permute-start.13 = (f32[56,128]{1,0:T(8,128)S(1)}, f32[56,128]{1,0:T(8,128)S(1)}, u32[]{:S(2)}, u32[]{:S(2)}) collective-permute-start(f32[56,128]{1,0:T(8,128)S(1)} %get-tuple-element.85), channel_id=1, source_target_pairs={{0,7},{1,6},{2,5},{3,4},{4,3},{5,2},{6,1},{7,0},{8,15},{9,14},{10,... | collective-permute-start | bytes 86024 | tf_op jit(solution)/shard_map/ppermute | solution.py:339
  41.1 0.6 shard_map.90
  41.7 0.6 collective-permute-start.28
  42.3 3.0 %collective-permute-start.30 = (f32[56,128]{1,0:T(8,128)S(1)}, f32[56,128]{1,0:T(8,128)S(1)}, u32[]{:S(2)}, u32[]{:S(2)}) collective-permute-start(f32[56,128]{1,0:T(8,128)S(1)} %get-tuple-element.106), channel_id=1, source_target_pairs={{0,3},{1,2},{2,1},{3,0},{4,7},{5,6},{6,5},{7,4},{8,11},{9,10},{10,... | collective-permute-start | bytes 86024 | tf_op jit(solution)/shard_map/ppermute | solution.py:339
  45.6 2.8 %collective-permute-start.32 = (f32[56,128]{1,0:T(8,128)S(1)}, f32[56,128]{1,0:T(8,128)S(1)}, u32[]{:S(2)}, u32[]{:S(2)}) collective-permute-start(f32[56,128]{1,0:T(8,128)S(1)} %get-tuple-element.108), channel_id=1, source_target_pairs={{0,5},{1,4},{2,7},{3,6},{4,1},{5,0},{6,3},{7,2},{8,13},{9,12},{10,... | collective-permute-start | bytes 86024 | tf_op jit(solution)/shard_map/ppermute | solution.py:339
  48.4 4.4 %shard_map.88 = (f32[6,16,16,128]{3,2,1,0:T(8,128)S(1)}, f32[56,128]{1,0:T(8,128)S(1)}, f32[56,128]{1,0:T(8,128)S(1)}, f32[56,128]{1,0:T(8,128)S(1)}, f32[56,128...) custom-call(s32[1]{0:T(128)} %bitcast.place, ...), custom_call_target="tpu_custom_call" | custom-call | flops 14155776 | bytes 3145728 | tf_op jit(solution)/shard_map/pallas_call | solution.py:368
  53.3 4.4 %collective-permute-start.34 = (f32[56,128]{1,0:T(8,128)S(1)}, f32[56,128]{1,0:T(8,128)S(1)}, u32[]{:S(2)}, u32[]{:S(2)}) collective-permute-start(f32[56,128]{1,0:T(8,128)S(1)} %get-tuple-element.110), channel_id=1, source_target_pairs={{0,7},{1,6},{2,5},{3,4},{4,3},{5,2},{6,1},{7,0},{8,15},{9,14},{10,... | collective-permute-start | bytes 86024 | tf_op jit(solution)/shard_map/ppermute | solution.py:339
  58.2 3.0 %collective-permute-start.16 = (f32[56,128]{1,0:T(8,128)S(1)}, f32[56,128]{1,0:T(8,128)S(1)}, u32[]{:S(2)}, u32[]{:S(2)}) collective-permute-start(f32[56,128]{1,0:T(8,128)S(1)} %get-tuple-element.90), channel_id=1, source_target_pairs={{0,3},{1,2},{2,1},{3,0},{4,7},{5,6},{6,5},{7,4},{8,11},{9,10},{10,... | collective-permute-start | bytes 86024 | tf_op jit(solution)/shard_map/ppermute | solution.py:339
  61.2 2.9 %collective-permute-start.18 = (f32[56,128]{1,0:T(8,128)S(1)}, f32[56,128]{1,0:T(8,128)S(1)}, u32[]{:S(2)}, u32[]{:S(2)}) collective-permute-start(f32[56,128]{1,0:T(8,128)S(1)} %get-tuple-element.92), channel_id=1, source_target_pairs={{0,5},{1,4},{2,7},{3,6},{4,1},{5,0},{6,3},{7,2},{8,13},{9,12},{10,... | collective-permute-start | bytes 86024 | tf_op jit(solution)/shard_map/ppermute | solution.py:339
  64.4 4.4 %collective-permute-start.20 = (f32[56,128]{1,0:T(8,128)S(1)}, f32[56,128]{1,0:T(8,128)S(1)}, u32[]{:S(2)}, u32[]{:S(2)}) collective-permute-start(f32[56,128]{1,0:T(8,128)S(1)} %get-tuple-element.94), channel_id=1, source_target_pairs={{0,7},{1,6},{2,5},{3,4},{4,3},{5,2},{6,1},{7,0},{8,15},{9,14},{10,... | collective-permute-start | bytes 86024 | tf_op jit(solution)/shard_map/ppermute | solution.py:339
  68.9 0.6 shard_map.91
  69.5 0.6 collective-permute-start.35
  70.1 3.0 %collective-permute-start.37 = (f32[56,128]{1,0:T(8,128)S(1)}, f32[56,128]{1,0:T(8,128)S(1)}, u32[]{:S(2)}, u32[]{:S(2)}) collective-permute-start(f32[56,128]{1,0:T(8,128)S(1)} %get-tuple-element.114), channel_id=1, source_target_pairs={{0,3},{1,2},{2,1},{3,0},{4,7},{5,6},{6,5},{7,4},{8,11},{9,10},{10,... | collective-permute-start | bytes 86024 | tf_op jit(solution)/shard_map/ppermute | solution.py:339
  73.1 2.9 %collective-permute-start.39 = (f32[56,128]{1,0:T(8,128)S(1)}, f32[56,128]{1,0:T(8,128)S(1)}, u32[]{:S(2)}, u32[]{:S(2)}) collective-permute-start(f32[56,128]{1,0:T(8,128)S(1)} %get-tuple-element.116), channel_id=1, source_target_pairs={{0,5},{1,4},{2,7},{3,6},{4,1},{5,0},{6,3},{7,2},{8,13},{9,12},{10,... | collective-permute-start | bytes 86024 | tf_op jit(solution)/shard_map/ppermute | solution.py:339
  76.0 0.6 shard_map.89
  77.0 4.4 %collective-permute-start.41 = (f32[56,128]{1,0:T(8,128)S(1)}, f32[56,128]{1,0:T(8,128)S(1)}, u32[]{:S(2)}, u32[]{:S(2)}) collective-permute-start(f32[56,128]{1,0:T(8,128)S(1)} %get-tuple-element.118), channel_id=1, source_target_pairs={{0,7},{1,6},{2,5},{3,4},{4,3},{5,2},{6,1},{7,0},{8,15},{9,14},{10,... | collective-permute-start | bytes 86024 | tf_op jit(solution)/shard_map/ppermute | solution.py:339
  82.0 3.0 %collective-permute-start.23 = (f32[56,128]{1,0:T(8,128)S(1)}, f32[56,128]{1,0:T(8,128)S(1)}, u32[]{:S(2)}, u32[]{:S(2)}) collective-permute-start(f32[56,128]{1,0:T(8,128)S(1)} %get-tuple-element.98), channel_id=1, source_target_pairs={{0,3},{1,2},{2,1},{3,0},{4,7},{5,6},{6,5},{7,4},{8,11},{9,10},{10,... | collective-permute-start | bytes 86024 | tf_op jit(solution)/shard_map/ppermute | solution.py:339
  85.0 2.9 %collective-permute-start.25 = (f32[56,128]{1,0:T(8,128)S(1)}, f32[56,128]{1,0:T(8,128)S(1)}, u32[]{:S(2)}, u32[]{:S(2)}) collective-permute-start(f32[56,128]{1,0:T(8,128)S(1)} %get-tuple-element.100), channel_id=1, source_target_pairs={{0,5},{1,4},{2,7},{3,6},{4,1},{5,0},{6,3},{7,2},{8,13},{9,12},{10,... | collective-permute-start | bytes 86024 | tf_op jit(solution)/shard_map/ppermute | solution.py:339
  88.2 4.4 %collective-permute-start.27 = (f32[56,128]{1,0:T(8,128)S(1)}, f32[56,128]{1,0:T(8,128)S(1)}, u32[]{:S(2)}, u32[]{:S(2)}) collective-permute-start(f32[56,128]{1,0:T(8,128)S(1)} %get-tuple-element.102), channel_id=1, source_target_pairs={{0,7},{1,6},{2,5},{3,4},{4,3},{5,2},{6,1},{7,0},{8,15},{9,14},{10,... | collective-permute-start | bytes 86024 | tf_op jit(solution)/shard_map/ppermute | solution.py:339
  92.6 1.0 collective-permute-done.26.rest_6_
  93.6 1.2 collective-permute-done.27.rest_7_
  94.8 6.2 %shard_map.92 = (f32[6,16,16,128]{3,2,1,0:T(8,128)S(1)}, f32[56,128]{1,0:T(8,128)S(1)}, f32[56,128]{1,0:T(8,128)S(1)}, f32[56,128]{1,0:T(8,128)S(1)}, f32[56,128...) custom-call(s32[1]{0:T(128)} %bitcast.place, ...), custom_call_target="tpu_custom_call" | custom-call | flops 28311552 | bytes 3145728 | tf_op jit(solution)/shard_map/pallas_call | solution.py:373
  100.9 1.5 %collective-permute-start.42 = (f32[56,128]{1,0:T(8,128)S(1)}, f32[56,128]{1,0:T(8,128)S(1)}, u32[]{:S(2)}, u32[]{:S(2)}) collective-permute-start(f32[56,128]{1,0:T(8,128)S(1)} %get-tuple-element.121), channel_id=1, source_target_pairs={{0,1},{1,0},{2,3},{3,2},{4,5},{5,4},{6,7},{7,6},{8,9},{9,8},{10,11... | collective-permute-start | bytes 86024 | tf_op jit(solution)/shard_map/ppermute | solution.py:339
  102.5 2.0 %collective-permute-start.44 = (f32[56,128]{1,0:T(8,128)S(1)}, f32[56,128]{1,0:T(8,128)S(1)}, u32[]{:S(2)}, u32[]{:S(2)}) collective-permute-start(f32[56,128]{1,0:T(8,128)S(1)} %get-tuple-element.123), channel_id=1, source_target_pairs={{0,3},{1,2},{2,1},{3,0},{4,7},{5,6},{6,5},{7,4},{8,11},{9,10},{10,... | collective-permute-start | bytes 86024 | tf_op jit(solution)/shard_map/ppermute | solution.py:339
  104.5 2.1 %collective-permute-start.45 = (f32[56,128]{1,0:T(8,128)S(1)}, f32[56,128]{1,0:T(8,128)S(1)}, u32[]{:S(2)}, u32[]{:S(2)}) collective-permute-start(f32[56,128]{1,0:T(8,128)S(1)} %get-tuple-element.124), channel_id=1, source_target_pairs={{0,4},{1,5},{2,6},{3,7},{4,0},{5,1},{6,2},{7,3},{8,12},{9,13},{10,... | collective-permute-start | bytes 86024 | tf_op jit(solution)/shard_map/ppermute | solution.py:339
  106.6 1.7 %collective-permute-start.46 = (f32[56,128]{1,0:T(8,128)S(1)}, f32[56,128]{1,0:T(8,128)S(1)}, u32[]{:S(2)}, u32[]{:S(2)}) collective-permute-start(f32[56,128]{1,0:T(8,128)S(1)} %get-tuple-element.125), channel_id=1, source_target_pairs={{0,5},{1,4},{2,7},{3,6},{4,1},{5,0},{6,3},{7,2},{8,13},{9,12},{10,... | collective-permute-start | bytes 86024 | tf_op jit(solution)/shard_map/ppermute | solution.py:339
  108.3 3.5 %collective-permute-start.47 = (f32[56,128]{1,0:T(8,128)S(1)}, f32[56,128]{1,0:T(8,128)S(1)}, u32[]{:S(2)}, u32[]{:S(2)}) collective-permute-start(f32[56,128]{1,0:T(8,128)S(1)} %get-tuple-element.126), channel_id=1, source_target_pairs={{0,6},{1,7},{2,4},{3,5},{4,2},{5,3},{6,0},{7,1},{8,14},{9,15},{10,... | collective-permute-start | bytes 86024 | tf_op jit(solution)/shard_map/ppermute | solution.py:339
  112.3 2.0 %collective-permute-done.47.rest_6_ = f32[56,128]{1,0:T(8,128)S(1)} collective-permute-done((f32[56,128]{1,0:T(8,128)S(1)}, f32[56,128]{1,0:T(8,128)S(1)}, u32[]{:S(2)}, u32[]{:S(2)}) %collective-permute-start.47) | collective-permute-done | bytes 28704 | tf_op jit(solution)/shard_map/ppermute | solution.py:339
  114.3 4.1 %collective-permute-done.48.rest_7_ = f32[56,128]{1,0:T(8,128)S(1)} collective-permute-done((f32[56,128]{1,0:T(8,128)S(1)}, f32[56,128]{1,0:T(8,128)S(1)}, u32[]{:S(2)}, u32[]{:S(2)}) %collective-permute-start.48) | collective-permute-done | bytes 28704 | tf_op jit(solution)/shard_map/ppermute | solution.py:339
  118.4 0.6 shard_map.93
  119.1 0.7 collective-permute-start.49
  119.7 2.9 %collective-permute-start.51 = (f32[56,128]{1,0:T(8,128)S(1)}, f32[56,128]{1,0:T(8,128)S(1)}, u32[]{:S(2)}, u32[]{:S(2)}) collective-permute-start(f32[56,128]{1,0:T(8,128)S(1)} %get-tuple-element.131), channel_id=1, source_target_pairs={{0,3},{1,2},{2,1},{3,0},{4,7},{5,6},{6,5},{7,4},{8,11},{9,10},{10,... | collective-permute-start | bytes 86024 | tf_op jit(solution)/shard_map/ppermute | solution.py:339
  122.6 3.0 %collective-permute-start.53 = (f32[56,128]{1,0:T(8,128)S(1)}, f32[56,128]{1,0:T(8,128)S(1)}, u32[]{:S(2)}, u32[]{:S(2)}) collective-permute-start(f32[56,128]{1,0:T(8,128)S(1)} %get-tuple-element.133), channel_id=1, source_target_pairs={{0,5},{1,4},{2,7},{3,6},{4,1},{5,0},{6,3},{7,2},{8,13},{9,12},{10,... | collective-permute-start | bytes 86024 | tf_op jit(solution)/shard_map/ppermute | solution.py:339
  126.0 4.3 %collective-permute-start.55 = (f32[56,128]{1,0:T(8,128)S(1)}, f32[56,128]{1,0:T(8,128)S(1)}, u32[]{:S(2)}, u32[]{:S(2)}) collective-permute-start(f32[56,128]{1,0:T(8,128)S(1)} %get-tuple-element.135), channel_id=1, source_target_pairs={{0,7},{1,6},{2,5},{3,4},{4,3},{5,2},{6,1},{7,0},{8,15},{9,14},{10,... | collective-permute-start | bytes 86024 | tf_op jit(solution)/shard_map/ppermute | solution.py:339
  130.3 4.8 %shard_map.95 = f32[6,16,16,128]{3,2,1,0:T(8,128)} custom-call(s32[1]{0:T(128)} %bitcast.place, s32[8]{0:T(128)S(1)} %copy-done.2, s32[48]{0:T(128)S(1)} %reshape.17.orientation, f32[108]{0:T(128)S(1)} %reshape.18.mats, f32[6,16,16,128]{3,2,1,0:T(8,128)S(1)} %get-tuple-element.86.block, f32[16,16,128]{2,1,0:T(8,128)S(1)} %bitcast.8, ...), custom_call_target="tpu_custom_call" | custom-call | flops 14155776 | bytes 3145728 | tf_op jit(solution)/shard_map/pallas_call | solution.py:381
  135.1 6.5 %shard_map.94 = f32[6,16,16,128]{3,2,1,0:T(8,128)} custom-call(s32[1]{0:T(128)} %bitcast.place, s32[8]{0:T(128)S(1)} %copy-done.2, s32[48]{0:T(128)S(1)} %reshape.17.orientation, f32[108]{0:T(128)S(1)} %reshape.18.mats, f32[6,16,16,128]{3,2,1,0:T(8,128)S(1)} %get-tuple-element.69.block, f32[6,16,16,128]{3,2,1,0:T(8,128)S(1)} %get-tuple-element.119.grads, ...), custom_call_target="tpu_custom_call" | custom-call | flops 28311552 | bytes 3145728 | tf_op jit(solution)/shard_map/pallas_call | solution.py:384
  (90 shorter events, 5.9 us)
Async XLA Ops:
  11.6 7.4 %collective-permute-start = (f32[56,128]{1,0:T(8,128)S(1)}, f32[56,128]{1,0:T(8,128)S(1)}, u32[]{:S(2)}, u32[]{:S(2)}) collective-permute-start(f32[56,128]{1,0:T(8,128)S(1)} %get-tuple-element.71), channel_id=1, source_target_pairs={{0,1},{1,0},{2,3},{3,2},{4,5},{5,4},{6,7},{7,6},{8,9},{9,8},{10,11... | collective-permute-start | bytes 86024 | tf_op jit(solution)/shard_map/ppermute | solution.py:339
  13.2 9.5 %collective-permute-start.1 = (f32[56,128]{1,0:T(8,128)S(1)}, f32[56,128]{1,0:T(8,128)S(1)}, u32[]{:S(2)}, u32[]{:S(2)}) collective-permute-start(f32[56,128]{1,0:T(8,128)S(1)} %get-tuple-element.72), channel_id=1, source_target_pairs={{0,2},{1,3},{2,0},{3,1},{4,6},{5,7},{6,4},{7,5},{8,10},{9,11},{10,... | collective-permute-start | bytes 86024 | tf_op jit(solution)/shard_map/ppermute | solution.py:339
  14.8 8.1 %collective-permute-start.2 = (f32[56,128]{1,0:T(8,128)S(1)}, f32[56,128]{1,0:T(8,128)S(1)}, u32[]{:S(2)}, u32[]{:S(2)}) collective-permute-start(f32[56,128]{1,0:T(8,128)S(1)} %get-tuple-element.73), channel_id=1, source_target_pairs={{0,3},{1,2},{2,1},{3,0},{4,7},{5,6},{6,5},{7,4},{8,11},{9,10},{10,... | collective-permute-start | bytes 86024 | tf_op jit(solution)/shard_map/ppermute | solution.py:339
  15.2 7.7 %collective-permute-start.3 = (f32[56,128]{1,0:T(8,128)S(1)}, f32[56,128]{1,0:T(8,128)S(1)}, u32[]{:S(2)}, u32[]{:S(2)}) collective-permute-start(f32[56,128]{1,0:T(8,128)S(1)} %get-tuple-element.74), channel_id=1, source_target_pairs={{0,4},{1,5},{2,6},{3,7},{4,0},{5,1},{6,2},{7,3},{8,12},{9,13},{10,... | collective-permute-start | bytes 86024 | tf_op jit(solution)/shard_map/ppermute | solution.py:339
  22.7 6.6 %collective-permute-start.6 = (f32[56,128]{1,0:T(8,128)S(1)}, f32[56,128]{1,0:T(8,128)S(1)}, u32[]{:S(2)}, u32[]{:S(2)}) collective-permute-start(f32[56,128]{1,0:T(8,128)S(1)} %get-tuple-element.77), channel_id=1, source_target_pairs={{0,7},{1,6},{2,5},{3,4},{4,3},{5,2},{6,1},{7,0},{8,15},{9,14},{10,... | collective-permute-start | bytes 86024 | tf_op jit(solution)/shard_map/ppermute | solution.py:339
  29.9 6.4 %collective-permute-start.7 = (f32[56,128]{1,0:T(8,128)S(1)}, f32[56,128]{1,0:T(8,128)S(1)}, u32[]{:S(2)}, u32[]{:S(2)}) collective-permute-start(f32[56,128]{1,0:T(8,128)S(1)} %get-tuple-element.79), channel_id=1, source_target_pairs={{0,1},{1,0},{2,3},{3,2},{4,5},{5,4},{6,7},{7,6},{8,9},{9,8},{10,11... | collective-permute-start | bytes 86024 | tf_op jit(solution)/shard_map/ppermute | solution.py:339
  30.5 11.3 %collective-permute-start.9 = (f32[56,128]{1,0:T(8,128)S(1)}, f32[56,128]{1,0:T(8,128)S(1)}, u32[]{:S(2)}, u32[]{:S(2)}) collective-permute-start(f32[56,128]{1,0:T(8,128)S(1)} %get-tuple-element.81), channel_id=1, source_target_pairs={{0,3},{1,2},{2,1},{3,0},{4,7},{5,6},{6,5},{7,4},{8,11},{9,10},{10,... | collective-permute-start | bytes 86024 | tf_op jit(solution)/shard_map/ppermute | solution.py:339
  33.4 8.9 %collective-permute-start.10 = (f32[56,128]{1,0:T(8,128)S(1)}, f32[56,128]{1,0:T(8,128)S(1)}, u32[]{:S(2)}, u32[]{:S(2)}) collective-permute-start(f32[56,128]{1,0:T(8,128)S(1)} %get-tuple-element.82), channel_id=1, source_target_pairs={{0,4},{1,5},{2,6},{3,7},{4,0},{5,1},{6,2},{7,3},{8,12},{9,13},{10,... | collective-permute-start | bytes 86024 | tf_op jit(solution)/shard_map/ppermute | solution.py:339
  33.4 8.9 %collective-permute-start.11 = (f32[56,128]{1,0:T(8,128)S(1)}, f32[56,128]{1,0:T(8,128)S(1)}, u32[]{:S(2)}, u32[]{:S(2)}) collective-permute-start(f32[56,128]{1,0:T(8,128)S(1)} %get-tuple-element.83), channel_id=1, source_target_pairs={{0,5},{1,4},{2,7},{3,6},{4,1},{5,0},{6,3},{7,2},{8,13},{9,12},{10,... | collective-permute-start | bytes 86024 | tf_op jit(solution)/shard_map/ppermute | solution.py:339
  36.3 9.2 %collective-permute-start.12 = (f32[56,128]{1,0:T(8,128)S(1)}, f32[56,128]{1,0:T(8,128)S(1)}, u32[]{:S(2)}, u32[]{:S(2)}) collective-permute-start(f32[56,128]{1,0:T(8,128)S(1)} %get-tuple-element.84), channel_id=1, source_target_pairs={{0,6},{1,7},{2,4},{3,5},{4,2},{5,3},{6,0},{7,1},{8,14},{9,15},{10,... | collective-permute-start | bytes 86024 | tf_op jit(solution)/shard_map/ppermute | solution.py:339
  36.7 8.9 %collective-permute-start.13 = (f32[56,128]{1,0:T(8,128)S(1)}, f32[56,128]{1,0:T(8,128)S(1)}, u32[]{:S(2)}, u32[]{:S(2)}) collective-permute-start(f32[56,128]{1,0:T(8,128)S(1)} %get-tuple-element.85), channel_id=1, source_target_pairs={{0,7},{1,6},{2,5},{3,4},{4,3},{5,2},{6,1},{7,0},{8,15},{9,14},{10,... | collective-permute-start | bytes 86024 | tf_op jit(solution)/shard_map/ppermute | solution.py:339
  41.7 11.1 %collective-permute-start.28 = (f32[56,128]{1,0:T(8,128)S(1)}, f32[56,128]{1,0:T(8,128)S(1)}, u32[]{:S(2)}, u32[]{:S(2)}) collective-permute-start(f32[56,128]{1,0:T(8,128)S(1)} %get-tuple-element.104), channel_id=1, source_target_pairs={{0,1},{1,0},{2,3},{3,2},{4,5},{5,4},{6,7},{7,6},{8,9},{9,8},{10,11... | collective-permute-start | bytes 86024 | tf_op jit(solution)/shard_map/ppermute | solution.py:339
  42.3 11.0 %collective-permute-start.29 = (f32[56,128]{1,0:T(8,128)S(1)}, f32[56,128]{1,0:T(8,128)S(1)}, u32[]{:S(2)}, u32[]{:S(2)}) collective-permute-start(f32[56,128]{1,0:T(8,128)S(1)} %get-tuple-element.105), channel_id=1, source_target_pairs={{0,2},{1,3},{2,0},{3,1},{4,6},{5,7},{6,4},{7,5},{8,10},{9,11},{10,... | collective-permute-start | bytes 86024 | tf_op jit(solution)/shard_map/ppermute | solution.py:339
  42.3 15.4 %collective-permute-start.30 = (f32[56,128]{1,0:T(8,128)S(1)}, f32[56,128]{1,0:T(8,128)S(1)}, u32[]{:S(2)}, u32[]{:S(2)}) collective-permute-start(f32[56,128]{1,0:T(8,128)S(1)} %get-tuple-element.106), channel_id=1, source_target_pairs={{0,3},{1,2},{2,1},{3,0},{4,7},{5,6},{6,5},{7,4},{8,11},{9,10},{10,... | collective-permute-start | bytes 86024 | tf_op jit(solution)/shard_map/ppermute | solution.py:339
  45.5 12.7 %collective-permute-start.31 = (f32[56,128]{1,0:T(8,128)S(1)}, f32[56,128]{1,0:T(8,128)S(1)}, u32[]{:S(2)}, u32[]{:S(2)}) collective-permute-start(f32[56,128]{1,0:T(8,128)S(1)} %get-tuple-element.107), channel_id=1, source_target_pairs={{0,4},{1,5},{2,6},{3,7},{4,0},{5,1},{6,2},{7,3},{8,12},{9,13},{10,... | collective-permute-start | bytes 86024 | tf_op jit(solution)/shard_map/ppermute | solution.py:339
  45.6 12.6 %collective-permute-start.32 = (f32[56,128]{1,0:T(8,128)S(1)}, f32[56,128]{1,0:T(8,128)S(1)}, u32[]{:S(2)}, u32[]{:S(2)}) collective-permute-start(f32[56,128]{1,0:T(8,128)S(1)} %get-tuple-element.108), channel_id=1, source_target_pairs={{0,5},{1,4},{2,7},{3,6},{4,1},{5,0},{6,3},{7,2},{8,13},{9,12},{10,... | collective-permute-start | bytes 86024 | tf_op jit(solution)/shard_map/ppermute | solution.py:339
  52.8 8.4 %collective-permute-start.33 = (f32[56,128]{1,0:T(8,128)S(1)}, f32[56,128]{1,0:T(8,128)S(1)}, u32[]{:S(2)}, u32[]{:S(2)}) collective-permute-start(f32[56,128]{1,0:T(8,128)S(1)} %get-tuple-element.109), channel_id=1, source_target_pairs={{0,6},{1,7},{2,4},{3,5},{4,2},{5,3},{6,0},{7,1},{8,14},{9,15},{10,... | collective-permute-start | bytes 86024 | tf_op jit(solution)/shard_map/ppermute | solution.py:339
  53.3 7.9 %collective-permute-start.34 = (f32[56,128]{1,0:T(8,128)S(1)}, f32[56,128]{1,0:T(8,128)S(1)}, u32[]{:S(2)}, u32[]{:S(2)}) collective-permute-start(f32[56,128]{1,0:T(8,128)S(1)} %get-tuple-element.110), channel_id=1, source_target_pairs={{0,7},{1,6},{2,5},{3,4},{4,3},{5,2},{6,1},{7,0},{8,15},{9,14},{10,... | collective-permute-start | bytes 86024 | tf_op jit(solution)/shard_map/ppermute | solution.py:339
  57.7 6.4 %collective-permute-start.14 = (f32[56,128]{1,0:T(8,128)S(1)}, f32[56,128]{1,0:T(8,128)S(1)}, u32[]{:S(2)}, u32[]{:S(2)}) collective-permute-start(f32[56,128]{1,0:T(8,128)S(1)} %get-tuple-element.88), channel_id=1, source_target_pairs={{0,1},{1,0},{2,3},{3,2},{4,5},{5,4},{6,7},{7,6},{8,9},{9,8},{10,11... | collective-permute-start | bytes 86024 | tf_op jit(solution)/shard_map/ppermute | solution.py:339
  58.2 6.2 %collective-permute-start.15 = (f32[56,128]{1,0:T(8,128)S(1)}, f32[56,128]{1,0:T(8,128)S(1)}, u32[]{:S(2)}, u32[]{:S(2)}) collective-permute-start(f32[56,128]{1,0:T(8,128)S(1)} %get-tuple-element.89), channel_id=1, source_target_pairs={{0,2},{1,3},{2,0},{3,1},{4,6},{5,7},{6,4},{7,5},{8,10},{9,11},{10,... | collective-permute-start | bytes 86024 | tf_op jit(solution)/shard_map/ppermute | solution.py:339
  58.2 11.3 %collective-permute-start.16 = (f32[56,128]{1,0:T(8,128)S(1)}, f32[56,128]{1,0:T(8,128)S(1)}, u32[]{:S(2)}, u32[]{:S(2)}) collective-permute-start(f32[56,128]{1,0:T(8,128)S(1)} %get-tuple-element.90), channel_id=1, source_target_pairs={{0,3},{1,2},{2,1},{3,0},{4,7},{5,6},{6,5},{7,4},{8,11},{9,10},{10,... | collective-permute-start | bytes 86024 | tf_op jit(solution)/shard_map/ppermute | solution.py:339
  61.2 8.9 %collective-permute-start.17 = (f32[56,128]{1,0:T(8,128)S(1)}, f32[56,128]{1,0:T(8,128)S(1)}, u32[]{:S(2)}, u32[]{:S(2)}) collective-permute-start(f32[56,128]{1,0:T(8,128)S(1)} %get-tuple-element.91), channel_id=1, source_target_pairs={{0,4},{1,5},{2,6},{3,7},{4,0},{5,1},{6,2},{7,3},{8,12},{9,13},{10,... | collective-permute-start | bytes 86024 | tf_op jit(solution)/shard_map/ppermute | solution.py:339
  61.2 8.9 %collective-permute-start.18 = (f32[56,128]{1,0:T(8,128)S(1)}, f32[56,128]{1,0:T(8,128)S(1)}, u32[]{:S(2)}, u32[]{:S(2)}) collective-permute-start(f32[56,128]{1,0:T(8,128)S(1)} %get-tuple-element.92), channel_id=1, source_target_pairs={{0,5},{1,4},{2,7},{3,6},{4,1},{5,0},{6,3},{7,2},{8,13},{9,12},{10,... | collective-permute-start | bytes 86024 | tf_op jit(solution)/shard_map/ppermute | solution.py:339
  64.1 9.0 %collective-permute-start.19 = (f32[56,128]{1,0:T(8,128)S(1)}, f32[56,128]{1,0:T(8,128)S(1)}, u32[]{:S(2)}, u32[]{:S(2)}) collective-permute-start(f32[56,128]{1,0:T(8,128)S(1)} %get-tuple-element.93), channel_id=1, source_target_pairs={{0,6},{1,7},{2,4},{3,5},{4,2},{5,3},{6,0},{7,1},{8,14},{9,15},{10,... | collective-permute-start | bytes 86024 | tf_op jit(solution)/shard_map/ppermute | solution.py:339
  64.4 8.7 %collective-permute-start.20 = (f32[56,128]{1,0:T(8,128)S(1)}, f32[56,128]{1,0:T(8,128)S(1)}, u32[]{:S(2)}, u32[]{:S(2)}) collective-permute-start(f32[56,128]{1,0:T(8,128)S(1)} %get-tuple-element.94), channel_id=1, source_target_pairs={{0,7},{1,6},{2,5},{3,4},{4,3},{5,2},{6,1},{7,0},{8,15},{9,14},{10,... | collective-permute-start | bytes 86024 | tf_op jit(solution)/shard_map/ppermute | solution.py:339
  69.5 7.1 %collective-permute-start.35 = (f32[56,128]{1,0:T(8,128)S(1)}, f32[56,128]{1,0:T(8,128)S(1)}, u32[]{:S(2)}, u32[]{:S(2)}) collective-permute-start(f32[56,128]{1,0:T(8,128)S(1)} %get-tuple-element.112), channel_id=1, source_target_pairs={{0,1},{1,0},{2,3},{3,2},{4,5},{5,4},{6,7},{7,6},{8,9},{9,8},{10,11... | collective-permute-start | bytes 86024 | tf_op jit(solution)/shard_map/ppermute | solution.py:339
  70.1 7.0 %collective-permute-start.36 = (f32[56,128]{1,0:T(8,128)S(1)}, f32[56,128]{1,0:T(8,128)S(1)}, u32[]{:S(2)}, u32[]{:S(2)}) collective-permute-start(f32[56,128]{1,0:T(8,128)S(1)} %get-tuple-element.113), channel_id=1, source_target_pairs={{0,2},{1,3},{2,0},{3,1},{4,6},{5,7},{6,4},{7,5},{8,10},{9,11},{10,... | collective-permute-start | bytes 86024 | tf_op jit(solution)/shard_map/ppermute | solution.py:339
  70.1 11.4 %collective-permute-start.37 = (f32[56,128]{1,0:T(8,128)S(1)}, f32[56,128]{1,0:T(8,128)S(1)}, u32[]{:S(2)}, u32[]{:S(2)}) collective-permute-start(f32[56,128]{1,0:T(8,128)S(1)} %get-tuple-element.114), channel_id=1, source_target_pairs={{0,3},{1,2},{2,1},{3,0},{4,7},{5,6},{6,5},{7,4},{8,11},{9,10},{10,... | collective-permute-start | bytes 86024 | tf_op jit(solution)/shard_map/ppermute | solution.py:339
  73.1 8.9 %collective-permute-start.38 = (f32[56,128]{1,0:T(8,128)S(1)}, f32[56,128]{1,0:T(8,128)S(1)}, u32[]{:S(2)}, u32[]{:S(2)}) collective-permute-start(f32[56,128]{1,0:T(8,128)S(1)} %get-tuple-element.115), channel_id=1, source_target_pairs={{0,4},{1,5},{2,6},{3,7},{4,0},{5,1},{6,2},{7,3},{8,12},{9,13},{10,... | collective-permute-start | bytes 86024 | tf_op jit(solution)/shard_map/ppermute | solution.py:339
  73.1 8.9 %collective-permute-start.39 = (f32[56,128]{1,0:T(8,128)S(1)}, f32[56,128]{1,0:T(8,128)S(1)}, u32[]{:S(2)}, u32[]{:S(2)}) collective-permute-start(f32[56,128]{1,0:T(8,128)S(1)} %get-tuple-element.116), channel_id=1, source_target_pairs={{0,5},{1,4},{2,7},{3,6},{4,1},{5,0},{6,3},{7,2},{8,13},{9,12},{10,... | collective-permute-start | bytes 86024 | tf_op jit(solution)/shard_map/ppermute | solution.py:339
  76.6 8.4 %collective-permute-start.40 = (f32[56,128]{1,0:T(8,128)S(1)}, f32[56,128]{1,0:T(8,128)S(1)}, u32[]{:S(2)}, u32[]{:S(2)}) collective-permute-start(f32[56,128]{1,0:T(8,128)S(1)} %get-tuple-element.117), channel_id=1, source_target_pairs={{0,6},{1,7},{2,4},{3,5},{4,2},{5,3},{6,0},{7,1},{8,14},{9,15},{10,... | collective-permute-start | bytes 86024 | tf_op jit(solution)/shard_map/ppermute | solution.py:339
  77.0 7.9 %collective-permute-start.41 = (f32[56,128]{1,0:T(8,128)S(1)}, f32[56,128]{1,0:T(8,128)S(1)}, u32[]{:S(2)}, u32[]{:S(2)}) collective-permute-start(f32[56,128]{1,0:T(8,128)S(1)} %get-tuple-element.118), channel_id=1, source_target_pairs={{0,7},{1,6},{2,5},{3,4},{4,3},{5,2},{6,1},{7,0},{8,15},{9,14},{10,... | collective-permute-start | bytes 86024 | tf_op jit(solution)/shard_map/ppermute | solution.py:339
  81.5 6.4 %collective-permute-start.21 = (f32[56,128]{1,0:T(8,128)S(1)}, f32[56,128]{1,0:T(8,128)S(1)}, u32[]{:S(2)}, u32[]{:S(2)}) collective-permute-start(f32[56,128]{1,0:T(8,128)S(1)} %get-tuple-element.96), channel_id=1, source_target_pairs={{0,1},{1,0},{2,3},{3,2},{4,5},{5,4},{6,7},{7,6},{8,9},{9,8},{10,11... | collective-permute-start | bytes 86024 | tf_op jit(solution)/shard_map/ppermute | solution.py:339
  82.0 10.6 %collective-permute-start.23 = (f32[56,128]{1,0:T(8,128)S(1)}, f32[56,128]{1,0:T(8,128)S(1)}, u32[]{:S(2)}, u32[]{:S(2)}) collective-permute-start(f32[56,128]{1,0:T(8,128)S(1)} %get-tuple-element.98), channel_id=1, source_target_pairs={{0,3},{1,2},{2,1},{3,0},{4,7},{5,6},{6,5},{7,4},{8,11},{9,10},{10,... | collective-permute-start | bytes 86024 | tf_op jit(solution)/shard_map/ppermute | solution.py:339
  85.0 7.7 %collective-permute-start.24 = (f32[56,128]{1,0:T(8,128)S(1)}, f32[56,128]{1,0:T(8,128)S(1)}, u32[]{:S(2)}, u32[]{:S(2)}) collective-permute-start(f32[56,128]{1,0:T(8,128)S(1)} %get-tuple-element.99), channel_id=1, source_target_pairs={{0,4},{1,5},{2,6},{3,7},{4,0},{5,1},{6,2},{7,3},{8,12},{9,13},{10,... | collective-permute-start | bytes 86024 | tf_op jit(solution)/shard_map/ppermute | solution.py:339
  85.0 7.7 %collective-permute-start.25 = (f32[56,128]{1,0:T(8,128)S(1)}, f32[56,128]{1,0:T(8,128)S(1)}, u32[]{:S(2)}, u32[]{:S(2)}) collective-permute-start(f32[56,128]{1,0:T(8,128)S(1)} %get-tuple-element.100), channel_id=1, source_target_pairs={{0,5},{1,4},{2,7},{3,6},{4,1},{5,0},{6,3},{7,2},{8,13},{9,12},{10,... | collective-permute-start | bytes 86024 | tf_op jit(solution)/shard_map/ppermute | solution.py:339
  88.2 6.6 %collective-permute-start.27 = (f32[56,128]{1,0:T(8,128)S(1)}, f32[56,128]{1,0:T(8,128)S(1)}, u32[]{:S(2)}, u32[]{:S(2)}) collective-permute-start(f32[56,128]{1,0:T(8,128)S(1)} %get-tuple-element.102), channel_id=1, source_target_pairs={{0,7},{1,6},{2,5},{3,4},{4,3},{5,2},{6,1},{7,0},{8,15},{9,14},{10,... | collective-permute-start | bytes 86024 | tf_op jit(solution)/shard_map/ppermute | solution.py:339
  100.9 7.4 %collective-permute-start.42 = (f32[56,128]{1,0:T(8,128)S(1)}, f32[56,128]{1,0:T(8,128)S(1)}, u32[]{:S(2)}, u32[]{:S(2)}) collective-permute-start(f32[56,128]{1,0:T(8,128)S(1)} %get-tuple-element.121), channel_id=1, source_target_pairs={{0,1},{1,0},{2,3},{3,2},{4,5},{5,4},{6,7},{7,6},{8,9},{9,8},{10,11... | collective-permute-start | bytes 86024 | tf_op jit(solution)/shard_map/ppermute | solution.py:339
  102.5 9.4 %collective-permute-start.43 = (f32[56,128]{1,0:T(8,128)S(1)}, f32[56,128]{1,0:T(8,128)S(1)}, u32[]{:S(2)}, u32[]{:S(2)}) collective-permute-start(f32[56,128]{1,0:T(8,128)S(1)} %get-tuple-element.122), channel_id=1, source_target_pairs={{0,2},{1,3},{2,0},{3,1},{4,6},{5,7},{6,4},{7,5},{8,10},{9,11},{10,... | collective-permute-start | bytes 86024 | tf_op jit(solution)/shard_map/ppermute | solution.py:339
  102.5 9.7 %collective-permute-start.44 = (f32[56,128]{1,0:T(8,128)S(1)}, f32[56,128]{1,0:T(8,128)S(1)}, u32[]{:S(2)}, u32[]{:S(2)}) collective-permute-start(f32[56,128]{1,0:T(8,128)S(1)} %get-tuple-element.123), channel_id=1, source_target_pairs={{0,3},{1,2},{2,1},{3,0},{4,7},{5,6},{6,5},{7,4},{8,11},{9,10},{10,... | collective-permute-start | bytes 86024 | tf_op jit(solution)/shard_map/ppermute | solution.py:339
  104.5 7.7 %collective-permute-start.45 = (f32[56,128]{1,0:T(8,128)S(1)}, f32[56,128]{1,0:T(8,128)S(1)}, u32[]{:S(2)}, u32[]{:S(2)}) collective-permute-start(f32[56,128]{1,0:T(8,128)S(1)} %get-tuple-element.124), channel_id=1, source_target_pairs={{0,4},{1,5},{2,6},{3,7},{4,0},{5,1},{6,2},{7,3},{8,12},{9,13},{10,... | collective-permute-start | bytes 86024 | tf_op jit(solution)/shard_map/ppermute | solution.py:339
  111.9 6.6 %collective-permute-start.48 = (f32[56,128]{1,0:T(8,128)S(1)}, f32[56,128]{1,0:T(8,128)S(1)}, u32[]{:S(2)}, u32[]{:S(2)}) collective-permute-start(f32[56,128]{1,0:T(8,128)S(1)} %get-tuple-element.127), channel_id=1, source_target_pairs={{0,7},{1,6},{2,5},{3,4},{4,3},{5,2},{6,1},{7,0},{8,15},{9,14},{10,... | collective-permute-start | bytes 86024 | tf_op jit(solution)/shard_map/ppermute | solution.py:339
  119.1 6.5 %collective-permute-start.49 = (f32[56,128]{1,0:T(8,128)S(1)}, f32[56,128]{1,0:T(8,128)S(1)}, u32[]{:S(2)}, u32[]{:S(2)}) collective-permute-start(f32[56,128]{1,0:T(8,128)S(1)} %get-tuple-element.129), channel_id=1, source_target_pairs={{0,1},{1,0},{2,3},{3,2},{4,5},{5,4},{6,7},{7,6},{8,9},{9,8},{10,11... | collective-permute-start | bytes 86024 | tf_op jit(solution)/shard_map/ppermute | solution.py:339
  119.7 15.3 %collective-permute-start.51 = (f32[56,128]{1,0:T(8,128)S(1)}, f32[56,128]{1,0:T(8,128)S(1)}, u32[]{:S(2)}, u32[]{:S(2)}) collective-permute-start(f32[56,128]{1,0:T(8,128)S(1)} %get-tuple-element.131), channel_id=1, source_target_pairs={{0,3},{1,2},{2,1},{3,0},{4,7},{5,6},{6,5},{7,4},{8,11},{9,10},{10,... | collective-permute-start | bytes 86024 | tf_op jit(solution)/shard_map/ppermute | solution.py:339
  122.6 12.4 %collective-permute-start.52 = (f32[56,128]{1,0:T(8,128)S(1)}, f32[56,128]{1,0:T(8,128)S(1)}, u32[]{:S(2)}, u32[]{:S(2)}) collective-permute-start(f32[56,128]{1,0:T(8,128)S(1)} %get-tuple-element.132), channel_id=1, source_target_pairs={{0,4},{1,5},{2,6},{3,7},{4,0},{5,1},{6,2},{7,3},{8,12},{9,13},{10,... | collective-permute-start | bytes 86024 | tf_op jit(solution)/shard_map/ppermute | solution.py:339
  122.6 12.4 %collective-permute-start.53 = (f32[56,128]{1,0:T(8,128)S(1)}, f32[56,128]{1,0:T(8,128)S(1)}, u32[]{:S(2)}, u32[]{:S(2)}) collective-permute-start(f32[56,128]{1,0:T(8,128)S(1)} %get-tuple-element.133), channel_id=1, source_target_pairs={{0,5},{1,4},{2,7},{3,6},{4,1},{5,0},{6,3},{7,2},{8,13},{9,12},{10,... | collective-permute-start | bytes 86024 | tf_op jit(solution)/shard_map/ppermute | solution.py:339
  125.6 9.5 %collective-permute-start.54 = (f32[56,128]{1,0:T(8,128)S(1)}, f32[56,128]{1,0:T(8,128)S(1)}, u32[]{:S(2)}, u32[]{:S(2)}) collective-permute-start(f32[56,128]{1,0:T(8,128)S(1)} %get-tuple-element.134), channel_id=1, source_target_pairs={{0,6},{1,7},{2,4},{3,5},{4,2},{5,3},{6,0},{7,1},{8,14},{9,15},{10,... | collective-permute-start | bytes 86024 | tf_op jit(solution)/shard_map/ppermute | solution.py:339
  126.0 9.1 %collective-permute-start.55 = (f32[56,128]{1,0:T(8,128)S(1)}, f32[56,128]{1,0:T(8,128)S(1)}, u32[]{:S(2)}, u32[]{:S(2)}) collective-permute-start(f32[56,128]{1,0:T(8,128)S(1)} %get-tuple-element.135), channel_id=1, source_target_pairs={{0,7},{1,6},{2,5},{3,4},{4,3},{5,2},{6,1},{7,0},{8,15},{9,14},{10,... | collective-permute-start | bytes 86024 | tf_op jit(solution)/shard_map/ppermute | solution.py:339
  (14 other events, 148.5 us)

commit v3 on v1

v3 whole, which is shorter than its diff:
```python
import functools

import jax
import jax.numpy as jnp
from jax import lax
from jax.experimental import pallas as pl
from jax.experimental.pallas import tpu as pltpu
from jax.sharding import PartitionSpec as P

STEPS = 2
time_step = 0.05
damping = 0.015

PAD = 8
VMEM = pl.BlockSpec(memory_space=pltpu.VMEM)
SMEM = pl.BlockSpec(memory_space=pltpu.SMEM)
VMEM_LIMIT = 32 * 1024 * 1024


class Geometry:
    def __init__(self, nvars, cx, cy, cz, count):
        self.v, self.x, self.y, self.z, self.n = nvars, cx, cy, cz, count
        self.rows = [nvars * cy] * 2 + [nvars * cx] * 2 + [cy] * 2
        self.runs = [-(-rows // count) for rows in self.rows]
        self.starts = [sum(self.runs[:side]) for side in range(6)]
        self.field = sum(self.runs)
        self.face_rows = -(-max(run * count for run in self.runs) // 8) * 8
        self.block = (nvars, cx, cy, cz)
        self.tall = (nvars, cx, cy + 2 * PAD, cz)
        self.faces = (6, self.face_rows, cz)
        self.rate_faces = (6, max(cx, cy), cz)

    def buffer(self, fields):
        return (self.n, -(-fields * self.field // 8) * 8, self.z)


def take_z_faces(geo, load):
    v, x, y, z = geo.block
    lane = lax.broadcasted_iota(jnp.int32, (y, z), 1)
    high = jnp.zeros((y, z), jnp.float32)
    low = jnp.zeros((y, z), jnp.float32)
    for var in range(v):
        for plane in range(x):
            place = var * x + plane
            tile = load(var, plane)
            here = lane == place
            high = jnp.where(here, pltpu.roll(tile, (place + 1) % z, 1), high)
            low = jnp.where(here, pltpu.roll(tile, place, 1) if place else tile, low)
    return high, low


def take_xy_faces(geo, source, faces):
    v, x, y, z = geo.block
    faces[0, : v * y] = source[:, x - 1].reshape(v * y, z)
    faces[1, : v * y] = source[:, 0].reshape(v * y, z)
    for var in range(v):
        faces[2, var * x : (var + 1) * x] = source[var, :, y - 1, :]
        faces[3, var * x : (var + 1) * x] = source[var, :, 0, :]


def cut(geo, faces, buffer, field):
    for side in range(6):
        run, start = geo.runs[side], field * geo.field + geo.starts[side]
        for slot in range(geo.n):
            buffer[slot, start : start + run] = faces[side, slot * run : (slot + 1) * run]


def own_codes(geo, place, owner, orientation):
    block = jnp.int32(0)
    for index in range(geo.n):
        block = jnp.where(owner[index] == place[0], index, block)
    return [orientation[block * 6 + side] for side in range(6)]


def flip_rows(values, flag, length):
    rows, z = values.shape
    grouped = values.reshape(rows // length, length // 8, 8, z)
    index = lax.broadcasted_iota(jnp.int32, (8, z), 0)
    index = jnp.where(flag == 1, 7 - index, index)
    tiles = length // 8
    out = []
    for group in range(rows // length):
        for tile in range(tiles):
            picked = jnp.where(flag == 1, grouped[group, tiles - 1 - tile], grouped[group, tile])
            out.append(jnp.take_along_axis(picked, index, axis=0))
    return jnp.stack(out).reshape(rows, z)


def flip_lanes(values, flag, length):
    rows, z = values.shape
    lane = lax.broadcasted_iota(jnp.int32, (8, z), 1)
    within = lax.rem(lane, length)
    index = jnp.where(flag == 1, lane + (length - 1) - 2 * within, lane)
    index = jnp.minimum(index, z - 1)
    tiles = values.reshape(rows // 8, 8, z)
    return jnp.stack(
        [jnp.take_along_axis(tiles[tile], index, axis=1) for tile in range(rows // 8)]
    ).reshape(rows, z)


def unpack(geo, codes, buffer, field, raw, ghosts):
    v, x, y, z = geo.block
    for side in range(6):
        run, start = geo.runs[side], field * geo.field + geo.starts[side]
        for slot in range(geo.n):
            raw[side, slot * run : (slot + 1) * run] = buffer[slot, start : start + run]
    for side in range(6):
        first, second = codes[side] & 1, (codes[side] >> 1) & 1
        layer = raw[side, : geo.rows[side]]
        if side < 4:
            layer = flip_lanes(flip_rows(layer, first, y if side < 2 else x), second, z)
        else:
            layer = flip_lanes(flip_rows(layer, second, y), first, x)
        ghosts[side, : geo.rows[side]] = layer


def face_values(geo, faces, side):
    v, x, y, z = geo.block
    if side < 4:
        depth = y if side < 2 else x
        return [faces[side, var * depth : (var + 1) * depth] for var in range(v)]
    layer = faces[side, :y]
    return [layer] + [pltpu.roll(layer, z - var * x, 1) for var in range(1, v)]


def add_xy_terms(geo, side, terms, result):
    v, x, y, z = geo.block
    for var in range(v):
        if side < 2:
            plane = x - 1 if side == 0 else 0
            result[var, plane] = result[var, plane] + terms[var]
        else:
            row = y - 1 if side == 2 else 0
            result[var, :, row, :] = result[var, :, row, :] + terms[var]


def add_z_terms(geo, high_terms, low_terms, result):
    v, x, y, z = geo.block
    lane = lax.broadcasted_iota(jnp.int32, (y, z), 1)
    zero = jnp.zeros((y, z), jnp.float32)
    for var in range(v):
        for plane in range(x):
            high = pltpu.roll(high_terms[var], z - 1 - plane, 1)
            low = pltpu.roll(low_terms[var], z - plane, 1) if plane else low_terms[var]
            change = jnp.where(lane == z - 1, high, jnp.where(lane == 0, low, zero))
            result[var, plane] = result[var, plane] + change


def fill_tall(geo, source, tall):
    v, x, y, z = geo.block
    tall[:, :, PAD : PAD + y, :] = source[...]
    for var in range(v):
        tall[var, :, PAD - 1, :] = source[var, :, 0, :]
        tall[var, :, PAD + y, :] = source[var, :, y - 1, :]


def around(geo, tall, plane):
    v, x, y, z = geo.block
    lane = lax.broadcasted_iota(jnp.int32, (y, z), 1)
    before, after = jnp.maximum(plane - 1, 0), jnp.minimum(plane + 1, x - 1)
    cells, low, high = [], [[], [], []], [[], [], []]
    for var in range(v):
        mid = tall[var, plane, PAD : PAD + y]
        cells.append(mid)
        low[0].append(tall[var, before, PAD : PAD + y])
        high[0].append(tall[var, after, PAD : PAD + y])
        low[1].append(tall[var, plane, PAD - 1 : PAD - 1 + y])
        high[1].append(tall[var, plane, PAD + 1 : PAD + 1 + y])
        low[2].append(jnp.where(lane == 0, mid, pltpu.roll(mid, 1, 1)))
        high[2].append(jnp.where(lane == z - 1, mid, pltpu.roll(mid, z - 1, 1)))
    return cells, low, high


def flux_entry(geo, mats, direction, row, column):
    return mats[(direction * geo.v + row) * geo.v + column]


def step_plane(geo, mats, cells, low, high, rate):
    v = geo.v
    total = [None] * v
    for direction in range(3):
        lows, highs = low[direction], high[direction]
        mean_low = 0.5 * (lows[0] + cells[0])
        mean_high = 0.5 * (cells[0] + highs[0])
        square_low = 1.0 + mean_low * mean_low
        square_high = 1.0 + mean_high * mean_high
        spread_low = square_low * lax.rsqrt(square_low)
        spread_high = square_high * lax.rsqrt(square_high)
        slopes = [highs[var] - lows[var] for var in range(v)]
        for var in range(v):
            term = spread_low * (cells[var] - lows[var]) - spread_high * (highs[var] - cells[var])
            for column in range(v):
                term = term + flux_entry(geo, mats, direction, var, column) * slopes[column]
            total[var] = term if total[var] is None else total[var] + term
    scale = (0.5 * time_step) * rate
    return [cells[var] - scale * total[var] - damping * jnp.tanh(cells[var]) for var in range(v)]


def adjoint_plane(geo, mats, cells, low, high, grads, weight, weight_low, weight_high):
    v = geo.v
    total = [None] * v
    extra = None
    for direction in range(3):
        spreads, steps = [], []
        for lower, upper, lower_weight, upper_weight in (
            (low[direction], cells, weight_low[direction], weight),
            (cells, high[direction], weight, weight_high[direction]),
        ):
            mean = 0.5 * (lower[0] + upper[0])
            square = 1.0 + mean * mean
            inverse = lax.rsqrt(square)
            jump = [lower_weight[var] - upper_weight[var] for var in range(v)]
            product = jump[0] * (upper[0] - lower[0])
            for var in range(1, v):
                product = product + jump[var] * (upper[var] - lower[var])
            product = product * (mean * inverse)
            extra = product if extra is None else extra + product
            spreads.append(square * inverse)
            steps.append(jump)
        slopes = [steps[0][var] + steps[1][var] for var in range(v)]
        for var in range(v):
            term = spreads[1] * steps[1][var] - spreads[0] * steps[0][var]
            for row in range(v):
                term = term + flux_entry(geo, mats, direction, row, var) * slopes[row]
            total[var] = term if total[var] is None else total[var] + term
    total[0] = total[0] - 0.5 * extra
    out = []
    for var in range(v):
        bend = jnp.tanh(cells[var])
        slope = (1.0 - damping) + damping * (bend * bend)
        out.append(grads[var] * slope - (0.5 * time_step) * total[var])
    return out


def step_face(geo, mats, side, cells, ghosts, rate):
    v = geo.v
    mean = 0.5 * (cells[0] + ghosts[0])
    square = 1.0 + mean * mean
    spread = square * lax.rsqrt(square)
    gap = [ghosts[var] - cells[var] for var in range(v)]
    scale = (0.5 * time_step) * rate
    out = []
    for var in range(v):
        total = flux_entry(geo, mats, side // 2, var, 0) * gap[0]
        for column in range(1, v):
            total = total + flux_entry(geo, mats, side // 2, var, column) * gap[column]
        if side % 2 == 0:
            out.append(scale * (spread * gap[var] - total))
        else:
            out.append(scale * (spread * gap[var] + total))
    return out


def adjoint_face(geo, mats, side, cells, ghosts, weight, ghost_weight):
    v = geo.v
    mean = 0.5 * (cells[0] + ghosts[0])
    square = 1.0 + mean * mean
    inverse = lax.rsqrt(square)
    spread = square * inverse
    jump = [weight[var] - ghost_weight[var] for var in range(v)]
    product = jump[0] * (ghosts[0] - cells[0])
    for var in range(1, v):
        product = product + jump[var] * (ghosts[var] - cells[var])
    product = (0.5 * product) * (mean * inverse)
    out = []
    for var in range(v):
        total = flux_entry(geo, mats, side // 2, 0, var) * jump[0]
        for row in range(1, v):
            total = total + flux_entry(geo, mats, side // 2, row, var) * jump[row]
        if side % 2 == 0:
            total = spread * jump[var] + total
        else:
            total = spread * jump[var] - total
        if var == 0:
            total = total - product
        out.append((-0.5 * time_step) * total)
    return out


def pack_kernel(geo, gathered, grads, rate, state, faces, weight_faces, rate_faces, buffer, weight):
    v, x, y, z = geo.block
    parts, depth = gathered.shape[0], gathered.shape[2]
    for part in range(parts):
        state[:, part * depth : (part + 1) * depth] = gathered[part]
    take_xy_faces(geo, state, faces)
    high, low = take_z_faces(geo, lambda var, plane: state[var, plane])
    faces[4, :y] = high
    faces[5, :y] = low
    cut(geo, faces, buffer, 0)
    rate_faces[0, :y] = rate[x - 1]
    rate_faces[1, :y] = rate[0]
    rate_faces[2, :x] = rate[:, y - 1, :]
    rate_faces[3, :x] = rate[:, 0, :]
    high, low = take_z_faces(geo, lambda var, plane: rate[plane])
    rate_faces[4, :y] = high
    rate_faces[5, :y] = low

    def body(plane, carry):
        for var in range(v):
            weight[var, plane] = rate[plane] * grads[var, plane]
        return carry

    lax.fori_loop(0, x, body, 0)
    take_xy_faces(geo, weight, weight_faces)
    high, low = take_z_faces(geo, lambda var, plane: weight[var, plane])
    weight_faces[4, :y] = high
    weight_faces[5, :y] = low
    cut(geo, weight_faces, buffer, 1)


def route_kernel(geo, fields, owner, neighbours, arrived, leaving):
    for block in range(geo.n):
        target = owner[block]
        for side in range(6):
            source = owner[neighbours[block * 6 + side]]
            for field in range(fields):
                run, base = geo.runs[side], field * geo.field
                start, far = base + geo.starts[side], base + geo.starts[side ^ 1]
                leaving[target, start : start + run] = arrived[source, far : far + run]


def step_inner_kernel(geo, mats, block, rate, result, tall):
    fill_tall(geo, block, tall)

    def body(plane, carry):
        cells, low, high = around(geo, tall, plane)
        for var, value in enumerate(step_plane(geo, mats, cells, low, high, rate[plane])):
            result[var, plane] = value
        return carry

    lax.fori_loop(0, geo.x, body, 0)


def adjoint_inner_kernel(geo, mats, block, grads, rate, result, tall, weights):
    v, x, y, z = geo.block
    fill_tall(geo, block, tall)

    def scale(plane, carry):
        for var in range(v):
            weights[var, plane, PAD : PAD + y] = rate[plane] * grads[var, plane]
        return carry

    lax.fori_loop(0, x, scale, 0)
    for var in range(v):
        weights[var, :, PAD - 1, :] = weights[var, :, PAD, :]
        weights[var, :, PAD + y, :] = weights[var, :, PAD + y - 1, :]

    def body(plane, carry):
        cells, low, high = around(geo, tall, plane)
        weight, weight_low, weight_high = around(geo, weights, plane)
        here = [grads[var, plane] for var in range(v)]
        values = adjoint_plane(geo, mats, cells, low, high, here, weight, weight_low, weight_high)
        for var, value in enumerate(values):
            result[var, plane] = value
        return carry

    lax.fori_loop(0, x, body, 0)


def step_edge_kernel(geo, packed, place, owner, orientation, mats, inner, faces, rate_faces, buffer, result, *rest):
    if packed:
        new_faces, sent, raw, ghosts = rest
    else:
        raw, ghosts = rest
    v, x, y, z = geo.block
    unpack(geo, own_codes(geo, place, owner, orientation), buffer, 0, raw, ghosts)
    result[...] = inner[...]
    terms = []
    for side in range(6):
        depth = y if side < 2 or side > 3 else x
        cells, outer = face_values(geo, faces, side), face_values(geo, ghosts, side)
        values = step_face(geo, mats, side, cells, outer, rate_faces[side, :depth])
        if side < 4:
            add_xy_terms(geo, side, values, result)
        else:
            terms.append(values)
    add_z_terms(geo, *terms, result)
    if packed:
        take_xy_faces(geo, result, new_faces)
        high, low = take_z_faces(geo, lambda var, plane: result[var, plane])
        new_faces[4, :y] = high
        new_faces[5, :y] = low
        cut(geo, new_faces, sent, 0)


def adjoint_edge_kernel(
    geo, packed, weight_field, place, owner, orientation, mats, inner, faces, weight_faces, *rest
):
    rate_faces, buffer, weight_buffer, result = rest[:4]
    if packed:
        new_faces, sent, raw, ghosts, weight_ghosts = rest[4:]
    else:
        raw, ghosts, weight_ghosts = rest[4:]
    v, x, y, z = geo.block
    codes = own_codes(geo, place, owner, orientation)
    unpack(geo, codes, buffer, 0, raw, ghosts)
    unpack(geo, codes, weight_buffer, weight_field, raw, weight_ghosts)
    result[...] = inner[...]
    terms = []
    for side in range(6):
        views = [face_values(geo, field, side) for field in (faces, ghosts, weight_faces, weight_ghosts)]
        values = adjoint_face(geo, mats, side, *views)
        if side < 4:
            add_xy_terms(geo, side, values, result)
        else:
            terms.append(values)
    add_z_terms(geo, *terms, result)
    if packed:
        take_xy_faces(geo, result, new_faces)
        high, low = take_z_faces(geo, lambda var, plane: result[var, plane])
        for side in range(4):
            depth = y if side < 2 else x
            for var in range(v):
                here = slice(var * depth, (var + 1) * depth)
                new_faces[side, here] = new_faces[side, here] * rate_faces[side, :depth]
        new_faces[4, :y] = high * rate_faces[4, :y]
        new_faces[5, :y] = low * rate_faces[5, :y]
        cut(geo, new_faces, sent, 0)


def call(kernel, specs, outs, scratch, flops):
    return pl.pallas_call(
        kernel,
        in_specs=specs,
        out_specs=[VMEM] * len(outs),
        out_shape=[jax.ShapeDtypeStruct(shape, jnp.float32) for shape in outs],
        scratch_shapes=[pltpu.VMEM(shape, jnp.float32) for shape in scratch],
        compiler_params=pltpu.CompilerParams(vmem_limit_bytes=VMEM_LIMIT),
        cost_estimate=pl.CostEstimate(flops=flops, bytes_accessed=3 << 20, transcendentals=0),
    )


def on_device(count, checkpoint, seeds, cell_rate, flux_mats, owner, neighbours, orientation):
    nvars, cx, cy, cz = seeds.shape[2:]
    geo = Geometry(nvars, cx, cy, cz, count)
    rate = cell_rate[0]
    grads = seeds[0, 0]
    place = lax.axis_index("space").astype(jnp.int32).reshape(1)
    mats = flux_mats.reshape(-1)
    neighbours = neighbours.reshape(-1)
    orientation = orientation.reshape(-1)
    work = nvars * nvars * 3 * 4 * cx * cy * cz
    few = work // 16

    def exchange(buffer, fields):
        arrived = lax.all_to_all(buffer, "space", 0, 0, tiled=True)
        (leaving,) = call(
            functools.partial(route_kernel, geo, fields), [SMEM, SMEM, VMEM], [geo.buffer(fields)], [], few
        )(owner, neighbours, arrived)
        return lax.all_to_all(leaving, "space", 0, 0, tiled=True)

    def step_inner(block):
        return call(
            functools.partial(step_inner_kernel, geo), [SMEM, VMEM, VMEM], [geo.block], [geo.tall], work
        )(mats, block, rate)[0]

    def adjoint_inner(block, grads):
        return call(
            functools.partial(adjoint_inner_kernel, geo), [SMEM] + [VMEM] * 3, [geo.block], [geo.tall] * 2, 2 * work
        )(mats, block, grads, rate)[0]

    def step_edge(inner, faces, buffer, packed):
        outs = [geo.block, geo.faces, geo.buffer(1)] if packed else [geo.block]
        return call(
            functools.partial(step_edge_kernel, geo, packed), [SMEM] * 4 + [VMEM] * 4, outs, [geo.faces] * 2, few
        )(*fixed, inner, faces, rate_faces, buffer)

    def adjoint_edge(inner, faces, weight_faces, buffer, weight_buffer, field, packed):
        outs = [geo.block, geo.faces, geo.buffer(1)] if packed else [geo.block]
        return call(
            functools.partial(adjoint_edge_kernel, geo, packed, field),
            [SMEM] * 4 + [VMEM] * 6,
            outs,
            [geo.faces] * 3,
            few,
        )(*fixed, inner, faces, weight_faces, rate_faces, buffer, weight_buffer)

    fixed = (place, owner, orientation, mats)
    gathered = lax.all_gather(checkpoint, "ckpt", axis=0, tiled=True)
    state, faces, weight_faces, rate_faces, sent = call(
        functools.partial(pack_kernel, geo),
        [VMEM] * 3,
        [geo.block, geo.faces, geo.faces, geo.rate_faces, geo.buffer(2)],
        [geo.block],
        few,
    )(gathered, grads, rate)
    ghosts = exchange(sent, 2)
    next_state, next_faces, sent = step_edge(step_inner(state), faces, ghosts, True)
    next_ghosts = exchange(sent, 1)
    inner = adjoint_inner(next_state, grads)
    grads_now, next_weight_faces, sent = adjoint_edge(
        inner, next_faces, weight_faces, next_ghosts, ghosts, 1, True
    )
    weight_ghosts = exchange(sent, 1)
    (final,) = step_edge(step_inner(next_state), next_faces, next_ghosts, False)
    inner = adjoint_inner(state, grads_now)
    (adjoint,) = adjoint_edge(inner, faces, next_weight_faces, ghosts, weight_ghosts, 0, False)
    return (adjoint[None, None], final[None])


def solution(mesh):
    return jax.shard_map(
        functools.partial(on_device, mesh.shape["space"]),
        mesh=mesh,
        in_specs=(
            P("space", None, "ckpt", None, None),
            P("ckpt", "space", None, None, None, None),
            P("space", None, None, None),
            P(),
            P(),
            P(),
            P(),
        ),
        out_specs=(P("ckpt", "space", None, None, None, None), P("space", None, None, None, None)),
        check_vma=False,
    )
```

time: 125 us -> 115 us (0.920)
  waiting for transfers between devices: 34.6 us -> 23.2 us
  starting transfers between devices: 23.6 us -> 17 us
  Pallas kernels: 28.6 us -> 32 us
  local copies, waits for them, and re-layouts: 4.32 us -> 6.95 us
  blocking collectives: 32.1 us -> 34.1 us
    all_to_all x1 -> x2, blocking collectives: 10.5 us -> 23.7 us  [exchange(): arrived = lax.all_to_all(buffer, 'space', 0, 0, tiled=True)]
    all_to_all x1 -> x0, blocking collectives: 11.3 us -> none  [exchange(): return lax.all_to_all(leaving, 'space', 0, 0, tiled=True)]
    all_to_all x3 -> x1, starting transfers between devices: 13.3 us -> 5.83 us  [exchange(): arrived = lax.all_to_all(buffer, 'space', 0, 0, tiled=True)]
    all_to_all x3, waiting for transfers between devices: 16.9 us -> 10.4 us  [exchange(): return lax.all_to_all(leaving, 'space', 0, 0, tiled=True)]
    all_to_all x3 -> x1, waiting for transfers between devices: 17.7 us -> 12.8 us  [exchange(): arrived = lax.all_to_all(buffer, 'space', 0, 0, tiled=True)]
    pallas_call x10 -> x12, Pallas kernels: 28.6 us -> 32 us  [the longest x2 9.65 us: adjoint_inner(): call(functools.partial(adjoint_inner_kernel, geo), [SMEM] + [VMEM] * 3, [...]
    unnamed x20 -> x32, local copies, waits for them, and re-layouts: 4.07 us -> 6.7 us
  transfers between devices with their start and end apart: 6 -> 4, of which waited for: 6 -> 3; matrix products, arithmetic and copies ran while one was open for 0% -> 0% of each run, Pallas kernels for 10% -> 17%
where the time goes in v3:
time: 115 us; the launch traced here: 114 us
  blocking collectives  34.1 us (30%)
  Pallas kernels  32 us (28%)
  waiting for transfers between devices  23.2 us (20%)
  starting transfers between devices  17 us (15%)
  local copies, waits for them, and re-layouts  6.95 us (6%)
    all_to_all x2, blocking collectives, exchange(): arrived = lax.all_to_all(buffer, 'space', 0, 0, tiled=True)  23.7 us
    all_to_all x1, waiting for transfers between devices, exchange(): arrived = lax.all_to_all(buffer, 'space', 0, 0, tiled=True)  12.8 us
    all_to_all x3, starting transfers between devices, exchange(): return lax.all_to_all(leaving, 'space', 0, 0, tiled=True)  11.2 us
    all_gather x1, blocking collectives, on_device(): gathered = lax.all_gather(checkpoint, 'ckpt', axis=0, tiled=True)  10.4 us
    all_to_all x3, waiting for transfers between devices, exchange(): return lax.all_to_all(leaving, 'space', 0, 0, tiled=True)  10.4 us
    pallas_call x2, Pallas kernels, adjoint_inner(): call(functools.partial(adjoint_inner_kernel, geo), [SMEM] + [VMEM] * 3, [...  9.65 us
    pallas_call x2, Pallas kernels, step_inner(): call(functools.partial(step_inner_kernel, geo), [SMEM, VMEM, VMEM], [geo....  7.07 us
    unnamed x32, local copies, waits for them, and re-layouts  6.7 us
  transfers between devices with their start and end apart: 4, of which 3 were waited for; matrix products, arithmetic and copies ran while one was open for 0% of the time, Pallas kernels for 17%

profile of v3, /device:TPU:0, one launch (start us, length us, event | category | flops | bytes accessed | tf_op | source)
XLA Modules:
  0.0 114.0 jit_solution(13380902653486694515)
XLA Ops:
  0.6 0.0 copy-start
  0.6 0.0 copy-start.1
  0.7 10.4 %all_gather.3.gathered = f32[4,6,4,16,128]{4,3,2,1,0:T(8,128)S(1)} all-gather(f32[1,6,4,16,128]{4,3,2,1,0:T(8,128)} %param.7), channel_id=1, replica_groups=mesh['ckpt'=4,'space'=8] {'ckpt'}, dimensions={0}, use_global_device_ids=true | all-gather | bytes 983040 | tf_op jit(solution)/shard_map/all_gather | solution.py:479
  11.0 0.0 copy-done
  11.0 0.0 copy-done.1
  11.0 2.4 %shard_map.86 = (f32[6,16,16,128]{3,2,1,0:T(8,128)S(1)}, f32[6,96,128]{2,1,0:T(8,128)S(1)}, f32[6,96,128]{2,1,0:T(8,128)S(1)}, f32[6,16,128]{2,1,0:T(8,128)S(1)}, f32[8,104,128]{2,1,0:T(8,128)}) custom-call(f32[4,6,4,16,128]{4,3,2,1,0:T(8,128)S(1)} %all_gather.3.gathered, f32[6,16,16,128]{3,2,1,0:T(8,128)S(1)} %bitcast.10, f32[16,16,128]{2,1,0:T(8,128)S(1)} %bitcast.5), custom_call_target="tpu_custom_call" | custom-call | flops 884736 | bytes 3145728 | tf_op jit(solution)/shard_map/pallas_call | solution.py:480
  13.4 0.7 copy-done.3
  14.1 0.7 copy-done.8
  14.8 5.8 %all-to-all-start = ((f32[8,104,128]{2,1,0:T(8,128)}), f32[8,104,128]{2,1,0:T(8,128)S(1)}, u32[]{:S(2)}, u32[]{:S(2)}) async-start(f32[8,104,128]{2,1,0:T(8,128)} %get-tuple-element.16), calls=%async_computation | async-start | bytes 851968 | tf_op jit(solution)/shard_map/all_to_all | solution.py:446
  20.7 0.0 copy-done.14
  20.7 0.0 copy-start.12
  20.7 0.1 reshape.19.neighbours
  20.8 12.8 %all-to-all-done.arrived = f32[8,104,128]{2,1,0:T(8,128)S(1)} async-done(((f32[8,104,128]{2,1,0:T(8,128)}), f32[8,104,128]{2,1,0:T(8,128)S(1)}, u32[]{:S(2)}, u32[]{:S(2)}) %all-to-all-start) | async-done | bytes 426016 | tf_op jit(solution)/shard_map/all_to_all | solution.py:446
  33.6 0.0 copy-done.12
  33.6 1.4 %shard_map.88 = f32[8,104,128]{2,1,0:T(8,128)} custom-call(s32[8]{0:T(128)S(1)} %copy-done.12, s32[48]{0:T(128)S(1)} %reshape.19.neighbours, f32[8,104,128]{2,1,0:T(8,128)S(1)} %all-to-all-done.arrived), custom_call_target="tpu_custom_call" | custom-call | flops 884736 | bytes 3145728 | tf_op jit(solution)/shard_map/pallas_call | solution.py:447
  35.0 3.8 %all-to-all-start.1 = ((f32[8,104,128]{2,1,0:T(8,128)}), f32[8,104,128]{2,1,0:T(8,128)S(1)}, u32[]{:S(2)}, u32[]{:S(2)}) async-start(f32[8,104,128]{2,1,0:T(8,128)} %shard_map.88), calls=%async_computation.1 | async-start | bytes 851968 | tf_op jit(solution)/shard_map/all_to_all | solution.py:450
  38.7 0.0 copy-done.13
  38.7 0.0 copy-start.15
  38.8 0.1 reshape.18.mats
  38.8 0.6 copy-done.15
  39.4 0.1 reshape.17.orientation
  39.5 3.5 %shard_map.87.inner = f32[6,16,16,128]{3,2,1,0:T(8,128)S(1)} custom-call(f32[108]{0:T(128)S(1)} %reshape.18.mats, f32[6,16,16,128]{3,2,1,0:T(8,128)S(1)} %get-tuple-element.13.block, f32[16,16,128]{2,1,0:T(8,128)S(1)} %bitcast.6), custom_call_target="tpu_custom_call" | custom-call | flops 14155776 | bytes 3145728 | tf_op jit(solution)/shard_map/pallas_call | solution.py:453
  43.1 8.3 %all-to-all-done.1.buffer.rest_2_.rest_1_ = f32[8,104,128]{2,1,0:T(8,128)S(1)} async-done(((f32[8,104,128]{2,1,0:T(8,128)}), f32[8,104,128]{2,1,0:T(8,128)S(1)}, u32[]{:S(2)}, u32[]{:S(2)}) %all-to-all-start.1) | async-done | bytes 426016 | tf_op jit(solution)/shard_map/all_to_all | solution.py:450
  51.3 1.0 copy-done.4
  52.3 1.9 %shard_map.89 = (f32[6,16,16,128]{3,2,1,0:T(8,128)S(1)}, f32[6,96,128]{2,1,0:T(8,128)S(1)}, f32[8,56,128]{2,1,0:T(8,128)S(1)}) custom-call(s32[1]{0:T(128)} %bitcast.place, s32[8]{0:T(128)S(1)} %copy-done.12, s32[48]{0:T(128)S(1)} %reshape.17.orientation, f32[108]{0:T(128)S(1)} %reshape.18.mats, f32[6,16,16,128]{3,2,1,0:T(8,128)S(1)} %shard_map.87.inner, ...), custom_call_target="tpu_custom_call" | custom-call | flops 884736 | bytes 3145728 | tf_op jit(solution)/shard_map/pallas_call | solution.py:464
  54.1 12.1 %all_to_all.30.arrived = f32[8,56,128]{2,1,0:T(8,128)S(1)} all-to-all(f32[8,56,128]{2,1,0:T(8,128)S(1)} %get-tuple-element.20), channel_id=1, replica_groups=mesh['ckpt'=4,'space'=8] {'space'}, dimensions={0} | all-to-all | bytes 458752 | tf_op jit(solution)/shard_map/all_to_all | solution.py:446
  66.2 1.3 %shard_map.91 = f32[8,56,128]{2,1,0:T(8,128)} custom-call(s32[8]{0:T(128)S(1)} %copy-done.12, s32[48]{0:T(128)S(1)} %reshape.19.neighbours, f32[8,56,128]{2,1,0:T(8,128)S(1)} %all_to_all.30.arrived), custom_call_target="tpu_custom_call" | custom-call | flops 884736 | bytes 3145728 | tf_op jit(solution)/shard_map/pallas_call | solution.py:447
  67.5 3.4 %all-to-all-start.3 = ((f32[8,56,128]{2,1,0:T(8,128)}), f32[8,56,128]{2,1,0:T(8,128)S(1)}, u32[]{:S(2)}, u32[]{:S(2)}) async-start(f32[8,56,128]{2,1,0:T(8,128)} %shard_map.91), calls=%async_computation.3 | async-start | bytes 458752 | tf_op jit(solution)/shard_map/all_to_all | solution.py:450
  70.9 0.0 copy-start.2
  70.9 1.1 copy-done.2
  72.0 4.8 %shard_map.90.inner = f32[6,16,16,128]{3,2,1,0:T(8,128)S(1)} custom-call(f32[108]{0:T(128)S(1)} %reshape.18.mats, f32[6,16,16,128]{3,2,1,0:T(8,128)S(1)} %get-tuple-element.17.block, f32[6,16,16,128]{3,2,1,0:T(8,128)S(1)} %bitcast.11, f32[16,16,128]{2,1,0:T(8,128)S(1)} %bitcast.7), custom_call_target="tpu_custom_call" | custom-call | flops 28311552 | bytes 3145728 | tf_op jit(solution)/shard_map/pallas_call | solution.py:458
  76.9 2.1 %all-to-all-done.3.rest_1_.buffer = f32[8,56,128]{2,1,0:T(8,128)S(1)} async-done(((f32[8,56,128]{2,1,0:T(8,128)}), f32[8,56,128]{2,1,0:T(8,128)S(1)}, u32[]{:S(2)}, u32[]{:S(2)}) %all-to-all-start.3) | async-done | bytes 229408 | tf_op jit(solution)/shard_map/all_to_all | solution.py:450
  79.0 1.0 copy-done.9
  80.0 2.0 %shard_map.92 = (f32[6,16,16,128]{3,2,1,0:T(8,128)S(1)}, f32[6,96,128]{2,1,0:T(8,128)S(1)}, f32[8,56,128]{2,1,0:T(8,128)S(1)}) custom-call(s32[1]{0:T(128)} %bitcast.place, s32[8]{0:T(128)S(1)} %copy-done.12, s32[48]{0:T(128)S(1)} %reshape.17.orientation, f32[108]{0:T(128)S(1)} %reshape.18.mats, f32[6,16,16,128]{3,2,1,0:T(8,128)S(1)} %shard_map.90.inner, ...), custom_call_target="tpu_custom_call" | custom-call | flops 884736 | bytes 3145728 | tf_op jit(solution)/shard_map/pallas_call | solution.py:470
  82.0 0.0 copy-start.6
  82.0 0.9 copy-done.6
  82.9 0.7 copy-done.10
  83.6 11.6 %all_to_all.31.arrived = f32[8,56,128]{2,1,0:T(8,128)S(1)} all-to-all(f32[8,56,128]{2,1,0:T(8,128)S(1)} %get-tuple-element.23), channel_id=1, replica_groups=mesh['ckpt'=4,'space'=8] {'space'}, dimensions={0} | all-to-all | bytes 458752 | tf_op jit(solution)/shard_map/all_to_all | solution.py:446
  95.2 1.3 %shard_map.94 = f32[8,56,128]{2,1,0:T(8,128)} custom-call(s32[8]{0:T(128)S(1)} %copy-done.12, s32[48]{0:T(128)S(1)} %reshape.19.neighbours, f32[8,56,128]{2,1,0:T(8,128)S(1)} %all_to_all.31.arrived), custom_call_target="tpu_custom_call" | custom-call | flops 884736 | bytes 3145728 | tf_op jit(solution)/shard_map/pallas_call | solution.py:447
  96.5 4.0 %all-to-all-start.5 = ((f32[8,56,128]{2,1,0:T(8,128)}), f32[8,56,128]{2,1,0:T(8,128)}, u32[]{:S(2)}, u32[]{:S(2)}) async-start(f32[8,56,128]{2,1,0:T(8,128)} %shard_map.94), calls=%async_computation.5 | async-start | bytes 458752 | tf_op jit(solution)/shard_map/all_to_all | solution.py:450
  100.6 3.5 %shard_map.96.inner = f32[6,16,16,128]{3,2,1,0:T(8,128)S(1)} custom-call(f32[108]{0:T(128)S(1)} %reshape.18.mats, f32[6,16,16,128]{3,2,1,0:T(8,128)S(1)} %get-tuple-element.17.block, f32[16,16,128]{2,1,0:T(8,128)S(1)} %bitcast.8), custom_call_target="tpu_custom_call" | custom-call | flops 14155776 | bytes 3145728 | tf_op jit(solution)/shard_map/pallas_call | solution.py:453
  104.1 0.0 copy-start.7
  104.1 2.2 %shard_map.97 = f32[6,16,16,128]{3,2,1,0:T(8,128)} custom-call(s32[1]{0:T(128)} %bitcast.place, s32[8]{0:T(128)S(1)} %copy-done.12, s32[48]{0:T(128)S(1)} %reshape.17.orientation, f32[108]{0:T(128)S(1)} %reshape.18.mats, f32[6,16,16,128]{3,2,1,0:T(8,128)S(1)} %shard_map.96.inner, f32[6,96,128]{2,1,0:T(8,128)S(1)} %get-tuple-element.18.faces, ...), custom_call_target="tpu_custom_call" | custom-call | flops 884736 | bytes 3145728 | tf_op jit(solution)/shard_map/pallas_call | solution.py:464
  106.4 0.0 copy-done.7
  106.4 4.8 %shard_map.93.inner = f32[6,16,16,128]{3,2,1,0:T(8,128)S(1)} custom-call(f32[108]{0:T(128)S(1)} %reshape.18.mats, f32[6,16,16,128]{3,2,1,0:T(8,128)S(1)} %get-tuple-element.13.block, f32[6,16,16,128]{3,2,1,0:T(8,128)S(1)} %copy-done.7, f32[16,16,128]{2,1,0:T(8,128)S(1)} %bitcast.9), custom_call_target="tpu_custom_call" | custom-call | flops 28311552 | bytes 3145728 | tf_op jit(solution)/shard_map/pallas_call | solution.py:458
  111.2 0.0 all-to-all-done.5.rest_2_
  111.2 0.0 copy-done.5
  111.2 2.8 %shard_map.95 = f32[6,16,16,128]{3,2,1,0:T(8,128)} custom-call(s32[1]{0:T(128)} %bitcast.place, s32[8]{0:T(128)S(1)} %copy-done.12, s32[48]{0:T(128)S(1)} %reshape.17.orientation, f32[108]{0:T(128)S(1)} %reshape.18.mats, f32[6,16,16,128]{3,2,1,0:T(8,128)S(1)} %shard_map.93.inner, f32[6,96,128]{2,1,0:T(8,128)S(1)} %copy-done.5, f32[6,96,128]{2,1,0:T(8,128)S(1)} %copy-done.11, ...), custom_call_target="tpu_custom_call" | custom-call | flops 884736 | bytes 3145728 | tf_op jit(solution)/shard_map/pallas_call | solution.py:470
  (10 shorter events, 0.0 us)
Async XLA Ops:
  0.6 10.4 %copy-start = (f32[1,16,16,128]{3,2,1,0:T(8,128)S(1)}, f32[1,16,16,128]{3,2,1,0:T(8,128)}, u32[]{:S(2)}) copy-start(f32[1,16,16,128]{3,2,1,0:T(8,128)} %param.9) | copy-start | bytes 393220
  0.6 10.4 %copy-start.1 = (f32[1,1,6,16,16,128]{5,4,3,2,1,0:T(8,128)S(1)}, f32[1,1,6,16,16,128]{5,4,3,2,1,0:T(8,128)}, u32[]{:S(2)}) copy-start(f32[1,1,6,16,16,128]{5,4,3,2,1,0:T(8,128)} %param.8) | copy-start | bytes 2359300
  13.4 0.7 copy-start.3
  14.1 0.7 copy-start.8
  14.1 6.5 %copy-start.14 = (s32[8,6]{1,0:T(8,128)S(1)}, s32[8,6]{1,0:T(8,128)}, u32[]{:S(2)}) copy-start(s32[8,6]{1,0:T(8,128)} %param.12) | copy-start | bytes 580
  14.8 18.7 %all-to-all-start = ((f32[8,104,128]{2,1,0:T(8,128)}), f32[8,104,128]{2,1,0:T(8,128)S(1)}, u32[]{:S(2)}, u32[]{:S(2)}) async-start(f32[8,104,128]{2,1,0:T(8,128)} %get-tuple-element.16), calls=%async_computation | async-start | bytes 851968 | tf_op jit(solution)/shard_map/all_to_all | solution.py:446
  20.7 12.9 %copy-start.12 = (s32[8]{0:T(128)S(1)}, s32[8]{0:T(128)}, u32[]{:S(2)}) copy-start(s32[8]{0:T(128)} %owner.13) | copy-start | bytes 100
  35.0 3.8 %copy-start.13 = (f32[3,6,6]{2,1,0:T(8,128)S(1)}, f32[3,6,6]{2,1,0:T(8,128)}, u32[]{:S(2)}) copy-start(f32[3,6,6]{2,1,0:T(8,128)} %param.10) | copy-start | bytes 1300
  35.0 16.3 %all-to-all-start.1 = ((f32[8,104,128]{2,1,0:T(8,128)}), f32[8,104,128]{2,1,0:T(8,128)S(1)}, u32[]{:S(2)}, u32[]{:S(2)}) async-start(f32[8,104,128]{2,1,0:T(8,128)} %shard_map.88), calls=%async_computation.1 | async-start | bytes 851968 | tf_op jit(solution)/shard_map/all_to_all | solution.py:450
  38.7 0.7 copy-start.15
  51.3 1.0 copy-start.4
  67.5 11.5 %all-to-all-start.3 = ((f32[8,56,128]{2,1,0:T(8,128)}), f32[8,56,128]{2,1,0:T(8,128)S(1)}, u32[]{:S(2)}, u32[]{:S(2)}) async-start(f32[8,56,128]{2,1,0:T(8,128)} %shard_map.91), calls=%async_computation.3 | async-start | bytes 458752 | tf_op jit(solution)/shard_map/all_to_all | solution.py:450
  70.9 1.1 copy-start.2
  79.0 1.0 copy-start.9
  82.0 0.9 copy-start.6
  82.9 0.7 copy-start.10
  96.5 14.7 %all-to-all-start.5 = ((f32[8,56,128]{2,1,0:T(8,128)}), f32[8,56,128]{2,1,0:T(8,128)}, u32[]{:S(2)}, u32[]{:S(2)}) async-start(f32[8,56,128]{2,1,0:T(8,128)} %shard_map.94), calls=%async_computation.5 | async-start | bytes 458752 | tf_op jit(solution)/shard_map/all_to_all | solution.py:450
  104.1 2.3 %copy-start.7 = (f32[6,16,16,128]{3,2,1,0:T(8,128)S(1)}, f32[6,16,16,128]{3,2,1,0:T(8,128)}, u32[]{:S(2)}) copy-start(f32[6,16,16,128]{3,2,1,0:T(8,128)} %copy-done.6) | copy-start | bytes 2359300
  106.4 4.8 %copy-start.5 = (f32[6,96,128]{2,1,0:T(8,128)S(1)}, f32[6,96,128]{2,1,0:T(8,128)}, u32[]{:S(2)}) copy-start(f32[6,96,128]{2,1,0:T(8,128)} %copy-done.3) | copy-start | bytes 884740
  106.4 4.9 %copy-start.11 = (f32[6,96,128]{2,1,0:T(8,128)S(1)}, f32[6,96,128]{2,1,0:T(8,128)}, u32[]{:S(2)}) copy-start(f32[6,96,128]{2,1,0:T(8,128)} %copy-done.10) | copy-start | bytes 884740

commit v4 on v3

--- a/solution.py
+++ b/solution.py
@@ -14,24 +14,32 @@
 PAD = 8
 VMEM = pl.BlockSpec(memory_space=pltpu.VMEM)
 SMEM = pl.BlockSpec(memory_space=pltpu.SMEM)
-VMEM_LIMIT = 32 * 1024 * 1024
+VMEM_LIMIT = 12 * 1024 * 1024
+
+
+class Pieces:
+    def __init__(self, rows, count):
+        self.rows = rows
+        self.runs = [-(-length // count) for length in rows]
+        self.starts = [sum(self.runs[:index]) for index in range(len(rows))]
+        self.total = sum(self.runs)
 
 
 class Geometry:
-    def __init__(self, nvars, cx, cy, cz, count):
-        self.v, self.x, self.y, self.z, self.n = nvars, cx, cy, cz, count
+    def __init__(self, nvars, cx, cy, cz, count, parts):
+        self.v, self.x, self.y, self.z, self.n, self.parts = nvars, cx, cy, cz, count, parts
+        self.depth = cx // parts
         self.rows = [nvars * cy] * 2 + [nvars * cx] * 2 + [cy] * 2
-        self.runs = [-(-rows // count) for rows in self.rows]
-        self.starts = [sum(self.runs[:side]) for side in range(6)]
-        self.field = sum(self.runs)
-        self.face_rows = -(-max(run * count for run in self.runs) // 8) * 8
+        self.whole = Pieces(self.rows, count)
+        self.part = Pieces([nvars * cy] + [nvars * self.depth] * 2 + [cy] * 2, count)
+        self.face_rows = -(-max(run * count for run in self.whole.runs) // 8) * 8
         self.block = (nvars, cx, cy, cz)
         self.tall = (nvars, cx, cy + 2 * PAD, cz)
         self.faces = (6, self.face_rows, cz)
         self.rate_faces = (6, max(cx, cy), cz)
 
-    def buffer(self, fields):
-        return (self.n, -(-fields * self.field // 8) * 8, self.z)
+    def buffer(self, rows):
+        return (self.n, -(-rows // 8) * 8, self.z)
 
 
 def take_z_faces(geo, load):
@@ -58,11 +66,10 @@
         faces[3, var * x : (var + 1) * x] = source[var, :, 0, :]
 
 
-def cut(geo, faces, buffer, field):
-    for side in range(6):
-        run, start = geo.runs[side], field * geo.field + geo.starts[side]
+def cut(geo, pieces, faces, buffer, base):
+    for index, (run, start) in enumerate(zip(pieces.runs, pieces.starts)):
         for slot in range(geo.n):
-            buffer[slot, start : start + run] = faces[side, slot * run : (slot + 1) * run]
+            buffer[slot, base + start : base + start + run] = faces[index, slot * run : (slot + 1) * run]
 
 
 def own_codes(geo, place, owner, orientation):
@@ -98,12 +105,38 @@
     ).reshape(rows, z)
 
 
-def unpack(geo, codes, buffer, field, raw, ghosts):
-    v, x, y, z = geo.block
+def join(geo, buffer, raw):
     for side in range(6):
-        run, start = geo.runs[side], field * geo.field + geo.starts[side]
+        run, start = geo.whole.runs[side], geo.whole.starts[side]
         for slot in range(geo.n):
             raw[side, slot * run : (slot + 1) * run] = buffer[slot, start : start + run]
+
+
+def join_parts(geo, buffer, raw, piece):
+    for side in range(6):
+        index = 0 if side < 2 else side - 1
+        run, start = geo.part.runs[index], geo.part.starts[index]
+        if side < 2:
+            part = 0 if side == 0 else geo.parts - 1
+            for slot in range(geo.n):
+                raw[side, slot * run : (slot + 1) * run] = buffer[part, slot, start : start + run]
+        elif side < 4:
+            for part in range(geo.parts):
+                for slot in range(geo.n):
+                    piece[slot * run : (slot + 1) * run] = buffer[part, slot, start : start + run]
+                for var in range(geo.v):
+                    row = var * geo.x + part * geo.depth
+                    raw[side, row : row + geo.depth] = piece[var * geo.depth : (var + 1) * geo.depth]
+        else:
+            for slot in range(geo.n):
+                total = buffer[0, slot, start : start + run]
+                for part in range(1, geo.parts):
+                    total = total + buffer[part, slot, start : start + run]
+                raw[side, slot * run : (slot + 1) * run] = total
+
+
+def turn(geo, codes, raw, ghosts):
+    v, x, y, z = geo.block
     for side in range(6):
         first, second = codes[side] & 1, (codes[side] >> 1) & 1
         layer = raw[side, : geo.rows[side]]
@@ -148,10 +181,15 @@
 
 def fill_tall(geo, source, tall):
     v, x, y, z = geo.block
-    tall[:, :, PAD : PAD + y, :] = source[...]
-    for var in range(v):
-        tall[var, :, PAD - 1, :] = source[var, :, 0, :]
-        tall[var, :, PAD + y, :] = source[var, :, y - 1, :]
+    if len(source.shape) == 5:
+        depth = geo.depth
+        for part in range(geo.parts):
+            tall[:, part * depth : (part + 1) * depth, PAD : PAD + y, :] = source[part]
+    else:
+        tall[:, :, PAD : PAD + y, :] = source[...]
+    for var in range(v):
+        tall[var, :, PAD - 1, :] = tall[var, :, PAD, :]
+        tall[var, :, PAD + y, :] = tall[var, :, PAD + y - 1, :]
 
 
 def around(geo, tall, plane):
@@ -277,16 +315,27 @@
     return out
 
 
-def pack_kernel(geo, gathered, grads, rate, state, faces, weight_faces, rate_faces, buffer, weight):
-    v, x, y, z = geo.block
-    parts, depth = gathered.shape[0], gathered.shape[2]
-    for part in range(parts):
-        state[:, part * depth : (part + 1) * depth] = gathered[part]
-    take_xy_faces(geo, state, faces)
-    high, low = take_z_faces(geo, lambda var, plane: state[var, plane])
-    faces[4, :y] = high
-    faces[5, :y] = low
-    cut(geo, faces, buffer, 0)
+def pack_kernel(geo, part, stored, grads, rate, kept, weight_faces, rate_faces, buffer, pieces):
+    v, x, y, z = geo.block
+    depth = geo.depth
+    kept[...] = stored[...]
+    lane = lax.broadcasted_iota(jnp.int32, (y, z), 1)
+    plane = jnp.where(part[0] == geo.parts - 1, depth - 1, 0)
+    high = jnp.zeros((y, z), jnp.float32)
+    low = jnp.zeros((y, z), jnp.float32)
+    for var in range(v):
+        pieces[0, var * y : (var + 1) * y] = stored[var, plane]
+        pieces[1, var * depth : (var + 1) * depth] = stored[var, :, y - 1, :]
+        pieces[2, var * depth : (var + 1) * depth] = stored[var, :, 0, :]
+        for step in range(depth):
+            place = var * x + part[0] * depth + step
+            tile = stored[var, step]
+            here = lane == place
+            high = jnp.where(here, pltpu.roll(tile, lax.rem(place + 1, z), 1), high)
+            low = jnp.where(here, pltpu.roll(tile, place, 1), low)
+    pieces[3, :y] = high
+    pieces[4, :y] = low
+    cut(geo, geo.part, pieces, buffer, 0)
     rate_faces[0, :y] = rate[x - 1]
     rate_faces[1, :y] = rate[0]
     rate_faces[2, :x] = rate[:, y - 1, :]
@@ -294,32 +343,50 @@
     high, low = take_z_faces(geo, lambda var, plane: rate[plane])
     rate_faces[4, :y] = high
     rate_faces[5, :y] = low
-
-    def body(plane, carry):
+    take_weight_faces(geo, grads, rate_faces, weight_faces)
+    cut(geo, geo.whole, weight_faces, buffer, geo.part.total)
+
+
+def take_weight_faces(geo, grads, rate_faces, faces):
+    v, x, y, z = geo.block
+    take_xy_faces(geo, grads, faces)
+    for side in range(4):
+        depth = y if side < 2 else x
         for var in range(v):
-            weight[var, plane] = rate[plane] * grads[var, plane]
-        return carry
-
-    lax.fori_loop(0, x, body, 0)
-    take_xy_faces(geo, weight, weight_faces)
-    high, low = take_z_faces(geo, lambda var, plane: weight[var, plane])
-    weight_faces[4, :y] = high
-    weight_faces[5, :y] = low
-    cut(geo, weight_faces, buffer, 1)
-
-
-def route_kernel(geo, fields, owner, neighbours, arrived, leaving):
+            here = slice(var * depth, (var + 1) * depth)
+            faces[side, here] = faces[side, here] * rate_faces[side, :depth]
+    high, low = take_z_faces(geo, lambda var, plane: grads[var, plane])
+    faces[4, :y] = high * rate_faces[4, :y]
+    faces[5, :y] = low * rate_faces[5, :y]
+
+
+def route_whole(geo, owner, neighbours, arrived, base, leaving):
     for block in range(geo.n):
         target = owner[block]
         for side in range(6):
             source = owner[neighbours[block * 6 + side]]
-            for field in range(fields):
-                run, base = geo.runs[side], field * geo.field
-                start, far = base + geo.starts[side], base + geo.starts[side ^ 1]
-                leaving[target, start : start + run] = arrived[source, far : far + run]
-
-
-def step_inner_kernel(geo, mats, block, rate, result, tall):
+            run, start, far = geo.whole.runs[side], geo.whole.starts[side], base + geo.whole.starts[side ^ 1]
+            leaving[target, start : start + run] = arrived[source, far : far + run]
+
+
+def route_kernel(geo, owner, neighbours, arrived, leaving):
+    route_whole(geo, owner, neighbours, arrived, 0, leaving)
+
+
+def route_first_kernel(geo, part, owner, neighbours, arrived, leaving, weight_leaving):
+    route_whole(geo, owner, neighbours, arrived, geo.part.total, weight_leaving)
+    x_side = jnp.where(part[0] == geo.parts - 1, 1, 0)
+    for block in range(geo.n):
+        target = owner[block]
+        for index in range(5):
+            side, far_index = (x_side, 0) if index == 0 else (index + 1, ((index + 1) ^ 1) - 1)
+            source = owner[neighbours[block * 6 + side]]
+            run, start, far = geo.part.runs[index], geo.part.starts[index], geo.part.starts[far_index]
+            leaving[target, start : start + run] = arrived[source, far : far + run]
+
+
+def step_inner_kernel(geo, mats, block, rate, result, *rest):
+    tall = rest[-1]
     fill_tall(geo, block, tall)
 
     def body(plane, carry):
@@ -329,6 +396,17 @@
         return carry
 
     lax.fori_loop(0, geo.x, body, 0)
+    if len(rest) == 2:
+        faces = rest[0]
+        v, x, y, z = geo.block
+        for var in range(v):
+            faces[0, var * y : (var + 1) * y] = tall[var, x - 1, PAD : PAD + y]
+            faces[1, var * y : (var + 1) * y] = tall[var, 0, PAD : PAD + y]
+            faces[2, var * x : (var + 1) * x] = tall[var, :, PAD + y - 1, :]
+            faces[3, var * x : (var + 1) * x] = tall[var, :, PAD, :]
+        high, low = take_z_faces(geo, lambda var, plane: tall[var, plane, PAD : PAD + y])
+        faces[4, :y] = high
+        faces[5, :y] = low
 
 
 def adjoint_inner_kernel(geo, mats, block, grads, rate, result, tall, weights):
@@ -357,13 +435,15 @@
     lax.fori_loop(0, x, body, 0)
 
 
-def step_edge_kernel(geo, packed, place, owner, orientation, mats, inner, faces, rate_faces, buffer, result, *rest):
-    if packed:
-        new_faces, sent, raw, ghosts = rest
+def step_edge_kernel(geo, first, place, owner, orientation, mats, inner, faces, rate_faces, buffer, result, *rest):
+    if first:
+        new_faces, sent, ghosts, raw, piece = rest
+        join_parts(geo, buffer, raw, piece)
     else:
-        raw, ghosts = rest
-    v, x, y, z = geo.block
-    unpack(geo, own_codes(geo, place, owner, orientation), buffer, 0, raw, ghosts)
+        ghosts, raw = rest
+        join(geo, buffer, raw)
+    v, x, y, z = geo.block
+    turn(geo, own_codes(geo, place, owner, orientation), raw, ghosts)
     result[...] = inner[...]
     terms = []
     for side in range(6):
@@ -375,26 +455,25 @@
         else:
             terms.append(values)
     add_z_terms(geo, *terms, result)
-    if packed:
+    if first:
         take_xy_faces(geo, result, new_faces)
         high, low = take_z_faces(geo, lambda var, plane: result[var, plane])
         new_faces[4, :y] = high
         new_faces[5, :y] = low
-        cut(geo, new_faces, sent, 0)
-
-
-def adjoint_edge_kernel(
-    geo, packed, weight_field, place, owner, orientation, mats, inner, faces, weight_faces, *rest
-):
-    rate_faces, buffer, weight_buffer, result = rest[:4]
-    if packed:
-        new_faces, sent, raw, ghosts, weight_ghosts = rest[4:]
+        cut(geo, geo.whole, new_faces, sent, 0)
+
+
+def adjoint_edge_kernel(geo, last, place, owner, orientation, mats, inner, faces, weight_faces, *rest):
+    v, x, y, z = geo.block
+    codes = own_codes(geo, place, owner, orientation)
+    if last:
+        ghosts, weight_buffer, result, raw, weight_ghosts = rest
     else:
-        raw, ghosts, weight_ghosts = rest[4:]
-    v, x, y, z = geo.block
-    codes = own_codes(geo, place, owner, orientation)
-    unpack(geo, codes, buffer, 0, raw, ghosts)
-    unpack(geo, codes, weight_buffer, weight_field, raw, weight_ghosts)
+        rate_faces, buffer, weight_buffer, result, new_faces, sent, raw, ghosts, weight_ghosts = rest
+        join(geo, buffer, raw)
+        turn(geo, codes, raw, ghosts)
+    join(geo, weight_buffer, raw)
+    turn(geo, codes, raw, weight_ghosts)
     result[...] = inner[...]
     terms = []
     for side in range(6):
@@ -405,17 +484,9 @@
         else:
             terms.append(values)
     add_z_terms(geo, *terms, result)
-    if packed:
-        take_xy_faces(geo, result, new_faces)
-        high, low = take_z_faces(geo, lambda var, plane: result[var, plane])
-        for side in range(4):
-            depth = y if side < 2 else x
-            for var in range(v):
-                here = slice(var * depth, (var + 1) * depth)
-                new_faces[side, here] = new_faces[side, here] * rate_faces[side, :depth]
-        new_faces[4, :y] = high * rate_faces[4, :y]
-        new_faces[5, :y] = low * rate_faces[5, :y]
-        cut(geo, new_faces, sent, 0)
+    if not last:
+        take_weight_faces(geo, result, rate_faces, new_faces)
+        cut(geo, geo.whole, new_faces, sent, 0)
 
 
 def call(kernel, specs, outs, scratch, flops):
@@ -430,77 +501,109 @@
     )
 
 
-def on_device(count, checkpoint, seeds, cell_rate, flux_mats, owner, neighbours, orientation):
+def on_device(count, parts, checkpoint, seeds, cell_rate, flux_mats, owner, neighbours, orientation):
     nvars, cx, cy, cz = seeds.shape[2:]
-    geo = Geometry(nvars, cx, cy, cz, count)
+    geo = Geometry(nvars, cx, cy, cz, count, parts)
     rate = cell_rate[0]
     grads = seeds[0, 0]
     place = lax.axis_index("space").astype(jnp.int32).reshape(1)
+    part = lax.axis_index("ckpt").astype(jnp.int32).reshape(1)
     mats = flux_mats.reshape(-1)
     neighbours = neighbours.reshape(-1)
     orientation = orientation.reshape(-1)
+    fixed = (place, owner, orientation, mats)
     work = nvars * nvars * 3 * 4 * cx * cy * cz
     few = work // 16
-
-    def exchange(buffer, fields):
-        arrived = lax.all_to_all(buffer, "space", 0, 0, tiled=True)
-        (leaving,) = call(
-            functools.partial(route_kernel, geo, fields), [SMEM, SMEM, VMEM], [geo.buffer(fields)], [], few
-        )(owner, neighbours, arrived)
-        return lax.all_to_all(leaving, "space", 0, 0, tiled=True)
-
-    def step_inner(block):
-        return call(
-            functools.partial(step_inner_kernel, geo), [SMEM, VMEM, VMEM], [geo.block], [geo.tall], work
-        )(mats, block, rate)[0]
+    whole, some = geo.buffer(geo.whole.total), geo.buffer(geo.part.total)
+
+    def swap(buffer):
+        return lax.all_to_all(buffer, "space", 0, 0, tiled=True)
+
+    def route(arrived):
+        return call(functools.partial(route_kernel, geo), [SMEM, SMEM, VMEM], [whole], [], few)(
+            owner, neighbours, arrived
+        )[0]
+
+    def step_inner(block, faces):
+        outs = [geo.block, geo.faces] if faces else [geo.block]
+        return call(functools.partial(step_inner_kernel, geo), [SMEM, VMEM, VMEM], outs, [geo.tall], work)(
+            mats, block, rate
+        )
 
     def adjoint_inner(block, grads):
         return call(
             functools.partial(adjoint_inner_kernel, geo), [SMEM] + [VMEM] * 3, [geo.block], [geo.tall] * 2, 2 * work
         )(mats, block, grads, rate)[0]
 
-    def step_edge(inner, faces, buffer, packed):
-        outs = [geo.block, geo.faces, geo.buffer(1)] if packed else [geo.block]
-        return call(
-            functools.partial(step_edge_kernel, geo, packed), [SMEM] * 4 + [VMEM] * 4, outs, [geo.faces] * 2, few
-        )(*fixed, inner, faces, rate_faces, buffer)
-
-    def adjoint_edge(inner, faces, weight_faces, buffer, weight_buffer, field, packed):
-        outs = [geo.block, geo.faces, geo.buffer(1)] if packed else [geo.block]
-        return call(
-            functools.partial(adjoint_edge_kernel, geo, packed, field),
-            [SMEM] * 4 + [VMEM] * 6,
-            outs,
-            [geo.faces] * 3,
-            few,
-        )(*fixed, inner, faces, weight_faces, rate_faces, buffer, weight_buffer)
-
-    fixed = (place, owner, orientation, mats)
-    gathered = lax.all_gather(checkpoint, "ckpt", axis=0, tiled=True)
-    state, faces, weight_faces, rate_faces, sent = call(
+    kept, weight_faces, rate_faces, sent = call(
         functools.partial(pack_kernel, geo),
-        [VMEM] * 3,
-        [geo.block, geo.faces, geo.faces, geo.rate_faces, geo.buffer(2)],
+        [SMEM] + [VMEM] * 3,
+        [checkpoint.shape[1:], geo.faces, geo.rate_faces, geo.buffer(geo.part.total + geo.whole.total)],
+        [geo.faces],
+        few,
+    )(part, checkpoint[0], grads, rate)
+    arrived = swap(sent)
+    state = lax.all_gather(kept, "ckpt", axis=0)
+    arrived, state = lax.optimization_barrier((arrived, state))
+    leaving, weight_leaving = call(
+        functools.partial(route_first_kernel, geo), [SMEM] * 3 + [VMEM], [some, whole], [], few
+    )(part, owner, neighbours, arrived)
+    part_ghosts = swap(leaving)
+    inner, faces = step_inner(state, True)
+    part_ghosts, inner, faces = lax.optimization_barrier((part_ghosts, inner, faces))
+    weight_ghosts = swap(weight_leaving)
+    gathered = lax.all_gather(part_ghosts, "ckpt", axis=0)
+    next_state, next_faces, sent, ghosts = call(
+        functools.partial(step_edge_kernel, geo, True),
+        [SMEM] * 4 + [VMEM] * 4,
+        [geo.block, geo.faces, whole, geo.faces],
+        [geo.faces, geo.faces[1:]],
+        few,
+    )(*fixed, inner, faces, rate_faces, gathered)
+
+    arrived = swap(sent)
+    inner = adjoint_inner(next_state, grads)
+    arrived, inner = lax.optimization_barrier((arrived, inner))
+    leaving = route(arrived)
+    later_state, leaving = lax.optimization_barrier((next_state, leaving))
+    next_ghosts = swap(leaving)
+    (final_inner,) = step_inner(later_state, False)
+    next_ghosts, final_inner = lax.optimization_barrier((next_ghosts, final_inner))
+    grads_now, next_weight_faces, sent = call(
+        functools.partial(adjoint_edge_kernel, geo, False),
+        [SMEM] * 4 + [VMEM] * 6,
+        [geo.block, geo.faces, whole],
+        [geo.faces] * 3,
+        few,
+    )(*fixed, inner, next_faces, weight_faces, rate_faces, next_ghosts, weight_ghosts)
+
+    arrived = swap(sent)
+    inner = adjoint_inner(state, grads_now)
+    arrived, inner = lax.optimization_barrier((arrived, inner))
+    leaving = route(arrived)
+    final_inner, leaving = lax.optimization_barrier((final_inner, leaving))
+    last_ghosts = swap(leaving)
+    (final,) = call(
+        functools.partial(step_edge_kernel, geo, False),
+        [SMEM] * 4 + [VMEM] * 4,
         [geo.block],
+        [geo.faces] * 2,
+        work,
+    )(*fixed, final_inner, next_faces, rate_faces, next_ghosts)
+    last_ghosts, final = lax.optimization_barrier((last_ghosts, final))
+    (adjoint,) = call(
+        functools.partial(adjoint_edge_kernel, geo, True),
+        [SMEM] * 4 + [VMEM] * 5,
+        [geo.block],
+        [geo.faces] * 2,
         few,
-    )(gathered, grads, rate)
-    ghosts = exchange(sent, 2)
-    next_state, next_faces, sent = step_edge(step_inner(state), faces, ghosts, True)
-    next_ghosts = exchange(sent, 1)
-    inner = adjoint_inner(next_state, grads)
-    grads_now, next_weight_faces, sent = adjoint_edge(
-        inner, next_faces, weight_faces, next_ghosts, ghosts, 1, True
-    )
-    weight_ghosts = exchange(sent, 1)
-    (final,) = step_edge(step_inner(next_state), next_faces, next_ghosts, False)
-    inner = adjoint_inner(state, grads_now)
-    (adjoint,) = adjoint_edge(inner, faces, next_weight_faces, ghosts, weight_ghosts, 0, False)
+    )(*fixed, inner, faces, next_weight_faces, ghosts, last_ghosts)
     return (adjoint[None, None], final[None])
 
 
 def solution(mesh):
     return jax.shard_map(
-        functools.partial(on_device, mesh.shape["space"]),
+        functools.partial(on_device, mesh.shape["space"], mesh.shape["ckpt"]),
         mesh=mesh,
         in_specs=(
             P("space", None, "ckpt", None, None),

time: 115 us -> 123 us (1.070)
  starting transfers between devices: 17 us -> 28.6 us
  local copies, waits for them, and re-layouts: 6.95 us -> 16.6 us
  blocking collectives: 34.1 us -> 26.3 us
  waiting for transfers between devices: 23.2 us -> 18.2 us
    all_to_all x2 -> x1, blocking collectives: 23.7 us -> 11.6 us  [swap(): return lax.all_to_all(buffer, 'space', 0, 0, tiled=True)]
    all_to_all x4 -> x6, starting transfers between devices: 17 us -> 28.6 us  [swap(): return lax.all_to_all(buffer, 'space', 0, 0, tiled=True)]
    unnamed x32 -> x72, local copies, waits for them, and re-layouts: 6.7 us -> 16.4 us
    all_to_all x4 -> x6, waiting for transfers between devices: 23.2 us -> 18.2 us  [swap(): return lax.all_to_all(buffer, 'space', 0, 0, tiled=True)]
    all_gather x1 -> x2, blocking collectives: 10.4 us -> 14.7 us  [the longest x1 8.59 us: on_device(): state = lax.all_gather(kept, 'ckpt', axis=0)]
  transfers between devices with their start and end apart: 4 -> 6, of which waited for: 3 -> 6; matrix products, arithmetic and copies ran while one was open for 0% -> 0% of each run, Pallas kernels for 17% -> 16%
where the time goes in v4:
time: 123 us; the launch traced here: 122 us
  Pallas kernels  31.7 us (26%)
  starting transfers between devices  28.6 us (23%)
  blocking collectives  26.3 us (21%)
  waiting for transfers between devices  18.2 us (15%)
  local copies, waits for them, and re-layouts  16.6 us (13%)
    all_to_all x6, starting transfers between devices, swap(): return lax.all_to_all(buffer, 'space', 0, 0, tiled=True)  28.6 us
    all_to_all x6, waiting for transfers between devices, swap(): return lax.all_to_all(buffer, 'space', 0, 0, tiled=True)  18.2 us
    unnamed x72, local copies, waits for them, and re-layouts  16.4 us
    all_to_all x1, blocking collectives, swap(): return lax.all_to_all(buffer, 'space', 0, 0, tiled=True)  11.6 us
    pallas_call x2, Pallas kernels, adjoint_inner(): call(functools.partial(adjoint_inner_kernel, geo), [SMEM] + [VMEM] * 3, [...  9.61 us
    all_gather x1, blocking collectives, on_device(): state = lax.all_gather(kept, 'ckpt', axis=0)  8.59 us
    pallas_call x2, Pallas kernels, step_inner(): call(functools.partial(step_inner_kernel, geo), [SMEM, VMEM, VMEM], outs,...  7.5 us
    all_gather x1, blocking collectives, on_device(): gathered = lax.all_gather(part_ghosts, 'ckpt', axis=0)  6.13 us
  transfers between devices with their start and end apart: 6, of which 6 were waited for; matrix products, arithmetic and copies ran while one was open for 0% of the time, Pallas kernels for 16%

profile of v4, /device:TPU:0, one launch (start us, length us, event | category | flops | bytes accessed | tf_op | source)
XLA Modules:
  0.0 122.2 jit_solution(1252303729173755217)
XLA Ops:
  0.6 0.9 copy-done
  1.5 1.1 copy-done.2
  2.7 0.9 copy-done.20
  3.6 1.8 %shard_map.86 = (f32[6,4,16,128]{3,2,1,0:T(8,128)S(1)}, f32[6,96,128]{2,1,0:T(8,128)S(1)}, f32[6,16,128]{2,1,0:T(8,128)S(1)}, f32[8,80,128]{2,1,0:T(8,128)}) custom-call(s32[1]{0:T(128)} %bitcast.1.part, f32[6,4,16,128]{3,2,1,0:T(8,128)S(1)} %bitcast.19, f32[6,16,16,128]{3,2,1,0:T(8,128)S(1)} %bitcast.16, f32[16,16,128]{2,1,0:T(8,128)S(1)} %bitcast.11), custom_call_target="tpu_custom_call" | custom-call | flops 884736 | bytes 3145728 | tf_op jit(solution)/shard_map/pallas_call | solution.py:538
  5.4 0.7 copy-done.17
  6.1 7.4 %all-to-all-start = ((f32[8,80,128]{2,1,0:T(8,128)}), f32[8,80,128]{2,1,0:T(8,128)S(1)}, u32[]{:S(2)}, u32[]{:S(2)}) async-start(f32[8,80,128]{2,1,0:T(8,128)} %get-tuple-element.34), calls=%async_computation | async-start | bytes 655360 | tf_op jit(solution)/shard_map/all_to_all | solution.py:520
  13.6 8.6 %all-gather = f32[24,4,16,128]{3,2,1,0:T(8,128)S(1)} all-gather(f32[6,4,16,128]{3,2,1,0:T(8,128)S(1)} %get-tuple-element.35), channel_id=2, replica_groups=mesh['ckpt'=4,'space'=8] {'ckpt'}, dimensions={0}, use_global_device_ids=true | all-gather | bytes 983040 | tf_op jit(solution)/shard_map/all_gather | solution.py:546
  22.2 1.6 %all-to-all-done.arrived = f32[8,80,128]{2,1,0:T(8,128)S(1)} async-done(((f32[8,80,128]{2,1,0:T(8,128)}), f32[8,80,128]{2,1,0:T(8,128)S(1)}, u32[]{:S(2)}, u32[]{:S(2)}) %all-to-all-start) | async-done | bytes 327712 | tf_op jit(solution)/shard_map/all_to_all | solution.py:520
  23.9 1.4 %shard_map.87 = (f32[8,24,128]{2,1,0:T(8,128)}, f32[8,56,128]{2,1,0:T(8,128)}) custom-call(s32[1]{0:T(128)} %bitcast.1.part, s32[8]{0:T(128)S(1)} %copy-done.25, s32[48]{0:T(128)S(1)} %reshape.23.neighbours, f32[8,80,128]{2,1,0:T(8,128)S(1)} %all-to-all-done.arrived), custom_call_target="tpu_custom_call" | custom-call | flops 884736 | bytes 3145728 | tf_op jit(solution)/shard_map/pallas_call | solution.py:548
  25.2 5.1 %all-to-all-start.1 = ((f32[8,24,128]{2,1,0:T(8,128)}), f32[8,24,128]{2,1,0:T(8,128)S(1)}, u32[]{:S(2)}, u32[]{:S(2)}) async-start(f32[8,24,128]{2,1,0:T(8,128)} %get-tuple-element.37), calls=%async_computation.1 | async-start | bytes 196608 | tf_op jit(solution)/shard_map/all_to_all | solution.py:520
  30.4 0.1 reshape.21.mats
  30.5 0.6 copy-done.35
  31.2 4.0 %shard_map.88 = (f32[6,16,16,128]{3,2,1,0:T(8,128)S(1)}, f32[6,96,128]{2,1,0:T(8,128)S(1)}) custom-call(f32[108]{0:T(128)S(1)} %reshape.21.mats, f32[4,6,4,16,128]{4,3,2,1,0:T(8,128)S(1)} %bitcast.9, f32[16,16,128]{2,1,0:T(8,128)S(1)} %bitcast.12), custom_call_target="tpu_custom_call" | custom-call | flops 14155776 | bytes 3145728 | tf_op jit(solution)/shard_map/pallas_call | solution.py:529
  35.2 0.9 copy-done.9
  36.0 1.5 %all-to-all-done.1 = f32[8,24,128]{2,1,0:T(8,128)S(1)} async-done(((f32[8,24,128]{2,1,0:T(8,128)}), f32[8,24,128]{2,1,0:T(8,128)S(1)}, u32[]{:S(2)}, u32[]{:S(2)}) %all-to-all-start.1) | async-done | bytes 98336 | tf_op jit(solution)/shard_map/all_to_all | solution.py:520
  37.5 6.1 %all-gather.1 = f32[32,24,128]{2,1,0:T(8,128)S(1)} all-gather(f32[8,24,128]{2,1,0:T(8,128)S(1)} %all-to-all-done.1), channel_id=3, replica_groups=mesh['ckpt'=4,'space'=8] {'ckpt'}, dimensions={0}, use_global_device_ids=true | all-gather | bytes 491520 | tf_op jit(solution)/shard_map/all_gather | solution.py:555
  43.6 1.1 copy-done.10
  44.8 1.9 %shard_map.89 = (f32[6,16,16,128]{3,2,1,0:T(8,128)S(1)}, f32[6,96,128]{2,1,0:T(8,128)S(1)}, f32[8,56,128]{2,1,0:T(8,128)S(1)}, f32[6,96,128]{2,1,0:T(8,128)S(1)}) custom-call(s32[1]{0:T(128)} %bitcast.place, s32[8]{0:T(128)S(1)} %copy-done.25, s32[48]{0:T(128)S(1)} %reshape.20.orientation, f32[108]{0:T(128)S(1)} %reshape.21.mats, ...), custom_call_target="tpu_custom_call" | custom-call | flops 884736 | bytes 3145728 | tf_op jit(solution)/shard_map/pallas_call | solution.py:556
  46.7 0.7 copy-done.6
  47.4 0.7 copy-done.13
  48.1 0.7 copy-done.19
  48.8 4.5 %all-to-all-start.2 = ((f32[8,56,128]{2,1,0:T(8,128)}), f32[8,56,128]{2,1,0:T(8,128)S(1)}, u32[]{:S(2)}, u32[]{:S(2)}) async-start(f32[8,56,128]{2,1,0:T(8,128)} %copy-done.19), calls=%async_computation.2 | async-start | bytes 458752 | tf_op jit(solution)/shard_map/all_to_all | solution.py:520
  53.4 0.6 copy-done.22
  54.0 4.8 %shard_map.90.inner = f32[6,16,16,128]{3,2,1,0:T(8,128)S(1)} custom-call(f32[108]{0:T(128)S(1)} %copy-done.22, f32[6,16,16,128]{3,2,1,0:T(8,128)S(1)} %get-tuple-element.52.block, f32[6,16,16,128]{3,2,1,0:T(8,128)S(1)} %bitcast.17, f32[16,16,128]{2,1,0:T(8,128)S(1)} %bitcast.13), custom_call_target="tpu_custom_call" | custom-call | flops 28311552 | bytes 3145728 | tf_op jit(solution)/shard_map/pallas_call | solution.py:534
  58.8 3.5 %all-to-all-done.2.arrived = f32[8,56,128]{2,1,0:T(8,128)S(1)} async-done(((f32[8,56,128]{2,1,0:T(8,128)}), f32[8,56,128]{2,1,0:T(8,128)S(1)}, u32[]{:S(2)}, u32[]{:S(2)}) %all-to-all-start.2) | async-done | bytes 229408 | tf_op jit(solution)/shard_map/all_to_all | solution.py:520
  62.3 0.7 copy-done.26
  63.0 0.7 copy-done.31
  63.6 0.6 shard_map.91
  64.2 11.6 %all_to_all.35.rest_1_.buffer = f32[8,56,128]{2,1,0:T(8,128)S(1)} all-to-all(f32[8,56,128]{2,1,0:T(8,128)S(1)} %shard_map.91), channel_id=1, replica_groups=mesh['ckpt'=4,'space'=8] {'space'}, dimensions={0} | all-to-all | bytes 458752 | tf_op jit(solution)/shard_map/all_to_all | solution.py:520
  75.8 4.0 %all-to-all-start.4 = ((f32[8,56,128]{2,1,0:T(8,128)}), f32[8,56,128]{2,1,0:T(8,128)}, u32[]{:S(2)}, u32[]{:S(2)}) async-start(f32[8,56,128]{2,1,0:T(8,128)} %get-tuple-element.54), calls=%async_computation.4 | async-start | bytes 458752 | tf_op jit(solution)/shard_map/all_to_all | solution.py:520
  79.9 0.6 copy-done.23
  80.5 3.5 %shard_map.92.inner = f32[6,16,16,128]{3,2,1,0:T(8,128)S(1)} custom-call(f32[108]{0:T(128)S(1)} %copy-done.23, f32[6,16,16,128]{3,2,1,0:T(8,128)S(1)} %get-tuple-element.52.block, f32[16,16,128]{2,1,0:T(8,128)S(1)} %bitcast.14), custom_call_target="tpu_custom_call" | custom-call | flops 14155776 | bytes 3145728 | tf_op jit(solution)/shard_map/pallas_call | solution.py:529
  84.1 3.8 %all-to-all-done.4.rest_2_ = f32[8,56,128]{2,1,0:T(8,128)} async-done(((f32[8,56,128]{2,1,0:T(8,128)}), f32[8,56,128]{2,1,0:T(8,128)}, u32[]{:S(2)}, u32[]{:S(2)}) %all-to-all-start.4) | async-done | bytes 229408 | tf_op jit(solution)/shard_map/all_to_all | solution.py:520
  87.9 0.7 copy-done.24
  88.6 1.0 copy-done.7
  89.6 1.0 copy-done.18
  90.5 3.1 %shard_map.93 = (f32[6,16,16,128]{3,2,1,0:T(8,128)S(1)}, f32[6,96,128]{2,1,0:T(8,128)S(1)}, f32[8,56,128]{2,1,0:T(8,128)}) custom-call(s32[1]{0:T(128)} %bitcast.place, s32[8]{0:T(128)S(1)} %copy-done.27, s32[48]{0:T(128)S(1)} %copy-done.29, f32[108]{0:T(128)S(1)} %copy-done.24, f32[6,16,16,128]{3,2,1,0:T(8,128)S(1)} %shard_map.90.inner, ...), custom_call_target="tpu_custom_call" | custom-call | flops 884736 | bytes 3145728 | tf_op jit(solution)/shard_map/pallas_call | solution.py:572
  93.6 0.9 copy-done.11
  94.5 0.7 copy-done.15
  95.2 3.4 %all-to-all-start.5 = ((f32[8,56,128]{2,1,0:T(8,128)}), f32[8,56,128]{2,1,0:T(8,128)S(1)}, u32[]{:S(2)}, u32[]{:S(2)}) async-start(f32[8,56,128]{2,1,0:T(8,128)} %get-tuple-element.55), calls=%async_computation.5 | async-start | bytes 458752 | tf_op jit(solution)/shard_map/all_to_all | solution.py:520
  98.6 1.1 copy-done.12
  99.8 4.8 %shard_map.94.inner = f32[6,16,16,128]{3,2,1,0:T(8,128)S(1)} custom-call(f32[108]{0:T(128)S(1)} %copy-done.24, f32[4,6,4,16,128]{4,3,2,1,0:T(8,128)S(1)} %bitcast.10, f32[6,16,16,128]{3,2,1,0:T(8,128)S(1)} %copy-done.12, f32[16,16,128]{2,1,0:T(8,128)S(1)} %bitcast.15), custom_call_target="tpu_custom_call" | custom-call | flops 28311552 | bytes 3145728 | tf_op jit(solution)/shard_map/pallas_call | solution.py:534
  104.6 2.0 %all-to-all-done.5.arrived = f32[8,56,128]{2,1,0:T(8,128)S(1)} async-done(((f32[8,56,128]{2,1,0:T(8,128)}), f32[8,56,128]{2,1,0:T(8,128)S(1)}, u32[]{:S(2)}, u32[]{:S(2)}) %all-to-all-start.5) | async-done | bytes 229408 | tf_op jit(solution)/shard_map/all_to_all | solution.py:520
  106.6 1.3 %shard_map.95 = f32[8,56,128]{2,1,0:T(8,128)} custom-call(s32[8]{0:T(128)S(1)} %copy-done.27, s32[48]{0:T(128)S(1)} %copy-done.32, f32[8,56,128]{2,1,0:T(8,128)S(1)} %all-to-all-done.5.arrived), custom_call_target="tpu_custom_call" | custom-call | flops 884736 | bytes 3145728 | tf_op jit(solution)/shard_map/pallas_call | solution.py:523
  107.9 4.1 %all-to-all-start.6 = ((f32[8,56,128]{2,1,0:T(8,128)}), f32[8,56,128]{2,1,0:T(8,128)S(1)}, u32[]{:S(2)}, u32[]{:S(2)}) async-start(f32[8,56,128]{2,1,0:T(8,128)} %shard_map.95), calls=%async_computation.6 | async-start | bytes 458752 | tf_op jit(solution)/shard_map/all_to_all | solution.py:520
  112.0 2.2 %shard_map.96 = f32[6,16,16,128]{3,2,1,0:T(8,128)} custom-call(s32[1]{0:T(128)} %bitcast.place, s32[8]{0:T(128)S(1)} %copy-done.27, s32[48]{0:T(128)S(1)} %copy-done.29, f32[108]{0:T(128)S(1)} %copy-done.24, f32[6,16,16,128]{3,2,1,0:T(8,128)S(1)} %shard_map.92.inner, f32[6,96,128]{2,1,0:T(8,128)S(1)} %copy-done.8, ...), custom_call_target="tpu_custom_call" | custom-call | flops 14155776 | bytes 3145728 | tf_op jit(solution)/shard_map/pallas_call | solution.py:586
  114.2 5.7 %all-to-all-done.6.rest_1_ = f32[8,56,128]{2,1,0:T(8,128)S(1)} async-done(((f32[8,56,128]{2,1,0:T(8,128)}), f32[8,56,128]{2,1,0:T(8,128)S(1)}, u32[]{:S(2)}, u32[]{:S(2)}) %all-to-all-start.6) | async-done | bytes 229408 | tf_op jit(solution)/shard_map/all_to_all | solution.py:520
  120.0 2.3 %shard_map.97 = f32[6,16,16,128]{3,2,1,0:T(8,128)} custom-call(s32[1]{0:T(128)} %bitcast.place, s32[8]{0:T(128)S(1)} %copy-done.27, s32[48]{0:T(128)S(1)} %copy-done.29, f32[108]{0:T(128)S(1)} %copy-done.24, f32[6,16,16,128]{3,2,1,0:T(8,128)S(1)} %shard_map.94.inner, f32[6,96,128]{2,1,0:T(8,128)S(1)} %copy-done.5, f32[6,96,128]{2,1,0:T(8,128)S(1)} %copy-done.16, ...), custom_call_target="tpu_custom_call" | custom-call | flops 884736 | bytes 3145728 | tf_op jit(solution)/shard_map/pallas_call | solution.py:594
  (54 shorter events, 0.3 us)
Async XLA Ops:
  0.6 0.9 copy-start
  1.5 1.1 copy-start.2
  2.7 0.9 copy-start.20
  5.4 0.7 copy-start.17
  6.1 7.4 %copy-start.34 = (s32[8,6]{1,0:T(8,128)S(1)}, s32[8,6]{1,0:T(8,128)}, u32[]{:S(2)}) copy-start(s32[8,6]{1,0:T(8,128)} %param.12) | copy-start | bytes 580
  6.1 17.7 %all-to-all-start = ((f32[8,80,128]{2,1,0:T(8,128)}), f32[8,80,128]{2,1,0:T(8,128)S(1)}, u32[]{:S(2)}, u32[]{:S(2)}) async-start(f32[8,80,128]{2,1,0:T(8,128)} %get-tuple-element.34), calls=%async_computation | async-start | bytes 655360 | tf_op jit(solution)/shard_map/all_to_all | solution.py:520
  13.6 10.2 %copy-start.30 = (s32[48]{0:T(128)}, s32[48]{0:T(128)S(1)}, u32[]{:S(2)}) copy-start(s32[48]{0:T(128)S(1)} %reshape.23.neighbours) | copy-start | bytes 580
  22.2 1.7 %copy-start.25 = (s32[8]{0:T(128)S(1)}, s32[8]{0:T(128)}, u32[]{:S(2)}) copy-start(s32[8]{0:T(128)} %owner.13) | copy-start | bytes 100
  25.2 5.9 %copy-start.1 = (f32[1,16,16,128]{3,2,1,0:T(8,128)S(1)}, f32[1,16,16,128]{3,2,1,0:T(8,128)}, u32[]{:S(2)}) copy-start(f32[1,16,16,128]{3,2,1,0:T(8,128)} %param.9) | copy-start | bytes 393220
  25.2 5.1 %copy-start.33 = (f32[3,6,6]{2,1,0:T(8,128)S(1)}, f32[3,6,6]{2,1,0:T(8,128)}, u32[]{:S(2)}) copy-start(f32[3,6,6]{2,1,0:T(8,128)} %param.10) | copy-start | bytes 1300
  25.2 12.3 %all-to-all-start.1 = ((f32[8,24,128]{2,1,0:T(8,128)}), f32[8,24,128]{2,1,0:T(8,128)S(1)}, u32[]{:S(2)}, u32[]{:S(2)}) async-start(f32[8,24,128]{2,1,0:T(8,128)} %get-tuple-element.37), calls=%async_computation.1 | async-start | bytes 196608 | tf_op jit(solution)/shard_map/all_to_all | solution.py:520
  30.4 0.7 copy-start.35
  31.1 12.6 %copy-start.21 = (f32[108]{0:T(128)}, f32[108]{0:T(128)S(1)}, u32[]{:S(2)}) copy-start(f32[108]{0:T(128)S(1)} %reshape.21.mats) | copy-start | bytes 1300
  31.2 12.5 %copy-start.28 = (s32[48]{0:T(128)}, s32[48]{0:T(128)S(1)}, u32[]{:S(2)}) copy-start(s32[48]{0:T(128)S(1)} %reshape.20.orientation) | copy-start | bytes 580
  35.1 0.9 copy-start.9
  36.0 10.7 %copy-start.4 = (f32[6,96,128]{2,1,0:T(8,128)}, f32[6,96,128]{2,1,0:T(8,128)S(1)}, u32[]{:S(2)}) copy-start(f32[6,96,128]{2,1,0:T(8,128)S(1)} %get-tuple-element.42.faces) | copy-start | bytes 884740
  43.6 1.1 copy-start.10
  44.8 8.6 %copy-start.3 = (f32[1,1,6,16,16,128]{5,4,3,2,1,0:T(8,128)S(1)}, f32[1,1,6,16,16,128]{5,4,3,2,1,0:T(8,128)}, u32[]{:S(2)}) copy-start(f32[1,1,6,16,16,128]{5,4,3,2,1,0:T(8,128)} %param.8) | copy-start | bytes 2359300
  46.7 0.7 copy-start.6
  47.4 0.7 copy-start.13
  48.1 0.7 copy-start.19
  48.8 13.5 %all-to-all-start.2 = ((f32[8,56,128]{2,1,0:T(8,128)}), f32[8,56,128]{2,1,0:T(8,128)S(1)}, u32[]{:S(2)}, u32[]{:S(2)}) async-start(f32[8,56,128]{2,1,0:T(8,128)} %copy-done.19), calls=%async_computation.2 | async-start | bytes 458752 | tf_op jit(solution)/shard_map/all_to_all | solution.py:520
  53.4 0.7 copy-start.22
  62.3 0.7 copy-start.26
  63.0 0.7 copy-start.31
  75.8 12.1 %all-to-all-start.4 = ((f32[8,56,128]{2,1,0:T(8,128)}), f32[8,56,128]{2,1,0:T(8,128)}, u32[]{:S(2)}, u32[]{:S(2)}) async-start(f32[8,56,128]{2,1,0:T(8,128)} %get-tuple-element.54), calls=%async_computation.4 | async-start | bytes 458752 | tf_op jit(solution)/shard_map/all_to_all | solution.py:520
  79.9 0.7 copy-start.23
  87.9 0.7 copy-start.24
  87.9 0.7 copy-start.27
  87.9 0.7 copy-start.29
  88.6 1.0 copy-start.7
  89.6 1.0 copy-start.18
  93.6 0.9 copy-start.11
  94.5 0.7 copy-start.15
  95.2 11.3 %all-to-all-start.5 = ((f32[8,56,128]{2,1,0:T(8,128)}), f32[8,56,128]{2,1,0:T(8,128)S(1)}, u32[]{:S(2)}, u32[]{:S(2)}) async-start(f32[8,56,128]{2,1,0:T(8,128)} %get-tuple-element.55), calls=%async_computation.5 | async-start | bytes 458752 | tf_op jit(solution)/shard_map/all_to_all | solution.py:520
  98.6 1.1 copy-start.12
  99.8 6.8 %copy-start.32 = (s32[48]{0:T(128)S(1)}, s32[48]{0:T(128)}, u32[]{:S(2)}) copy-start(s32[48]{0:T(128)} %copy-done.30) | copy-start | bytes 580
  107.9 4.1 %copy-start.8 = (f32[6,96,128]{2,1,0:T(8,128)S(1)}, f32[6,96,128]{2,1,0:T(8,128)}, u32[]{:S(2)}) copy-start(f32[6,96,128]{2,1,0:T(8,128)} %copy-done.6) | copy-start | bytes 884740
  107.9 12.1 %all-to-all-start.6 = ((f32[8,56,128]{2,1,0:T(8,128)}), f32[8,56,128]{2,1,0:T(8,128)S(1)}, u32[]{:S(2)}, u32[]{:S(2)}) async-start(f32[8,56,128]{2,1,0:T(8,128)} %shard_map.95), calls=%async_computation.6 | async-start | bytes 458752 | tf_op jit(solution)/shard_map/all_to_all | solution.py:520
  112.0 8.0 %copy-start.5 = (f32[6,96,128]{2,1,0:T(8,128)S(1)}, f32[6,96,128]{2,1,0:T(8,128)}, u32[]{:S(2)}) copy-start(f32[6,96,128]{2,1,0:T(8,128)} %copy-done.4) | copy-start | bytes 884740
  112.0 8.0 %copy-start.14 = (f32[6,96,128]{2,1,0:T(8,128)S(1)}, f32[6,96,128]{2,1,0:T(8,128)}, u32[]{:S(2)}) copy-start(f32[6,96,128]{2,1,0:T(8,128)} %copy-done.13) | copy-start | bytes 884740
  112.0 8.0 %copy-start.16 = (f32[6,96,128]{2,1,0:T(8,128)S(1)}, f32[6,96,128]{2,1,0:T(8,128)}, u32[]{:S(2)}) copy-start(f32[6,96,128]{2,1,0:T(8,128)} %copy-done.15) | copy-start | bytes 884740

commit v5 on v4

--- a/solution.py
+++ b/solution.py
@@ -14,7 +14,7 @@
 PAD = 8
 VMEM = pl.BlockSpec(memory_space=pltpu.VMEM)
 SMEM = pl.BlockSpec(memory_space=pltpu.SMEM)
-VMEM_LIMIT = 12 * 1024 * 1024
+VMEM_LIMIT = 16 * 1024 * 1024
 
 
 class Pieces:
@@ -315,10 +315,10 @@
     return out
 
 
-def pack_kernel(geo, part, stored, grads, rate, kept, weight_faces, rate_faces, buffer, pieces):
+def pack_kernel(geo, late, part, stored, grads, rate, weight_faces, rate_faces, buffer, pieces):
     v, x, y, z = geo.block
     depth = geo.depth
-    kept[...] = stored[...]
+    late.wait(1)
     lane = lax.broadcasted_iota(jnp.int32, (y, z), 1)
     plane = jnp.where(part[0] == geo.parts - 1, depth - 1, 0)
     high = jnp.zeros((y, z), jnp.float32)
@@ -336,6 +336,8 @@
     pieces[3, :y] = high
     pieces[4, :y] = low
     cut(geo, geo.part, pieces, buffer, 0)
+    late.wait(2)
+    late.wait(3)
     rate_faces[0, :y] = rate[x - 1]
     rate_faces[1, :y] = rate[0]
     rate_faces[2, :x] = rate[:, y - 1, :]
@@ -343,7 +345,9 @@
     high, low = take_z_faces(geo, lambda var, plane: rate[plane])
     rate_faces[4, :y] = high
     rate_faces[5, :y] = low
+    late.leave(1)
     take_weight_faces(geo, grads, rate_faces, weight_faces)
+    late.leave(0)
     cut(geo, geo.whole, weight_faces, buffer, geo.part.total)
 
 
@@ -369,11 +373,11 @@
             leaving[target, start : start + run] = arrived[source, far : far + run]
 
 
-def route_kernel(geo, owner, neighbours, arrived, leaving):
+def route_kernel(geo, late, owner, neighbours, arrived, leaving):
     route_whole(geo, owner, neighbours, arrived, 0, leaving)
 
 
-def route_first_kernel(geo, part, owner, neighbours, arrived, leaving, weight_leaving):
+def route_first_kernel(geo, late, part, owner, neighbours, arrived, leaving, weight_leaving):
     route_whole(geo, owner, neighbours, arrived, geo.part.total, weight_leaving)
     x_side = jnp.where(part[0] == geo.parts - 1, 1, 0)
     for block in range(geo.n):
@@ -385,8 +389,10 @@
             leaving[target, start : start + run] = arrived[source, far : far + run]
 
 
-def step_inner_kernel(geo, mats, block, rate, result, *rest):
+def step_inner_kernel(geo, late, mats, block, rate, result, *rest):
     tall = rest[-1]
+    late.wait(1)
+    late.wait(2)
     fill_tall(geo, block, tall)
 
     def body(plane, carry):
@@ -409,8 +415,10 @@
         faces[5, :y] = low
 
 
-def adjoint_inner_kernel(geo, mats, block, grads, rate, result, tall, weights):
-    v, x, y, z = geo.block
+def adjoint_inner_kernel(geo, late, mats, block, grads, rate, result, tall, weights):
+    v, x, y, z = geo.block
+    for index in range(1, 4):
+        late.wait(index)
     fill_tall(geo, block, tall)
 
     def scale(plane, carry):
@@ -435,15 +443,15 @@
     lax.fori_loop(0, x, body, 0)
 
 
-def step_edge_kernel(geo, first, place, owner, orientation, mats, inner, faces, rate_faces, buffer, result, *rest):
+def step_edge_kernel(geo, first, late, place, owner, orientation, mats, inner, faces, rate_faces, arrived, result, *rest):
+    v, x, y, z = geo.block
     if first:
         new_faces, sent, ghosts, raw, piece = rest
-        join_parts(geo, buffer, raw, piece)
+        join_parts(geo, arrived, raw, piece)
+        turn(geo, own_codes(geo, place, owner, orientation), raw, ghosts)
+        late.leave(2)
     else:
-        ghosts, raw = rest
-        join(geo, buffer, raw)
-    v, x, y, z = geo.block
-    turn(geo, own_codes(geo, place, owner, orientation), raw, ghosts)
+        ghosts = arrived
     result[...] = inner[...]
     terms = []
     for side in range(6):
@@ -455,25 +463,30 @@
         else:
             terms.append(values)
     add_z_terms(geo, *terms, result)
+    late.leave(0)
     if first:
         take_xy_faces(geo, result, new_faces)
         high, low = take_z_faces(geo, lambda var, plane: result[var, plane])
         new_faces[4, :y] = high
         new_faces[5, :y] = low
+        late.leave(1)
         cut(geo, geo.whole, new_faces, sent, 0)
 
 
-def adjoint_edge_kernel(geo, last, place, owner, orientation, mats, inner, faces, weight_faces, *rest):
+def adjoint_edge_kernel(geo, last, late, place, owner, orientation, mats, inner, faces, weight_faces, *rest):
     v, x, y, z = geo.block
     codes = own_codes(geo, place, owner, orientation)
     if last:
         ghosts, weight_buffer, result, raw, weight_ghosts = rest
+        join(geo, weight_buffer, raw)
+        turn(geo, codes, raw, weight_ghosts)
     else:
-        rate_faces, buffer, weight_buffer, result, new_faces, sent, raw, ghosts, weight_ghosts = rest
+        rate_faces, buffer, weight_buffer, result, new_faces, sent, ghosts, raw, weight_ghosts = rest
         join(geo, buffer, raw)
         turn(geo, codes, raw, ghosts)
-    join(geo, weight_buffer, raw)
-    turn(geo, codes, raw, weight_ghosts)
+        late.leave(2)
+        join(geo, weight_buffer, raw)
+        turn(geo, codes, raw, weight_ghosts)
     result[...] = inner[...]
     terms = []
     for side in range(6):
@@ -484,21 +497,79 @@
         else:
             terms.append(values)
     add_z_terms(geo, *terms, result)
+    late.leave(0)
     if not last:
         take_weight_faces(geo, result, rate_faces, new_faces)
+        late.leave(1)
         cut(geo, geo.whole, new_faces, sent, 0)
 
 
-def call(kernel, specs, outs, scratch, flops):
-    return pl.pallas_call(
-        kernel,
-        in_specs=specs,
-        out_specs=[VMEM] * len(outs),
-        out_shape=[jax.ShapeDtypeStruct(shape, jnp.float32) for shape in outs],
-        scratch_shapes=[pltpu.VMEM(shape, jnp.float32) for shape in scratch],
+class Late:
+    def __init__(self, arrivals, departures):
+        self.arrivals, self.departures = arrivals, departures
+
+    def wait(self, index):
+        if index in self.arrivals:
+            self.arrivals[index].wait()
+
+    def leave(self, index):
+        if index in self.departures:
+            self.departures[index].start()
+
+
+def call(kernel, ins, outs, scratch, flops):
+    late_in = [(index, shape) for index, (kind, shape) in enumerate(ins) if kind == "H"]
+    late_out = [(index, shape) for index, (kind, shape) in enumerate(outs) if kind == "H"]
+    count_in, count_out = len(late_in), len(late_out)
+
+    def body(*refs):
+        given = list(refs[: len(ins)])
+        made = list(refs[len(ins) : len(ins) + len(outs)])
+        rest = list(refs[len(ins) + len(outs) :])
+        own = rest[: len(scratch)]
+        stage = rest[len(scratch) : len(scratch) + count_in + count_out]
+        sems = rest[-1] if count_in + count_out else None
+        arrivals, departures = {}, {}
+        for slot, (index, _) in enumerate(late_in):
+            copy = pltpu.make_async_copy(given[index], stage[slot], sems.at[slot])
+            copy.start()
+            arrivals[index] = copy
+            given[index] = stage[slot]
+        for slot, (index, _) in enumerate(late_out):
+            spot = count_in + slot
+            departures[index] = pltpu.make_async_copy(stage[spot], made[index], sems.at[spot])
+            made[index] = stage[spot]
+        kernel(Late(arrivals, departures), *given, *made, *own)
+        for copy in departures.values():
+            copy.wait()
+
+    hbm = pl.BlockSpec(memory_space=pltpu.HBM)
+    specs = {"S": SMEM, "V": VMEM, "R": VMEM, "H": hbm}
+    scratch_shapes = [pltpu.VMEM(shape, jnp.float32) for shape in scratch]
+    scratch_shapes += [pltpu.VMEM(shape, jnp.float32) for _, shape in late_in + late_out]
+    if count_in + count_out:
+        scratch_shapes.append(pltpu.SemaphoreType.DMA((count_in + count_out,)))
+    shapes = {"V": jax.ShapeDtypeStruct, "R": pltpu.VMEM, "H": pltpu.HBM}
+    invoke = pl.pallas_call(
+        body,
+        in_specs=[specs[kind] for kind, _ in ins],
+        out_specs=[specs[kind] for kind, _ in outs],
+        out_shape=[shapes[kind](shape, jnp.float32) for kind, shape in outs],
+        scratch_shapes=scratch_shapes,
         compiler_params=pltpu.CompilerParams(vmem_limit_bytes=VMEM_LIMIT),
         cost_estimate=pl.CostEstimate(flops=flops, bytes_accessed=3 << 20, transcendentals=0),
     )
+
+    def run(*operands):
+        placed = {"H": pltpu.HBM, "R": pltpu.VMEM}
+        return invoke(
+            *[
+                pltpu.with_memory_space_constraint(operand, placed[kind]) if kind in placed else operand
+                for operand, (kind, _) in zip(operands, ins)
+            ]
+        )
+
+    return run
 
 
 def on_device(count, parts, checkpoint, seeds, cell_rate, flux_mats, owner, neighbours, orientation):
@@ -516,86 +587,105 @@
     few = work // 16
     whole, some = geo.buffer(geo.whole.total), geo.buffer(geo.part.total)
 
+    stored_shape, block, faces_shape = checkpoint.shape[1:], geo.block, geo.faces
+    rate_block = cell_rate.shape[1:]
+    scalar, near, kept_near = ("S", None), ("V", None), ("R", None)
+
+    def far(shape):
+        return ("H", shape)
+
     def swap(buffer):
         return lax.all_to_all(buffer, "space", 0, 0, tiled=True)
 
     def route(arrived):
-        return call(functools.partial(route_kernel, geo), [SMEM, SMEM, VMEM], [whole], [], few)(
+        return call(functools.partial(route_kernel, geo), [scalar, scalar, near], [("V", whole)], [], few)(
             owner, neighbours, arrived
         )[0]
 
-    def step_inner(block, faces):
-        outs = [geo.block, geo.faces] if faces else [geo.block]
-        return call(functools.partial(step_inner_kernel, geo), [SMEM, VMEM, VMEM], outs, [geo.tall], work)(
-            mats, block, rate
-        )
-
-    def adjoint_inner(block, grads):
+    def adjoint_inner(state, state_kind, grads, grads_kind):
         return call(
-            functools.partial(adjoint_inner_kernel, geo), [SMEM] + [VMEM] * 3, [geo.block], [geo.tall] * 2, 2 * work
-        )(mats, block, grads, rate)[0]
-
-    kept, weight_faces, rate_faces, sent = call(
+            functools.partial(adjoint_inner_kernel, geo),
+            [scalar, state_kind, grads_kind, far(rate_block)],
+            [("R", block)],
+            [geo.tall] * 2,
+            2 * work,
+        )(mats, state, grads, rate)[0]
+
+    weight_faces, rate_faces, sent = call(
         functools.partial(pack_kernel, geo),
-        [SMEM] + [VMEM] * 3,
-        [checkpoint.shape[1:], geo.faces, geo.rate_faces, geo.buffer(geo.part.total + geo.whole.total)],
-        [geo.faces],
+        [scalar, far(stored_shape), far(block), far(rate_block)],
+        [("R", faces_shape), ("R", geo.rate_faces), ("V", geo.buffer(geo.part.total + geo.whole.total))],
+        [faces_shape],
         few,
     )(part, checkpoint[0], grads, rate)
+    kept, sent = lax.optimization_barrier((checkpoint[0], sent))
     arrived = swap(sent)
     state = lax.all_gather(kept, "ckpt", axis=0)
     arrived, state = lax.optimization_barrier((arrived, state))
     leaving, weight_leaving = call(
-        functools.partial(route_first_kernel, geo), [SMEM] * 3 + [VMEM], [some, whole], [], few
+        functools.partial(route_first_kernel, geo), [scalar] * 3 + [near], [("V", some), ("V", whole)], [], few
     )(part, owner, neighbours, arrived)
     part_ghosts = swap(leaving)
-    inner, faces = step_inner(state, True)
+    inner, faces = call(
+        functools.partial(step_inner_kernel, geo),
+        [scalar, far(state.shape), far(rate_block)],
+        [("R", block), ("R", faces_shape)],
+        [geo.tall],
+        work,
+    )(mats, state, rate)
     part_ghosts, inner, faces = lax.optimization_barrier((part_ghosts, inner, faces))
     weight_ghosts = swap(weight_leaving)
     gathered = lax.all_gather(part_ghosts, "ckpt", axis=0)
     next_state, next_faces, sent, ghosts = call(
         functools.partial(step_edge_kernel, geo, True),
-        [SMEM] * 4 + [VMEM] * 4,
-        [geo.block, geo.faces, whole, geo.faces],
-        [geo.faces, geo.faces[1:]],
+        [scalar] * 4 + [kept_near] * 3 + [near],
+        [("R", block), ("R", faces_shape), ("V", whole), ("R", faces_shape)],
+        [faces_shape, faces_shape[1:]],
         few,
     )(*fixed, inner, faces, rate_faces, gathered)
 
+    sent, weight_ghosts = lax.optimization_barrier((sent, weight_ghosts))
     arrived = swap(sent)
-    inner = adjoint_inner(next_state, grads)
+    inner = adjoint_inner(next_state, kept_near, grads, far(block))
     arrived, inner = lax.optimization_barrier((arrived, inner))
     leaving = route(arrived)
     later_state, leaving = lax.optimization_barrier((next_state, leaving))
     next_ghosts = swap(leaving)
-    (final_inner,) = step_inner(later_state, False)
+    (final_inner,) = call(
+        functools.partial(step_inner_kernel, geo),
+        [scalar, kept_near, far(rate_block)],
+        [("R", block)],
+        [geo.tall],
+        work,
+    )(mats, later_state, rate)
     next_ghosts, final_inner = lax.optimization_barrier((next_ghosts, final_inner))
-    grads_now, next_weight_faces, sent = call(
+    grads_now, next_weight_faces, sent, turned = call(
         functools.partial(adjoint_edge_kernel, geo, False),
-        [SMEM] * 4 + [VMEM] * 6,
-        [geo.block, geo.faces, whole],
-        [geo.faces] * 3,
+        [scalar] * 4 + [kept_near] * 4 + [near, near],
+        [("R", block), ("R", faces_shape), ("V", whole), ("R", faces_shape)],
+        [faces_shape] * 2,
         few,
     )(*fixed, inner, next_faces, weight_faces, rate_faces, next_ghosts, weight_ghosts)
 
     arrived = swap(sent)
-    inner = adjoint_inner(state, grads_now)
+    inner = adjoint_inner(state, far(state.shape), grads_now, kept_near)
     arrived, inner = lax.optimization_barrier((arrived, inner))
     leaving = route(arrived)
     final_inner, leaving = lax.optimization_barrier((final_inner, leaving))
     last_ghosts = swap(leaving)
     (final,) = call(
         functools.partial(step_edge_kernel, geo, False),
-        [SMEM] * 4 + [VMEM] * 4,
-        [geo.block],
-        [geo.faces] * 2,
+        [scalar] * 4 + [kept_near] * 4,
+        [("V", block)],
+        [],
         work,
-    )(*fixed, final_inner, next_faces, rate_faces, next_ghosts)
+    )(*fixed, final_inner, next_faces, rate_faces, turned)
     last_ghosts, final = lax.optimization_barrier((last_ghosts, final))
     (adjoint,) = call(
         functools.partial(adjoint_edge_kernel, geo, True),
-        [SMEM] * 4 + [VMEM] * 5,
-        [geo.block],
-        [geo.faces] * 2,
+        [scalar] * 4 + [kept_near] * 4 + [near],
+        [("V", block)],
+        [faces_shape] * 2,
         few,
     )(*fixed, inner, faces, next_weight_faces, ghosts, last_ghosts)
     return (adjoint[None, None], final[None])

time: 123 us -> 118 us (0.959)
  local copies, waits for them, and re-layouts: 16.6 us -> 8.32 us
  Pallas kernels: 31.7 us -> 37.3 us
  waiting for transfers between devices: 18.2 us -> 14.1 us
    unnamed x72 -> x32, local copies, waits for them, and re-layouts: 16.4 us -> 8.08 us
    pallas_call x12, Pallas kernels: 31.7 us -> 37.3 us  [run(): invoke(*[pltpu.with_memory_space_constraint(operand, placed[kind]) if kin...]
    all_to_all x6, waiting for transfers between devices: 18.2 us -> 14.1 us  [swap(): return lax.all_to_all(buffer, 'space', 0, 0, tiled=True)]
  transfers between devices with their start and end apart: 6 -> 6, of which waited for: 6 -> 5; matrix products, arithmetic and copies ran while one was open for 0% -> 0% of each run, Pallas kernels for 16% -> 22%
where the time goes in v5:
time: 118 us; the launch traced here: 117 us
  Pallas kernels  37.3 us (32%)
  starting transfers between devices  28.7 us (24%)
  blocking collectives  27.5 us (23%)
  waiting for transfers between devices  14.1 us (12%)
  local copies, waits for them, and re-layouts  8.32 us (7%)
    pallas_call x12, Pallas kernels, run(): invoke(*[pltpu.with_memory_space_constraint(operand, placed[kind]) if kin...  37.3 us
    all_to_all x6, starting transfers between devices, swap(): return lax.all_to_all(buffer, 'space', 0, 0, tiled=True)  28.7 us
    all_to_all x6, waiting for transfers between devices, swap(): return lax.all_to_all(buffer, 'space', 0, 0, tiled=True)  14.1 us
    all_to_all x1, blocking collectives, swap(): return lax.all_to_all(buffer, 'space', 0, 0, tiled=True)  12.4 us
    all_gather x1, blocking collectives, on_device(): state = lax.all_gather(kept, 'ckpt', axis=0)  9.04 us
    unnamed x32, local copies, waits for them, and re-layouts  8.08 us
    all_gather x1, blocking collectives, on_device(): gathered = lax.all_gather(part_ghosts, 'ckpt', axis=0)  6.15 us
  transfers between devices with their start and end apart: 6, of which 5 were waited for; matrix products, arithmetic and copies ran while one was open for 0% of the time, Pallas kernels for 22%

profile of v5, /device:TPU:0, one launch (start us, length us, event | category | flops | bytes accessed | tf_op | source)
XLA Modules:
  0.0 116.7 jit_solution(15689050094416054290)
XLA Ops:
  0.6 2.9 %shard_map.86 = (f32[6,96,128]{2,1,0:T(8,128)S(1)}, f32[6,16,128]{2,1,0:T(8,128)S(1)}, f32[8,80,128]{2,1,0:T(8,128)}) custom-call(s32[1]{0:T(128)} %bitcast.1.refs_0_, f32[6,4,16,128]{3,2,1,0:T(8,128)} %bitcast.21, f32[6,16,16,128]{3,2,1,0:T(8,128)} %bitcast.17, f32[16,16,128]{2,1,0:T(8,128)} %bitcast.12), custom_call_target="tpu_custom_call" | custom-call | flops 884736 | bytes 3145728 | tf_op jit(solution)/shard_map/pallas_call | solution.py:565
  3.6 0.0 copy-start.8
  3.6 0.7 copy-done.8
  4.3 7.4 %all-to-all-start = ((f32[8,80,128]{2,1,0:T(8,128)}), f32[8,80,128]{2,1,0:T(8,128)S(1)}, u32[]{:S(2)}, u32[]{:S(2)}) async-start(f32[8,80,128]{2,1,0:T(8,128)} %get-tuple-element.39), calls=%async_computation | async-start | bytes 655360 | tf_op jit(solution)/shard_map/all_to_all | solution.py:598
  11.7 0.0 copy-done.14
  11.7 0.1 reshape.23.refs_2_.refs_1_
  11.8 0.0 copy-done.12
  11.8 9.0 %all-gather = f32[24,4,16,128]{3,2,1,0:T(8,128)} all-gather(f32[6,4,16,128]{3,2,1,0:T(8,128)S(1)} %bitcast.22), channel_id=2, replica_groups=mesh['ckpt'=4,'space'=8] {'ckpt'}, dimensions={0}, use_global_device_ids=true | all-gather | bytes 983040 | tf_op jit(solution)/shard_map/all_gather | solution.py:623
  20.8 1.2 %all-to-all-done.refs_3_ = f32[8,80,128]{2,1,0:T(8,128)S(1)} async-done(((f32[8,80,128]{2,1,0:T(8,128)}), f32[8,80,128]{2,1,0:T(8,128)S(1)}, u32[]{:S(2)}, u32[]{:S(2)}) %all-to-all-start) | async-done | bytes 327712 | tf_op jit(solution)/shard_map/all_to_all | solution.py:598
  22.0 0.0 copy-done.11
  22.0 1.3 %shard_map.87 = (f32[8,24,128]{2,1,0:T(8,128)S(1)}, f32[8,56,128]{2,1,0:T(8,128)}) custom-call(s32[1]{0:T(128)} %bitcast.1.refs_0_, s32[8]{0:T(128)S(1)} %copy-done.11, s32[48]{0:T(128)S(1)} %reshape.23.refs_2_.refs_1_, f32[8,80,128]{2,1,0:T(8,128)S(1)} %all-to-all-done.refs_3_), custom_call_target="tpu_custom_call" | custom-call | flops 884736 | bytes 3145728 | tf_op jit(solution)/shard_map/pallas_call | solution.py:565
  23.4 12.4 %all_to_all.35 = f32[8,24,128]{2,1,0:T(8,128)S(1)} all-to-all(f32[8,24,128]{2,1,0:T(8,128)S(1)} %get-tuple-element.42), channel_id=1, replica_groups=mesh['ckpt'=4,'space'=8] {'space'}, dimensions={0} | all-to-all | bytes 196608 | tf_op jit(solution)/shard_map/all_to_all | solution.py:598
  35.8 3.5 %all-to-all-start.2 = ((f32[8,56,128]{2,1,0:T(8,128)}), f32[8,56,128]{2,1,0:T(8,128)S(1)}, u32[]{:S(2)}, u32[]{:S(2)}) async-start(f32[8,56,128]{2,1,0:T(8,128)} %get-tuple-element.51), calls=%async_computation.2 | async-start | bytes 458752 | tf_op jit(solution)/shard_map/all_to_all | solution.py:598
  39.3 0.0 copy-start.15
  39.3 0.1 reshape.21.refs_0_.refs_3_
  39.4 0.6 copy-done.15
  40.0 0.1 reshape.20.refs_2_
  40.1 5.1 %shard_map.88 = (f32[6,16,16,128]{3,2,1,0:T(8,128)S(1)}, f32[6,96,128]{2,1,0:T(8,128)S(1)}) custom-call(f32[108]{0:T(128)S(1)} %reshape.21.refs_0_.refs_3_, f32[4,6,4,16,128]{4,3,2,1,0:T(8,128)} %bitcast.10, f32[16,16,128]{2,1,0:T(8,128)} %bitcast.13), custom_call_target="tpu_custom_call" | custom-call | flops 14155776 | bytes 3145728 | tf_op jit(solution)/shard_map/pallas_call | solution.py:565
  45.2 6.1 %all-gather.1 = f32[32,24,128]{2,1,0:T(8,128)S(1)} all-gather(f32[8,24,128]{2,1,0:T(8,128)S(1)} %all_to_all.35), channel_id=3, replica_groups=mesh['ckpt'=4,'space'=8] {'ckpt'}, dimensions={0}, use_global_device_ids=true | all-gather | bytes 491520 | tf_op jit(solution)/shard_map/all_gather | solution.py:638
  51.4 2.6 %shard_map.89 = (f32[6,16,16,128]{3,2,1,0:T(8,128)S(1)}, f32[6,96,128]{2,1,0:T(8,128)S(1)}, f32[8,56,128]{2,1,0:T(8,128)}, f32[6,96,128]{2,1,0:T(8,128)S(1)}) custom-call(s32[1]{0:T(128)} %bitcast.refs_0_, s32[8]{0:T(128)S(1)} %copy-done.11, s32[48]{0:T(128)S(1)} %reshape.20.refs_2_, f32[108]{0:T(128)S(1)} %reshape.21.refs_0_.refs_3_, ...), custom_call_target="tpu_custom_call" | custom-call | flops 884736 | bytes 3145728 | tf_op jit(solution)/shard_map/pallas_call | solution.py:565
  54.0 0.7 copy-done.2
  54.7 0.0 all-to-all-done.2.refs_9_
  54.7 5.9 %all-to-all-start.3 = ((f32[8,56,128]{2,1,0:T(8,128)}), f32[8,56,128]{2,1,0:T(8,128)S(1)}, u32[]{:S(2)}, u32[]{:S(2)}) async-start(f32[8,56,128]{2,1,0:T(8,128)} %get-tuple-element.52), calls=%async_computation.3 | async-start | bytes 458752 | tf_op jit(solution)/shard_map/all_to_all | solution.py:598
  60.6 6.0 %shard_map.90.refs_4_ = f32[6,16,16,128]{3,2,1,0:T(8,128)S(1)} custom-call(f32[108]{0:T(128)S(1)} %reshape.21.refs_0_.refs_3_, f32[6,16,16,128]{3,2,1,0:T(8,128)S(1)} %get-tuple-element.59.refs_1_, f32[6,16,16,128]{3,2,1,0:T(8,128)} %bitcast.18, f32[16,16,128]{2,1,0:T(8,128)} %bitcast.14), custom_call_target="tpu_custom_call" | custom-call | flops 28311552 | bytes 3145728 | tf_op jit(solution)/shard_map/pallas_call | solution.py:565
  66.6 3.0 %all-to-all-done.3.refs_2_ = f32[8,56,128]{2,1,0:T(8,128)S(1)} async-done(((f32[8,56,128]{2,1,0:T(8,128)}), f32[8,56,128]{2,1,0:T(8,128)S(1)}, u32[]{:S(2)}, u32[]{:S(2)}) %all-to-all-start.3) | async-done | bytes 229408 | tf_op jit(solution)/shard_map/all_to_all | solution.py:598
  69.6 1.3 %shard_map.91 = f32[8,56,128]{2,1,0:T(8,128)} custom-call(s32[8]{0:T(128)S(1)} %copy-done.11, s32[48]{0:T(128)S(1)} %reshape.23.refs_2_.refs_1_, f32[8,56,128]{2,1,0:T(8,128)S(1)} %all-to-all-done.3.refs_2_), custom_call_target="tpu_custom_call" | custom-call | flops 884736 | bytes 3145728 | tf_op jit(solution)/shard_map/pallas_call | solution.py:565
  70.9 3.4 %all-to-all-start.4 = ((f32[8,56,128]{2,1,0:T(8,128)}), f32[8,56,128]{2,1,0:T(8,128)S(1)}, u32[]{:S(2)}, u32[]{:S(2)}) async-start(f32[8,56,128]{2,1,0:T(8,128)} %shard_map.91), calls=%async_computation.4 | async-start | bytes 458752 | tf_op jit(solution)/shard_map/all_to_all | solution.py:598
  74.3 4.4 %shard_map.92.refs_4_ = f32[6,16,16,128]{3,2,1,0:T(8,128)S(1)} custom-call(f32[108]{0:T(128)S(1)} %reshape.21.refs_0_.refs_3_, f32[6,16,16,128]{3,2,1,0:T(8,128)S(1)} %get-tuple-element.59.refs_1_, f32[16,16,128]{2,1,0:T(8,128)} %bitcast.15), custom_call_target="tpu_custom_call" | custom-call | flops 14155776 | bytes 3145728 | tf_op jit(solution)/shard_map/pallas_call | solution.py:565
  78.7 4.0 %all-to-all-done.4.refs_8_ = f32[8,56,128]{2,1,0:T(8,128)S(1)} async-done(((f32[8,56,128]{2,1,0:T(8,128)}), f32[8,56,128]{2,1,0:T(8,128)S(1)}, u32[]{:S(2)}, u32[]{:S(2)}) %all-to-all-start.4) | async-done | bytes 229408 | tf_op jit(solution)/shard_map/all_to_all | solution.py:598
  82.7 1.0 copy-done.9
  83.6 2.0 %shard_map.93 = (f32[6,16,16,128]{3,2,1,0:T(8,128)S(1)}, f32[6,96,128]{2,1,0:T(8,128)S(1)}, f32[8,56,128]{2,1,0:T(8,128)S(1)}, f32[6,96,128]{2,1,0:T(8,128)S(1)}) custom-call(s32[1]{0:T(128)} %bitcast.refs_0_, s32[8]{0:T(128)S(1)} %copy-done.11, s32[48]{0:T(128)S(1)} %reshape.20.refs_2_, f32[108]{0:T(128)S(1)} %reshape.21.refs_0_.refs_3_, ...), custom_call_target="tpu_custom_call" | custom-call | flops 884736 | bytes 3145728 | tf_op jit(solution)/shard_map/pallas_call | solution.py:565
  85.6 0.0 copy-start
  85.7 0.9 copy-done
  86.5 0.7 copy-done.4
  87.2 0.7 copy-done.6
  88.0 0.7 copy-done.10
  88.6 3.4 %all-to-all-start.5 = ((f32[8,56,128]{2,1,0:T(8,128)}), f32[8,56,128]{2,1,0:T(8,128)S(1)}, u32[]{:S(2)}, u32[]{:S(2)}) async-start(f32[8,56,128]{2,1,0:T(8,128)} %copy-done.10), calls=%async_computation.5 | async-start | bytes 458752 | tf_op jit(solution)/shard_map/all_to_all | solution.py:598
  92.0 0.0 copy-start.1
  92.1 1.1 copy-done.1
  93.2 6.0 %shard_map.94.refs_4_ = f32[6,16,16,128]{3,2,1,0:T(8,128)S(1)} custom-call(f32[108]{0:T(128)S(1)} %reshape.21.refs_0_.refs_3_, f32[4,6,4,16,128]{4,3,2,1,0:T(8,128)} %bitcast.11, f32[6,16,16,128]{3,2,1,0:T(8,128)S(1)} %copy-done.1, f32[16,16,128]{2,1,0:T(8,128)} %bitcast.16), custom_call_target="tpu_custom_call" | custom-call | flops 28311552 | bytes 3145728 | tf_op jit(solution)/shard_map/pallas_call | solution.py:565
  99.2 1.0 all-to-all-done.5.refs_2_
  100.1 1.3 %shard_map.95 = f32[8,56,128]{2,1,0:T(8,128)} custom-call(s32[8]{0:T(128)S(1)} %copy-done.11, s32[48]{0:T(128)S(1)} %reshape.23.refs_2_.refs_1_, f32[8,56,128]{2,1,0:T(8,128)S(1)} %all-to-all-done.5.refs_2_), custom_call_target="tpu_custom_call" | custom-call | flops 884736 | bytes 3145728 | tf_op jit(solution)/shard_map/pallas_call | solution.py:565
  101.4 5.0 %all-to-all-start.6 = ((f32[8,56,128]{2,1,0:T(8,128)}), f32[8,56,128]{2,1,0:T(8,128)S(1)}, u32[]{:S(2)}, u32[]{:S(2)}) async-start(f32[8,56,128]{2,1,0:T(8,128)} %shard_map.95), calls=%async_computation.6 | async-start | bytes 458752 | tf_op jit(solution)/shard_map/all_to_all | solution.py:598
  106.4 1.0 copy-done.7
  107.4 2.1 %shard_map.96 = f32[6,16,16,128]{3,2,1,0:T(8,128)} custom-call(s32[1]{0:T(128)} %bitcast.refs_0_, s32[8]{0:T(128)S(1)} %copy-done.11, s32[48]{0:T(128)S(1)} %reshape.20.refs_2_, f32[108]{0:T(128)S(1)} %reshape.21.refs_0_.refs_3_, f32[6,16,16,128]{3,2,1,0:T(8,128)S(1)} %shard_map.92.refs_4_, f32[6,96,128]{2,1,0:T(8,128)S(1)} %get-tuple-element.55.refs_5_, ...), custom_call_target="tpu_custom_call" | custom-call | flops 14155776 | bytes 3145728 | tf_op jit(solution)/shard_map/pallas_call | solution.py:565
  109.4 5.0 %all-to-all-done.6.refs_8_ = f32[8,56,128]{2,1,0:T(8,128)S(1)} async-done(((f32[8,56,128]{2,1,0:T(8,128)}), f32[8,56,128]{2,1,0:T(8,128)S(1)}, u32[]{:S(2)}, u32[]{:S(2)}) %all-to-all-start.6) | async-done | bytes 229408 | tf_op jit(solution)/shard_map/all_to_all | solution.py:598
  114.4 0.0 copy-done.3
  114.4 2.3 %shard_map.97 = f32[6,16,16,128]{3,2,1,0:T(8,128)} custom-call(s32[1]{0:T(128)} %bitcast.refs_0_, s32[8]{0:T(128)S(1)} %copy-done.11, s32[48]{0:T(128)S(1)} %reshape.20.refs_2_, f32[108]{0:T(128)S(1)} %reshape.21.refs_0_.refs_3_, f32[6,16,16,128]{3,2,1,0:T(8,128)S(1)} %shard_map.94.refs_4_, f32[6,96,128]{2,1,0:T(8,128)S(1)} %get-tuple-element.47.refs_5_, ...), custom_call_target="tpu_custom_call" | custom-call | flops 884736 | bytes 3145728 | tf_op jit(solution)/shard_map/pallas_call | solution.py:565
  (14 shorter events, 0.0 us)
Async XLA Ops:
  3.6 0.7 copy-start.8
  4.3 7.4 %copy-start.14 = (s32[8,6]{1,0:T(8,128)S(1)}, s32[8,6]{1,0:T(8,128)}, u32[]{:S(2)}) copy-start(s32[8,6]{1,0:T(8,128)} %param.12) | copy-start | bytes 580
  4.3 7.5 %copy-start.12 = (f32[1,6,4,16,128]{4,3,2,1,0:T(8,128)S(1)}, f32[1,6,4,16,128]{4,3,2,1,0:T(8,128)}, u32[]{:S(2)}) copy-start(f32[1,6,4,16,128]{4,3,2,1,0:T(8,128)} %param.7) | copy-start | bytes 589828
  4.3 17.7 %all-to-all-start = ((f32[8,80,128]{2,1,0:T(8,128)}), f32[8,80,128]{2,1,0:T(8,128)S(1)}, u32[]{:S(2)}, u32[]{:S(2)}) async-start(f32[8,80,128]{2,1,0:T(8,128)} %get-tuple-element.39), calls=%async_computation | async-start | bytes 655360 | tf_op jit(solution)/shard_map/all_to_all | solution.py:598
  20.8 1.2 %copy-start.11 = (s32[8]{0:T(128)S(1)}, s32[8]{0:T(128)}, u32[]{:S(2)}) copy-start(s32[8]{0:T(128)} %refs_1_.9) | copy-start | bytes 100
  35.8 3.6 %copy-start.13 = (f32[3,6,6]{2,1,0:T(8,128)S(1)}, f32[3,6,6]{2,1,0:T(8,128)}, u32[]{:S(2)}) copy-start(f32[3,6,6]{2,1,0:T(8,128)} %param.10) | copy-start | bytes 1300
  35.8 18.9 %all-to-all-start.2 = ((f32[8,56,128]{2,1,0:T(8,128)}), f32[8,56,128]{2,1,0:T(8,128)S(1)}, u32[]{:S(2)}, u32[]{:S(2)}) async-start(f32[8,56,128]{2,1,0:T(8,128)} %get-tuple-element.51), calls=%async_computation.2 | async-start | bytes 458752 | tf_op jit(solution)/shard_map/all_to_all | solution.py:598
  39.3 0.7 copy-start.15
  54.0 0.7 copy-start.2
  54.7 14.9 %all-to-all-start.3 = ((f32[8,56,128]{2,1,0:T(8,128)}), f32[8,56,128]{2,1,0:T(8,128)S(1)}, u32[]{:S(2)}, u32[]{:S(2)}) async-start(f32[8,56,128]{2,1,0:T(8,128)} %get-tuple-element.52), calls=%async_computation.3 | async-start | bytes 458752 | tf_op jit(solution)/shard_map/all_to_all | solution.py:598
  70.9 11.8 %all-to-all-start.4 = ((f32[8,56,128]{2,1,0:T(8,128)}), f32[8,56,128]{2,1,0:T(8,128)S(1)}, u32[]{:S(2)}, u32[]{:S(2)}) async-start(f32[8,56,128]{2,1,0:T(8,128)} %shard_map.91), calls=%async_computation.4 | async-start | bytes 458752 | tf_op jit(solution)/shard_map/all_to_all | solution.py:598
  82.7 1.0 copy-start.9
  85.6 0.9 copy-start
  86.5 0.7 copy-start.4
  87.2 0.7 copy-start.6
  88.0 0.7 copy-start.10
  88.6 11.5 %all-to-all-start.5 = ((f32[8,56,128]{2,1,0:T(8,128)}), f32[8,56,128]{2,1,0:T(8,128)S(1)}, u32[]{:S(2)}, u32[]{:S(2)}) async-start(f32[8,56,128]{2,1,0:T(8,128)} %copy-done.10), calls=%async_computation.5 | async-start | bytes 458752 | tf_op jit(solution)/shard_map/all_to_all | solution.py:598
  92.0 1.1 copy-start.1
  101.4 13.0 %all-to-all-start.6 = ((f32[8,56,128]{2,1,0:T(8,128)}), f32[8,56,128]{2,1,0:T(8,128)S(1)}, u32[]{:S(2)}, u32[]{:S(2)}) async-start(f32[8,56,128]{2,1,0:T(8,128)} %shard_map.95), calls=%async_computation.6 | async-start | bytes 458752 | tf_op jit(solution)/shard_map/all_to_all | solution.py:598
  106.4 1.0 copy-start.7
  107.4 7.0 %copy-start.3 = (f32[6,96,128]{2,1,0:T(8,128)S(1)}, f32[6,96,128]{2,1,0:T(8,128)}, u32[]{:S(2)}) copy-start(f32[6,96,128]{2,1,0:T(8,128)} %copy-done.2) | copy-start | bytes 884740
  107.4 7.0 %copy-start.5 = (f32[6,96,128]{2,1,0:T(8,128)S(1)}, f32[6,96,128]{2,1,0:T(8,128)}, u32[]{:S(2)}) copy-start(f32[6,96,128]{2,1,0:T(8,128)} %copy-done.4) | copy-start | bytes 884740

commit v6 on v5

--- a/solution.py
+++ b/solution.py
@@ -105,9 +105,9 @@
     ).reshape(rows, z)
 
 
-def join(geo, buffer, raw):
+def join(geo, buffer, raw, base=0):
     for side in range(6):
-        run, start = geo.whole.runs[side], geo.whole.starts[side]
+        run, start = geo.whole.runs[side], base + geo.whole.starts[side]
         for slot in range(geo.n):
             raw[side, slot * run : (slot + 1) * run] = buffer[slot, start : start + run]
 
@@ -349,6 +349,7 @@
     take_weight_faces(geo, grads, rate_faces, weight_faces)
     late.leave(0)
     cut(geo, geo.whole, weight_faces, buffer, geo.part.total)
+    late.leave(2)
 
 
 def take_weight_faces(geo, grads, rate_faces, faces):
@@ -364,21 +365,22 @@
     faces[5, :y] = low * rate_faces[5, :y]
 
 
-def route_whole(geo, owner, neighbours, arrived, base, leaving):
+def route_whole(geo, owner, neighbours, arrived, leaving, base):
     for block in range(geo.n):
         target = owner[block]
         for side in range(6):
             source = owner[neighbours[block * 6 + side]]
-            run, start, far = geo.whole.runs[side], geo.whole.starts[side], base + geo.whole.starts[side ^ 1]
+            run, start, far = geo.whole.runs[side], base + geo.whole.starts[side], base + geo.whole.starts[side ^ 1]
             leaving[target, start : start + run] = arrived[source, far : far + run]
 
 
 def route_kernel(geo, late, owner, neighbours, arrived, leaving):
-    route_whole(geo, owner, neighbours, arrived, 0, leaving)
-
-
-def route_first_kernel(geo, late, part, owner, neighbours, arrived, leaving, weight_leaving):
-    route_whole(geo, owner, neighbours, arrived, geo.part.total, weight_leaving)
+    route_whole(geo, owner, neighbours, arrived, leaving, 0)
+    late.leave(0)
+
+
+def route_first_kernel(geo, late, part, owner, neighbours, arrived, leaving):
+    route_whole(geo, owner, neighbours, arrived, leaving, geo.part.total)
     x_side = jnp.where(part[0] == geo.parts - 1, 1, 0)
     for block in range(geo.n):
         target = owner[block]
@@ -387,6 +389,7 @@
             source = owner[neighbours[block * 6 + side]]
             run, start, far = geo.part.runs[index], geo.part.starts[index], geo.part.starts[far_index]
             leaving[target, start : start + run] = arrived[source, far : far + run]
+    late.leave(0)
 
 
 def step_inner_kernel(geo, late, mats, block, rate, result, *rest):
@@ -402,6 +405,7 @@
         return carry
 
     lax.fori_loop(0, geo.x, body, 0)
+    late.leave(0)
     if len(rest) == 2:
         faces = rest[0]
         v, x, y, z = geo.block
@@ -413,6 +417,7 @@
         high, low = take_z_faces(geo, lambda var, plane: tall[var, plane, PAD : PAD + y])
         faces[4, :y] = high
         faces[5, :y] = low
+        late.leave(1)
 
 
 def adjoint_inner_kernel(geo, late, mats, block, grads, rate, result, tall, weights):
@@ -449,9 +454,12 @@
         new_faces, sent, ghosts, raw, piece = rest
         join_parts(geo, arrived, raw, piece)
         turn(geo, own_codes(geo, place, owner, orientation), raw, ghosts)
-        late.leave(2)
+        late.leave(3)
     else:
         ghosts = arrived
+        late.wait(4)
+        late.wait(7)
+    late.wait(5)
     result[...] = inner[...]
     terms = []
     for side in range(6):
@@ -471,6 +479,7 @@
         new_faces[5, :y] = low
         late.leave(1)
         cut(geo, geo.whole, new_faces, sent, 0)
+        late.leave(2)
 
 
 def adjoint_edge_kernel(geo, last, late, place, owner, orientation, mats, inner, faces, weight_faces, *rest):
@@ -484,9 +493,11 @@
         rate_faces, buffer, weight_buffer, result, new_faces, sent, ghosts, raw, weight_ghosts = rest
         join(geo, buffer, raw)
         turn(geo, codes, raw, ghosts)
-        late.leave(2)
-        join(geo, weight_buffer, raw)
+        late.leave(3)
+        join(geo, weight_buffer, raw, geo.part.total)
         turn(geo, codes, raw, weight_ghosts)
+    for index in range(5, 8):
+        late.wait(index)
     result[...] = inner[...]
     terms = []
     for side in range(6):
@@ -502,6 +513,7 @@
         take_weight_faces(geo, result, rate_faces, new_faces)
         late.leave(1)
         cut(geo, geo.whole, new_faces, sent, 0)
+        late.leave(2)
 
 
 class Late:
@@ -585,7 +597,8 @@
     fixed = (place, owner, orientation, mats)
     work = nvars * nvars * 3 * 4 * cx * cy * cz
     few = work // 16
-    whole, some = geo.buffer(geo.whole.total), geo.buffer(geo.part.total)
+    whole, both = geo.buffer(geo.whole.total), geo.buffer(geo.part.total + geo.whole.total)
+    some = -(-geo.part.total // 8) * 8
 
     stored_shape, block, faces_shape = checkpoint.shape[1:], geo.block, geo.faces
     rate_block = cell_rate.shape[1:]
@@ -598,7 +611,7 @@
         return lax.all_to_all(buffer, "space", 0, 0, tiled=True)
 
     def route(arrived):
-        return call(functools.partial(route_kernel, geo), [scalar, scalar, near], [("V", whole)], [], few)(
+        return call(functools.partial(route_kernel, geo), [scalar, scalar, near], [far(whole)], [], few)(
             owner, neighbours, arrived
         )[0]
 
@@ -614,7 +627,7 @@
     weight_faces, rate_faces, sent = call(
         functools.partial(pack_kernel, geo),
         [scalar, far(stored_shape), far(block), far(rate_block)],
-        [("R", faces_shape), ("R", geo.rate_faces), ("V", geo.buffer(geo.part.total + geo.whole.total))],
+        [far(faces_shape), ("R", geo.rate_faces), far(both)],
         [faces_shape],
         few,
     )(part, checkpoint[0], grads, rate)
@@ -622,60 +635,58 @@
     arrived = swap(sent)
     state = lax.all_gather(kept, "ckpt", axis=0)
     arrived, state = lax.optimization_barrier((arrived, state))
-    leaving, weight_leaving = call(
-        functools.partial(route_first_kernel, geo), [scalar] * 3 + [near], [("V", some), ("V", whole)], [], few
-    )(part, owner, neighbours, arrived)
-    part_ghosts = swap(leaving)
+    (leaving,) = call(functools.partial(route_first_kernel, geo), [scalar] * 3 + [near], [far(both)], [], few)(
+        part, owner, neighbours, arrived
+    )
+    first_ghosts = swap(leaving)
     inner, faces = call(
         functools.partial(step_inner_kernel, geo),
         [scalar, far(state.shape), far(rate_block)],
-        [("R", block), ("R", faces_shape)],
+        [("R", block), far(faces_shape)],
         [geo.tall],
         work,
     )(mats, state, rate)
-    part_ghosts, inner, faces = lax.optimization_barrier((part_ghosts, inner, faces))
-    weight_ghosts = swap(weight_leaving)
-    gathered = lax.all_gather(part_ghosts, "ckpt", axis=0)
+    first_ghosts, inner, faces = lax.optimization_barrier((first_ghosts, inner, faces))
+    gathered = lax.all_gather(first_ghosts[:, :some], "ckpt", axis=0)
     next_state, next_faces, sent, ghosts = call(
         functools.partial(step_edge_kernel, geo, True),
-        [scalar] * 4 + [kept_near] * 3 + [near],
-        [("R", block), ("R", faces_shape), ("V", whole), ("R", faces_shape)],
+        [scalar] * 4 + [kept_near, far(faces_shape), kept_near, near],
+        [far(block), far(faces_shape), far(whole), far(faces_shape)],
         [faces_shape, faces_shape[1:]],
         few,
     )(*fixed, inner, faces, rate_faces, gathered)
 
-    sent, weight_ghosts = lax.optimization_barrier((sent, weight_ghosts))
     arrived = swap(sent)
-    inner = adjoint_inner(next_state, kept_near, grads, far(block))
+    inner = adjoint_inner(next_state, far(block), grads, far(block))
     arrived, inner = lax.optimization_barrier((arrived, inner))
     leaving = route(arrived)
     later_state, leaving = lax.optimization_barrier((next_state, leaving))
     next_ghosts = swap(leaving)
     (final_inner,) = call(
         functools.partial(step_inner_kernel, geo),
-        [scalar, kept_near, far(rate_block)],
-        [("R", block)],
+        [scalar, far(block), far(rate_block)],
+        [far(block)],
         [geo.tall],
         work,
     )(mats, later_state, rate)
     next_ghosts, final_inner = lax.optimization_barrier((next_ghosts, final_inner))
     grads_now, next_weight_faces, sent, turned = call(
         functools.partial(adjoint_edge_kernel, geo, False),
-        [scalar] * 4 + [kept_near] * 4 + [near, near],
-        [("R", block), ("R", faces_shape), ("V", whole), ("R", faces_shape)],
+        [scalar] * 4 + [kept_near, far(faces_shape), far(faces_shape), kept_near, near, near],
+        [far(block), far(faces_shape), far(whole), far(faces_shape)],
         [faces_shape] * 2,
         few,
-    )(*fixed, inner, next_faces, weight_faces, rate_faces, next_ghosts, weight_ghosts)
+    )(*fixed, inner, next_faces, weight_faces, rate_faces, next_ghosts, first_ghosts)
 
     arrived = swap(sent)
-    inner = adjoint_inner(state, far(state.shape), grads_now, kept_near)
+    inner = adjoint_inner(state, far(state.shape), grads_now, far(block))
     arrived, inner = lax.optimization_barrier((arrived, inner))
     leaving = route(arrived)
     final_inner, leaving = lax.optimization_barrier((final_inner, leaving))
     last_ghosts = swap(leaving)
     (final,) = call(
         functools.partial(step_edge_kernel, geo, False),
-        [scalar] * 4 + [kept_near] * 4,
+        [scalar] * 4 + [far(block), far(faces_shape), kept_near, far(faces_shape)],
         [("V", block)],
         [],
         work,
@@ -683,7 +694,7 @@
     last_ghosts, final = lax.optimization_barrier((last_ghosts, final))
     (adjoint,) = call(
         functools.partial(adjoint_edge_kernel, geo, True),
-        [scalar] * 4 + [kept_near] * 4 + [near],
+        [scalar] * 4 + [kept_near] + [far(faces_shape)] * 3 + [near],
         [("V", block)],
         [faces_shape] * 2,
         few,

time: 118 us -> 108 us (0.915)
  blocking collectives: 27.5 us -> 15.2 us
  Pallas kernels: 37.3 us -> 45 us
  local copies, waits for them, and re-layouts: 8.32 us -> 0.87 us
  waiting for transfers between devices: 14.1 us -> 17.4 us
    all_to_all x1 -> x0, blocking collectives: 12.4 us -> none  [swap(): return lax.all_to_all(buffer, 'space', 0, 0, tiled=True)]
    pallas_call x12, Pallas kernels: 37.3 us -> 45 us  [run(): invoke(*[pltpu.with_memory_space_constraint(operand, placed[kind]) if kin...]
    unnamed x32 -> x10, local copies, waits for them, and re-layouts: 8.08 us -> 0.62 us
    all_to_all x6, waiting for transfers between devices: 14.1 us -> 17.4 us  [swap(): return lax.all_to_all(buffer, 'space', 0, 0, tiled=True)]
  transfers between devices with their start and end apart: 6 -> 6, of which waited for: 5 -> 6; matrix products, arithmetic and copies ran while one was open for 0% -> 0% of each run, Pallas kernels for 22% -> 25%
where the time goes in v6:
time: 108 us; the launch traced here: 107 us
  Pallas kernels  45 us (42%)
  starting transfers between devices  27.6 us (26%)
  waiting for transfers between devices  17.4 us (16%)
  blocking collectives  15.2 us (14%)
    pallas_call x12, Pallas kernels, run(): invoke(*[pltpu.with_memory_space_constraint(operand, placed[kind]) if kin...  45 us
    all_to_all x6, starting transfers between devices, swap(): return lax.all_to_all(buffer, 'space', 0, 0, tiled=True)  27.6 us
    all_to_all x6, waiting for transfers between devices, swap(): return lax.all_to_all(buffer, 'space', 0, 0, tiled=True)  17.4 us
    all_gather x1, blocking collectives, on_device(): state = lax.all_gather(kept, 'ckpt', axis=0)  9.04 us
    all_gather x1, blocking collectives, on_device(): gathered = lax.all_gather(first_ghosts[:, :some], 'ckpt', axis=0)  6.15 us
  transfers between devices with their start and end apart: 6, of which 6 were waited for; matrix products, arithmetic and copies ran while one was open for 0% of the time, Pallas kernels for 25%

profile of v6, /device:TPU:0, one launch (start us, length us, event | category | flops | bytes accessed | tf_op | source)
XLA Modules:
  0.0 106.8 jit_solution(15063306259319139660)
XLA Ops:
  0.6 3.0 %shard_map.86 = (f32[6,96,128]{2,1,0:T(8,128)}, f32[6,16,128]{2,1,0:T(8,128)S(1)}, f32[8,80,128]{2,1,0:T(8,128)}) custom-call(s32[1]{0:T(128)} %bitcast.1.refs_0_, f32[6,4,16,128]{3,2,1,0:T(8,128)} %bitcast.21, f32[6,16,16,128]{3,2,1,0:T(8,128)} %bitcast.17, f32[16,16,128]{2,1,0:T(8,128)} %bitcast.12), custom_call_target="tpu_custom_call" | custom-call | flops 884736 | bytes 3145728 | tf_op jit(solution)/shard_map/pallas_call | solution.py:577
  3.7 0.0 copy-start.3
  3.7 0.0 copy-start.1
  3.7 7.4 %all-to-all-start = ((f32[8,80,128]{2,1,0:T(8,128)}), f32[8,80,128]{2,1,0:T(8,128)S(1)}, u32[]{:S(2)}, u32[]{:S(2)}) async-start(f32[8,80,128]{2,1,0:T(8,128)} %get-tuple-element.35), calls=%async_computation | async-start | bytes 655360 | tf_op jit(solution)/shard_map/all_to_all | solution.py:611
  11.1 0.0 copy-done.3
  11.1 0.1 reshape.23.refs_2_.refs_1_
  11.2 0.0 copy-done.1
  11.2 9.0 %all-gather = f32[24,4,16,128]{3,2,1,0:T(8,128)} all-gather(f32[6,4,16,128]{3,2,1,0:T(8,128)S(1)} %bitcast.22), channel_id=2, replica_groups=mesh['ckpt'=4,'space'=8] {'ckpt'}, dimensions={0}, use_global_device_ids=true | all-gather | bytes 983040 | tf_op jit(solution)/shard_map/all_gather | solution.py:636
  20.3 0.0 copy-start
  20.3 1.2 %all-to-all-done.refs_3_ = f32[8,80,128]{2,1,0:T(8,128)S(1)} async-done(((f32[8,80,128]{2,1,0:T(8,128)}), f32[8,80,128]{2,1,0:T(8,128)S(1)}, u32[]{:S(2)}, u32[]{:S(2)}) %all-to-all-start) | async-done | bytes 327712 | tf_op jit(solution)/shard_map/all_to_all | solution.py:611
  21.5 0.0 copy-done
  21.5 1.4 %shard_map.87 = f32[8,80,128]{2,1,0:T(8,128)} custom-call(s32[1]{0:T(128)} %bitcast.1.refs_0_, s32[8]{0:T(128)S(1)} %copy-done, s32[48]{0:T(128)S(1)} %reshape.23.refs_2_.refs_1_, f32[8,80,128]{2,1,0:T(8,128)S(1)} %all-to-all-done.refs_3_), custom_call_target="tpu_custom_call" | custom-call | flops 884736 | bytes 3145728 | tf_op jit(solution)/shard_map/pallas_call | solution.py:577
  22.9 0.0 copy-start.2
  22.9 5.5 %all-to-all-start.1 = ((f32[8,80,128]{2,1,0:T(8,128)}), f32[8,80,128]{2,1,0:T(8,128)S(1)}, u32[]{:S(2)}, u32[]{:S(2)}) async-start(f32[8,80,128]{2,1,0:T(8,128)} %shard_map.87), calls=%async_computation.1 | async-start | bytes 655360 | tf_op jit(solution)/shard_map/all_to_all | solution.py:611
  28.3 0.0 copy-done.2
  28.4 0.0 copy-start.4
  28.4 0.1 reshape.21.refs_0_.refs_3_
  28.5 0.6 copy-done.4
  29.0 0.1 reshape.20.refs_2_
  29.1 5.9 %shard_map.88 = (f32[6,16,16,128]{3,2,1,0:T(8,128)S(1)}, f32[6,96,128]{2,1,0:T(8,128)}) custom-call(f32[108]{0:T(128)S(1)} %reshape.21.refs_0_.refs_3_, f32[4,6,4,16,128]{4,3,2,1,0:T(8,128)} %bitcast.10, f32[16,16,128]{2,1,0:T(8,128)} %bitcast.13), custom_call_target="tpu_custom_call" | custom-call | flops 14155776 | bytes 3145728 | tf_op jit(solution)/shard_map/pallas_call | solution.py:577
  35.0 4.2 %all-to-all-done.1.refs_9_ = f32[8,80,128]{2,1,0:T(8,128)S(1)} async-done(((f32[8,80,128]{2,1,0:T(8,128)}), f32[8,80,128]{2,1,0:T(8,128)S(1)}, u32[]{:S(2)}, u32[]{:S(2)}) %all-to-all-start.1) | async-done | bytes 327712 | tf_op jit(solution)/shard_map/all_to_all | solution.py:611
  39.1 6.1 %all-gather.1 = f32[32,24,128]{2,1,0:T(8,128)S(1)} all-gather(f32[8,24,128]{2,1,0:T(8,128)S(1)} %slice.3), channel_id=3, replica_groups=mesh['ckpt'=4,'space'=8] {'ckpt'}, dimensions={0}, use_global_device_ids=true | all-gather | bytes 491520 | tf_op jit(solution)/shard_map/all_gather | solution.py:650
  45.3 3.6 %shard_map.89 = (f32[6,16,16,128]{3,2,1,0:T(8,128)}, f32[6,96,128]{2,1,0:T(8,128)}, f32[8,56,128]{2,1,0:T(8,128)}, f32[6,96,128]{2,1,0:T(8,128)}) custom-call(s32[1]{0:T(128)} %bitcast.refs_0_, s32[8]{0:T(128)S(1)} %copy-done, s32[48]{0:T(128)S(1)} %reshape.20.refs_2_, f32[108]{0:T(128)S(1)} %reshape.21.refs_0_.refs_3_, ...), custom_call_target="tpu_custom_call" | custom-call | flops 884736 | bytes 3145728 | tf_op jit(solution)/shard_map/pallas_call | solution.py:577
  48.9 3.8 %all-to-all-start.2 = ((f32[8,56,128]{2,1,0:T(8,128)}), f32[8,56,128]{2,1,0:T(8,128)S(1)}, u32[]{:S(2)}, u32[]{:S(2)}) async-start(f32[8,56,128]{2,1,0:T(8,128)} %get-tuple-element.45), calls=%async_computation.2 | async-start | bytes 458752 | tf_op jit(solution)/shard_map/all_to_all | solution.py:611
  52.7 6.2 %shard_map.90.refs_4_ = f32[6,16,16,128]{3,2,1,0:T(8,128)S(1)} custom-call(f32[108]{0:T(128)S(1)} %reshape.21.refs_0_.refs_3_, f32[6,16,16,128]{3,2,1,0:T(8,128)} %get-tuple-element.52.refs_1_, f32[6,16,16,128]{3,2,1,0:T(8,128)} %bitcast.18, f32[16,16,128]{2,1,0:T(8,128)} %bitcast.14), custom_call_target="tpu_custom_call" | custom-call | flops 28311552 | bytes 3145728 | tf_op jit(solution)/shard_map/pallas_call | solution.py:577
  58.9 2.7 %all-to-all-done.2.refs_2_ = f32[8,56,128]{2,1,0:T(8,128)S(1)} async-done(((f32[8,56,128]{2,1,0:T(8,128)}), f32[8,56,128]{2,1,0:T(8,128)S(1)}, u32[]{:S(2)}, u32[]{:S(2)}) %all-to-all-start.2) | async-done | bytes 229408 | tf_op jit(solution)/shard_map/all_to_all | solution.py:611
  61.6 1.3 %shard_map.91 = f32[8,56,128]{2,1,0:T(8,128)} custom-call(s32[8]{0:T(128)S(1)} %copy-done, s32[48]{0:T(128)S(1)} %reshape.23.refs_2_.refs_1_, f32[8,56,128]{2,1,0:T(8,128)S(1)} %all-to-all-done.2.refs_2_), custom_call_target="tpu_custom_call" | custom-call | flops 884736 | bytes 3145728 | tf_op jit(solution)/shard_map/pallas_call | solution.py:577
  62.9 3.4 %all-to-all-start.3 = ((f32[8,56,128]{2,1,0:T(8,128)}), f32[8,56,128]{2,1,0:T(8,128)S(1)}, u32[]{:S(2)}, u32[]{:S(2)}) async-start(f32[8,56,128]{2,1,0:T(8,128)} %shard_map.91), calls=%async_computation.3 | async-start | bytes 458752 | tf_op jit(solution)/shard_map/all_to_all | solution.py:611
  66.3 5.6 %shard_map.92.refs_4_ = f32[6,16,16,128]{3,2,1,0:T(8,128)} custom-call(f32[108]{0:T(128)S(1)} %reshape.21.refs_0_.refs_3_, f32[6,16,16,128]{3,2,1,0:T(8,128)} %get-tuple-element.52.refs_1_, f32[16,16,128]{2,1,0:T(8,128)} %bitcast.15), custom_call_target="tpu_custom_call" | custom-call | flops 14155776 | bytes 3145728 | tf_op jit(solution)/shard_map/pallas_call | solution.py:577
  71.9 2.8 %all-to-all-done.3.refs_8_ = f32[8,56,128]{2,1,0:T(8,128)S(1)} async-done(((f32[8,56,128]{2,1,0:T(8,128)}), f32[8,56,128]{2,1,0:T(8,128)S(1)}, u32[]{:S(2)}, u32[]{:S(2)}) %all-to-all-start.3) | async-done | bytes 229408 | tf_op jit(solution)/shard_map/all_to_all | solution.py:611
  74.7 3.9 %shard_map.93 = (f32[6,16,16,128]{3,2,1,0:T(8,128)}, f32[6,96,128]{2,1,0:T(8,128)}, f32[8,56,128]{2,1,0:T(8,128)}, f32[6,96,128]{2,1,0:T(8,128)}) custom-call(s32[1]{0:T(128)} %bitcast.refs_0_, s32[8]{0:T(128)S(1)} %copy-done, s32[48]{0:T(128)S(1)} %reshape.20.refs_2_, f32[108]{0:T(128)S(1)} %reshape.21.refs_0_.refs_3_, ...), custom_call_target="tpu_custom_call" | custom-call | flops 884736 | bytes 3145728 | tf_op jit(solution)/shard_map/pallas_call | solution.py:577
  78.6 3.4 %all-to-all-start.4 = ((f32[8,56,128]{2,1,0:T(8,128)}), f32[8,56,128]{2,1,0:T(8,128)S(1)}, u32[]{:S(2)}, u32[]{:S(2)}) async-start(f32[8,56,128]{2,1,0:T(8,128)} %get-tuple-element.54), calls=%async_computation.4 | async-start | bytes 458752 | tf_op jit(solution)/shard_map/all_to_all | solution.py:611
  82.0 6.2 %shard_map.94.refs_4_ = f32[6,16,16,128]{3,2,1,0:T(8,128)S(1)} custom-call(f32[108]{0:T(128)S(1)} %reshape.21.refs_0_.refs_3_, f32[4,6,4,16,128]{4,3,2,1,0:T(8,128)} %bitcast.11, f32[6,16,16,128]{3,2,1,0:T(8,128)} %get-tuple-element.55.refs_2_, f32[16,16,128]{2,1,0:T(8,128)} %bitcast.16), custom_call_target="tpu_custom_call" | custom-call | flops 28311552 | bytes 3145728 | tf_op jit(solution)/shard_map/pallas_call | solution.py:577
  88.2 1.9 %all-to-all-done.4.refs_2_ = f32[8,56,128]{2,1,0:T(8,128)S(1)} async-done(((f32[8,56,128]{2,1,0:T(8,128)}), f32[8,56,128]{2,1,0:T(8,128)S(1)}, u32[]{:S(2)}, u32[]{:S(2)}) %all-to-all-start.4) | async-done | bytes 229408 | tf_op jit(solution)/shard_map/all_to_all | solution.py:611
  90.1 1.3 %shard_map.95 = f32[8,56,128]{2,1,0:T(8,128)} custom-call(s32[8]{0:T(128)S(1)} %copy-done, s32[48]{0:T(128)S(1)} %reshape.23.refs_2_.refs_1_, f32[8,56,128]{2,1,0:T(8,128)S(1)} %all-to-all-done.4.refs_2_), custom_call_target="tpu_custom_call" | custom-call | flops 884736 | bytes 3145728 | tf_op jit(solution)/shard_map/pallas_call | solution.py:577
  91.4 4.1 %all-to-all-start.5 = ((f32[8,56,128]{2,1,0:T(8,128)}), f32[8,56,128]{2,1,0:T(8,128)S(1)}, u32[]{:S(2)}, u32[]{:S(2)}) async-start(f32[8,56,128]{2,1,0:T(8,128)} %shard_map.95), calls=%async_computation.5 | async-start | bytes 458752 | tf_op jit(solution)/shard_map/all_to_all | solution.py:611
  95.5 3.4 %shard_map.96 = f32[6,16,16,128]{3,2,1,0:T(8,128)} custom-call(s32[1]{0:T(128)} %bitcast.refs_0_, s32[8]{0:T(128)S(1)} %copy-done, s32[48]{0:T(128)S(1)} %reshape.20.refs_2_, f32[108]{0:T(128)S(1)} %reshape.21.refs_0_.refs_3_, f32[6,16,16,128]{3,2,1,0:T(8,128)} %shard_map.92.refs_4_, f32[6,96,128]{2,1,0:T(8,128)} %get-tuple-element.48.refs_5_, ...), custom_call_target="tpu_custom_call" | custom-call | flops 14155776 | bytes 3145728 | tf_op jit(solution)/shard_map/pallas_call | solution.py:577
  98.9 4.6 %all-to-all-done.5.refs_8_ = f32[8,56,128]{2,1,0:T(8,128)S(1)} async-done(((f32[8,56,128]{2,1,0:T(8,128)}), f32[8,56,128]{2,1,0:T(8,128)S(1)}, u32[]{:S(2)}, u32[]{:S(2)}) %all-to-all-start.5) | async-done | bytes 229408 | tf_op jit(solution)/shard_map/all_to_all | solution.py:611
  103.5 3.3 %shard_map.97 = f32[6,16,16,128]{3,2,1,0:T(8,128)} custom-call(s32[1]{0:T(128)} %bitcast.refs_0_, s32[8]{0:T(128)S(1)} %copy-done, s32[48]{0:T(128)S(1)} %reshape.20.refs_2_, f32[108]{0:T(128)S(1)} %reshape.21.refs_0_.refs_3_, f32[6,16,16,128]{3,2,1,0:T(8,128)S(1)} %shard_map.94.refs_4_, f32[6,96,128]{2,1,0:T(8,128)} %get-tuple-element.42.refs_5_, ...), custom_call_target="tpu_custom_call" | custom-call | flops 884736 | bytes 3145728 | tf_op jit(solution)/shard_map/pallas_call | solution.py:577
  (1 shorter events, 0.0 us)
Async XLA Ops:
  3.7 7.5 %copy-start.3 = (s32[8,6]{1,0:T(8,128)S(1)}, s32[8,6]{1,0:T(8,128)}, u32[]{:S(2)}) copy-start(s32[8,6]{1,0:T(8,128)} %param.12) | copy-start | bytes 580
  3.7 7.5 %copy-start.1 = (f32[1,6,4,16,128]{4,3,2,1,0:T(8,128)S(1)}, f32[1,6,4,16,128]{4,3,2,1,0:T(8,128)}, u32[]{:S(2)}) copy-start(f32[1,6,4,16,128]{4,3,2,1,0:T(8,128)} %param.7) | copy-start | bytes 589828
  3.7 17.7 %all-to-all-start = ((f32[8,80,128]{2,1,0:T(8,128)}), f32[8,80,128]{2,1,0:T(8,128)S(1)}, u32[]{:S(2)}, u32[]{:S(2)}) async-start(f32[8,80,128]{2,1,0:T(8,128)} %get-tuple-element.35), calls=%async_computation | async-start | bytes 655360 | tf_op jit(solution)/shard_map/all_to_all | solution.py:611
  20.3 1.2 %copy-start = (s32[8]{0:T(128)S(1)}, s32[8]{0:T(128)}, u32[]{:S(2)}) copy-start(s32[8]{0:T(128)} %refs_1_.9) | copy-start | bytes 100
  22.9 5.5 %copy-start.2 = (f32[3,6,6]{2,1,0:T(8,128)S(1)}, f32[3,6,6]{2,1,0:T(8,128)}, u32[]{:S(2)}) copy-start(f32[3,6,6]{2,1,0:T(8,128)} %param.10) | copy-start | bytes 1300
  22.9 16.3 %all-to-all-start.1 = ((f32[8,80,128]{2,1,0:T(8,128)}), f32[8,80,128]{2,1,0:T(8,128)S(1)}, u32[]{:S(2)}, u32[]{:S(2)}) async-start(f32[8,80,128]{2,1,0:T(8,128)} %shard_map.87), calls=%async_computation.1 | async-start | bytes 655360 | tf_op jit(solution)/shard_map/all_to_all | solution.py:611
  28.4 0.7 copy-start.4
  48.9 12.7 %all-to-all-start.2 = ((f32[8,56,128]{2,1,0:T(8,128)}), f32[8,56,128]{2,1,0:T(8,128)S(1)}, u32[]{:S(2)}, u32[]{:S(2)}) async-start(f32[8,56,128]{2,1,0:T(8,128)} %get-tuple-element.45), calls=%async_computation.2 | async-start | bytes 458752 | tf_op jit(solution)/shard_map/all_to_all | solution.py:611
  62.9 11.8 %all-to-all-start.3 = ((f32[8,56,128]{2,1,0:T(8,128)}), f32[8,56,128]{2,1,0:T(8,128)S(1)}, u32[]{:S(2)}, u32[]{:S(2)}) async-start(f32[8,56,128]{2,1,0:T(8,128)} %shard_map.91), calls=%async_computation.3 | async-start | bytes 458752 | tf_op jit(solution)/shard_map/all_to_all | solution.py:611
  78.6 11.5 %all-to-all-start.4 = ((f32[8,56,128]{2,1,0:T(8,128)}), f32[8,56,128]{2,1,0:T(8,128)S(1)}, u32[]{:S(2)}, u32[]{:S(2)}) async-start(f32[8,56,128]{2,1,0:T(8,128)} %get-tuple-element.54), calls=%async_computation.4 | async-start | bytes 458752 | tf_op jit(solution)/shard_map/all_to_all | solution.py:611
  91.4 12.1 %all-to-all-start.5 = ((f32[8,56,128]{2,1,0:T(8,128)}), f32[8,56,128]{2,1,0:T(8,128)S(1)}, u32[]{:S(2)}, u32[]{:S(2)}) async-start(f32[8,56,128]{2,1,0:T(8,128)} %shard_map.95), calls=%async_computation.5 | async-start | bytes 458752 | tf_op jit(solution)/shard_map/all_to_all | solution.py:611

commit v7 on v6

--- a/solution.py
+++ b/solution.py
@@ -66,10 +66,12 @@
         faces[3, var * x : (var + 1) * x] = source[var, :, 0, :]
 
 
-def cut(geo, pieces, faces, buffer, base):
-    for index, (run, start) in enumerate(zip(pieces.runs, pieces.starts)):
-        for slot in range(geo.n):
+def cut(geo, pieces, faces, buffer, base, leave=None):
+    for slot in range(geo.n):
+        for index, (run, start) in enumerate(zip(pieces.runs, pieces.starts)):
             buffer[slot, base + start : base + start + run] = faces[index, slot * run : (slot + 1) * run]
+        if leave:
+            leave(slot)
 
 
 def own_codes(geo, place, owner, orientation):
@@ -167,7 +169,7 @@
             result[var, :, row, :] = result[var, :, row, :] + terms[var]
 
 
-def add_z_terms(geo, high_terms, low_terms, result):
+def add_z_terms(geo, high_terms, low_terms, inner, result):
     v, x, y, z = geo.block
     lane = lax.broadcasted_iota(jnp.int32, (y, z), 1)
     zero = jnp.zeros((y, z), jnp.float32)
@@ -176,7 +178,7 @@
             high = pltpu.roll(high_terms[var], z - 1 - plane, 1)
             low = pltpu.roll(low_terms[var], z - plane, 1) if plane else low_terms[var]
             change = jnp.where(lane == z - 1, high, jnp.where(lane == 0, low, zero))
-            result[var, plane] = result[var, plane] + change
+            result[var, plane] = inner[var, plane] + change
 
 
 def fill_tall(geo, source, tall):
@@ -348,8 +350,7 @@
     late.leave(1)
     take_weight_faces(geo, grads, rate_faces, weight_faces)
     late.leave(0)
-    cut(geo, geo.whole, weight_faces, buffer, geo.part.total)
-    late.leave(2)
+    cut(geo, geo.whole, weight_faces, buffer, geo.part.total, functools.partial(late.leave, 2))
 
 
 def take_weight_faces(geo, grads, rate_faces, faces):
@@ -365,31 +366,29 @@
     faces[5, :y] = low * rate_faces[5, :y]
 
 
-def route_whole(geo, owner, neighbours, arrived, leaving, base):
+def route_whole(geo, owner, neighbours, block, arrived, leaving, base):
+    for side in range(6):
+        source = owner[neighbours[block * 6 + side]]
+        run, start, far = geo.whole.runs[side], base + geo.whole.starts[side], base + geo.whole.starts[side ^ 1]
+        leaving[owner[block], start : start + run] = arrived[source, far : far + run]
+
+
+def route_kernel(geo, late, owner, neighbours, arrived, leaving):
     for block in range(geo.n):
-        target = owner[block]
-        for side in range(6):
-            source = owner[neighbours[block * 6 + side]]
-            run, start, far = geo.whole.runs[side], base + geo.whole.starts[side], base + geo.whole.starts[side ^ 1]
-            leaving[target, start : start + run] = arrived[source, far : far + run]
-
-
-def route_kernel(geo, late, owner, neighbours, arrived, leaving):
-    route_whole(geo, owner, neighbours, arrived, leaving, 0)
-    late.leave(0)
+        route_whole(geo, owner, neighbours, block, arrived, leaving, 0)
+        late.leave(0, owner[block])
 
 
 def route_first_kernel(geo, late, part, owner, neighbours, arrived, leaving):
-    route_whole(geo, owner, neighbours, arrived, leaving, geo.part.total)
     x_side = jnp.where(part[0] == geo.parts - 1, 1, 0)
     for block in range(geo.n):
-        target = owner[block]
+        route_whole(geo, owner, neighbours, block, arrived, leaving, geo.part.total)
         for index in range(5):
             side, far_index = (x_side, 0) if index == 0 else (index + 1, ((index + 1) ^ 1) - 1)
             source = owner[neighbours[block * 6 + side]]
             run, start, far = geo.part.runs[index], geo.part.starts[index], geo.part.starts[far_index]
-            leaving[target, start : start + run] = arrived[source, far : far + run]
-    late.leave(0)
+            leaving[owner[block], start : start + run] = arrived[source, far : far + run]
+        late.leave(0, owner[block])
 
 
 def step_inner_kernel(geo, late, mats, block, rate, result, *rest):
@@ -460,9 +459,8 @@
         late.wait(4)
         late.wait(7)
     late.wait(5)
-    result[...] = inner[...]
     terms = []
-    for side in range(6):
+    for side in (4, 5, 0, 1, 2, 3):
         depth = y if side < 2 or side > 3 else x
         cells, outer = face_values(geo, faces, side), face_values(geo, ghosts, side)
         values = step_face(geo, mats, side, cells, outer, rate_faces[side, :depth])
@@ -470,7 +468,8 @@
             add_xy_terms(geo, side, values, result)
         else:
             terms.append(values)
-    add_z_terms(geo, *terms, result)
+            if side == 5:
+                add_z_terms(geo, *terms, inner, result)
     late.leave(0)
     if first:
         take_xy_faces(geo, result, new_faces)
@@ -478,8 +477,7 @@
         new_faces[4, :y] = high
         new_faces[5, :y] = low
         late.leave(1)
-        cut(geo, geo.whole, new_faces, sent, 0)
-        late.leave(2)
+        cut(geo, geo.whole, new_faces, sent, 0, functools.partial(late.leave, 2))
 
 
 def adjoint_edge_kernel(geo, last, late, place, owner, orientation, mats, inner, faces, weight_faces, *rest):
@@ -498,41 +496,46 @@
         turn(geo, codes, raw, weight_ghosts)
     for index in range(5, 8):
         late.wait(index)
-    result[...] = inner[...]
     terms = []
-    for side in range(6):
+    for side in (4, 5, 0, 1, 2, 3):
         views = [face_values(geo, field, side) for field in (faces, ghosts, weight_faces, weight_ghosts)]
         values = adjoint_face(geo, mats, side, *views)
         if side < 4:
             add_xy_terms(geo, side, values, result)
         else:
             terms.append(values)
-    add_z_terms(geo, *terms, result)
+            if side == 5:
+                add_z_terms(geo, *terms, inner, result)
     late.leave(0)
     if not last:
         take_weight_faces(geo, result, rate_faces, new_faces)
         late.leave(1)
-        cut(geo, geo.whole, new_faces, sent, 0)
-        late.leave(2)
+        cut(geo, geo.whole, new_faces, sent, 0, functools.partial(late.leave, 2))
 
 
 class Late:
-    def __init__(self, arrivals, departures):
-        self.arrivals, self.departures = arrivals, departures
+    def __init__(self, arrivals, departures, sems):
+        self.arrivals, self.departures, self.sems, self.started = arrivals, departures, sems, []
 
     def wait(self, index):
         if index in self.arrivals:
             self.arrivals[index].wait()
 
-    def leave(self, index):
+    def leave(self, index, slot=None):
         if index in self.departures:
-            self.departures[index].start()
+            source, target = self.departures[index]
+            if slot is not None:
+                source, target = source.at[slot], target.at[slot]
+            copy = pltpu.make_async_copy(source, target, self.sems.at[len(self.started)])
+            copy.start()
+            self.started.append(copy)
 
 
 def call(kernel, ins, outs, scratch, flops):
     late_in = [(index, shape) for index, (kind, shape) in enumerate(ins) if kind == "H"]
-    late_out = [(index, shape) for index, (kind, shape) in enumerate(outs) if kind == "H"]
+    late_out = [(index, shape) for index, (kind, shape) in enumerate(outs) if kind in "HB"]
     count_in, count_out = len(late_in), len(late_out)
+    sends = sum(shape[0] if kind == "B" else 1 for kind, shape in outs if kind in "HB")
 
     def body(*refs):
         given = list(refs[: len(ins)])
@@ -540,28 +543,32 @@
         rest = list(refs[len(ins) + len(outs) :])
         own = rest[: len(scratch)]
         stage = rest[len(scratch) : len(scratch) + count_in + count_out]
-        sems = rest[-1] if count_in + count_out else None
+        sems_in = rest[len(scratch) + count_in + count_out] if count_in else None
+        sems_out = rest[-1] if count_out else None
         arrivals, departures = {}, {}
         for slot, (index, _) in enumerate(late_in):
-            copy = pltpu.make_async_copy(given[index], stage[slot], sems.at[slot])
+            copy = pltpu.make_async_copy(given[index], stage[slot], sems_in.at[slot])
             copy.start()
             arrivals[index] = copy
             given[index] = stage[slot]
         for slot, (index, _) in enumerate(late_out):
-            spot = count_in + slot
-            departures[index] = pltpu.make_async_copy(stage[spot], made[index], sems.at[spot])
-            made[index] = stage[spot]
-        kernel(Late(arrivals, departures), *given, *made, *own)
-        for copy in departures.values():
+            departures[index] = (stage[count_in + slot], made[index])
+            made[index] = stage[count_in + slot]
+        late = Late(arrivals, departures, sems_out)
+        kernel(late, *given, *made, *own)
+        assert len(late.started) == sends
+        for copy in late.started:
             copy.wait()
 
     hbm = pl.BlockSpec(memory_space=pltpu.HBM)
-    specs = {"S": SMEM, "V": VMEM, "R": VMEM, "H": hbm}
+    specs = {"S": SMEM, "V": VMEM, "R": VMEM, "H": hbm, "B": hbm}
     scratch_shapes = [pltpu.VMEM(shape, jnp.float32) for shape in scratch]
     scratch_shapes += [pltpu.VMEM(shape, jnp.float32) for _, shape in late_in + late_out]
-    if count_in + count_out:
-        scratch_shapes.append(pltpu.SemaphoreType.DMA((count_in + count_out,)))
-    shapes = {"V": jax.ShapeDtypeStruct, "R": pltpu.VMEM, "H": pltpu.HBM}
+    if count_in:
+        scratch_shapes.append(pltpu.SemaphoreType.DMA((count_in,)))
+    if count_out:
+        scratch_shapes.append(pltpu.SemaphoreType.DMA((sends,)))
+    shapes = {"V": jax.ShapeDtypeStruct, "R": pltpu.VMEM, "H": pltpu.HBM, "B": pltpu.HBM}
     invoke = pl.pallas_call(
         body,
         in_specs=[specs[kind] for kind, _ in ins],
@@ -611,7 +618,7 @@
         return lax.all_to_all(buffer, "space", 0, 0, tiled=True)
 
     def route(arrived):
-        return call(functools.partial(route_kernel, geo), [scalar, scalar, near], [far(whole)], [], few)(
+        return call(functools.partial(route_kernel, geo), [scalar, scalar, near], [("B", whole)], [], few)(
             owner, neighbours, arrived
         )[0]
 
@@ -627,7 +634,7 @@
     weight_faces, rate_faces, sent = call(
         functools.partial(pack_kernel, geo),
         [scalar, far(stored_shape), far(block), far(rate_block)],
-        [far(faces_shape), ("R", geo.rate_faces), far(both)],
+        [far(faces_shape), ("R", geo.rate_faces), ("B", both)],
         [faces_shape],
         few,
     )(part, checkpoint[0], grads, rate)
@@ -635,7 +642,7 @@
     arrived = swap(sent)
     state = lax.all_gather(kept, "ckpt", axis=0)
     arrived, state = lax.optimization_barrier((arrived, state))
-    (leaving,) = call(functools.partial(route_first_kernel, geo), [scalar] * 3 + [near], [far(both)], [], few)(
+    (leaving,) = call(functools.partial(route_first_kernel, geo), [scalar] * 3 + [near], [("B", both)], [], few)(
         part, owner, neighbours, arrived
     )
     first_ghosts = swap(leaving)
@@ -651,20 +658,20 @@
     next_state, next_faces, sent, ghosts = call(
         functools.partial(step_edge_kernel, geo, True),
         [scalar] * 4 + [kept_near, far(faces_shape), kept_near, near],
-        [far(block), far(faces_shape), far(whole), far(faces_shape)],
+        [("R", block), far(faces_shape), ("B", whole), far(faces_shape)],
         [faces_shape, faces_shape[1:]],
         few,
     )(*fixed, inner, faces, rate_faces, gathered)
 
     arrived = swap(sent)
-    inner = adjoint_inner(next_state, far(block), grads, far(block))
+    inner = adjoint_inner(next_state, kept_near, grads, far(block))
     arrived, inner = lax.optimization_barrier((arrived, inner))
     leaving = route(arrived)
     later_state, leaving = lax.optimization_barrier((next_state, leaving))
     next_ghosts = swap(leaving)
     (final_inner,) = call(
         functools.partial(step_inner_kernel, geo),
-        [scalar, far(block), far(rate_block)],
+        [scalar, kept_near, far(rate_block)],
         [far(block)],
         [geo.tall],
         work,
@@ -673,13 +680,13 @@
     grads_now, next_weight_faces, sent, turned = call(
         functools.partial(adjoint_edge_kernel, geo, False),
         [scalar] * 4 + [kept_near, far(faces_shape), far(faces_shape), kept_near, near, near],
-        [far(block), far(faces_shape), far(whole), far(faces_shape)],
+        [("R", block), far(faces_shape), ("B", whole), far(faces_shape)],
         [faces_shape] * 2,
         few,
     )(*fixed, inner, next_faces, weight_faces, rate_faces, next_ghosts, first_ghosts)
 
     arrived = swap(sent)
-    inner = adjoint_inner(state, far(state.shape), grads_now, far(block))
+    inner = adjoint_inner(state, far(state.shape), grads_now, kept_near)
     arrived, inner = lax.optimization_barrier((arrived, inner))
     leaving = route(arrived)
     final_inner, leaving = lax.optimization_barrier((final_inner, leaving))

time: 108 us -> 108 us (level)
  no operation moved by 1% of the time
where the time goes in v7:
time: 108 us; the launch traced here: 106 us
  Pallas kernels  44.2 us (41%)
  starting transfers between devices  27.3 us (25%)
  waiting for transfers between devices  18.1 us (17%)
  blocking collectives  15.2 us (14%)
    pallas_call x12, Pallas kernels, run(): invoke(*[pltpu.with_memory_space_constraint(operand, placed[kind]) if kin...  44.2 us
    all_to_all x6, starting transfers between devices, swap(): return lax.all_to_all(buffer, 'space', 0, 0, tiled=True)  27.3 us
    all_to_all x6, waiting for transfers between devices, swap(): return lax.all_to_all(buffer, 'space', 0, 0, tiled=True)  18.1 us
    all_gather x1, blocking collectives, on_device(): state = lax.all_gather(kept, 'ckpt', axis=0)  9.04 us
    all_gather x1, blocking collectives, on_device(): gathered = lax.all_gather(first_ghosts[:, :some], 'ckpt', axis=0)  6.15 us
  transfers between devices with their start and end apart: 6, of which 6 were waited for; matrix products, arithmetic and copies ran while one was open for 0% of the time, Pallas kernels for 25%

profile of v7, /device:TPU:0, one launch (start us, length us, event | category | flops | bytes accessed | tf_op | source)
XLA Modules:
  0.0 106.5 jit_solution(12632102484932560942)
XLA Ops:
  0.6 3.1 %shard_map.86 = (f32[6,96,128]{2,1,0:T(8,128)}, f32[6,16,128]{2,1,0:T(8,128)S(1)}, f32[8,80,128]{2,1,0:T(8,128)}) custom-call(s32[1]{0:T(128)} %bitcast.1.refs_0_, f32[6,4,16,128]{3,2,1,0:T(8,128)} %bitcast.21, f32[6,16,16,128]{3,2,1,0:T(8,128)} %bitcast.17, f32[16,16,128]{2,1,0:T(8,128)} %bitcast.12), custom_call_target="tpu_custom_call" | custom-call | flops 884736 | bytes 3145728 | tf_op jit(solution)/shard_map/pallas_call | solution.py:584
  3.7 0.0 copy-start.3
  3.7 0.0 copy-start.1
  3.7 7.4 %all-to-all-start = ((f32[8,80,128]{2,1,0:T(8,128)}), f32[8,80,128]{2,1,0:T(8,128)S(1)}, u32[]{:S(2)}, u32[]{:S(2)}) async-start(f32[8,80,128]{2,1,0:T(8,128)} %get-tuple-element.35), calls=%async_computation | async-start | bytes 655360 | tf_op jit(solution)/shard_map/all_to_all | solution.py:618
  11.2 0.0 copy-done.3
  11.2 0.1 reshape.23.refs_2_.refs_1_
  11.3 0.0 copy-done.1
  11.3 9.0 %all-gather = f32[24,4,16,128]{3,2,1,0:T(8,128)} all-gather(f32[6,4,16,128]{3,2,1,0:T(8,128)S(1)} %bitcast.22), channel_id=2, replica_groups=mesh['ckpt'=4,'space'=8] {'ckpt'}, dimensions={0}, use_global_device_ids=true | all-gather | bytes 983040 | tf_op jit(solution)/shard_map/all_gather | solution.py:643
  20.3 0.0 copy-start
  20.3 1.2 %all-to-all-done.refs_3_ = f32[8,80,128]{2,1,0:T(8,128)S(1)} async-done(((f32[8,80,128]{2,1,0:T(8,128)}), f32[8,80,128]{2,1,0:T(8,128)S(1)}, u32[]{:S(2)}, u32[]{:S(2)}) %all-to-all-start) | async-done | bytes 327712 | tf_op jit(solution)/shard_map/all_to_all | solution.py:618
  21.5 0.0 copy-done
  21.5 1.3 %shard_map.87 = f32[8,80,128]{2,1,0:T(8,128)} custom-call(s32[1]{0:T(128)} %bitcast.1.refs_0_, s32[8]{0:T(128)S(1)} %copy-done, s32[48]{0:T(128)S(1)} %reshape.23.refs_2_.refs_1_, f32[8,80,128]{2,1,0:T(8,128)S(1)} %all-to-all-done.refs_3_), custom_call_target="tpu_custom_call" | custom-call | flops 884736 | bytes 3145728 | tf_op jit(solution)/shard_map/pallas_call | solution.py:584
  22.9 0.0 copy-start.2
  22.9 5.5 %all-to-all-start.1 = ((f32[8,80,128]{2,1,0:T(8,128)}), f32[8,80,128]{2,1,0:T(8,128)S(1)}, u32[]{:S(2)}, u32[]{:S(2)}) async-start(f32[8,80,128]{2,1,0:T(8,128)} %shard_map.87), calls=%async_computation.1 | async-start | bytes 655360 | tf_op jit(solution)/shard_map/all_to_all | solution.py:618
  28.3 0.0 copy-done.2
  28.3 0.0 copy-start.4
  28.3 0.1 reshape.21.refs_0_.refs_3_
  28.4 0.6 copy-done.4
  29.0 0.1 reshape.20.refs_2_
  29.1 5.9 %shard_map.88 = (f32[6,16,16,128]{3,2,1,0:T(8,128)S(1)}, f32[6,96,128]{2,1,0:T(8,128)}) custom-call(f32[108]{0:T(128)S(1)} %reshape.21.refs_0_.refs_3_, f32[4,6,4,16,128]{4,3,2,1,0:T(8,128)} %bitcast.10, f32[16,16,128]{2,1,0:T(8,128)} %bitcast.13), custom_call_target="tpu_custom_call" | custom-call | flops 14155776 | bytes 3145728 | tf_op jit(solution)/shard_map/pallas_call | solution.py:584
  35.0 4.2 %all-to-all-done.1.refs_9_ = f32[8,80,128]{2,1,0:T(8,128)S(1)} async-done(((f32[8,80,128]{2,1,0:T(8,128)}), f32[8,80,128]{2,1,0:T(8,128)S(1)}, u32[]{:S(2)}, u32[]{:S(2)}) %all-to-all-start.1) | async-done | bytes 327712 | tf_op jit(solution)/shard_map/all_to_all | solution.py:618
  39.1 6.1 %all-gather.1 = f32[32,24,128]{2,1,0:T(8,128)S(1)} all-gather(f32[8,24,128]{2,1,0:T(8,128)S(1)} %slice.3), channel_id=3, replica_groups=mesh['ckpt'=4,'space'=8] {'ckpt'}, dimensions={0}, use_global_device_ids=true | all-gather | bytes 491520 | tf_op jit(solution)/shard_map/all_gather | solution.py:657
  45.3 3.6 %shard_map.89 = (f32[6,16,16,128]{3,2,1,0:T(8,128)S(1)}, f32[6,96,128]{2,1,0:T(8,128)}, f32[8,56,128]{2,1,0:T(8,128)}, f32[6,96,128]{2,1,0:T(8,128)}) custom-call(s32[1]{0:T(128)} %bitcast.refs_0_, s32[8]{0:T(128)S(1)} %copy-done, s32[48]{0:T(128)S(1)} %reshape.20.refs_2_, f32[108]{0:T(128)S(1)} %reshape.21.refs_0_.refs_3_, ...), custom_call_target="tpu_custom_call" | custom-call | flops 884736 | bytes 3145728 | tf_op jit(solution)/shard_map/pallas_call | solution.py:584
  48.8 3.8 %all-to-all-start.2 = ((f32[8,56,128]{2,1,0:T(8,128)}), f32[8,56,128]{2,1,0:T(8,128)S(1)}, u32[]{:S(2)}, u32[]{:S(2)}) async-start(f32[8,56,128]{2,1,0:T(8,128)} %get-tuple-element.45), calls=%async_computation.2 | async-start | bytes 458752 | tf_op jit(solution)/shard_map/all_to_all | solution.py:618
  52.6 6.0 %shard_map.90.refs_4_ = f32[6,16,16,128]{3,2,1,0:T(8,128)S(1)} custom-call(f32[108]{0:T(128)S(1)} %reshape.21.refs_0_.refs_3_, f32[6,16,16,128]{3,2,1,0:T(8,128)S(1)} %get-tuple-element.52.refs_1_, f32[6,16,16,128]{3,2,1,0:T(8,128)} %bitcast.18, f32[16,16,128]{2,1,0:T(8,128)} %bitcast.14), custom_call_target="tpu_custom_call" | custom-call | flops 28311552 | bytes 3145728 | tf_op jit(solution)/shard_map/pallas_call | solution.py:584
  58.6 3.0 %all-to-all-done.2.refs_2_ = f32[8,56,128]{2,1,0:T(8,128)S(1)} async-done(((f32[8,56,128]{2,1,0:T(8,128)}), f32[8,56,128]{2,1,0:T(8,128)S(1)}, u32[]{:S(2)}, u32[]{:S(2)}) %all-to-all-start.2) | async-done | bytes 229408 | tf_op jit(solution)/shard_map/all_to_all | solution.py:618
  61.5 1.3 %shard_map.91 = f32[8,56,128]{2,1,0:T(8,128)} custom-call(s32[8]{0:T(128)S(1)} %copy-done, s32[48]{0:T(128)S(1)} %reshape.23.refs_2_.refs_1_, f32[8,56,128]{2,1,0:T(8,128)S(1)} %all-to-all-done.2.refs_2_), custom_call_target="tpu_custom_call" | custom-call | flops 884736 | bytes 3145728 | tf_op jit(solution)/shard_map/pallas_call | solution.py:584
  62.9 3.4 %all-to-all-start.3 = ((f32[8,56,128]{2,1,0:T(8,128)}), f32[8,56,128]{2,1,0:T(8,128)S(1)}, u32[]{:S(2)}, u32[]{:S(2)}) async-start(f32[8,56,128]{2,1,0:T(8,128)} %shard_map.91), calls=%async_computation.3 | async-start | bytes 458752 | tf_op jit(solution)/shard_map/all_to_all | solution.py:618
  66.3 5.3 %shard_map.92.refs_4_ = f32[6,16,16,128]{3,2,1,0:T(8,128)} custom-call(f32[108]{0:T(128)S(1)} %reshape.21.refs_0_.refs_3_, f32[6,16,16,128]{3,2,1,0:T(8,128)S(1)} %get-tuple-element.52.refs_1_, f32[16,16,128]{2,1,0:T(8,128)} %bitcast.15), custom_call_target="tpu_custom_call" | custom-call | flops 14155776 | bytes 3145728 | tf_op jit(solution)/shard_map/pallas_call | solution.py:584
  71.6 3.1 %all-to-all-done.3.refs_8_ = f32[8,56,128]{2,1,0:T(8,128)S(1)} async-done(((f32[8,56,128]{2,1,0:T(8,128)}), f32[8,56,128]{2,1,0:T(8,128)S(1)}, u32[]{:S(2)}, u32[]{:S(2)}) %all-to-all-start.3) | async-done | bytes 229408 | tf_op jit(solution)/shard_map/all_to_all | solution.py:618
  74.7 3.8 %shard_map.93 = (f32[6,16,16,128]{3,2,1,0:T(8,128)S(1)}, f32[6,96,128]{2,1,0:T(8,128)}, f32[8,56,128]{2,1,0:T(8,128)}, f32[6,96,128]{2,1,0:T(8,128)}) custom-call(s32[1]{0:T(128)} %bitcast.refs_0_, s32[8]{0:T(128)S(1)} %copy-done, s32[48]{0:T(128)S(1)} %reshape.20.refs_2_, f32[108]{0:T(128)S(1)} %reshape.21.refs_0_.refs_3_, ...), custom_call_target="tpu_custom_call" | custom-call | flops 884736 | bytes 3145728 | tf_op jit(solution)/shard_map/pallas_call | solution.py:584
  78.5 3.4 %all-to-all-start.4 = ((f32[8,56,128]{2,1,0:T(8,128)}), f32[8,56,128]{2,1,0:T(8,128)S(1)}, u32[]{:S(2)}, u32[]{:S(2)}) async-start(f32[8,56,128]{2,1,0:T(8,128)} %get-tuple-element.54), calls=%async_computation.4 | async-start | bytes 458752 | tf_op jit(solution)/shard_map/all_to_all | solution.py:618
  81.9 6.0 %shard_map.94.refs_4_ = f32[6,16,16,128]{3,2,1,0:T(8,128)S(1)} custom-call(f32[108]{0:T(128)S(1)} %reshape.21.refs_0_.refs_3_, f32[4,6,4,16,128]{4,3,2,1,0:T(8,128)} %bitcast.11, f32[6,16,16,128]{3,2,1,0:T(8,128)S(1)} %get-tuple-element.55.refs_2_, f32[16,16,128]{2,1,0:T(8,128)} %bitcast.16), custom_call_target="tpu_custom_call" | custom-call | flops 28311552 | bytes 3145728 | tf_op jit(solution)/shard_map/pallas_call | solution.py:584
  87.9 2.1 %all-to-all-done.4.refs_2_ = f32[8,56,128]{2,1,0:T(8,128)S(1)} async-done(((f32[8,56,128]{2,1,0:T(8,128)}), f32[8,56,128]{2,1,0:T(8,128)S(1)}, u32[]{:S(2)}, u32[]{:S(2)}) %all-to-all-start.4) | async-done | bytes 229408 | tf_op jit(solution)/shard_map/all_to_all | solution.py:618
  90.0 1.3 %shard_map.95 = f32[8,56,128]{2,1,0:T(8,128)} custom-call(s32[8]{0:T(128)S(1)} %copy-done, s32[48]{0:T(128)S(1)} %reshape.23.refs_2_.refs_1_, f32[8,56,128]{2,1,0:T(8,128)S(1)} %all-to-all-done.4.refs_2_), custom_call_target="tpu_custom_call" | custom-call | flops 884736 | bytes 3145728 | tf_op jit(solution)/shard_map/pallas_call | solution.py:584
  91.3 3.9 %all-to-all-start.5 = ((f32[8,56,128]{2,1,0:T(8,128)}), f32[8,56,128]{2,1,0:T(8,128)S(1)}, u32[]{:S(2)}, u32[]{:S(2)}) async-start(f32[8,56,128]{2,1,0:T(8,128)} %shard_map.95), calls=%async_computation.5 | async-start | bytes 458752 | tf_op jit(solution)/shard_map/all_to_all | solution.py:618
  95.2 3.4 %shard_map.96 = f32[6,16,16,128]{3,2,1,0:T(8,128)} custom-call(s32[1]{0:T(128)} %bitcast.refs_0_, s32[8]{0:T(128)S(1)} %copy-done, s32[48]{0:T(128)S(1)} %reshape.20.refs_2_, f32[108]{0:T(128)S(1)} %reshape.21.refs_0_.refs_3_, f32[6,16,16,128]{3,2,1,0:T(8,128)} %shard_map.92.refs_4_, f32[6,96,128]{2,1,0:T(8,128)} %get-tuple-element.48.refs_5_, ...), custom_call_target="tpu_custom_call" | custom-call | flops 14155776 | bytes 3145728 | tf_op jit(solution)/shard_map/pallas_call | solution.py:584
  98.6 4.6 %all-to-all-done.5.refs_8_ = f32[8,56,128]{2,1,0:T(8,128)S(1)} async-done(((f32[8,56,128]{2,1,0:T(8,128)}), f32[8,56,128]{2,1,0:T(8,128)S(1)}, u32[]{:S(2)}, u32[]{:S(2)}) %all-to-all-start.5) | async-done | bytes 229408 | tf_op jit(solution)/shard_map/all_to_all | solution.py:618
  103.2 3.3 %shard_map.97 = f32[6,16,16,128]{3,2,1,0:T(8,128)} custom-call(s32[1]{0:T(128)} %bitcast.refs_0_, s32[8]{0:T(128)S(1)} %copy-done, s32[48]{0:T(128)S(1)} %reshape.20.refs_2_, f32[108]{0:T(128)S(1)} %reshape.21.refs_0_.refs_3_, f32[6,16,16,128]{3,2,1,0:T(8,128)S(1)} %shard_map.94.refs_4_, f32[6,96,128]{2,1,0:T(8,128)} %get-tuple-element.42.refs_5_, ...), custom_call_target="tpu_custom_call" | custom-call | flops 884736 | bytes 3145728 | tf_op jit(solution)/shard_map/pallas_call | solution.py:584
  (1 shorter events, 0.0 us)
Async XLA Ops:
  3.7 7.5 %copy-start.3 = (s32[8,6]{1,0:T(8,128)S(1)}, s32[8,6]{1,0:T(8,128)}, u32[]{:S(2)}) copy-start(s32[8,6]{1,0:T(8,128)} %param.12) | copy-start | bytes 580
  3.7 7.5 %copy-start.1 = (f32[1,6,4,16,128]{4,3,2,1,0:T(8,128)S(1)}, f32[1,6,4,16,128]{4,3,2,1,0:T(8,128)}, u32[]{:S(2)}) copy-start(f32[1,6,4,16,128]{4,3,2,1,0:T(8,128)} %param.7) | copy-start | bytes 589828
  3.7 17.7 %all-to-all-start = ((f32[8,80,128]{2,1,0:T(8,128)}), f32[8,80,128]{2,1,0:T(8,128)S(1)}, u32[]{:S(2)}, u32[]{:S(2)}) async-start(f32[8,80,128]{2,1,0:T(8,128)} %get-tuple-element.35), calls=%async_computation | async-start | bytes 655360 | tf_op jit(solution)/shard_map/all_to_all | solution.py:618
  20.3 1.2 %copy-start = (s32[8]{0:T(128)S(1)}, s32[8]{0:T(128)}, u32[]{:S(2)}) copy-start(s32[8]{0:T(128)} %refs_1_.9) | copy-start | bytes 100
  22.9 5.5 %copy-start.2 = (f32[3,6,6]{2,1,0:T(8,128)S(1)}, f32[3,6,6]{2,1,0:T(8,128)}, u32[]{:S(2)}) copy-start(f32[3,6,6]{2,1,0:T(8,128)} %param.10) | copy-start | bytes 1300
  22.9 16.3 %all-to-all-start.1 = ((f32[8,80,128]{2,1,0:T(8,128)}), f32[8,80,128]{2,1,0:T(8,128)S(1)}, u32[]{:S(2)}, u32[]{:S(2)}) async-start(f32[8,80,128]{2,1,0:T(8,128)} %shard_map.87), calls=%async_computation.1 | async-start | bytes 655360 | tf_op jit(solution)/shard_map/all_to_all | solution.py:618
  28.3 0.7 copy-start.4
  48.8 12.7 %all-to-all-start.2 = ((f32[8,56,128]{2,1,0:T(8,128)}), f32[8,56,128]{2,1,0:T(8,128)S(1)}, u32[]{:S(2)}, u32[]{:S(2)}) async-start(f32[8,56,128]{2,1,0:T(8,128)} %get-tuple-element.45), calls=%async_computation.2 | async-start | bytes 458752 | tf_op jit(solution)/shard_map/all_to_all | solution.py:618
  62.9 11.8 %all-to-all-start.3 = ((f32[8,56,128]{2,1,0:T(8,128)}), f32[8,56,128]{2,1,0:T(8,128)S(1)}, u32[]{:S(2)}, u32[]{:S(2)}) async-start(f32[8,56,128]{2,1,0:T(8,128)} %shard_map.91), calls=%async_computation.3 | async-start | bytes 458752 | tf_op jit(solution)/shard_map/all_to_all | solution.py:618
  78.5 11.5 %all-to-all-start.4 = ((f32[8,56,128]{2,1,0:T(8,128)}), f32[8,56,128]{2,1,0:T(8,128)S(1)}, u32[]{:S(2)}, u32[]{:S(2)}) async-start(f32[8,56,128]{2,1,0:T(8,128)} %get-tuple-element.54), calls=%async_computation.4 | async-start | bytes 458752 | tf_op jit(solution)/shard_map/all_to_all | solution.py:618
  91.3 11.9 %all-to-all-start.5 = ((f32[8,56,128]{2,1,0:T(8,128)}), f32[8,56,128]{2,1,0:T(8,128)S(1)}, u32[]{:S(2)}, u32[]{:S(2)}) async-start(f32[8,56,128]{2,1,0:T(8,128)} %shard_map.95), calls=%async_computation.5 | async-start | bytes 458752 | tf_op jit(solution)/shard_map/all_to_all | solution.py:618

commit v8 on v7

--- a/solution.py
+++ b/solution.py
@@ -156,29 +156,6 @@
         return [faces[side, var * depth : (var + 1) * depth] for var in range(v)]
     layer = faces[side, :y]
     return [layer] + [pltpu.roll(layer, z - var * x, 1) for var in range(1, v)]
-
-
-def add_xy_terms(geo, side, terms, result):
-    v, x, y, z = geo.block
-    for var in range(v):
-        if side < 2:
-            plane = x - 1 if side == 0 else 0
-            result[var, plane] = result[var, plane] + terms[var]
-        else:
-            row = y - 1 if side == 2 else 0
-            result[var, :, row, :] = result[var, :, row, :] + terms[var]
-
-
-def add_z_terms(geo, high_terms, low_terms, inner, result):
-    v, x, y, z = geo.block
-    lane = lax.broadcasted_iota(jnp.int32, (y, z), 1)
-    zero = jnp.zeros((y, z), jnp.float32)
-    for var in range(v):
-        for plane in range(x):
-            high = pltpu.roll(high_terms[var], z - 1 - plane, 1)
-            low = pltpu.roll(low_terms[var], z - plane, 1) if plane else low_terms[var]
-            change = jnp.where(lane == z - 1, high, jnp.where(lane == 0, low, zero))
-            result[var, plane] = inner[var, plane] + change
 
 
 def fill_tall(geo, source, tall):
@@ -416,7 +393,7 @@
         high, low = take_z_faces(geo, lambda var, plane: tall[var, plane, PAD : PAD + y])
         faces[4, :y] = high
         faces[5, :y] = low
-        late.leave(1)
+        late.leave(2)
 
 
 def adjoint_inner_kernel(geo, late, mats, block, grads, rate, result, tall, weights):
@@ -447,37 +424,51 @@
     lax.fori_loop(0, x, body, 0)
 
 
+def add_terms(geo, values, inner, result, leave=None):
+    v, x, y, z = geo.block
+    lane = lax.broadcasted_iota(jnp.int32, (y, z), 1)
+    zero = jnp.zeros((y, z), jnp.float32)
+    for var in range(v):
+        for plane in range(x):
+            high = pltpu.roll(values[4][var], z - 1 - plane, 1)
+            low = pltpu.roll(values[5][var], z - plane, 1) if plane else values[5][var]
+            change = jnp.where(lane == z - 1, high, jnp.where(lane == 0, low, zero))
+            if plane == 0:
+                change = change + values[1][var]
+            if plane == x - 1:
+                change = change + values[0][var]
+            result[var, plane] = inner[var, plane] + change
+        result[var, :, y - 1, :] = result[var, :, y - 1, :] + values[2][var]
+        result[var, :, 0, :] = result[var, :, 0, :] + values[3][var]
+        if leave:
+            leave(var)
+
+
 def step_edge_kernel(geo, first, late, place, owner, orientation, mats, inner, faces, rate_faces, arrived, result, *rest):
     v, x, y, z = geo.block
     if first:
         new_faces, sent, ghosts, raw, piece = rest
         join_parts(geo, arrived, raw, piece)
         turn(geo, own_codes(geo, place, owner, orientation), raw, ghosts)
-        late.leave(3)
+        late.leave(4)
     else:
         ghosts = arrived
         late.wait(4)
         late.wait(7)
     late.wait(5)
-    terms = []
-    for side in (4, 5, 0, 1, 2, 3):
+    values = []
+    for side in range(6):
         depth = y if side < 2 or side > 3 else x
         cells, outer = face_values(geo, faces, side), face_values(geo, ghosts, side)
-        values = step_face(geo, mats, side, cells, outer, rate_faces[side, :depth])
-        if side < 4:
-            add_xy_terms(geo, side, values, result)
-        else:
-            terms.append(values)
-            if side == 5:
-                add_z_terms(geo, *terms, inner, result)
-    late.leave(0)
+        values.append(step_face(geo, mats, side, cells, outer, rate_faces[side, :depth]))
+    add_terms(geo, values, inner, result)
     if first:
         take_xy_faces(geo, result, new_faces)
         high, low = take_z_faces(geo, lambda var, plane: result[var, plane])
         new_faces[4, :y] = high
         new_faces[5, :y] = low
-        late.leave(1)
-        cut(geo, geo.whole, new_faces, sent, 0, functools.partial(late.leave, 2))
+        cut(geo, geo.whole, new_faces, sent, 0, functools.partial(late.leave, 3))
+        late.leave(2)
 
 
 def adjoint_edge_kernel(geo, last, late, place, owner, orientation, mats, inner, faces, weight_faces, *rest):
@@ -494,22 +485,13 @@
         late.leave(3)
         join(geo, weight_buffer, raw, geo.part.total)
         turn(geo, codes, raw, weight_ghosts)
-    for index in range(5, 8):
-        late.wait(index)
-    terms = []
-    for side in (4, 5, 0, 1, 2, 3):
+    values = []
+    for side in range(6):
         views = [face_values(geo, field, side) for field in (faces, ghosts, weight_faces, weight_ghosts)]
-        values = adjoint_face(geo, mats, side, *views)
-        if side < 4:
-            add_xy_terms(geo, side, values, result)
-        else:
-            terms.append(values)
-            if side == 5:
-                add_z_terms(geo, *terms, inner, result)
-    late.leave(0)
+        values.append(adjoint_face(geo, mats, side, *views))
+    add_terms(geo, values, inner, result, functools.partial(late.leave, 0) if last else None)
     if not last:
         take_weight_faces(geo, result, rate_faces, new_faces)
-        late.leave(1)
         cut(geo, geo.whole, new_faces, sent, 0, functools.partial(late.leave, 2))
 
 
@@ -531,11 +513,11 @@
             self.started.append(copy)
 
 
-def call(kernel, ins, outs, scratch, flops):
+def call(kernel, ins, outs, scratch, flops, fetch=()):
     late_in = [(index, shape) for index, (kind, shape) in enumerate(ins) if kind == "H"]
     late_out = [(index, shape) for index, (kind, shape) in enumerate(outs) if kind in "HB"]
     count_in, count_out = len(late_in), len(late_out)
-    sends = sum(shape[0] if kind == "B" else 1 for kind, shape in outs if kind in "HB")
+    sends = sum(shape[0] if kind == "B" else 1 for kind, shape in outs if kind in "HBD")
 
     def body(*refs):
         given = list(refs[: len(ins)])
@@ -543,8 +525,8 @@
         rest = list(refs[len(ins) + len(outs) :])
         own = rest[: len(scratch)]
         stage = rest[len(scratch) : len(scratch) + count_in + count_out]
-        sems_in = rest[len(scratch) + count_in + count_out] if count_in else None
-        sems_out = rest[-1] if count_out else None
+        sems_in = rest[len(scratch) + count_in + count_out] if count_in or fetch else None
+        sems_out = rest[-1] if sends else None
         arrivals, departures = {}, {}
         for slot, (index, _) in enumerate(late_in):
             copy = pltpu.make_async_copy(given[index], stage[slot], sems_in.at[slot])
@@ -554,21 +536,36 @@
         for slot, (index, _) in enumerate(late_out):
             departures[index] = (stage[count_in + slot], made[index])
             made[index] = stage[count_in + slot]
+        for index, (kind, _) in enumerate(outs):
+            if kind == "D":
+                departures[index] = (made[index - 1], made[index])
+        fetched = []
+        for slot, (source, target) in enumerate(fetch):
+            copy = pltpu.make_async_copy(given[source], made[target], sems_in.at[count_in + slot])
+            copy.start()
+            fetched.append(copy)
         late = Late(arrivals, departures, sems_out)
-        kernel(late, *given, *made, *own)
+        hidden_in = {source for source, _ in fetch}
+        hidden_out = {target for _, target in fetch}
+        kernel(
+            late,
+            *[ref for index, ref in enumerate(given) if index not in hidden_in],
+            *[ref for index, ref in enumerate(made) if index not in hidden_out and outs[index][0] != "D"],
+            *own,
+        )
         assert len(late.started) == sends
-        for copy in late.started:
+        for copy in fetched + late.started:
             copy.wait()
 
     hbm = pl.BlockSpec(memory_space=pltpu.HBM)
-    specs = {"S": SMEM, "V": VMEM, "R": VMEM, "H": hbm, "B": hbm}
+    specs = {"S": SMEM, "V": VMEM, "R": VMEM, "H": hbm, "B": hbm, "D": hbm, "P": hbm}
     scratch_shapes = [pltpu.VMEM(shape, jnp.float32) for shape in scratch]
     scratch_shapes += [pltpu.VMEM(shape, jnp.float32) for _, shape in late_in + late_out]
-    if count_in:
-        scratch_shapes.append(pltpu.SemaphoreType.DMA((count_in,)))
-    if count_out:
+    if count_in or fetch:
+        scratch_shapes.append(pltpu.SemaphoreType.DMA((count_in + len(fetch),)))
+    if sends:
         scratch_shapes.append(pltpu.SemaphoreType.DMA((sends,)))
-    shapes = {"V": jax.ShapeDtypeStruct, "R": pltpu.VMEM, "H": pltpu.HBM, "B": pltpu.HBM}
+    shapes = {"V": jax.ShapeDtypeStruct, "R": pltpu.VMEM, "H": pltpu.HBM, "B": pltpu.HBM, "D": pltpu.HBM}
     invoke = pl.pallas_call(
         body,
         in_specs=[specs[kind] for kind, _ in ins],
@@ -580,7 +577,7 @@
     )
 
     def run(*operands):
-        placed = {"H": pltpu.HBM, "R": pltpu.VMEM}
+        placed = {"H": pltpu.HBM, "R": pltpu.VMEM, "P": pltpu.HBM}
         return invoke(
             *[
                 pltpu.with_memory_space_constraint(operand, placed[kind]) if kind in placed else operand
@@ -646,19 +643,19 @@
         part, owner, neighbours, arrived
     )
     first_ghosts = swap(leaving)
-    inner, faces = call(
+    inner, faces, kept_faces = call(
         functools.partial(step_inner_kernel, geo),
         [scalar, far(state.shape), far(rate_block)],
-        [("R", block), far(faces_shape)],
+        [("R", block), ("R", faces_shape), ("D", faces_shape)],
         [geo.tall],
         work,
     )(mats, state, rate)
     first_ghosts, inner, faces = lax.optimization_barrier((first_ghosts, inner, faces))
     gathered = lax.all_gather(first_ghosts[:, :some], "ckpt", axis=0)
-    next_state, next_faces, sent, ghosts = call(
+    next_state, next_faces, kept_next_faces, sent, ghosts = call(
         functools.partial(step_edge_kernel, geo, True),
-        [scalar] * 4 + [kept_near, far(faces_shape), kept_near, near],
-        [("R", block), far(faces_shape), ("B", whole), far(faces_shape)],
+        [scalar] * 4 + [kept_near] * 3 + [near],
+        [("R", block), ("R", faces_shape), ("D", faces_shape), ("B", whole), far(faces_shape)],
         [faces_shape, faces_shape[1:]],
         few,
     )(*fixed, inner, faces, rate_faces, gathered)
@@ -669,18 +666,19 @@
     leaving = route(arrived)
     later_state, leaving = lax.optimization_barrier((next_state, leaving))
     next_ghosts = swap(leaving)
-    (final_inner,) = call(
+    final_inner, weight_faces = call(
         functools.partial(step_inner_kernel, geo),
-        [scalar, kept_near, far(rate_block)],
-        [far(block)],
+        [scalar, kept_near, far(rate_block), ("P", None)],
+        [far(block), ("R", faces_shape)],
         [geo.tall],
         work,
-    )(mats, later_state, rate)
-    next_ghosts, final_inner = lax.optimization_barrier((next_ghosts, final_inner))
+        fetch=((3, 1),),
+    )(mats, later_state, rate, weight_faces)
+    next_ghosts, final_inner, weight_faces = lax.optimization_barrier((next_ghosts, final_inner, weight_faces))
     grads_now, next_weight_faces, sent, turned = call(
         functools.partial(adjoint_edge_kernel, geo, False),
-        [scalar] * 4 + [kept_near, far(faces_shape), far(faces_shape), kept_near, near, near],
-        [("R", block), far(faces_shape), ("B", whole), far(faces_shape)],
+        [scalar] * 4 + [kept_near] * 4 + [near, near],
+        [("R", block), ("R", faces_shape), ("B", whole), far(faces_shape)],
         [faces_shape] * 2,
         few,
     )(*fixed, inner, next_faces, weight_faces, rate_faces, next_ghosts, first_ghosts)
@@ -691,18 +689,19 @@
     leaving = route(arrived)
     final_inner, leaving = lax.optimization_barrier((final_inner, leaving))
     last_ghosts = swap(leaving)
-    (final,) = call(
+    final, faces, ghosts = call(
         functools.partial(step_edge_kernel, geo, False),
-        [scalar] * 4 + [far(block), far(faces_shape), kept_near, far(faces_shape)],
-        [("V", block)],
+        [scalar] * 4 + [far(block), far(faces_shape), kept_near, far(faces_shape), ("P", None), ("P", None)],
+        [("V", block), ("R", faces_shape), ("R", faces_shape)],
         [],
         work,
-    )(*fixed, final_inner, next_faces, rate_faces, turned)
-    last_ghosts, final = lax.optimization_barrier((last_ghosts, final))
+        fetch=((8, 1), (9, 2)),
+    )(*fixed, final_inner, kept_next_faces, rate_faces, turned, kept_faces, ghosts)
+    last_ghosts, final, faces, ghosts = lax.optimization_barrier((last_ghosts, final, faces, ghosts))
     (adjoint,) = call(
         functools.partial(adjoint_edge_kernel, geo, True),
-        [scalar] * 4 + [kept_near] + [far(faces_shape)] * 3 + [near],
-        [("V", block)],
+        [scalar] * 4 + [kept_near] * 4 + [near],
+        [("B", block)],
         [faces_shape] * 2,
         few,
     )(*fixed, inner, faces, next_weight_faces, ghosts, last_ghosts)

time: 108 us -> 105 us (0.972)
  Pallas kernels: 44.2 us -> 41 us
  local copies, waits for them, and re-layouts: 0.87 us -> 2.19 us
    pallas_call x12, Pallas kernels: 44.2 us -> 41 us  [run(): invoke(*[pltpu.with_memory_space_constraint(operand, placed[kind]) if kin...]
    unnamed x10 -> x30, local copies, waits for them, and re-layouts: 0.62 us -> 1.94 us
where the time goes in v8:
time: 105 us; the launch traced here: 104 us
  Pallas kernels  41 us (39%)
  starting transfers between devices  27.4 us (26%)
  waiting for transfers between devices  17.4 us (17%)
  blocking collectives  15.2 us (14%)
  local copies, waits for them, and re-layouts  2.19 us (2%)
    pallas_call x12, Pallas kernels, run(): invoke(*[pltpu.with_memory_space_constraint(operand, placed[kind]) if kin...  41 us
    all_to_all x6, starting transfers between devices, swap(): return lax.all_to_all(buffer, 'space', 0, 0, tiled=True)  27.4 us
    all_to_all x6, waiting for transfers between devices, swap(): return lax.all_to_all(buffer, 'space', 0, 0, tiled=True)  17.4 us
    all_gather x1, blocking collectives, on_device(): state = lax.all_gather(kept, 'ckpt', axis=0)  9.05 us
    all_gather x1, blocking collectives, on_device(): gathered = lax.all_gather(first_ghosts[:, :some], 'ckpt', axis=0)  6.15 us
  transfers between devices with their start and end apart: 6, of which 6 were waited for; matrix products, arithmetic and copies ran while one was open for 0% of the time, Pallas kernels for 25%

profile of v8, /device:TPU:0, one launch (start us, length us, event | category | flops | bytes accessed | tf_op | source)
XLA Modules:
  0.0 104.0 jit_solution(9926853497095614447)
XLA Ops:
  0.6 3.1 %shard_map.86 = (f32[6,96,128]{2,1,0:T(8,128)}, f32[6,16,128]{2,1,0:T(8,128)S(1)}, f32[8,80,128]{2,1,0:T(8,128)}) custom-call(s32[1]{0:T(128)} %bitcast.1.refs_0_, f32[6,4,16,128]{3,2,1,0:T(8,128)} %bitcast.20, f32[6,16,16,128]{3,2,1,0:T(8,128)} %bitcast.17, f32[16,16,128]{2,1,0:T(8,128)} %bitcast.12), custom_call_target="tpu_custom_call" | custom-call | flops 884736 | bytes 3145728 | tf_op jit(solution)/shard_map/pallas_call | solution.py:581
  3.7 0.0 copy-start.13
  3.7 0.0 copy-start.11
  3.7 7.4 %all-to-all-start = ((f32[8,80,128]{2,1,0:T(8,128)}), f32[8,80,128]{2,1,0:T(8,128)S(1)}, u32[]{:S(2)}, u32[]{:S(2)}) async-start(f32[8,80,128]{2,1,0:T(8,128)} %get-tuple-element.45), calls=%async_computation | async-start | bytes 655360 | tf_op jit(solution)/shard_map/all_to_all | solution.py:615
  11.2 0.0 copy-done.13
  11.2 0.1 reshape.23.refs_2_.refs_1_
  11.3 0.0 copy-done.11
  11.3 9.0 %all-gather = f32[24,4,16,128]{3,2,1,0:T(8,128)} all-gather(f32[6,4,16,128]{3,2,1,0:T(8,128)S(1)} %bitcast.21), channel_id=2, replica_groups=mesh['ckpt'=4,'space'=8] {'ckpt'}, dimensions={0}, use_global_device_ids=true | all-gather | bytes 983040 | tf_op jit(solution)/shard_map/all_gather | solution.py:640
  20.3 1.2 %all-to-all-done.refs_3_ = f32[8,80,128]{2,1,0:T(8,128)S(1)} async-done(((f32[8,80,128]{2,1,0:T(8,128)}), f32[8,80,128]{2,1,0:T(8,128)S(1)}, u32[]{:S(2)}, u32[]{:S(2)}) %all-to-all-start) | async-done | bytes 327712 | tf_op jit(solution)/shard_map/all_to_all | solution.py:615
  21.5 0.0 copy-done.3
  21.5 1.3 %shard_map.87 = f32[8,80,128]{2,1,0:T(8,128)} custom-call(s32[1]{0:T(128)} %bitcast.1.refs_0_, s32[8]{0:T(128)S(1)} %copy-done.3, s32[48]{0:T(128)S(1)} %reshape.23.refs_2_.refs_1_, f32[8,80,128]{2,1,0:T(8,128)S(1)} %all-to-all-done.refs_3_), custom_call_target="tpu_custom_call" | custom-call | flops 884736 | bytes 3145728 | tf_op jit(solution)/shard_map/pallas_call | solution.py:581
  22.9 0.0 copy-start.12
  22.9 5.5 %all-to-all-start.1 = ((f32[8,80,128]{2,1,0:T(8,128)}), f32[8,80,128]{2,1,0:T(8,128)S(1)}, u32[]{:S(2)}, u32[]{:S(2)}) async-start(f32[8,80,128]{2,1,0:T(8,128)} %shard_map.87), calls=%async_computation.1 | async-start | bytes 655360 | tf_op jit(solution)/shard_map/all_to_all | solution.py:615
  28.3 0.0 copy-done.12
  28.3 0.0 copy-start.14
  28.4 0.1 reshape.21.refs_0_.refs_3_
  28.4 0.6 copy-done.14
  29.0 0.1 reshape.20.refs_2_
  29.1 5.9 %shard_map.88 = (f32[6,16,16,128]{3,2,1,0:T(8,128)S(1)}, f32[6,96,128]{2,1,0:T(8,128)S(1)}, f32[6,96,128]{2,1,0:T(8,128)}) custom-call(f32[108]{0:T(128)S(1)} %reshape.21.refs_0_.refs_3_, f32[4,6,4,16,128]{4,3,2,1,0:T(8,128)} %bitcast.10, f32[16,16,128]{2,1,0:T(8,128)} %bitcast.13), custom_call_target="tpu_custom_call" | custom-call | flops 14155776 | bytes 3145728 | tf_op jit(solution)/shard_map/pallas_call | solution.py:581
  35.0 4.1 %all-to-all-done.1.refs_9_ = f32[8,80,128]{2,1,0:T(8,128)S(1)} async-done(((f32[8,80,128]{2,1,0:T(8,128)}), f32[8,80,128]{2,1,0:T(8,128)S(1)}, u32[]{:S(2)}, u32[]{:S(2)}) %all-to-all-start.1) | async-done | bytes 327712 | tf_op jit(solution)/shard_map/all_to_all | solution.py:615
  39.1 6.1 %all-gather.1 = f32[32,24,128]{2,1,0:T(8,128)S(1)} all-gather(f32[8,24,128]{2,1,0:T(8,128)S(1)} %slice.3), channel_id=3, replica_groups=mesh['ckpt'=4,'space'=8] {'ckpt'}, dimensions={0}, use_global_device_ids=true | all-gather | bytes 491520 | tf_op jit(solution)/shard_map/all_gather | solution.py:654
  45.3 0.0 copy-done.6
  45.3 2.7 %shard_map.89 = (f32[6,16,16,128]{3,2,1,0:T(8,128)S(1)}, f32[6,96,128]{2,1,0:T(8,128)S(1)}, f32[6,96,128]{2,1,0:T(8,128)}, f32[8,56,128]{2,1,0:T(8,128)}, f32[6,96,128]{2,1,0:T(8,128)}) custom-call(s32[1]{0:T(128)} %bitcast.refs_0_, s32[8]{0:T(128)S(1)} %copy-done.3, s32[48]{0:T(128)S(1)} %reshape.20.refs_2_, f32[108]{0:T(128)S(1)} %reshape.21.refs_0_.refs_3_, ...), custom_call_target="tpu_custom_call" | custom-call | flops 884736 | bytes 3145728 | tf_op jit(solution)/shard_map/pallas_call | solution.py:581
  48.0 3.8 %all-to-all-start.2 = ((f32[8,56,128]{2,1,0:T(8,128)}), f32[8,56,128]{2,1,0:T(8,128)S(1)}, u32[]{:S(2)}, u32[]{:S(2)}) async-start(f32[8,56,128]{2,1,0:T(8,128)} %get-tuple-element.55), calls=%async_computation.2 | async-start | bytes 458752 | tf_op jit(solution)/shard_map/all_to_all | solution.py:615
  51.8 6.0 %shard_map.90.refs_4_ = f32[6,16,16,128]{3,2,1,0:T(8,128)S(1)} custom-call(f32[108]{0:T(128)S(1)} %reshape.21.refs_0_.refs_3_, f32[6,16,16,128]{3,2,1,0:T(8,128)S(1)} %get-tuple-element.61.refs_1_, f32[6,16,16,128]{3,2,1,0:T(8,128)} %bitcast.18, f32[16,16,128]{2,1,0:T(8,128)} %bitcast.14), custom_call_target="tpu_custom_call" | custom-call | flops 28311552 | bytes 3145728 | tf_op jit(solution)/shard_map/pallas_call | solution.py:581
  57.7 3.0 %all-to-all-done.2.refs_2_ = f32[8,56,128]{2,1,0:T(8,128)S(1)} async-done(((f32[8,56,128]{2,1,0:T(8,128)}), f32[8,56,128]{2,1,0:T(8,128)S(1)}, u32[]{:S(2)}, u32[]{:S(2)}) %all-to-all-start.2) | async-done | bytes 229408 | tf_op jit(solution)/shard_map/all_to_all | solution.py:615
  60.7 0.0 copy-done.9
  60.7 1.3 %shard_map.91 = f32[8,56,128]{2,1,0:T(8,128)} custom-call(s32[8]{0:T(128)S(1)} %copy-done.3, s32[48]{0:T(128)S(1)} %reshape.23.refs_2_.refs_1_, f32[8,56,128]{2,1,0:T(8,128)S(1)} %all-to-all-done.2.refs_2_), custom_call_target="tpu_custom_call" | custom-call | flops 884736 | bytes 3145728 | tf_op jit(solution)/shard_map/pallas_call | solution.py:581
  62.0 3.4 %all-to-all-start.3 = ((f32[8,56,128]{2,1,0:T(8,128)}), f32[8,56,128]{2,1,0:T(8,128)S(1)}, u32[]{:S(2)}, u32[]{:S(2)}) async-start(f32[8,56,128]{2,1,0:T(8,128)} %shard_map.91), calls=%async_computation.3 | async-start | bytes 458752 | tf_op jit(solution)/shard_map/all_to_all | solution.py:615
  65.5 0.0 copy-done
  65.5 5.3 %shard_map.92 = (f32[6,16,16,128]{3,2,1,0:T(8,128)}, f32[6,96,128]{2,1,0:T(8,128)S(1)}) custom-call(f32[108]{0:T(128)S(1)} %reshape.21.refs_0_.refs_3_, f32[6,16,16,128]{3,2,1,0:T(8,128)S(1)} %get-tuple-element.61.refs_1_, f32[16,16,128]{2,1,0:T(8,128)} %bitcast.15, f32[6,96,128]{2,1,0:T(8,128)} %get-tuple-element.62.refs_3_), custom_call_target="tpu_custom_call" | custom-call | flops 14155776 | bytes 3145728 | tf_op jit(solution)/shard_map/pallas_call | solution.py:581
  70.8 3.0 %all-to-all-done.3.refs_8_ = f32[8,56,128]{2,1,0:T(8,128)S(1)} async-done(((f32[8,56,128]{2,1,0:T(8,128)}), f32[8,56,128]{2,1,0:T(8,128)S(1)}, u32[]{:S(2)}, u32[]{:S(2)}) %all-to-all-start.3) | async-done | bytes 229408 | tf_op jit(solution)/shard_map/all_to_all | solution.py:615
  73.8 0.6 copy-done.1
  74.5 0.0 copy-done.4
  74.5 0.0 copy-done.7
  74.5 2.7 %shard_map.93 = (f32[6,16,16,128]{3,2,1,0:T(8,128)S(1)}, f32[6,96,128]{2,1,0:T(8,128)S(1)}, f32[8,56,128]{2,1,0:T(8,128)}, f32[6,96,128]{2,1,0:T(8,128)}) custom-call(s32[1]{0:T(128)} %bitcast.refs_0_, s32[8]{0:T(128)S(1)} %copy-done.4, s32[48]{0:T(128)S(1)} %copy-done.7, f32[108]{0:T(128)S(1)} %copy-done.1, f32[6,16,16,128]{3,2,1,0:T(8,128)S(1)} %shard_map.90.refs_4_, ...), custom_call_target="tpu_custom_call" | custom-call | flops 884736 | bytes 3145728 | tf_op jit(solution)/shard_map/pallas_call | solution.py:581
  77.2 3.4 %all-to-all-start.4 = ((f32[8,56,128]{2,1,0:T(8,128)}), f32[8,56,128]{2,1,0:T(8,128)S(1)}, u32[]{:S(2)}, u32[]{:S(2)}) async-start(f32[8,56,128]{2,1,0:T(8,128)} %get-tuple-element.67), calls=%async_computation.4 | async-start | bytes 458752 | tf_op jit(solution)/shard_map/all_to_all | solution.py:615
  80.6 6.0 %shard_map.94.refs_4_ = f32[6,16,16,128]{3,2,1,0:T(8,128)S(1)} custom-call(f32[108]{0:T(128)S(1)} %copy-done.1, f32[4,6,4,16,128]{4,3,2,1,0:T(8,128)} %bitcast.11, f32[6,16,16,128]{3,2,1,0:T(8,128)S(1)} %get-tuple-element.68.refs_2_, f32[16,16,128]{2,1,0:T(8,128)} %bitcast.16), custom_call_target="tpu_custom_call" | custom-call | flops 28311552 | bytes 3145728 | tf_op jit(solution)/shard_map/pallas_call | solution.py:581
  86.6 2.1 %all-to-all-done.4.refs_2_ = f32[8,56,128]{2,1,0:T(8,128)S(1)} async-done(((f32[8,56,128]{2,1,0:T(8,128)}), f32[8,56,128]{2,1,0:T(8,128)S(1)}, u32[]{:S(2)}, u32[]{:S(2)}) %all-to-all-start.4) | async-done | bytes 229408 | tf_op jit(solution)/shard_map/all_to_all | solution.py:615
  88.7 0.0 copy-done.10
  88.7 1.3 %shard_map.95 = f32[8,56,128]{2,1,0:T(8,128)} custom-call(s32[8]{0:T(128)S(1)} %copy-done.4, s32[48]{0:T(128)S(1)} %copy-done.10, f32[8,56,128]{2,1,0:T(8,128)S(1)} %all-to-all-done.4.refs_2_), custom_call_target="tpu_custom_call" | custom-call | flops 884736 | bytes 3145728 | tf_op jit(solution)/shard_map/pallas_call | solution.py:581
  90.0 3.9 %all-to-all-start.5 = ((f32[8,56,128]{2,1,0:T(8,128)}), f32[8,56,128]{2,1,0:T(8,128)S(1)}, u32[]{:S(2)}, u32[]{:S(2)}) async-start(f32[8,56,128]{2,1,0:T(8,128)} %shard_map.95), calls=%async_computation.5 | async-start | bytes 458752 | tf_op jit(solution)/shard_map/all_to_all | solution.py:615
  93.9 0.0 copy-start.5
  93.9 0.6 copy-done.2
  94.5 0.0 copy-done.5
  94.5 3.4 %shard_map.96 = (f32[6,16,16,128]{3,2,1,0:T(8,128)}, f32[6,96,128]{2,1,0:T(8,128)S(1)}, f32[6,96,128]{2,1,0:T(8,128)S(1)}) custom-call(s32[1]{0:T(128)} %bitcast.refs_0_, s32[8]{0:T(128)S(1)} %copy-done.5, s32[48]{0:T(128)S(1)} %copy-done.8, f32[108]{0:T(128)S(1)} %copy-done.2, f32[6,16,16,128]{3,2,1,0:T(8,128)} %get-tuple-element.73.refs_4_, ...), custom_call_target="tpu_custom_call" | custom-call | flops 14155776 | bytes 3145728 | tf_op jit(solution)/shard_map/pallas_call | solution.py:581
  98.0 3.9 %all-to-all-done.5.refs_8_ = f32[8,56,128]{2,1,0:T(8,128)S(1)} async-done(((f32[8,56,128]{2,1,0:T(8,128)}), f32[8,56,128]{2,1,0:T(8,128)S(1)}, u32[]{:S(2)}, u32[]{:S(2)}) %all-to-all-start.5) | async-done | bytes 229408 | tf_op jit(solution)/shard_map/all_to_all | solution.py:615
  101.9 2.1 %shard_map.97 = f32[6,16,16,128]{3,2,1,0:T(8,128)} custom-call(s32[1]{0:T(128)} %bitcast.refs_0_, s32[8]{0:T(128)S(1)} %copy-done.5, s32[48]{0:T(128)S(1)} %copy-done.8, f32[108]{0:T(128)S(1)} %copy-done.2, f32[6,16,16,128]{3,2,1,0:T(8,128)S(1)} %shard_map.94.refs_4_, f32[6,96,128]{2,1,0:T(8,128)S(1)} %get-tuple-element.81.refs_5_, ...), custom_call_target="tpu_custom_call" | custom-call | flops 884736 | bytes 3145728 | tf_op jit(solution)/shard_map/pallas_call | solution.py:581
  (12 shorter events, 0.0 us)
Async XLA Ops:
  3.7 7.5 %copy-start.13 = (s32[8,6]{1,0:T(8,128)S(1)}, s32[8,6]{1,0:T(8,128)}, u32[]{:S(2)}) copy-start(s32[8,6]{1,0:T(8,128)} %param.12) | copy-start | bytes 580
  3.7 7.5 %copy-start.11 = (f32[1,6,4,16,128]{4,3,2,1,0:T(8,128)S(1)}, f32[1,6,4,16,128]{4,3,2,1,0:T(8,128)}, u32[]{:S(2)}) copy-start(f32[1,6,4,16,128]{4,3,2,1,0:T(8,128)} %param.7) | copy-start | bytes 589828
  3.7 17.7 %all-to-all-start = ((f32[8,80,128]{2,1,0:T(8,128)}), f32[8,80,128]{2,1,0:T(8,128)S(1)}, u32[]{:S(2)}, u32[]{:S(2)}) async-start(f32[8,80,128]{2,1,0:T(8,128)} %get-tuple-element.45), calls=%async_computation | async-start | bytes 655360 | tf_op jit(solution)/shard_map/all_to_all | solution.py:615
  11.3 49.5 %copy-start.9 = (s32[48]{0:T(128)}, s32[48]{0:T(128)S(1)}, u32[]{:S(2)}) copy-start(s32[48]{0:T(128)S(1)} %reshape.23.refs_2_.refs_1_) | copy-start | bytes 580
  20.3 1.2 %copy-start.3 = (s32[8]{0:T(128)S(1)}, s32[8]{0:T(128)}, u32[]{:S(2)}) copy-start(s32[8]{0:T(128)} %refs_1_.9) | copy-start | bytes 100
  22.9 5.5 %copy-start.12 = (f32[3,6,6]{2,1,0:T(8,128)S(1)}, f32[3,6,6]{2,1,0:T(8,128)}, u32[]{:S(2)}) copy-start(f32[3,6,6]{2,1,0:T(8,128)} %param.10) | copy-start | bytes 1300
  22.9 16.3 %all-to-all-start.1 = ((f32[8,80,128]{2,1,0:T(8,128)}), f32[8,80,128]{2,1,0:T(8,128)S(1)}, u32[]{:S(2)}, u32[]{:S(2)}) async-start(f32[8,80,128]{2,1,0:T(8,128)} %shard_map.87), calls=%async_computation.1 | async-start | bytes 655360 | tf_op jit(solution)/shard_map/all_to_all | solution.py:615
  28.3 0.7 copy-start.14
  29.0 36.4 %copy-start = (f32[108]{0:T(128)}, f32[108]{0:T(128)S(1)}, u32[]{:S(2)}) copy-start(f32[108]{0:T(128)S(1)} %reshape.21.refs_0_.refs_3_) | copy-start | bytes 1300
  29.1 16.2 %copy-start.6 = (s32[48]{0:T(128)}, s32[48]{0:T(128)S(1)}, u32[]{:S(2)}) copy-start(s32[48]{0:T(128)S(1)} %reshape.20.refs_2_) | copy-start | bytes 580
  48.0 12.7 %all-to-all-start.2 = ((f32[8,56,128]{2,1,0:T(8,128)}), f32[8,56,128]{2,1,0:T(8,128)S(1)}, u32[]{:S(2)}, u32[]{:S(2)}) async-start(f32[8,56,128]{2,1,0:T(8,128)} %get-tuple-element.55), calls=%async_computation.2 | async-start | bytes 458752 | tf_op jit(solution)/shard_map/all_to_all | solution.py:615
  62.0 11.8 %all-to-all-start.3 = ((f32[8,56,128]{2,1,0:T(8,128)}), f32[8,56,128]{2,1,0:T(8,128)S(1)}, u32[]{:S(2)}, u32[]{:S(2)}) async-start(f32[8,56,128]{2,1,0:T(8,128)} %shard_map.91), calls=%async_computation.3 | async-start | bytes 458752 | tf_op jit(solution)/shard_map/all_to_all | solution.py:615
  73.8 0.6 copy-start.1
  73.8 0.7 copy-start.4
  73.8 0.7 copy-start.7
  77.2 11.5 %all-to-all-start.4 = ((f32[8,56,128]{2,1,0:T(8,128)}), f32[8,56,128]{2,1,0:T(8,128)S(1)}, u32[]{:S(2)}, u32[]{:S(2)}) async-start(f32[8,56,128]{2,1,0:T(8,128)} %get-tuple-element.67), calls=%async_computation.4 | async-start | bytes 458752 | tf_op jit(solution)/shard_map/all_to_all | solution.py:615
  80.6 8.1 %copy-start.10 = (s32[48]{0:T(128)S(1)}, s32[48]{0:T(128)}, u32[]{:S(2)}) copy-start(s32[48]{0:T(128)} %copy-done.9) | copy-start | bytes 580
  90.0 11.9 %all-to-all-start.5 = ((f32[8,56,128]{2,1,0:T(8,128)}), f32[8,56,128]{2,1,0:T(8,128)S(1)}, u32[]{:S(2)}, u32[]{:S(2)}) async-start(f32[8,56,128]{2,1,0:T(8,128)} %shard_map.95), calls=%async_computation.5 | async-start | bytes 458752 | tf_op jit(solution)/shard_map/all_to_all | solution.py:615
  93.9 0.6 copy-start.2
  93.9 0.7 copy-start.5
  93.9 0.6 copy-start.8

commit v9 on v8

--- a/solution.py
+++ b/solution.py
@@ -42,19 +42,25 @@
         return (self.n, -(-rows // 8) * 8, self.z)
 
 
-def take_z_faces(geo, load):
+def take_z_faces(geo, load, variables=None):
     v, x, y, z = geo.block
     lane = lax.broadcasted_iota(jnp.int32, (y, z), 1)
     high = jnp.zeros((y, z), jnp.float32)
     low = jnp.zeros((y, z), jnp.float32)
-    for var in range(v):
+    for var in range(variables or v):
         for plane in range(x):
             place = var * x + plane
-            tile = load(var, plane)
-            here = lane == place
-            high = jnp.where(here, pltpu.roll(tile, (place + 1) % z, 1), high)
-            low = jnp.where(here, pltpu.roll(tile, place, 1) if place else tile, low)
-    return high, low
+            tile = pltpu.roll(load(var, plane), place + 1, 1)
+            high = jnp.where(lane == place, tile, high)
+            low = jnp.where(lane == place + 1, tile, low)
+    return high, pltpu.roll(low, z - 1, 1)
+
+
+def repeat_lanes(geo, layer):
+    total = layer
+    for var in range(1, geo.v):
+        total = total + pltpu.roll(layer, var * geo.x, 1)
+    return total
 
 
 def take_xy_faces(geo, source, faces):
@@ -321,9 +327,9 @@
     rate_faces[1, :y] = rate[0]
     rate_faces[2, :x] = rate[:, y - 1, :]
     rate_faces[3, :x] = rate[:, 0, :]
-    high, low = take_z_faces(geo, lambda var, plane: rate[plane])
-    rate_faces[4, :y] = high
-    rate_faces[5, :y] = low
+    high, low = take_z_faces(geo, lambda var, plane: rate[plane], 1)
+    rate_faces[4, :y] = repeat_lanes(geo, high)
+    rate_faces[5, :y] = repeat_lanes(geo, low)
     late.leave(1)
     take_weight_faces(geo, grads, rate_faces, weight_faces)
     late.leave(0)
@@ -366,6 +372,12 @@
             run, start, far = geo.part.runs[index], geo.part.starts[index], geo.part.starts[far_index]
             leaving[owner[block], start : start + run] = arrived[source, far : far + run]
         late.leave(0, owner[block])
+
+
+def turn_weights_kernel(geo, late, mats, block, rate, place, owner, orientation, buffer, result, ghosts, tall, raw):
+    join(geo, buffer, raw, geo.part.total)
+    turn(geo, own_codes(geo, place, owner, orientation), raw, ghosts)
+    step_inner_kernel(geo, late, mats, block, rate, result, tall)
 
 
 def step_inner_kernel(geo, late, mats, block, rate, result, *rest):
@@ -428,11 +440,13 @@
     v, x, y, z = geo.block
     lane = lax.broadcasted_iota(jnp.int32, (y, z), 1)
     zero = jnp.zeros((y, z), jnp.float32)
-    for var in range(v):
+    ends = (lane == 0) | (lane == z - 1)
+    even = lane % 2 == 0
+    for var in range(v):
+        high, low = values[4][var], pltpu.roll(values[5][var], 1, 1)
+        mixed = (jnp.where(even, high, low), jnp.where(even, low, high))
         for plane in range(x):
-            high = pltpu.roll(values[4][var], z - 1 - plane, 1)
-            low = pltpu.roll(values[5][var], z - plane, 1) if plane else values[5][var]
-            change = jnp.where(lane == z - 1, high, jnp.where(lane == 0, low, zero))
+            change = jnp.where(ends, pltpu.roll(mixed[plane % 2], z - 1 - plane, 1), zero)
             if plane == 0:
                 change = change + values[1][var]
             if plane == x - 1:
@@ -479,12 +493,10 @@
         join(geo, weight_buffer, raw)
         turn(geo, codes, raw, weight_ghosts)
     else:
-        rate_faces, buffer, weight_buffer, result, new_faces, sent, ghosts, raw, weight_ghosts = rest
+        rate_faces, buffer, weight_ghosts, result, new_faces, sent, ghosts, raw = rest
         join(geo, buffer, raw)
         turn(geo, codes, raw, ghosts)
         late.leave(3)
-        join(geo, weight_buffer, raw, geo.part.total)
-        turn(geo, codes, raw, weight_ghosts)
     values = []
     for side in range(6):
         views = [face_values(geo, field, side) for field in (faces, ghosts, weight_faces, weight_ghosts)]
@@ -666,22 +678,24 @@
     leaving = route(arrived)
     later_state, leaving = lax.optimization_barrier((next_state, leaving))
     next_ghosts = swap(leaving)
-    final_inner, weight_faces = call(
-        functools.partial(step_inner_kernel, geo),
-        [scalar, kept_near, far(rate_block), ("P", None)],
-        [far(block), ("R", faces_shape)],
-        [geo.tall],
+    final_inner, weight_ghosts, weight_faces = call(
+        functools.partial(turn_weights_kernel, geo),
+        [scalar, kept_near, far(rate_block)] + [scalar] * 3 + [near, ("P", None)],
+        [far(block), ("R", faces_shape), ("R", faces_shape)],
+        [geo.tall, faces_shape],
         work,
-        fetch=((3, 1),),
-    )(mats, later_state, rate, weight_faces)
-    next_ghosts, final_inner, weight_faces = lax.optimization_barrier((next_ghosts, final_inner, weight_faces))
+        fetch=((7, 2),),
+    )(mats, later_state, rate, place, owner, orientation, first_ghosts, weight_faces)
+    next_ghosts, final_inner, weight_ghosts, weight_faces = lax.optimization_barrier(
+        (next_ghosts, final_inner, weight_ghosts, weight_faces)
+    )
     grads_now, next_weight_faces, sent, turned = call(
         functools.partial(adjoint_edge_kernel, geo, False),
-        [scalar] * 4 + [kept_near] * 4 + [near, near],
+        [scalar] * 4 + [kept_near] * 4 + [near, kept_near],
         [("R", block), ("R", faces_shape), ("B", whole), far(faces_shape)],
-        [faces_shape] * 2,
+        [faces_shape],
         few,
-    )(*fixed, inner, next_faces, weight_faces, rate_faces, next_ghosts, first_ghosts)
+    )(*fixed, inner, next_faces, weight_faces, rate_faces, next_ghosts, weight_ghosts)
 
     arrived = swap(sent)
     inner = adjoint_inner(state, far(state.shape), grads_now, kept_near)

time: 105 us -> 105 us (level)
  local copies, waits for them, and re-layouts: 2.19 us -> 3.86 us
    unnamed x30 -> x34, local copies, waits for them, and re-layouts: 1.94 us -> 3.61 us
where the time goes in v9:
time: 105 us; the launch traced here: 104 us
  Pallas kernels  40.1 us (38%)
  starting transfers between devices  27.7 us (26%)
  waiting for transfers between devices  16.7 us (16%)
  blocking collectives  15.2 us (14%)
  local copies, waits for them, and re-layouts  3.86 us (4%)
    pallas_call x12, Pallas kernels, run(): invoke(*[pltpu.with_memory_space_constraint(operand, placed[kind]) if kin...  40.1 us
    all_to_all x6, starting transfers between devices, swap(): return lax.all_to_all(buffer, 'space', 0, 0, tiled=True)  27.7 us
    all_to_all x6, waiting for transfers between devices, swap(): return lax.all_to_all(buffer, 'space', 0, 0, tiled=True)  16.7 us
    all_gather x1, blocking collectives, on_device(): state = lax.all_gather(kept, 'ckpt', axis=0)  9.05 us
    all_gather x1, blocking collectives, on_device(): gathered = lax.all_gather(first_ghosts[:, :some], 'ckpt', axis=0)  6.15 us
    unnamed x34, local copies, waits for them, and re-layouts  3.61 us
  transfers between devices with their start and end apart: 6, of which 6 were waited for; matrix products, arithmetic and copies ran while one was open for 0% of the time, Pallas kernels for 25%

profile of v9, /device:TPU:0, one launch (start us, length us, event | category | flops | bytes accessed | tf_op | source)
XLA Modules:
  0.0 104.4 jit_solution(3489651399439504267)
XLA Ops:
  0.6 2.6 %shard_map.86 = (f32[6,96,128]{2,1,0:T(8,128)}, f32[6,16,128]{2,1,0:T(8,128)S(1)}, f32[8,80,128]{2,1,0:T(8,128)}) custom-call(s32[1]{0:T(128)} %bitcast.1.refs_0_, f32[6,4,16,128]{3,2,1,0:T(8,128)} %bitcast.20, f32[6,16,16,128]{3,2,1,0:T(8,128)} %bitcast.17, f32[16,16,128]{2,1,0:T(8,128)} %bitcast.12), custom_call_target="tpu_custom_call" | custom-call | flops 884736 | bytes 3145728 | tf_op jit(solution)/shard_map/pallas_call | solution.py:593
  3.2 0.0 copy-start.15
  3.2 0.0 copy-start.13
  3.3 7.4 %all-to-all-start = ((f32[8,80,128]{2,1,0:T(8,128)}), f32[8,80,128]{2,1,0:T(8,128)S(1)}, u32[]{:S(2)}, u32[]{:S(2)}) async-start(f32[8,80,128]{2,1,0:T(8,128)} %get-tuple-element.47), calls=%async_computation | async-start | bytes 655360 | tf_op jit(solution)/shard_map/all_to_all | solution.py:627
  10.7 0.0 copy-done.15
  10.7 0.1 reshape.23.refs_2_.refs_1_
  10.8 0.0 copy-done.13
  10.8 9.0 %all-gather = f32[24,4,16,128]{3,2,1,0:T(8,128)} all-gather(f32[6,4,16,128]{3,2,1,0:T(8,128)S(1)} %bitcast.21), channel_id=2, replica_groups=mesh['ckpt'=4,'space'=8] {'ckpt'}, dimensions={0}, use_global_device_ids=true | all-gather | bytes 983040 | tf_op jit(solution)/shard_map/all_gather | solution.py:652
  19.8 1.2 %all-to-all-done.refs_3_ = f32[8,80,128]{2,1,0:T(8,128)S(1)} async-done(((f32[8,80,128]{2,1,0:T(8,128)}), f32[8,80,128]{2,1,0:T(8,128)S(1)}, u32[]{:S(2)}, u32[]{:S(2)}) %all-to-all-start) | async-done | bytes 327712 | tf_op jit(solution)/shard_map/all_to_all | solution.py:627
  21.0 0.0 copy-done.5
  21.0 1.3 %shard_map.87 = f32[8,80,128]{2,1,0:T(8,128)} custom-call(s32[1]{0:T(128)} %bitcast.1.refs_0_, s32[8]{0:T(128)S(1)} %copy-done.5, s32[48]{0:T(128)S(1)} %reshape.23.refs_2_.refs_1_, f32[8,80,128]{2,1,0:T(8,128)S(1)} %all-to-all-done.refs_3_), custom_call_target="tpu_custom_call" | custom-call | flops 884736 | bytes 3145728 | tf_op jit(solution)/shard_map/pallas_call | solution.py:593
  22.4 0.0 copy-start.14
  22.4 5.5 %all-to-all-start.1 = ((f32[8,80,128]{2,1,0:T(8,128)}), f32[8,80,128]{2,1,0:T(8,128)S(1)}, u32[]{:S(2)}, u32[]{:S(2)}) async-start(f32[8,80,128]{2,1,0:T(8,128)} %shard_map.87), calls=%async_computation.1 | async-start | bytes 655360 | tf_op jit(solution)/shard_map/all_to_all | solution.py:627
  27.9 0.0 copy-done.14
  27.9 0.0 copy-start.16
  27.9 0.1 reshape.21.refs_0_.refs_3_
  28.0 0.6 copy-done.16
  28.5 0.1 reshape.20.refs_2_.refs_5_
  28.6 5.7 %shard_map.88 = (f32[6,16,16,128]{3,2,1,0:T(8,128)S(1)}, f32[6,96,128]{2,1,0:T(8,128)S(1)}, f32[6,96,128]{2,1,0:T(8,128)}) custom-call(f32[108]{0:T(128)S(1)} %reshape.21.refs_0_.refs_3_, f32[4,6,4,16,128]{4,3,2,1,0:T(8,128)} %bitcast.10, f32[16,16,128]{2,1,0:T(8,128)} %bitcast.13), custom_call_target="tpu_custom_call" | custom-call | flops 14155776 | bytes 3145728 | tf_op jit(solution)/shard_map/pallas_call | solution.py:593
  34.4 4.3 %all-to-all-done.1.refs_6_ = f32[8,80,128]{2,1,0:T(8,128)S(1)} async-done(((f32[8,80,128]{2,1,0:T(8,128)}), f32[8,80,128]{2,1,0:T(8,128)S(1)}, u32[]{:S(2)}, u32[]{:S(2)}) %all-to-all-start.1) | async-done | bytes 327712 | tf_op jit(solution)/shard_map/all_to_all | solution.py:627
  38.6 6.1 %all-gather.1 = f32[32,24,128]{2,1,0:T(8,128)S(1)} all-gather(f32[8,24,128]{2,1,0:T(8,128)S(1)} %slice.3), channel_id=3, replica_groups=mesh['ckpt'=4,'space'=8] {'ckpt'}, dimensions={0}, use_global_device_ids=true | all-gather | bytes 491520 | tf_op jit(solution)/shard_map/all_gather | solution.py:666
  44.8 2.5 %shard_map.89 = (f32[6,16,16,128]{3,2,1,0:T(8,128)S(1)}, f32[6,96,128]{2,1,0:T(8,128)S(1)}, f32[6,96,128]{2,1,0:T(8,128)}, f32[8,56,128]{2,1,0:T(8,128)}, f32[6,96,128]{2,1,0:T(8,128)}) custom-call(s32[1]{0:T(128)} %bitcast.refs_0_.refs_3_, s32[8]{0:T(128)S(1)} %copy-done.5, s32[48]{0:T(128)S(1)} %reshape.20.refs_2_.refs_5_, ...), custom_call_target="tpu_custom_call" | custom-call | flops 884736 | bytes 3145728 | tf_op jit(solution)/shard_map/pallas_call | solution.py:593
  47.3 3.8 %all-to-all-start.2 = ((f32[8,56,128]{2,1,0:T(8,128)}), f32[8,56,128]{2,1,0:T(8,128)S(1)}, u32[]{:S(2)}, u32[]{:S(2)}) async-start(f32[8,56,128]{2,1,0:T(8,128)} %get-tuple-element.57), calls=%async_computation.2 | async-start | bytes 458752 | tf_op jit(solution)/shard_map/all_to_all | solution.py:627
  51.1 6.0 %shard_map.90.refs_4_ = f32[6,16,16,128]{3,2,1,0:T(8,128)S(1)} custom-call(f32[108]{0:T(128)S(1)} %reshape.21.refs_0_.refs_3_, f32[6,16,16,128]{3,2,1,0:T(8,128)S(1)} %get-tuple-element.63.refs_1_, f32[6,16,16,128]{3,2,1,0:T(8,128)} %bitcast.18, f32[16,16,128]{2,1,0:T(8,128)} %bitcast.14), custom_call_target="tpu_custom_call" | custom-call | flops 28311552 | bytes 3145728 | tf_op jit(solution)/shard_map/pallas_call | solution.py:593
  57.1 3.0 %all-to-all-done.2.refs_2_ = f32[8,56,128]{2,1,0:T(8,128)S(1)} async-done(((f32[8,56,128]{2,1,0:T(8,128)}), f32[8,56,128]{2,1,0:T(8,128)S(1)}, u32[]{:S(2)}, u32[]{:S(2)}) %all-to-all-start.2) | async-done | bytes 229408 | tf_op jit(solution)/shard_map/all_to_all | solution.py:627
  60.1 0.0 copy-done.11
  60.1 1.3 %shard_map.91 = f32[8,56,128]{2,1,0:T(8,128)} custom-call(s32[8]{0:T(128)S(1)} %copy-done.5, s32[48]{0:T(128)S(1)} %reshape.23.refs_2_.refs_1_, f32[8,56,128]{2,1,0:T(8,128)S(1)} %all-to-all-done.2.refs_2_), custom_call_target="tpu_custom_call" | custom-call | flops 884736 | bytes 3145728 | tf_op jit(solution)/shard_map/pallas_call | solution.py:593
  61.4 3.4 %all-to-all-start.3 = ((f32[8,56,128]{2,1,0:T(8,128)}), f32[8,56,128]{2,1,0:T(8,128)S(1)}, u32[]{:S(2)}, u32[]{:S(2)}) async-start(f32[8,56,128]{2,1,0:T(8,128)} %shard_map.91), calls=%async_computation.3 | async-start | bytes 458752 | tf_op jit(solution)/shard_map/all_to_all | solution.py:627
  64.8 5.3 %shard_map.92 = (f32[6,16,16,128]{3,2,1,0:T(8,128)}, f32[6,96,128]{2,1,0:T(8,128)S(1)}, f32[6,96,128]{2,1,0:T(8,128)S(1)}) custom-call(f32[108]{0:T(128)S(1)} %reshape.21.refs_0_.refs_3_, f32[6,16,16,128]{3,2,1,0:T(8,128)S(1)} %get-tuple-element.63.refs_1_, f32[16,16,128]{2,1,0:T(8,128)} %bitcast.15, s32[1]{0:T(128)} %bitcast.refs_0_.refs_3_, ...), custom_call_target="tpu_custom_call" | custom-call | flops 14155776 | bytes 3145728 | tf_op jit(solution)/shard_map/pallas_call | solution.py:593
  70.2 0.0 copy-start
  70.2 0.7 copy-done
  70.9 2.3 %all-to-all-done.3.refs_8_ = f32[8,56,128]{2,1,0:T(8,128)S(1)} async-done(((f32[8,56,128]{2,1,0:T(8,128)}), f32[8,56,128]{2,1,0:T(8,128)S(1)}, u32[]{:S(2)}, u32[]{:S(2)}) %all-to-all-start.3) | async-done | bytes 229408 | tf_op jit(solution)/shard_map/all_to_all | solution.py:627
  73.2 0.6 copy-done.3
  73.8 0.1 copy-done.6
  73.9 1.0 copy-done.1
  74.8 2.6 %shard_map.93 = (f32[6,16,16,128]{3,2,1,0:T(8,128)S(1)}, f32[6,96,128]{2,1,0:T(8,128)S(1)}, f32[8,56,128]{2,1,0:T(8,128)}, f32[6,96,128]{2,1,0:T(8,128)}) custom-call(s32[1]{0:T(128)} %bitcast.refs_0_.refs_3_, s32[8]{0:T(128)S(1)} %copy-done.6, s32[48]{0:T(128)S(1)} %copy-done.9, f32[108]{0:T(128)S(1)} %copy-done.3, ...), custom_call_target="tpu_custom_call" | custom-call | flops 884736 | bytes 3145728 | tf_op jit(solution)/shard_map/pallas_call | solution.py:593
  77.4 3.7 %all-to-all-start.4 = ((f32[8,56,128]{2,1,0:T(8,128)}), f32[8,56,128]{2,1,0:T(8,128)S(1)}, u32[]{:S(2)}, u32[]{:S(2)}) async-start(f32[8,56,128]{2,1,0:T(8,128)} %get-tuple-element.71), calls=%async_computation.4 | async-start | bytes 458752 | tf_op jit(solution)/shard_map/all_to_all | solution.py:627
  81.1 6.0 %shard_map.94.refs_4_ = f32[6,16,16,128]{3,2,1,0:T(8,128)S(1)} custom-call(f32[108]{0:T(128)S(1)} %copy-done.3, f32[4,6,4,16,128]{4,3,2,1,0:T(8,128)} %bitcast.11, f32[6,16,16,128]{3,2,1,0:T(8,128)S(1)} %get-tuple-element.72.refs_2_, f32[16,16,128]{2,1,0:T(8,128)} %bitcast.16), custom_call_target="tpu_custom_call" | custom-call | flops 28311552 | bytes 3145728 | tf_op jit(solution)/shard_map/pallas_call | solution.py:593
  87.1 2.0 %all-to-all-done.4.refs_2_ = f32[8,56,128]{2,1,0:T(8,128)S(1)} async-done(((f32[8,56,128]{2,1,0:T(8,128)}), f32[8,56,128]{2,1,0:T(8,128)S(1)}, u32[]{:S(2)}, u32[]{:S(2)}) %all-to-all-start.4) | async-done | bytes 229408 | tf_op jit(solution)/shard_map/all_to_all | solution.py:627
  89.1 0.0 copy-done.12
  89.1 1.3 %shard_map.95 = f32[8,56,128]{2,1,0:T(8,128)} custom-call(s32[8]{0:T(128)S(1)} %copy-done.6, s32[48]{0:T(128)S(1)} %copy-done.12, f32[8,56,128]{2,1,0:T(8,128)S(1)} %all-to-all-done.4.refs_2_), custom_call_target="tpu_custom_call" | custom-call | flops 884736 | bytes 3145728 | tf_op jit(solution)/shard_map/pallas_call | solution.py:593
  90.4 4.0 %all-to-all-start.5 = ((f32[8,56,128]{2,1,0:T(8,128)}), f32[8,56,128]{2,1,0:T(8,128)S(1)}, u32[]{:S(2)}, u32[]{:S(2)}) async-start(f32[8,56,128]{2,1,0:T(8,128)} %shard_map.95), calls=%async_computation.5 | async-start | bytes 458752 | tf_op jit(solution)/shard_map/all_to_all | solution.py:627
  94.4 0.0 copy-start.7
  94.4 0.6 copy-done.4
  95.0 0.1 copy-done.7
  95.1 3.4 %shard_map.96 = (f32[6,16,16,128]{3,2,1,0:T(8,128)}, f32[6,96,128]{2,1,0:T(8,128)S(1)}, f32[6,96,128]{2,1,0:T(8,128)S(1)}) custom-call(s32[1]{0:T(128)} %bitcast.refs_0_.refs_3_, s32[8]{0:T(128)S(1)} %copy-done.7, s32[48]{0:T(128)S(1)} %copy-done.10, f32[108]{0:T(128)S(1)} %copy-done.4, f32[6,16,16,128]{3,2,1,0:T(8,128)} %get-tuple-element.77.refs_4_, ...), custom_call_target="tpu_custom_call" | custom-call | flops 14155776 | bytes 3145728 | tf_op jit(solution)/shard_map/pallas_call | solution.py:593
  98.5 3.9 %all-to-all-done.5.refs_8_ = f32[8,56,128]{2,1,0:T(8,128)S(1)} async-done(((f32[8,56,128]{2,1,0:T(8,128)}), f32[8,56,128]{2,1,0:T(8,128)S(1)}, u32[]{:S(2)}, u32[]{:S(2)}) %all-to-all-start.5) | async-done | bytes 229408 | tf_op jit(solution)/shard_map/all_to_all | solution.py:627
  102.4 2.0 %shard_map.97 = f32[6,16,16,128]{3,2,1,0:T(8,128)} custom-call(s32[1]{0:T(128)} %bitcast.refs_0_.refs_3_, s32[8]{0:T(128)S(1)} %copy-done.7, s32[48]{0:T(128)S(1)} %copy-done.10, f32[108]{0:T(128)S(1)} %copy-done.4, f32[6,16,16,128]{3,2,1,0:T(8,128)S(1)} %shard_map.94.refs_4_, f32[6,96,128]{2,1,0:T(8,128)S(1)} %get-tuple-element.85.refs_5_, ...), custom_call_target="tpu_custom_call" | custom-call | flops 884736 | bytes 3145728 | tf_op jit(solution)/shard_map/pallas_call | solution.py:593
  (16 shorter events, 0.0 us)
Async XLA Ops:
  3.2 7.5 %copy-start.15 = (s32[8,6]{1,0:T(8,128)S(1)}, s32[8,6]{1,0:T(8,128)}, u32[]{:S(2)}) copy-start(s32[8,6]{1,0:T(8,128)} %param.12) | copy-start | bytes 580
  3.2 7.5 %copy-start.13 = (f32[1,6,4,16,128]{4,3,2,1,0:T(8,128)S(1)}, f32[1,6,4,16,128]{4,3,2,1,0:T(8,128)}, u32[]{:S(2)}) copy-start(f32[1,6,4,16,128]{4,3,2,1,0:T(8,128)} %param.7) | copy-start | bytes 589828
  3.3 17.7 %all-to-all-start = ((f32[8,80,128]{2,1,0:T(8,128)}), f32[8,80,128]{2,1,0:T(8,128)S(1)}, u32[]{:S(2)}, u32[]{:S(2)}) async-start(f32[8,80,128]{2,1,0:T(8,128)} %get-tuple-element.47), calls=%async_computation | async-start | bytes 655360 | tf_op jit(solution)/shard_map/all_to_all | solution.py:627
  10.8 49.3 %copy-start.11 = (s32[48]{0:T(128)}, s32[48]{0:T(128)S(1)}, u32[]{:S(2)}) copy-start(s32[48]{0:T(128)S(1)} %reshape.23.refs_2_.refs_1_) | copy-start | bytes 580
  19.8 1.2 %copy-start.5 = (s32[8]{0:T(128)S(1)}, s32[8]{0:T(128)}, u32[]{:S(2)}) copy-start(s32[8]{0:T(128)} %refs_1_.9) | copy-start | bytes 100
  22.4 5.5 %copy-start.14 = (f32[3,6,6]{2,1,0:T(8,128)S(1)}, f32[3,6,6]{2,1,0:T(8,128)}, u32[]{:S(2)}) copy-start(f32[3,6,6]{2,1,0:T(8,128)} %param.10) | copy-start | bytes 1300
  22.4 16.3 %all-to-all-start.1 = ((f32[8,80,128]{2,1,0:T(8,128)}), f32[8,80,128]{2,1,0:T(8,128)S(1)}, u32[]{:S(2)}, u32[]{:S(2)}) async-start(f32[8,80,128]{2,1,0:T(8,128)} %shard_map.87), calls=%async_computation.1 | async-start | bytes 655360 | tf_op jit(solution)/shard_map/all_to_all | solution.py:627
  27.9 0.7 copy-start.16
  28.5 36.3 %copy-start.2 = (f32[108]{0:T(128)}, f32[108]{0:T(128)S(1)}, u32[]{:S(2)}) copy-start(f32[108]{0:T(128)S(1)} %reshape.21.refs_0_.refs_3_) | copy-start | bytes 1300
  28.6 36.2 %copy-start.8 = (s32[48]{0:T(128)}, s32[48]{0:T(128)S(1)}, u32[]{:S(2)}) copy-start(s32[48]{0:T(128)S(1)} %reshape.20.refs_2_.refs_5_) | copy-start | bytes 580
  47.3 12.7 %all-to-all-start.2 = ((f32[8,56,128]{2,1,0:T(8,128)}), f32[8,56,128]{2,1,0:T(8,128)S(1)}, u32[]{:S(2)}, u32[]{:S(2)}) async-start(f32[8,56,128]{2,1,0:T(8,128)} %get-tuple-element.57), calls=%async_computation.2 | async-start | bytes 458752 | tf_op jit(solution)/shard_map/all_to_all | solution.py:627
  61.4 11.8 %all-to-all-start.3 = ((f32[8,56,128]{2,1,0:T(8,128)}), f32[8,56,128]{2,1,0:T(8,128)S(1)}, u32[]{:S(2)}, u32[]{:S(2)}) async-start(f32[8,56,128]{2,1,0:T(8,128)} %shard_map.91), calls=%async_computation.3 | async-start | bytes 458752 | tf_op jit(solution)/shard_map/all_to_all | solution.py:627
  70.2 0.7 copy-start
  73.2 0.6 copy-start.3
  73.2 0.7 copy-start.6
  73.2 0.7 copy-start.9
  73.9 1.0 copy-start.1
  77.4 11.7 %all-to-all-start.4 = ((f32[8,56,128]{2,1,0:T(8,128)}), f32[8,56,128]{2,1,0:T(8,128)S(1)}, u32[]{:S(2)}, u32[]{:S(2)}) async-start(f32[8,56,128]{2,1,0:T(8,128)} %get-tuple-element.71), calls=%async_computation.4 | async-start | bytes 458752 | tf_op jit(solution)/shard_map/all_to_all | solution.py:627
  81.1 8.0 %copy-start.12 = (s32[48]{0:T(128)S(1)}, s32[48]{0:T(128)}, u32[]{:S(2)}) copy-start(s32[48]{0:T(128)} %copy-done.11) | copy-start | bytes 580
  90.4 12.0 %all-to-all-start.5 = ((f32[8,56,128]{2,1,0:T(8,128)}), f32[8,56,128]{2,1,0:T(8,128)S(1)}, u32[]{:S(2)}, u32[]{:S(2)}) async-start(f32[8,56,128]{2,1,0:T(8,128)} %shard_map.95), calls=%async_computation.5 | async-start | bytes 458752 | tf_op jit(solution)/shard_map/all_to_all | solution.py:627
  94.4 0.6 copy-start.4
  94.4 0.7 copy-start.7
  94.4 0.6 copy-start.10

commit v10 on v9

--- a/solution.py
+++ b/solution.py
@@ -80,11 +80,32 @@
             leave(slot)
 
 
-def own_codes(geo, place, owner, orientation):
+class Table:
+    def __init__(self, geo, ref):
+        self.ref, self.n = ref, geo.n
+
+    def place(self):
+        return self.ref[0]
+
+    def part(self):
+        return self.ref[1]
+
+    def owner(self, block):
+        return self.ref[2 + block]
+
+    def neighbour(self, block, side):
+        return self.ref[2 + self.n + block * 6 + side]
+
+    def orientation(self, block, side):
+        return self.ref[2 + 7 * self.n + block * 6 + side]
+
+
+def own_codes(geo, table):
+    table = Table(geo, table)
     block = jnp.int32(0)
     for index in range(geo.n):
-        block = jnp.where(owner[index] == place[0], index, block)
-    return [orientation[block * 6 + side] for side in range(6)]
+        block = jnp.where(table.owner(index) == table.place(), index, block)
+    return [table.orientation(block, side) for side in range(6)]
 
 
 def flip_rows(values, flag, length):
@@ -349,34 +370,36 @@
     faces[5, :y] = low * rate_faces[5, :y]
 
 
-def route_whole(geo, owner, neighbours, block, arrived, leaving, base):
+def route_whole(geo, table, block, arrived, leaving, base):
     for side in range(6):
-        source = owner[neighbours[block * 6 + side]]
+        source = table.owner(table.neighbour(block, side))
         run, start, far = geo.whole.runs[side], base + geo.whole.starts[side], base + geo.whole.starts[side ^ 1]
-        leaving[owner[block], start : start + run] = arrived[source, far : far + run]
-
-
-def route_kernel(geo, late, owner, neighbours, arrived, leaving):
+        leaving[table.owner(block), start : start + run] = arrived[source, far : far + run]
+
+
+def route_kernel(geo, late, table, arrived, leaving):
+    table = Table(geo, table)
     for block in range(geo.n):
-        route_whole(geo, owner, neighbours, block, arrived, leaving, 0)
-        late.leave(0, owner[block])
-
-
-def route_first_kernel(geo, late, part, owner, neighbours, arrived, leaving):
-    x_side = jnp.where(part[0] == geo.parts - 1, 1, 0)
+        route_whole(geo, table, block, arrived, leaving, 0)
+        late.leave(0, table.owner(block))
+
+
+def route_first_kernel(geo, late, table, arrived, leaving):
+    table = Table(geo, table)
+    x_side = jnp.where(table.part() == geo.parts - 1, 1, 0)
     for block in range(geo.n):
-        route_whole(geo, owner, neighbours, block, arrived, leaving, geo.part.total)
+        route_whole(geo, table, block, arrived, leaving, geo.part.total)
         for index in range(5):
             side, far_index = (x_side, 0) if index == 0 else (index + 1, ((index + 1) ^ 1) - 1)
-            source = owner[neighbours[block * 6 + side]]
+            source = table.owner(table.neighbour(block, side))
             run, start, far = geo.part.runs[index], geo.part.starts[index], geo.part.starts[far_index]
-            leaving[owner[block], start : start + run] = arrived[source, far : far + run]
-        late.leave(0, owner[block])
-
-
-def turn_weights_kernel(geo, late, mats, block, rate, place, owner, orientation, buffer, result, ghosts, tall, raw):
+            leaving[table.owner(block), start : start + run] = arrived[source, far : far + run]
+        late.leave(0, table.owner(block))
+
+
+def turn_weights_kernel(geo, late, mats, block, rate, table, buffer, result, ghosts, tall, raw):
     join(geo, buffer, raw, geo.part.total)
-    turn(geo, own_codes(geo, place, owner, orientation), raw, ghosts)
+    turn(geo, own_codes(geo, table), raw, ghosts)
     step_inner_kernel(geo, late, mats, block, rate, result, tall)
 
 
@@ -458,18 +481,18 @@
             leave(var)
 
 
-def step_edge_kernel(geo, first, late, place, owner, orientation, mats, inner, faces, rate_faces, arrived, result, *rest):
+def step_edge_kernel(geo, first, late, table, mats, inner, faces, rate_faces, arrived, result, *rest):
     v, x, y, z = geo.block
     if first:
         new_faces, sent, ghosts, raw, piece = rest
         join_parts(geo, arrived, raw, piece)
-        turn(geo, own_codes(geo, place, owner, orientation), raw, ghosts)
+        turn(geo, own_codes(geo, table), raw, ghosts)
         late.leave(4)
     else:
         ghosts = arrived
-        late.wait(4)
-        late.wait(7)
-    late.wait(5)
+        late.wait(2)
+        late.wait(5)
+    late.wait(3)
     values = []
     for side in range(6):
         depth = y if side < 2 or side > 3 else x
@@ -485,9 +508,9 @@
         late.leave(2)
 
 
-def adjoint_edge_kernel(geo, last, late, place, owner, orientation, mats, inner, faces, weight_faces, *rest):
-    v, x, y, z = geo.block
-    codes = own_codes(geo, place, owner, orientation)
+def adjoint_edge_kernel(geo, last, late, table, mats, inner, faces, weight_faces, *rest):
+    v, x, y, z = geo.block
+    codes = own_codes(geo, table)
     if last:
         ghosts, weight_buffer, result, raw, weight_ghosts = rest
         join(geo, weight_buffer, raw)
@@ -525,7 +548,7 @@
             self.started.append(copy)
 
 
-def call(kernel, ins, outs, scratch, flops, fetch=()):
+def call(kernel, ins, outs, scratch, flops, fetch=(), aliases=None):
     late_in = [(index, shape) for index, (kind, shape) in enumerate(ins) if kind == "H"]
     late_out = [(index, shape) for index, (kind, shape) in enumerate(outs) if kind in "HB"]
     count_in, count_out = len(late_in), len(late_out)
@@ -584,12 +607,13 @@
         out_specs=[specs[kind] for kind, _ in outs],
         out_shape=[shapes[kind](shape, jnp.float32) for kind, shape in outs],
         scratch_shapes=scratch_shapes,
+        input_output_aliases=aliases or {},
         compiler_params=pltpu.CompilerParams(vmem_limit_bytes=VMEM_LIMIT),
         cost_estimate=pl.CostEstimate(flops=flops, bytes_accessed=3 << 20, transcendentals=0),
     )
 
     def run(*operands):
-        placed = {"H": pltpu.HBM, "R": pltpu.VMEM, "P": pltpu.HBM}
+        placed = {"S": pltpu.HBM, "H": pltpu.HBM, "R": pltpu.VMEM, "P": pltpu.HBM}
         return invoke(
             *[
                 pltpu.with_memory_space_constraint(operand, placed[kind]) if kind in placed else operand
@@ -608,9 +632,8 @@
     place = lax.axis_index("space").astype(jnp.int32).reshape(1)
     part = lax.axis_index("ckpt").astype(jnp.int32).reshape(1)
     mats = flux_mats.reshape(-1)
-    neighbours = neighbours.reshape(-1)
-    orientation = orientation.reshape(-1)
-    fixed = (place, owner, orientation, mats)
+    table = jnp.concatenate([place, part, owner, neighbours.reshape(-1), orientation.reshape(-1)])
+    fixed = (table, mats)
     work = nvars * nvars * 3 * 4 * cx * cy * cz
     few = work // 16
     whole, both = geo.buffer(geo.whole.total), geo.buffer(geo.part.total + geo.whole.total)
@@ -627,8 +650,8 @@
         return lax.all_to_all(buffer, "space", 0, 0, tiled=True)
 
     def route(arrived):
-        return call(functools.partial(route_kernel, geo), [scalar, scalar, near], [("B", whole)], [], few)(
-            owner, neighbours, arrived
+        return call(functools.partial(route_kernel, geo), [scalar, near], [("B", whole)], [], few)(
+            table, arrived
         )[0]
 
     def adjoint_inner(state, state_kind, grads, grads_kind):
@@ -651,8 +674,8 @@
     arrived = swap(sent)
     state = lax.all_gather(kept, "ckpt", axis=0)
     arrived, state = lax.optimization_barrier((arrived, state))
-    (leaving,) = call(functools.partial(route_first_kernel, geo), [scalar] * 3 + [near], [("B", both)], [], few)(
-        part, owner, neighbours, arrived
+    (leaving,) = call(functools.partial(route_first_kernel, geo), [scalar, near], [("B", both)], [], few)(
+        table, arrived
     )
     first_ghosts = swap(leaving)
     inner, faces, kept_faces = call(
@@ -666,10 +689,11 @@
     gathered = lax.all_gather(first_ghosts[:, :some], "ckpt", axis=0)
     next_state, next_faces, kept_next_faces, sent, ghosts = call(
         functools.partial(step_edge_kernel, geo, True),
-        [scalar] * 4 + [kept_near] * 3 + [near],
+        [scalar] * 2 + [kept_near] * 3 + [near],
         [("R", block), ("R", faces_shape), ("D", faces_shape), ("B", whole), far(faces_shape)],
         [faces_shape, faces_shape[1:]],
         few,
+        aliases={2: 0},
     )(*fixed, inner, faces, rate_faces, gathered)
 
     arrived = swap(sent)
@@ -680,21 +704,22 @@
     next_ghosts = swap(leaving)
     final_inner, weight_ghosts, weight_faces = call(
         functools.partial(turn_weights_kernel, geo),
-        [scalar, kept_near, far(rate_block)] + [scalar] * 3 + [near, ("P", None)],
+        [scalar, kept_near, far(rate_block), scalar, near, ("P", None)],
         [far(block), ("R", faces_shape), ("R", faces_shape)],
         [geo.tall, faces_shape],
         work,
-        fetch=((7, 2),),
-    )(mats, later_state, rate, place, owner, orientation, first_ghosts, weight_faces)
+        fetch=((5, 2),),
+    )(mats, later_state, rate, table, first_ghosts, weight_faces)
     next_ghosts, final_inner, weight_ghosts, weight_faces = lax.optimization_barrier(
         (next_ghosts, final_inner, weight_ghosts, weight_faces)
     )
     grads_now, next_weight_faces, sent, turned = call(
         functools.partial(adjoint_edge_kernel, geo, False),
-        [scalar] * 4 + [kept_near] * 4 + [near, kept_near],
+        [scalar] * 2 + [kept_near] * 4 + [near, kept_near],
         [("R", block), ("R", faces_shape), ("B", whole), far(faces_shape)],
         [faces_shape],
         few,
+        aliases={2: 0},
     )(*fixed, inner, next_faces, weight_faces, rate_faces, next_ghosts, weight_ghosts)
 
     arrived = swap(sent)
@@ -705,16 +730,16 @@
     last_ghosts = swap(leaving)
     final, faces, ghosts = call(
         functools.partial(step_edge_kernel, geo, False),
-        [scalar] * 4 + [far(block), far(faces_shape), kept_near, far(faces_shape), ("P", None), ("P", None)],
+        [scalar] * 2 + [far(block), far(faces_shape), kept_near, far(faces_shape), ("P", None), ("P", None)],
         [("V", block), ("R", faces_shape), ("R", faces_shape)],
         [],
         work,
-        fetch=((8, 1), (9, 2)),
+        fetch=((6, 1), (7, 2)),
     )(*fixed, final_inner, kept_next_faces, rate_faces, turned, kept_faces, ghosts)
     last_ghosts, final, faces, ghosts = lax.optimization_barrier((last_ghosts, final, faces, ghosts))
     (adjoint,) = call(
         functools.partial(adjoint_edge_kernel, geo, True),
-        [scalar] * 4 + [kept_near] * 4 + [near],
+        [scalar] * 2 + [kept_near] * 4 + [near],
         [("B", block)],
         [faces_shape] * 2,
         few,

time: 105 us -> 106 us (level)
  Pallas kernels: 40.1 us -> 42.2 us
  local copies, waits for them, and re-layouts: 3.86 us -> 2.66 us
    unnamed x34 -> x10, local copies, waits for them, and re-layouts: 3.61 us -> 1.27 us
    pallas_call x12, Pallas kernels: 40.1 us -> 42.2 us  [run(): invoke(*[pltpu.with_memory_space_constraint(operand, placed[kind]) if kin...]
  transfers between devices with their start and end apart: 6 -> 6, of which waited for: 6 -> 5; matrix products, arithmetic and copies ran while one was open for 0% -> 1% of each run, Pallas kernels for 25% -> 26%
where the time goes in v10:
time: 106 us; the launch traced here: 105 us
  Pallas kernels  42.2 us (40%)
  starting transfers between devices  28 us (26%)
  waiting for transfers between devices  16.6 us (16%)
  blocking collectives  15.2 us (14%)
  local copies, waits for them, and re-layouts  2.66 us (3%)
    pallas_call x12, Pallas kernels, run(): invoke(*[pltpu.with_memory_space_constraint(operand, placed[kind]) if kin...  42.2 us
    all_to_all x6, starting transfers between devices, swap(): return lax.all_to_all(buffer, 'space', 0, 0, tiled=True)  28 us
    all_to_all x6, waiting for transfers between devices, swap(): return lax.all_to_all(buffer, 'space', 0, 0, tiled=True)  16.6 us
    all_gather x1, blocking collectives, on_device(): state = lax.all_gather(kept, 'ckpt', axis=0)  9.03 us
    all_gather x1, blocking collectives, on_device(): gathered = lax.all_gather(first_ghosts[:, :some], 'ckpt', axis=0)  6.15 us
  transfers between devices with their start and end apart: 6, of which 5 were waited for; matrix products, arithmetic and copies ran while one was open for 1% of the time, Pallas kernels for 26%

profile of v10, /device:TPU:0, one launch (start us, length us, event | category | flops | bytes accessed | tf_op | source)
XLA Modules:
  0.0 105.4 jit_solution(9920290475151842780)
XLA Ops:
  0.6 2.6 %shard_map.86 = (f32[6,96,128]{2,1,0:T(8,128)}, f32[6,16,128]{2,1,0:T(8,128)S(1)}, f32[8,80,128]{2,1,0:T(8,128)}) custom-call(s32[1]{0:T(128)} %bitcast.1.refs_0_, f32[6,4,16,128]{3,2,1,0:T(8,128)} %bitcast.20, f32[6,16,16,128]{3,2,1,0:T(8,128)} %bitcast.17, f32[16,16,128]{2,1,0:T(8,128)} %bitcast.12), custom_call_target="tpu_custom_call" | custom-call | flops 884736 | bytes 3145728 | tf_op jit(solution)/shard_map/pallas_call | solution.py:617
  3.2 0.0 copy-start.2
  3.2 0.0 copy-start
  3.3 7.4 %all-to-all-start = ((f32[8,80,128]{2,1,0:T(8,128)}), f32[8,80,128]{2,1,0:T(8,128)S(1)}, u32[]{:S(2)}, u32[]{:S(2)}) async-start(f32[8,80,128]{2,1,0:T(8,128)} %get-tuple-element.47), calls=%async_computation | async-start | bytes 655360 | tf_op jit(solution)/shard_map/all_to_all | solution.py:650
  10.7 0.0 copy-start.3
  10.7 0.0 copy-done.2
  10.7 0.1 reshape.21
  10.8 0.6 copy-done.3
  11.4 0.1 reshape.22
  11.4 0.0 copy-start.4
  11.4 0.7 copy-done.4
  12.1 0.6 concatenate.3.refs_0_.refs_3_
  12.7 0.0 copy-done
  12.7 9.0 %all-gather = f32[24,4,16,128]{3,2,1,0:T(8,128)} all-gather(f32[6,4,16,128]{3,2,1,0:T(8,128)S(1)} %bitcast.21), channel_id=2, replica_groups=mesh['ckpt'=4,'space'=8] {'ckpt'}, dimensions={0}, use_global_device_ids=true | all-gather | bytes 983040 | tf_op jit(solution)/shard_map/all_gather | solution.py:675
  21.8 0.0 all-to-all-done.refs_1_
  21.8 1.5 %shard_map.87 = f32[8,80,128]{2,1,0:T(8,128)} custom-call(s32[106]{0:T(128)} %concatenate.3.refs_0_.refs_3_, f32[8,80,128]{2,1,0:T(8,128)S(1)} %all-to-all-done.refs_1_), custom_call_target="tpu_custom_call" | custom-call | flops 884736 | bytes 3145728 | tf_op jit(solution)/shard_map/pallas_call | solution.py:617
  23.3 0.0 copy-start.1
  23.3 6.0 %all-to-all-start.1 = ((f32[8,80,128]{2,1,0:T(8,128)}), f32[8,80,128]{2,1,0:T(8,128)S(1)}, u32[]{:S(2)}, u32[]{:S(2)}) async-start(f32[8,80,128]{2,1,0:T(8,128)} %shard_map.87), calls=%async_computation.1 | async-start | bytes 655360 | tf_op jit(solution)/shard_map/all_to_all | solution.py:650
  29.3 0.0 copy-done.1
  29.3 0.6 reshape.23.refs_0_.refs_1_
  29.9 5.8 %shard_map.88 = (f32[6,16,16,128]{3,2,1,0:T(8,128)S(1)}, f32[6,96,128]{2,1,0:T(8,128)S(1)}, f32[6,96,128]{2,1,0:T(8,128)}) custom-call(f32[108]{0:T(128)} %reshape.23.refs_0_.refs_1_, f32[4,6,4,16,128]{4,3,2,1,0:T(8,128)} %bitcast.10, f32[16,16,128]{2,1,0:T(8,128)} %bitcast.13), custom_call_target="tpu_custom_call" | custom-call | flops 14155776 | bytes 3145728 | tf_op jit(solution)/shard_map/pallas_call | solution.py:617
  35.7 4.3 %all-to-all-done.1.refs_4_ = f32[8,80,128]{2,1,0:T(8,128)S(1)} async-done(((f32[8,80,128]{2,1,0:T(8,128)}), f32[8,80,128]{2,1,0:T(8,128)S(1)}, u32[]{:S(2)}, u32[]{:S(2)}) %all-to-all-start.1) | async-done | bytes 327712 | tf_op jit(solution)/shard_map/all_to_all | solution.py:650
  40.1 6.1 %all-gather.1 = f32[32,24,128]{2,1,0:T(8,128)S(1)} all-gather(f32[8,24,128]{2,1,0:T(8,128)S(1)} %slice.3), channel_id=3, replica_groups=mesh['ckpt'=4,'space'=8] {'ckpt'}, dimensions={0}, use_global_device_ids=true | all-gather | bytes 491520 | tf_op jit(solution)/shard_map/all_gather | solution.py:689
  46.2 3.0 %shard_map.89 = (f32[6,16,16,128]{3,2,1,0:T(8,128)S(1)}, f32[6,96,128]{2,1,0:T(8,128)S(1)}, f32[6,96,128]{2,1,0:T(8,128)}, f32[8,56,128]{2,1,0:T(8,128)}, f32[6,96,128]{2,1,0:T(8,128)}) custom-call(s32[106]{0:T(128)} %concatenate.3.refs_0_.refs_3_, f32[108]{0:T(128)} %reshape.23.refs_0_.refs_1_, ...), custom_call_target="tpu_custom_call", output_to_operand_aliasing={{0}: (2, {})} | custom-call | flops 884736 | bytes 3145728 | tf_op jit(solution)/shard_map/pallas_call | solution.py:617
  49.3 3.8 %all-to-all-start.2 = ((f32[8,56,128]{2,1,0:T(8,128)}), f32[8,56,128]{2,1,0:T(8,128)S(1)}, u32[]{:S(2)}, u32[]{:S(2)}) async-start(f32[8,56,128]{2,1,0:T(8,128)} %get-tuple-element.57), calls=%async_computation.2 | async-start | bytes 458752 | tf_op jit(solution)/shard_map/all_to_all | solution.py:650
  53.0 6.1 %shard_map.90.refs_2_ = f32[6,16,16,128]{3,2,1,0:T(8,128)S(1)} custom-call(f32[108]{0:T(128)} %reshape.23.refs_0_.refs_1_, f32[6,16,16,128]{3,2,1,0:T(8,128)S(1)} %get-tuple-element.63.refs_1_, f32[6,16,16,128]{3,2,1,0:T(8,128)} %bitcast.18, f32[16,16,128]{2,1,0:T(8,128)} %bitcast.14), custom_call_target="tpu_custom_call" | custom-call | flops 28311552 | bytes 3145728 | tf_op jit(solution)/shard_map/pallas_call | solution.py:617
  59.1 2.9 %all-to-all-done.2.refs_1_ = f32[8,56,128]{2,1,0:T(8,128)S(1)} async-done(((f32[8,56,128]{2,1,0:T(8,128)}), f32[8,56,128]{2,1,0:T(8,128)S(1)}, u32[]{:S(2)}, u32[]{:S(2)}) %all-to-all-start.2) | async-done | bytes 229408 | tf_op jit(solution)/shard_map/all_to_all | solution.py:650
  62.0 1.5 %shard_map.91 = f32[8,56,128]{2,1,0:T(8,128)} custom-call(s32[106]{0:T(128)} %concatenate.3.refs_0_.refs_3_, f32[8,56,128]{2,1,0:T(8,128)S(1)} %all-to-all-done.2.refs_1_), custom_call_target="tpu_custom_call" | custom-call | flops 884736 | bytes 3145728 | tf_op jit(solution)/shard_map/pallas_call | solution.py:617
  63.4 3.4 %all-to-all-start.3 = ((f32[8,56,128]{2,1,0:T(8,128)}), f32[8,56,128]{2,1,0:T(8,128)S(1)}, u32[]{:S(2)}, u32[]{:S(2)}) async-start(f32[8,56,128]{2,1,0:T(8,128)} %shard_map.91), calls=%async_computation.3 | async-start | bytes 458752 | tf_op jit(solution)/shard_map/all_to_all | solution.py:650
  66.9 5.5 %shard_map.92 = (f32[6,16,16,128]{3,2,1,0:T(8,128)}, f32[6,96,128]{2,1,0:T(8,128)S(1)}, f32[6,96,128]{2,1,0:T(8,128)S(1)}) custom-call(f32[108]{0:T(128)} %reshape.23.refs_0_.refs_1_, f32[6,16,16,128]{3,2,1,0:T(8,128)S(1)} %get-tuple-element.63.refs_1_, f32[16,16,128]{2,1,0:T(8,128)} %bitcast.15, s32[106]{0:T(128)} %concatenate.3.refs_0_.refs_3_, ...), custom_call_target="tpu_custom_call" | custom-call | flops 14155776 | bytes 3145728 | tf_op jit(solution)/shard_map/pallas_call | solution.py:617
  72.3 2.9 %all-to-all-done.3.refs_6_ = f32[8,56,128]{2,1,0:T(8,128)S(1)} async-done(((f32[8,56,128]{2,1,0:T(8,128)}), f32[8,56,128]{2,1,0:T(8,128)S(1)}, u32[]{:S(2)}, u32[]{:S(2)}) %all-to-all-start.3) | async-done | bytes 229408 | tf_op jit(solution)/shard_map/all_to_all | solution.py:650
  75.2 3.0 %shard_map.93 = (f32[6,16,16,128]{3,2,1,0:T(8,128)S(1)}, f32[6,96,128]{2,1,0:T(8,128)S(1)}, f32[8,56,128]{2,1,0:T(8,128)}, f32[6,96,128]{2,1,0:T(8,128)}) custom-call(s32[106]{0:T(128)} %concatenate.3.refs_0_.refs_3_, f32[108]{0:T(128)} %reshape.23.refs_0_.refs_1_, f32[6,16,16,128]{3,2,1,0:T(8,128)S(1)} %shard_map.90.refs_2_, ...), custom_call_target="tpu_custom_call", output_to_operand_aliasing={{0}: (2, {})} | custom-call | flops 884736 | bytes 3145728 | tf_op jit(solution)/shard_map/pallas_call | solution.py:617
  78.3 3.4 %all-to-all-start.4 = ((f32[8,56,128]{2,1,0:T(8,128)}), f32[8,56,128]{2,1,0:T(8,128)S(1)}, u32[]{:S(2)}, u32[]{:S(2)}) async-start(f32[8,56,128]{2,1,0:T(8,128)} %get-tuple-element.71), calls=%async_computation.4 | async-start | bytes 458752 | tf_op jit(solution)/shard_map/all_to_all | solution.py:650
  81.7 6.1 %shard_map.94.refs_2_ = f32[6,16,16,128]{3,2,1,0:T(8,128)S(1)} custom-call(f32[108]{0:T(128)} %reshape.23.refs_0_.refs_1_, f32[4,6,4,16,128]{4,3,2,1,0:T(8,128)} %bitcast.11, f32[6,16,16,128]{3,2,1,0:T(8,128)S(1)} %get-tuple-element.72.refs_2_, f32[16,16,128]{2,1,0:T(8,128)} %bitcast.16), custom_call_target="tpu_custom_call" | custom-call | flops 28311552 | bytes 3145728 | tf_op jit(solution)/shard_map/pallas_call | solution.py:617
  87.8 2.0 %all-to-all-done.4.refs_1_ = f32[8,56,128]{2,1,0:T(8,128)S(1)} async-done(((f32[8,56,128]{2,1,0:T(8,128)}), f32[8,56,128]{2,1,0:T(8,128)S(1)}, u32[]{:S(2)}, u32[]{:S(2)}) %all-to-all-start.4) | async-done | bytes 229408 | tf_op jit(solution)/shard_map/all_to_all | solution.py:650
  89.8 1.4 %shard_map.95 = f32[8,56,128]{2,1,0:T(8,128)} custom-call(s32[106]{0:T(128)} %concatenate.3.refs_0_.refs_3_, f32[8,56,128]{2,1,0:T(8,128)S(1)} %all-to-all-done.4.refs_1_), custom_call_target="tpu_custom_call" | custom-call | flops 884736 | bytes 3145728 | tf_op jit(solution)/shard_map/pallas_call | solution.py:617
  91.2 4.0 %all-to-all-start.5 = ((f32[8,56,128]{2,1,0:T(8,128)}), f32[8,56,128]{2,1,0:T(8,128)S(1)}, u32[]{:S(2)}, u32[]{:S(2)}) async-start(f32[8,56,128]{2,1,0:T(8,128)} %shard_map.95), calls=%async_computation.5 | async-start | bytes 458752 | tf_op jit(solution)/shard_map/all_to_all | solution.py:650
  95.2 3.5 %shard_map.96 = (f32[6,16,16,128]{3,2,1,0:T(8,128)}, f32[6,96,128]{2,1,0:T(8,128)S(1)}, f32[6,96,128]{2,1,0:T(8,128)S(1)}) custom-call(s32[106]{0:T(128)} %concatenate.3.refs_0_.refs_3_, f32[108]{0:T(128)} %reshape.23.refs_0_.refs_1_, f32[6,16,16,128]{3,2,1,0:T(8,128)} %get-tuple-element.77.refs_2_, f32[6,96,128]{2,1,0:T(8,128)} %get-tuple-element.78.refs_3_, ...), custom_call_target="tpu_custom_call" | custom-call | flops 14155776 | bytes 3145728 | tf_op jit(solution)/shard_map/pallas_call | solution.py:617
  98.7 4.5 %all-to-all-done.5.refs_6_ = f32[8,56,128]{2,1,0:T(8,128)S(1)} async-done(((f32[8,56,128]{2,1,0:T(8,128)}), f32[8,56,128]{2,1,0:T(8,128)S(1)}, u32[]{:S(2)}, u32[]{:S(2)}) %all-to-all-start.5) | async-done | bytes 229408 | tf_op jit(solution)/shard_map/all_to_all | solution.py:650
  103.2 2.2 %shard_map.97 = f32[6,16,16,128]{3,2,1,0:T(8,128)} custom-call(s32[106]{0:T(128)} %concatenate.3.refs_0_.refs_3_, f32[108]{0:T(128)} %reshape.23.refs_0_.refs_1_, f32[6,16,16,128]{3,2,1,0:T(8,128)S(1)} %shard_map.94.refs_2_, f32[6,96,128]{2,1,0:T(8,128)S(1)} %get-tuple-element.85.refs_3_, f32[6,96,128]{2,1,0:T(8,128)S(1)} %get-tuple-element.86.refs_4_, ...), custom_call_target="tpu_custom_call" | custom-call | flops 884736 | bytes 3145728 | tf_op jit(solution)/shard_map/pallas_call | solution.py:617
  (1 shorter events, 0.0 us)
Async XLA Ops:
  3.2 7.5 %copy-start.2 = (s32[8,6]{1,0:T(8,128)S(1)}, s32[8,6]{1,0:T(8,128)}, u32[]{:S(2)}) copy-start(s32[8,6]{1,0:T(8,128)} %param.12) | copy-start | bytes 580
  3.2 9.5 %copy-start = (f32[1,6,4,16,128]{4,3,2,1,0:T(8,128)S(1)}, f32[1,6,4,16,128]{4,3,2,1,0:T(8,128)}, u32[]{:S(2)}) copy-start(f32[1,6,4,16,128]{4,3,2,1,0:T(8,128)} %param.7) | copy-start | bytes 589828
  3.3 18.5 %all-to-all-start = ((f32[8,80,128]{2,1,0:T(8,128)}), f32[8,80,128]{2,1,0:T(8,128)S(1)}, u32[]{:S(2)}, u32[]{:S(2)}) async-start(f32[8,80,128]{2,1,0:T(8,128)} %get-tuple-element.47), calls=%async_computation | async-start | bytes 655360 | tf_op jit(solution)/shard_map/all_to_all | solution.py:650
  10.7 0.7 copy-start.3
  11.4 0.7 copy-start.4
  23.3 6.0 %copy-start.1 = (f32[3,6,6]{2,1,0:T(8,128)S(1)}, f32[3,6,6]{2,1,0:T(8,128)}, u32[]{:S(2)}) copy-start(f32[3,6,6]{2,1,0:T(8,128)} %param.10) | copy-start | bytes 1300
  23.3 16.8 %all-to-all-start.1 = ((f32[8,80,128]{2,1,0:T(8,128)}), f32[8,80,128]{2,1,0:T(8,128)S(1)}, u32[]{:S(2)}, u32[]{:S(2)}) async-start(f32[8,80,128]{2,1,0:T(8,128)} %shard_map.87), calls=%async_computation.1 | async-start | bytes 655360 | tf_op jit(solution)/shard_map/all_to_all | solution.py:650
  49.3 12.7 %all-to-all-start.2 = ((f32[8,56,128]{2,1,0:T(8,128)}), f32[8,56,128]{2,1,0:T(8,128)S(1)}, u32[]{:S(2)}, u32[]{:S(2)}) async-start(f32[8,56,128]{2,1,0:T(8,128)} %get-tuple-element.57), calls=%async_computation.2 | async-start | bytes 458752 | tf_op jit(solution)/shard_map/all_to_all | solution.py:650
  63.4 11.8 %all-to-all-start.3 = ((f32[8,56,128]{2,1,0:T(8,128)}), f32[8,56,128]{2,1,0:T(8,128)S(1)}, u32[]{:S(2)}, u32[]{:S(2)}) async-start(f32[8,56,128]{2,1,0:T(8,128)} %shard_map.91), calls=%async_computation.3 | async-start | bytes 458752 | tf_op jit(solution)/shard_map/all_to_all | solution.py:650
  78.3 11.5 %all-to-all-start.4 = ((f32[8,56,128]{2,1,0:T(8,128)}), f32[8,56,128]{2,1,0:T(8,128)S(1)}, u32[]{:S(2)}, u32[]{:S(2)}) async-start(f32[8,56,128]{2,1,0:T(8,128)} %get-tuple-element.71), calls=%async_computation.4 | async-start | bytes 458752 | tf_op jit(solution)/shard_map/all_to_all | solution.py:650
  91.2 12.0 %all-to-all-start.5 = ((f32[8,56,128]{2,1,0:T(8,128)}), f32[8,56,128]{2,1,0:T(8,128)S(1)}, u32[]{:S(2)}, u32[]{:S(2)}) async-start(f32[8,56,128]{2,1,0:T(8,128)} %shard_map.95), calls=%async_computation.5 | async-start | bytes 458752 | tf_op jit(solution)/shard_map/all_to_all | solution.py:650

commit v11 on v10

--- a/solution.py
+++ b/solution.py
@@ -80,32 +80,41 @@
             leave(slot)
 
 
+class Links:
+    def __init__(self, owner, neighbours):
+        self.owner, self.neighbours = owner, neighbours
+
+    def target(self, block):
+        return self.owner[block]
+
+    def source(self, block, side):
+        return self.owner[self.neighbours[block, side]]
+
+
 class Table:
     def __init__(self, geo, ref):
         self.ref, self.n = ref, geo.n
 
-    def place(self):
-        return self.ref[0]
-
-    def part(self):
-        return self.ref[1]
-
-    def owner(self, block):
-        return self.ref[2 + block]
-
-    def neighbour(self, block, side):
-        return self.ref[2 + self.n + block * 6 + side]
-
-    def orientation(self, block, side):
-        return self.ref[2 + 7 * self.n + block * 6 + side]
-
-
-def own_codes(geo, table):
-    table = Table(geo, table)
-    block = jnp.int32(0)
-    for index in range(geo.n):
-        block = jnp.where(table.owner(index) == table.place(), index, block)
-    return [table.orientation(block, side) for side in range(6)]
+    def codes(self):
+        return [self.ref[side] for side in range(6)]
+
+    def target(self, block):
+        return self.ref[6 + block]
+
+    def source(self, block, side):
+        return self.ref[6 + self.n + block * 6 + side]
+
+
+def fill_table(geo, place, owner, neighbours, orientation, table):
+    links = Links(owner, neighbours)
+    own = jnp.int32(0)
+    for block in range(geo.n):
+        own = jnp.where(owner[block] == place[0], block, own)
+        table[6 + block] = links.target(block)
+        for side in range(6):
+            table[6 + geo.n + block * 6 + side] = links.source(block, side)
+    for side in range(6):
+        table[side] = orientation[own, side]
 
 
 def flip_rows(values, flag, length):
@@ -370,36 +379,47 @@
     faces[5, :y] = low * rate_faces[5, :y]
 
 
-def route_whole(geo, table, block, arrived, leaving, base):
+def route_whole(geo, links, block, arrived, leaving, base):
     for side in range(6):
-        source = table.owner(table.neighbour(block, side))
+        source = links.source(block, side)
         run, start, far = geo.whole.runs[side], base + geo.whole.starts[side], base + geo.whole.starts[side ^ 1]
-        leaving[table.owner(block), start : start + run] = arrived[source, far : far + run]
+        leaving[links.target(block), start : start + run] = arrived[source, far : far + run]
 
 
 def route_kernel(geo, late, table, arrived, leaving):
-    table = Table(geo, table)
+    links = Table(geo, table)
     for block in range(geo.n):
-        route_whole(geo, table, block, arrived, leaving, 0)
-        late.leave(0, table.owner(block))
-
-
-def route_first_kernel(geo, late, table, arrived, leaving):
-    table = Table(geo, table)
-    x_side = jnp.where(table.part() == geo.parts - 1, 1, 0)
+        route_whole(geo, links, block, arrived, leaving, 0)
+        late.leave(0, links.target(block))
+
+
+def route_first_kernel(geo, late, part, owner, neighbours, arrived, leaving):
+    links = Links(owner, neighbours)
+    x_side = jnp.where(part[0] == geo.parts - 1, 1, 0)
     for block in range(geo.n):
-        route_whole(geo, table, block, arrived, leaving, geo.part.total)
+        route_whole(geo, links, block, arrived, leaving, geo.part.total)
         for index in range(5):
             side, far_index = (x_side, 0) if index == 0 else (index + 1, ((index + 1) ^ 1) - 1)
-            source = table.owner(table.neighbour(block, side))
+            source = links.source(block, side)
             run, start, far = geo.part.runs[index], geo.part.starts[index], geo.part.starts[far_index]
-            leaving[table.owner(block), start : start + run] = arrived[source, far : far + run]
-        late.leave(0, table.owner(block))
+            leaving[links.target(block), start : start + run] = arrived[source, far : far + run]
+        late.leave(0, links.target(block))
+
+
+def first_inner_kernel(
+    geo, late, mats, block, rate, place, owner, neighbours, orientation, result, faces, table, flat, tall
+):
+    fill_table(geo, place, owner, neighbours, orientation, table)
+    for direction in range(3):
+        for row in range(geo.v):
+            for column in range(geo.v):
+                flat[(direction * geo.v + row) * geo.v + column] = mats[direction, row, column]
+    step_inner_kernel(geo, late, flat, block, rate, result, faces, tall)
 
 
 def turn_weights_kernel(geo, late, mats, block, rate, table, buffer, result, ghosts, tall, raw):
     join(geo, buffer, raw, geo.part.total)
-    turn(geo, own_codes(geo, table), raw, ghosts)
+    turn(geo, Table(geo, table).codes(), raw, ghosts)
     step_inner_kernel(geo, late, mats, block, rate, result, tall)
 
 
@@ -486,7 +506,7 @@
     if first:
         new_faces, sent, ghosts, raw, piece = rest
         join_parts(geo, arrived, raw, piece)
-        turn(geo, own_codes(geo, table), raw, ghosts)
+        turn(geo, Table(geo, table).codes(), raw, ghosts)
         late.leave(4)
     else:
         ghosts = arrived
@@ -510,7 +530,7 @@
 
 def adjoint_edge_kernel(geo, last, late, table, mats, inner, faces, weight_faces, *rest):
     v, x, y, z = geo.block
-    codes = own_codes(geo, table)
+    codes = Table(geo, table).codes()
     if last:
         ghosts, weight_buffer, result, raw, weight_ghosts = rest
         join(geo, weight_buffer, raw)
@@ -593,7 +613,7 @@
             copy.wait()
 
     hbm = pl.BlockSpec(memory_space=pltpu.HBM)
-    specs = {"S": SMEM, "V": VMEM, "R": VMEM, "H": hbm, "B": hbm, "D": hbm, "P": hbm}
+    specs = {"S": SMEM, "V": VMEM, "R": VMEM, "H": hbm, "B": hbm, "D": hbm, "P": hbm, "M": SMEM, "I": SMEM}
     scratch_shapes = [pltpu.VMEM(shape, jnp.float32) for shape in scratch]
     scratch_shapes += [pltpu.VMEM(shape, jnp.float32) for _, shape in late_in + late_out]
     if count_in or fetch:
@@ -601,11 +621,12 @@
     if sends:
         scratch_shapes.append(pltpu.SemaphoreType.DMA((sends,)))
     shapes = {"V": jax.ShapeDtypeStruct, "R": pltpu.VMEM, "H": pltpu.HBM, "B": pltpu.HBM, "D": pltpu.HBM}
+    shapes.update({"M": pltpu.SMEM, "I": pltpu.SMEM})
     invoke = pl.pallas_call(
         body,
         in_specs=[specs[kind] for kind, _ in ins],
         out_specs=[specs[kind] for kind, _ in outs],
-        out_shape=[shapes[kind](shape, jnp.float32) for kind, shape in outs],
+        out_shape=[shapes[kind](shape, jnp.int32 if kind == "I" else jnp.float32) for kind, shape in outs],
         scratch_shapes=scratch_shapes,
         input_output_aliases=aliases or {},
         compiler_params=pltpu.CompilerParams(vmem_limit_bytes=VMEM_LIMIT),
@@ -613,7 +634,7 @@
     )
 
     def run(*operands):
-        placed = {"S": pltpu.HBM, "H": pltpu.HBM, "R": pltpu.VMEM, "P": pltpu.HBM}
+        placed = {"M": pltpu.SMEM, "H": pltpu.HBM, "R": pltpu.VMEM, "P": pltpu.HBM}
         return invoke(
             *[
                 pltpu.with_memory_space_constraint(operand, placed[kind]) if kind in placed else operand
@@ -631,9 +652,6 @@
     grads = seeds[0, 0]
     place = lax.axis_index("space").astype(jnp.int32).reshape(1)
     part = lax.axis_index("ckpt").astype(jnp.int32).reshape(1)
-    mats = flux_mats.reshape(-1)
-    table = jnp.concatenate([place, part, owner, neighbours.reshape(-1), orientation.reshape(-1)])
-    fixed = (table, mats)
     work = nvars * nvars * 3 * 4 * cx * cy * cz
     few = work // 16
     whole, both = geo.buffer(geo.whole.total), geo.buffer(geo.part.total + geo.whole.total)
@@ -641,7 +659,7 @@
 
     stored_shape, block, faces_shape = checkpoint.shape[1:], geo.block, geo.faces
     rate_block = cell_rate.shape[1:]
-    scalar, near, kept_near = ("S", None), ("V", None), ("R", None)
+    scalar, near, kept_near, kept_scalar = ("S", None), ("V", None), ("R", None), ("M", None)
 
     def far(shape):
         return ("H", shape)
@@ -650,14 +668,14 @@
         return lax.all_to_all(buffer, "space", 0, 0, tiled=True)
 
     def route(arrived):
-        return call(functools.partial(route_kernel, geo), [scalar, near], [("B", whole)], [], few)(
+        return call(functools.partial(route_kernel, geo), [kept_scalar, near], [("B", whole)], [], few)(
             table, arrived
         )[0]
 
     def adjoint_inner(state, state_kind, grads, grads_kind):
         return call(
             functools.partial(adjoint_inner_kernel, geo),
-            [scalar, state_kind, grads_kind, far(rate_block)],
+            [kept_scalar, state_kind, grads_kind, far(rate_block)],
             [("R", block)],
             [geo.tall] * 2,
             2 * work,
@@ -674,22 +692,23 @@
     arrived = swap(sent)
     state = lax.all_gather(kept, "ckpt", axis=0)
     arrived, state = lax.optimization_barrier((arrived, state))
-    (leaving,) = call(functools.partial(route_first_kernel, geo), [scalar, near], [("B", both)], [], few)(
-        table, arrived
+    (leaving,) = call(functools.partial(route_first_kernel, geo), [scalar] * 3 + [near], [("B", both)], [], few)(
+        part, owner, neighbours, arrived
     )
     first_ghosts = swap(leaving)
-    inner, faces, kept_faces = call(
-        functools.partial(step_inner_kernel, geo),
-        [scalar, far(state.shape), far(rate_block)],
-        [("R", block), ("R", faces_shape), ("D", faces_shape)],
+    inner, faces, kept_faces, table, mats = call(
+        functools.partial(first_inner_kernel, geo),
+        [scalar, far(state.shape), far(rate_block)] + [scalar] * 4,
+        [("R", block), ("R", faces_shape), ("D", faces_shape), ("I", (6 + 7 * count,)), ("M", (3 * nvars * nvars,))],
         [geo.tall],
         work,
-    )(mats, state, rate)
+    )(flux_mats, state, rate, place, owner, neighbours, orientation)
+    fixed = (table, mats)
     first_ghosts, inner, faces = lax.optimization_barrier((first_ghosts, inner, faces))
     gathered = lax.all_gather(first_ghosts[:, :some], "ckpt", axis=0)
     next_state, next_faces, kept_next_faces, sent, ghosts = call(
         functools.partial(step_edge_kernel, geo, True),
-        [scalar] * 2 + [kept_near] * 3 + [near],
+        [kept_scalar] * 2 + [kept_near] * 3 + [near],
         [("R", block), ("R", faces_shape), ("D", faces_shape), ("B", whole), far(faces_shape)],
         [faces_shape, faces_shape[1:]],
         few,
@@ -704,7 +723,7 @@
     next_ghosts = swap(leaving)
     final_inner, weight_ghosts, weight_faces = call(
         functools.partial(turn_weights_kernel, geo),
-        [scalar, kept_near, far(rate_block), scalar, near, ("P", None)],
+        [kept_scalar, kept_near, far(rate_block), kept_scalar, near, ("P", None)],
         [far(block), ("R", faces_shape), ("R", faces_shape)],
         [geo.tall, faces_shape],
         work,
@@ -715,7 +734,7 @@
     )
     grads_now, next_weight_faces, sent, turned = call(
         functools.partial(adjoint_edge_kernel, geo, False),
-        [scalar] * 2 + [kept_near] * 4 + [near, kept_near],
+        [kept_scalar] * 2 + [kept_near] * 4 + [near, kept_near],
         [("R", block), ("R", faces_shape), ("B", whole), far(faces_shape)],
         [faces_shape],
         few,
@@ -730,7 +749,7 @@
     last_ghosts = swap(leaving)
     final, faces, ghosts = call(
         functools.partial(step_edge_kernel, geo, False),
-        [scalar] * 2 + [far(block), far(faces_shape), kept_near, far(faces_shape), ("P", None), ("P", None)],
+        [kept_scalar] * 2 + [far(block), far(faces_shape), kept_near, far(faces_shape), ("P", None), ("P", None)],
         [("V", block), ("R", faces_shape), ("R", faces_shape)],
         [],
         work,
@@ -739,7 +758,7 @@
     last_ghosts, final, faces, ghosts = lax.optimization_barrier((last_ghosts, final, faces, ghosts))
     (adjoint,) = call(
         functools.partial(adjoint_edge_kernel, geo, True),
-        [scalar] * 2 + [kept_near] * 4 + [near],
+        [kept_scalar] * 2 + [kept_near] * 4 + [near],
         [("B", block)],
         [faces_shape] * 2,
         few,

time: 106 us -> 101 us (0.953)
  Pallas kernels: 42.2 us -> 37.2 us
  waiting for transfers between devices: 16.6 us -> 19.1 us
  local copies, waits for them, and re-layouts: 2.66 us -> 0.7 us
    pallas_call x12, Pallas kernels: 42.2 us -> 37.2 us  [run(): invoke(*[pltpu.with_memory_space_constraint(operand, placed[kind]) if kin...]
    all_to_all x6, waiting for transfers between devices: 16.6 us -> 19.1 us  [swap(): return lax.all_to_all(buffer, 'space', 0, 0, tiled=True)]
  transfers between devices with their start and end apart: 6 -> 6, of which waited for: 5 -> 6; matrix products, arithmetic and copies ran while one was open for 1% -> 0% of each run, Pallas kernels for 26% -> 26%
where the time goes in v11:
time: 101 us; the launch traced here: 100 us
  Pallas kernels  37.2 us (37%)
  starting transfers between devices  27 us (27%)
  waiting for transfers between devices  19.1 us (19%)
  blocking collectives  15.2 us (15%)
    pallas_call x12, Pallas kernels, run(): invoke(*[pltpu.with_memory_space_constraint(operand, placed[kind]) if kin...  37.2 us
    all_to_all x6, starting transfers between devices, swap(): return lax.all_to_all(buffer, 'space', 0, 0, tiled=True)  27 us
    all_to_all x6, waiting for transfers between devices, swap(): return lax.all_to_all(buffer, 'space', 0, 0, tiled=True)  19.1 us
    all_gather x1, blocking collectives, on_device(): state = lax.all_gather(kept, 'ckpt', axis=0)  9.05 us
    all_gather x1, blocking collectives, on_device(): gathered = lax.all_gather(first_ghosts[:, :some], 'ckpt', axis=0)  6.15 us
  transfers between devices with their start and end apart: 6, of which 6 were waited for; matrix products, arithmetic and copies ran while one was open for 0% of the time, Pallas kernels for 26%

profile of v11, /device:TPU:0, one launch (start us, length us, event | category | flops | bytes accessed | tf_op | source)
XLA Modules:
  0.0 100.0 jit_solution(7006639936180833536)
XLA Ops:
  0.6 2.6 %shard_map.86 = (f32[6,96,128]{2,1,0:T(8,128)}, f32[6,16,128]{2,1,0:T(8,128)S(1)}, f32[8,80,128]{2,1,0:T(8,128)}) custom-call(s32[1]{0:T(128)} %bitcast.1.refs_0_, f32[6,4,16,128]{3,2,1,0:T(8,128)} %bitcast.20, f32[6,16,16,128]{3,2,1,0:T(8,128)} %bitcast.17, f32[16,16,128]{2,1,0:T(8,128)} %bitcast.12), custom_call_target="tpu_custom_call" | custom-call | flops 884736 | bytes 3145728 | tf_op jit(solution)/shard_map/pallas_call | solution.py:638
  3.2 0.0 copy-start.4
  3.2 7.4 %all-to-all-start = ((f32[8,80,128]{2,1,0:T(8,128)}), f32[8,80,128]{2,1,0:T(8,128)S(1)}, u32[]{:S(2)}, u32[]{:S(2)}) async-start(f32[8,80,128]{2,1,0:T(8,128)} %get-tuple-element.49), calls=%async_computation | async-start | bytes 655360 | tf_op jit(solution)/shard_map/all_to_all | solution.py:668
  10.7 0.0 copy-done.4
  10.7 0.0 copy-start
  10.7 9.0 %all-gather = f32[24,4,16,128]{3,2,1,0:T(8,128)} all-gather(f32[6,4,16,128]{3,2,1,0:T(8,128)S(1)} %bitcast.21), channel_id=2, replica_groups=mesh['ckpt'=4,'space'=8] {'ckpt'}, dimensions={0}, use_global_device_ids=true | all-gather | bytes 983040 | tf_op jit(solution)/shard_map/all_gather | solution.py:693
  19.7 0.0 copy-start.3
  19.7 1.3 %all-to-all-done.refs_3_ = f32[8,80,128]{2,1,0:T(8,128)S(1)} async-done(((f32[8,80,128]{2,1,0:T(8,128)}), f32[8,80,128]{2,1,0:T(8,128)S(1)}, u32[]{:S(2)}, u32[]{:S(2)}) %all-to-all-start) | async-done | bytes 327712 | tf_op jit(solution)/shard_map/all_to_all | solution.py:668
  21.0 0.0 copy-done
  21.0 0.0 copy-done.3
  21.0 1.4 %shard_map.88 = f32[8,80,128]{2,1,0:T(8,128)} custom-call(s32[1]{0:T(128)} %bitcast.1.refs_0_, s32[8]{0:T(128)S(1)} %copy-done.3, s32[8,6]{1,0:T(8,128)S(1)} %copy-done, f32[8,80,128]{2,1,0:T(8,128)S(1)} %all-to-all-done.refs_3_), custom_call_target="tpu_custom_call" | custom-call | flops 884736 | bytes 3145728 | tf_op jit(solution)/shard_map/pallas_call | solution.py:638
  22.4 0.0 copy-start.1
  22.4 5.5 %all-to-all-start.1 = ((f32[8,80,128]{2,1,0:T(8,128)}), f32[8,80,128]{2,1,0:T(8,128)S(1)}, u32[]{:S(2)}, u32[]{:S(2)}) async-start(f32[8,80,128]{2,1,0:T(8,128)} %shard_map.88), calls=%async_computation.1 | async-start | bytes 655360 | tf_op jit(solution)/shard_map/all_to_all | solution.py:668
  27.9 0.0 copy-start.2
  28.0 0.0 copy-done.1
  28.0 0.7 copy-done.2
  28.6 6.5 %shard_map.87 = (f32[6,16,16,128]{3,2,1,0:T(8,128)S(1)}, f32[6,96,128]{2,1,0:T(8,128)S(1)}, f32[6,96,128]{2,1,0:T(8,128)}, s32[62]{0:T(128)S(4)}, f32[108]{0:T(128)S(4)}) custom-call(f32[3,6,6]{2,1,0:T(8,128)S(1)} %copy-done.1, f32[4,6,4,16,128]{4,3,2,1,0:T(8,128)} %bitcast.10, f32[16,16,128]{2,1,0:T(8,128)} %bitcast.13, s32[1]{0:T(128)} %bitcast.5.refs_3_, ...), custom_call_target="tpu_custom_call" | custom-call | flops 14155776 | bytes 3145728 | tf_op jit(solution)/shard_map/pallas_call | solution.py:638
  35.2 3.6 %all-to-all-done.1.refs_4_ = f32[8,80,128]{2,1,0:T(8,128)S(1)} async-done(((f32[8,80,128]{2,1,0:T(8,128)}), f32[8,80,128]{2,1,0:T(8,128)S(1)}, u32[]{:S(2)}, u32[]{:S(2)}) %all-to-all-start.1) | async-done | bytes 327712 | tf_op jit(solution)/shard_map/all_to_all | solution.py:668
  38.7 6.1 %all-gather.1 = f32[32,24,128]{2,1,0:T(8,128)S(1)} all-gather(f32[8,24,128]{2,1,0:T(8,128)S(1)} %slice.3), channel_id=3, replica_groups=mesh['ckpt'=4,'space'=8] {'ckpt'}, dimensions={0}, use_global_device_ids=true | all-gather | bytes 491520 | tf_op jit(solution)/shard_map/all_gather | solution.py:708
  44.9 2.2 %shard_map.89 = (f32[6,16,16,128]{3,2,1,0:T(8,128)S(1)}, f32[6,96,128]{2,1,0:T(8,128)S(1)}, f32[6,96,128]{2,1,0:T(8,128)}, f32[8,56,128]{2,1,0:T(8,128)}, f32[6,96,128]{2,1,0:T(8,128)}) custom-call(s32[62]{0:T(128)S(4)} %get-tuple-element.52.refs_0_.refs_3_, f32[108]{0:T(128)S(4)} %get-tuple-element.53.refs_1_.refs_0_, ...), custom_call_target="tpu_custom_call", output_to_operand_aliasing={{0}: (2, {})} | custom-call | flops 884736 | bytes 3145728 | tf_op jit(solution)/shard_map/pallas_call | solution.py:638
  47.1 3.8 %all-to-all-start.2 = ((f32[8,56,128]{2,1,0:T(8,128)}), f32[8,56,128]{2,1,0:T(8,128)S(1)}, u32[]{:S(2)}, u32[]{:S(2)}) async-start(f32[8,56,128]{2,1,0:T(8,128)} %get-tuple-element.61), calls=%async_computation.2 | async-start | bytes 458752 | tf_op jit(solution)/shard_map/all_to_all | solution.py:668
  50.9 5.5 %shard_map.90.refs_2_ = f32[6,16,16,128]{3,2,1,0:T(8,128)S(1)} custom-call(f32[108]{0:T(128)S(4)} %get-tuple-element.53.refs_1_.refs_0_, f32[6,16,16,128]{3,2,1,0:T(8,128)S(1)} %get-tuple-element.67.refs_1_, f32[6,16,16,128]{3,2,1,0:T(8,128)} %bitcast.18, f32[16,16,128]{2,1,0:T(8,128)} %bitcast.14), custom_call_target="tpu_custom_call" | custom-call | flops 28311552 | bytes 3145728 | tf_op jit(solution)/shard_map/pallas_call | solution.py:638
  56.4 3.5 %all-to-all-done.2.refs_1_ = f32[8,56,128]{2,1,0:T(8,128)S(1)} async-done(((f32[8,56,128]{2,1,0:T(8,128)}), f32[8,56,128]{2,1,0:T(8,128)S(1)}, u32[]{:S(2)}, u32[]{:S(2)}) %all-to-all-start.2) | async-done | bytes 229408 | tf_op jit(solution)/shard_map/all_to_all | solution.py:668
  59.8 0.8 shard_map.91
  60.6 3.4 %all-to-all-start.3 = ((f32[8,56,128]{2,1,0:T(8,128)}), f32[8,56,128]{2,1,0:T(8,128)S(1)}, u32[]{:S(2)}, u32[]{:S(2)}) async-start(f32[8,56,128]{2,1,0:T(8,128)} %shard_map.91), calls=%async_computation.3 | async-start | bytes 458752 | tf_op jit(solution)/shard_map/all_to_all | solution.py:668
  64.0 5.3 %shard_map.92 = (f32[6,16,16,128]{3,2,1,0:T(8,128)}, f32[6,96,128]{2,1,0:T(8,128)S(1)}, f32[6,96,128]{2,1,0:T(8,128)S(1)}) custom-call(f32[108]{0:T(128)S(4)} %get-tuple-element.53.refs_1_.refs_0_, f32[6,16,16,128]{3,2,1,0:T(8,128)S(1)} %get-tuple-element.67.refs_1_, f32[16,16,128]{2,1,0:T(8,128)} %bitcast.15, s32[62]{0:T(128)S(4)} %get-tuple-element.52.refs_0_.refs_3_, ...), custom_call_target="tpu_custom_call" | custom-call | flops 14155776 | bytes 3145728 | tf_op jit(solution)/shard_map/pallas_call | solution.py:638
  69.3 3.1 %all-to-all-done.3.refs_6_ = f32[8,56,128]{2,1,0:T(8,128)S(1)} async-done(((f32[8,56,128]{2,1,0:T(8,128)}), f32[8,56,128]{2,1,0:T(8,128)S(1)}, u32[]{:S(2)}, u32[]{:S(2)}) %all-to-all-start.3) | async-done | bytes 229408 | tf_op jit(solution)/shard_map/all_to_all | solution.py:668
  72.4 2.3 %shard_map.93 = (f32[6,16,16,128]{3,2,1,0:T(8,128)S(1)}, f32[6,96,128]{2,1,0:T(8,128)S(1)}, f32[8,56,128]{2,1,0:T(8,128)}, f32[6,96,128]{2,1,0:T(8,128)}) custom-call(s32[62]{0:T(128)S(4)} %get-tuple-element.52.refs_0_.refs_3_, f32[108]{0:T(128)S(4)} %get-tuple-element.53.refs_1_.refs_0_, ...), custom_call_target="tpu_custom_call", output_to_operand_aliasing={{0}: (2, {})} | custom-call | flops 884736 | bytes 3145728 | tf_op jit(solution)/shard_map/pallas_call | solution.py:638
  74.7 3.4 %all-to-all-start.4 = ((f32[8,56,128]{2,1,0:T(8,128)}), f32[8,56,128]{2,1,0:T(8,128)S(1)}, u32[]{:S(2)}, u32[]{:S(2)}) async-start(f32[8,56,128]{2,1,0:T(8,128)} %get-tuple-element.75), calls=%async_computation.4 | async-start | bytes 458752 | tf_op jit(solution)/shard_map/all_to_all | solution.py:668
  78.2 5.5 %shard_map.94.refs_2_ = f32[6,16,16,128]{3,2,1,0:T(8,128)S(1)} custom-call(f32[108]{0:T(128)S(4)} %get-tuple-element.53.refs_1_.refs_0_, f32[4,6,4,16,128]{4,3,2,1,0:T(8,128)} %bitcast.11, f32[6,16,16,128]{3,2,1,0:T(8,128)S(1)} %get-tuple-element.76.refs_2_, f32[16,16,128]{2,1,0:T(8,128)} %bitcast.16), custom_call_target="tpu_custom_call" | custom-call | flops 28311552 | bytes 3145728 | tf_op jit(solution)/shard_map/pallas_call | solution.py:638
  83.7 2.6 %all-to-all-done.4.refs_1_ = f32[8,56,128]{2,1,0:T(8,128)S(1)} async-done(((f32[8,56,128]{2,1,0:T(8,128)}), f32[8,56,128]{2,1,0:T(8,128)S(1)}, u32[]{:S(2)}, u32[]{:S(2)}) %all-to-all-start.4) | async-done | bytes 229408 | tf_op jit(solution)/shard_map/all_to_all | solution.py:668
  86.3 0.8 shard_map.95
  87.0 3.5 %all-to-all-start.5 = ((f32[8,56,128]{2,1,0:T(8,128)}), f32[8,56,128]{2,1,0:T(8,128)S(1)}, u32[]{:S(2)}, u32[]{:S(2)}) async-start(f32[8,56,128]{2,1,0:T(8,128)} %shard_map.95), calls=%async_computation.5 | async-start | bytes 458752 | tf_op jit(solution)/shard_map/all_to_all | solution.py:668
  90.5 2.8 %shard_map.96 = (f32[6,16,16,128]{3,2,1,0:T(8,128)}, f32[6,96,128]{2,1,0:T(8,128)S(1)}, f32[6,96,128]{2,1,0:T(8,128)S(1)}) custom-call(s32[62]{0:T(128)S(4)} %get-tuple-element.52.refs_0_.refs_3_, f32[108]{0:T(128)S(4)} %get-tuple-element.53.refs_1_.refs_0_, f32[6,16,16,128]{3,2,1,0:T(8,128)} %get-tuple-element.81.refs_2_, ...), custom_call_target="tpu_custom_call" | custom-call | flops 14155776 | bytes 3145728 | tf_op jit(solution)/shard_map/pallas_call | solution.py:638
  93.4 5.2 %all-to-all-done.5.refs_6_ = f32[8,56,128]{2,1,0:T(8,128)S(1)} async-done(((f32[8,56,128]{2,1,0:T(8,128)}), f32[8,56,128]{2,1,0:T(8,128)S(1)}, u32[]{:S(2)}, u32[]{:S(2)}) %all-to-all-start.5) | async-done | bytes 229408 | tf_op jit(solution)/shard_map/all_to_all | solution.py:668
  98.5 1.5 %shard_map.97 = f32[6,16,16,128]{3,2,1,0:T(8,128)} custom-call(s32[62]{0:T(128)S(4)} %get-tuple-element.52.refs_0_.refs_3_, f32[108]{0:T(128)S(4)} %get-tuple-element.53.refs_1_.refs_0_, f32[6,16,16,128]{3,2,1,0:T(8,128)S(1)} %shard_map.94.refs_2_, f32[6,96,128]{2,1,0:T(8,128)S(1)} %get-tuple-element.89.refs_3_, ...), custom_call_target="tpu_custom_call" | custom-call | flops 884736 | bytes 3145728 | tf_op jit(solution)/shard_map/pallas_call | solution.py:638
  (1 shorter events, 0.0 us)
Async XLA Ops:
  3.2 7.4 %copy-start.4 = (f32[1,6,4,16,128]{4,3,2,1,0:T(8,128)S(1)}, f32[1,6,4,16,128]{4,3,2,1,0:T(8,128)}, u32[]{:S(2)}) copy-start(f32[1,6,4,16,128]{4,3,2,1,0:T(8,128)} %param.7) | copy-start | bytes 589828
  3.2 17.7 %all-to-all-start = ((f32[8,80,128]{2,1,0:T(8,128)}), f32[8,80,128]{2,1,0:T(8,128)S(1)}, u32[]{:S(2)}, u32[]{:S(2)}) async-start(f32[8,80,128]{2,1,0:T(8,128)} %get-tuple-element.49), calls=%async_computation | async-start | bytes 655360 | tf_op jit(solution)/shard_map/all_to_all | solution.py:668
  10.7 10.3 %copy-start = (s32[8,6]{1,0:T(8,128)S(1)}, s32[8,6]{1,0:T(8,128)}, u32[]{:S(2)}) copy-start(s32[8,6]{1,0:T(8,128)} %refs_2_.1) | copy-start | bytes 580
  19.7 1.3 %copy-start.3 = (s32[8]{0:T(128)S(1)}, s32[8]{0:T(128)}, u32[]{:S(2)}) copy-start(s32[8]{0:T(128)} %refs_1_.1) | copy-start | bytes 100
  22.4 5.5 %copy-start.1 = (f32[3,6,6]{2,1,0:T(8,128)S(1)}, f32[3,6,6]{2,1,0:T(8,128)}, u32[]{:S(2)}) copy-start(f32[3,6,6]{2,1,0:T(8,128)} %refs_0_.1) | copy-start | bytes 1300
  22.4 16.3 %all-to-all-start.1 = ((f32[8,80,128]{2,1,0:T(8,128)}), f32[8,80,128]{2,1,0:T(8,128)S(1)}, u32[]{:S(2)}, u32[]{:S(2)}) async-start(f32[8,80,128]{2,1,0:T(8,128)} %shard_map.88), calls=%async_computation.1 | async-start | bytes 655360 | tf_op jit(solution)/shard_map/all_to_all | solution.py:668
  27.9 0.7 copy-start.2
  47.1 12.7 %all-to-all-start.2 = ((f32[8,56,128]{2,1,0:T(8,128)}), f32[8,56,128]{2,1,0:T(8,128)S(1)}, u32[]{:S(2)}, u32[]{:S(2)}) async-start(f32[8,56,128]{2,1,0:T(8,128)} %get-tuple-element.61), calls=%async_computation.2 | async-start | bytes 458752 | tf_op jit(solution)/shard_map/all_to_all | solution.py:668
  60.6 11.8 %all-to-all-start.3 = ((f32[8,56,128]{2,1,0:T(8,128)}), f32[8,56,128]{2,1,0:T(8,128)S(1)}, u32[]{:S(2)}, u32[]{:S(2)}) async-start(f32[8,56,128]{2,1,0:T(8,128)} %shard_map.91), calls=%async_computation.3 | async-start | bytes 458752 | tf_op jit(solution)/shard_map/all_to_all | solution.py:668
  74.7 11.5 %all-to-all-start.4 = ((f32[8,56,128]{2,1,0:T(8,128)}), f32[8,56,128]{2,1,0:T(8,128)S(1)}, u32[]{:S(2)}, u32[]{:S(2)}) async-start(f32[8,56,128]{2,1,0:T(8,128)} %get-tuple-element.75), calls=%async_computation.4 | async-start | bytes 458752 | tf_op jit(solution)/shard_map/all_to_all | solution.py:668
  87.0 11.5 %all-to-all-start.5 = ((f32[8,56,128]{2,1,0:T(8,128)}), f32[8,56,128]{2,1,0:T(8,128)S(1)}, u32[]{:S(2)}, u32[]{:S(2)}) async-start(f32[8,56,128]{2,1,0:T(8,128)} %shard_map.95), calls=%async_computation.5 | async-start | bytes 458752 | tf_op jit(solution)/shard_map/all_to_all | solution.py:668

commit v12 on v11

--- a/solution.py
+++ b/solution.py
@@ -80,17 +80,6 @@
             leave(slot)
 
 
-class Links:
-    def __init__(self, owner, neighbours):
-        self.owner, self.neighbours = owner, neighbours
-
-    def target(self, block):
-        return self.owner[block]
-
-    def source(self, block, side):
-        return self.owner[self.neighbours[block, side]]
-
-
 class Table:
     def __init__(self, geo, ref):
         self.ref, self.n = ref, geo.n
@@ -98,21 +87,24 @@
     def codes(self):
         return [self.ref[side] for side in range(6)]
 
+    def part(self):
+        return self.ref[6]
+
     def target(self, block):
-        return self.ref[6 + block]
+        return self.ref[7 + block]
 
     def source(self, block, side):
-        return self.ref[6 + self.n + block * 6 + side]
-
-
-def fill_table(geo, place, owner, neighbours, orientation, table):
-    links = Links(owner, neighbours)
+        return self.ref[7 + self.n + block * 6 + side]
+
+
+def fill_table(geo, place, part, owner, neighbours, orientation, table):
     own = jnp.int32(0)
+    table[6] = part[0]
     for block in range(geo.n):
         own = jnp.where(owner[block] == place[0], block, own)
-        table[6 + block] = links.target(block)
+        table[7 + block] = owner[block]
         for side in range(6):
-            table[6 + geo.n + block * 6 + side] = links.source(block, side)
+            table[7 + geo.n + block * 6 + side] = owner[neighbours[block, side]]
     for side in range(6):
         table[side] = orientation[own, side]
 
@@ -330,10 +322,18 @@
     return out
 
 
-def pack_kernel(geo, late, part, stored, grads, rate, weight_faces, rate_faces, buffer, pieces):
+def pack_kernel(geo, late, part, place, owner, neighbours, orientation, mats, stored, grads, rate, *rest):
+    weight_faces, rate_faces, buffer, table, flat, pieces = rest
     v, x, y, z = geo.block
     depth = geo.depth
-    late.wait(1)
+    for index in range(2, 6):
+        late.wait(index)
+    fill_table(geo, place, part, owner, neighbours, orientation, table)
+    for direction in range(3):
+        for row in range(v):
+            for column in range(v):
+                flat[(direction * v + row) * v + column] = mats[direction, row, column]
+    late.wait(6)
     lane = lax.broadcasted_iota(jnp.int32, (y, z), 1)
     plane = jnp.where(part[0] == geo.parts - 1, depth - 1, 0)
     high = jnp.zeros((y, z), jnp.float32)
@@ -343,16 +343,14 @@
         pieces[1, var * depth : (var + 1) * depth] = stored[var, :, y - 1, :]
         pieces[2, var * depth : (var + 1) * depth] = stored[var, :, 0, :]
         for step in range(depth):
-            place = var * x + part[0] * depth + step
-            tile = stored[var, step]
-            here = lane == place
-            high = jnp.where(here, pltpu.roll(tile, lax.rem(place + 1, z), 1), high)
-            low = jnp.where(here, pltpu.roll(tile, place, 1), low)
+            place_now = var * x + part[0] * depth + step
+            tile = pltpu.roll(stored[var, step], place_now + 1, 1)
+            high = jnp.where(lane == place_now, tile, high)
+            low = jnp.where(lane == place_now + 1, tile, low)
     pieces[3, :y] = high
-    pieces[4, :y] = low
+    pieces[4, :y] = pltpu.roll(low, z - 1, 1)
     cut(geo, geo.part, pieces, buffer, 0)
-    late.wait(2)
-    late.wait(3)
+    late.wait(8)
     rate_faces[0, :y] = rate[x - 1]
     rate_faces[1, :y] = rate[0]
     rate_faces[2, :x] = rate[:, y - 1, :]
@@ -360,23 +358,30 @@
     high, low = take_z_faces(geo, lambda var, plane: rate[plane], 1)
     rate_faces[4, :y] = repeat_lanes(geo, high)
     rate_faces[5, :y] = repeat_lanes(geo, low)
-    late.leave(1)
-    take_weight_faces(geo, grads, rate_faces, weight_faces)
+    take_weight_faces(geo, grads, rate_faces, weight_faces, functools.partial(late.wait, 7))
     late.leave(0)
     cut(geo, geo.whole, weight_faces, buffer, geo.part.total, functools.partial(late.leave, 2))
 
 
-def take_weight_faces(geo, grads, rate_faces, faces):
-    v, x, y, z = geo.block
-    take_xy_faces(geo, grads, faces)
-    for side in range(4):
-        depth = y if side < 2 else x
-        for var in range(v):
-            here = slice(var * depth, (var + 1) * depth)
-            faces[side, here] = faces[side, here] * rate_faces[side, :depth]
-    high, low = take_z_faces(geo, lambda var, plane: grads[var, plane])
+def take_weight_faces(geo, grads, rate_faces, faces, wait=None):
+    v, x, y, z = geo.block
+    lane = lax.broadcasted_iota(jnp.int32, (y, z), 1)
+    high = jnp.zeros((y, z), jnp.float32)
+    low = jnp.zeros((y, z), jnp.float32)
+    for var in range(v):
+        if wait:
+            wait(var)
+        faces[0, var * y : (var + 1) * y] = grads[var, x - 1] * rate_faces[0, :y]
+        faces[1, var * y : (var + 1) * y] = grads[var, 0] * rate_faces[1, :y]
+        faces[2, var * x : (var + 1) * x] = grads[var, :, y - 1, :] * rate_faces[2, :x]
+        faces[3, var * x : (var + 1) * x] = grads[var, :, 0, :] * rate_faces[3, :x]
+        for plane in range(x):
+            place = var * x + plane
+            tile = pltpu.roll(grads[var, plane], place + 1, 1)
+            high = jnp.where(lane == place, tile, high)
+            low = jnp.where(lane == place + 1, tile, low)
     faces[4, :y] = high * rate_faces[4, :y]
-    faces[5, :y] = low * rate_faces[5, :y]
+    faces[5, :y] = pltpu.roll(low, z - 1, 1) * rate_faces[5, :y]
 
 
 def route_whole(geo, links, block, arrived, leaving, base):
@@ -393,9 +398,9 @@
         late.leave(0, links.target(block))
 
 
-def route_first_kernel(geo, late, part, owner, neighbours, arrived, leaving):
-    links = Links(owner, neighbours)
-    x_side = jnp.where(part[0] == geo.parts - 1, 1, 0)
+def route_first_kernel(geo, late, table, arrived, leaving):
+    links = Table(geo, table)
+    x_side = jnp.where(links.part() == geo.parts - 1, 1, 0)
     for block in range(geo.n):
         route_whole(geo, links, block, arrived, leaving, geo.part.total)
         for index in range(5):
@@ -404,17 +409,6 @@
             run, start, far = geo.part.runs[index], geo.part.starts[index], geo.part.starts[far_index]
             leaving[links.target(block), start : start + run] = arrived[source, far : far + run]
         late.leave(0, links.target(block))
-
-
-def first_inner_kernel(
-    geo, late, mats, block, rate, place, owner, neighbours, orientation, result, faces, table, flat, tall
-):
-    fill_table(geo, place, owner, neighbours, orientation, table)
-    for direction in range(3):
-        for row in range(geo.v):
-            for column in range(geo.v):
-                flat[(direction * geo.v + row) * geo.v + column] = mats[direction, row, column]
-    step_inner_kernel(geo, late, flat, block, rate, result, faces, tall)
 
 
 def turn_weights_kernel(geo, late, mats, block, rate, table, buffer, result, ghosts, tall, raw):
@@ -524,8 +518,8 @@
         high, low = take_z_faces(geo, lambda var, plane: result[var, plane])
         new_faces[4, :y] = high
         new_faces[5, :y] = low
+        late.leave(2)
         cut(geo, geo.whole, new_faces, sent, 0, functools.partial(late.leave, 3))
-        late.leave(2)
 
 
 def adjoint_edge_kernel(geo, last, late, table, mats, inner, faces, weight_faces, *rest):
@@ -554,9 +548,9 @@
     def __init__(self, arrivals, departures, sems):
         self.arrivals, self.departures, self.sems, self.started = arrivals, departures, sems, []
 
-    def wait(self, index):
+    def wait(self, index, slot=0):
         if index in self.arrivals:
-            self.arrivals[index].wait()
+            self.arrivals[index][slot].wait()
 
     def leave(self, index, slot=None):
         if index in self.departures:
@@ -569,7 +563,8 @@
 
 
 def call(kernel, ins, outs, scratch, flops, fetch=(), aliases=None):
-    late_in = [(index, shape) for index, (kind, shape) in enumerate(ins) if kind == "H"]
+    late_in = [(index, kind, shape) for index, (kind, shape) in enumerate(ins) if kind in "HCTF"]
+    arrive = sum(shape[0] if kind == "C" else 1 for _, kind, shape in late_in)
     late_out = [(index, shape) for index, (kind, shape) in enumerate(outs) if kind in "HB"]
     count_in, count_out = len(late_in), len(late_out)
     sends = sum(shape[0] if kind == "B" else 1 for kind, shape in outs if kind in "HBD")
@@ -583,10 +578,17 @@
         sems_in = rest[len(scratch) + count_in + count_out] if count_in or fetch else None
         sems_out = rest[-1] if sends else None
         arrivals, departures = {}, {}
-        for slot, (index, _) in enumerate(late_in):
-            copy = pltpu.make_async_copy(given[index], stage[slot], sems_in.at[slot])
-            copy.start()
-            arrivals[index] = copy
+        used = 0
+        for slot, (index, kind, shape) in enumerate(late_in):
+            pairs = [(given[index], stage[slot])]
+            if kind == "C":
+                pairs = [(given[index].at[chunk], stage[slot].at[chunk]) for chunk in range(shape[0])]
+            arrivals[index] = []
+            for source, target in pairs:
+                copy = pltpu.make_async_copy(source, target, sems_in.at[used])
+                copy.start()
+                arrivals[index].append(copy)
+                used += 1
             given[index] = stage[slot]
         for slot, (index, _) in enumerate(late_out):
             departures[index] = (stage[count_in + slot], made[index])
@@ -596,7 +598,7 @@
                 departures[index] = (made[index - 1], made[index])
         fetched = []
         for slot, (source, target) in enumerate(fetch):
-            copy = pltpu.make_async_copy(given[source], made[target], sems_in.at[count_in + slot])
+            copy = pltpu.make_async_copy(given[source], made[target], sems_in.at[arrive + slot])
             copy.start()
             fetched.append(copy)
         late = Late(arrivals, departures, sems_out)
@@ -613,11 +615,15 @@
             copy.wait()
 
     hbm = pl.BlockSpec(memory_space=pltpu.HBM)
-    specs = {"S": SMEM, "V": VMEM, "R": VMEM, "H": hbm, "B": hbm, "D": hbm, "P": hbm, "M": SMEM, "I": SMEM}
+    specs = {"C": hbm, "T": hbm, "F": hbm, "S": SMEM, "V": VMEM, "R": VMEM, "H": hbm, "B": hbm, "D": hbm, "P": hbm, "M": SMEM, "I": SMEM}
     scratch_shapes = [pltpu.VMEM(shape, jnp.float32) for shape in scratch]
-    scratch_shapes += [pltpu.VMEM(shape, jnp.float32) for _, shape in late_in + late_out]
+    stages = {"T": (pltpu.SMEM, jnp.int32), "F": (pltpu.SMEM, jnp.float32)}
+    for _, kind, shape in late_in:
+        memory, dtype = stages.get(kind, (pltpu.VMEM, jnp.float32))
+        scratch_shapes.append(memory(shape, dtype))
+    scratch_shapes += [pltpu.VMEM(shape, jnp.float32) for _, shape in late_out]
     if count_in or fetch:
-        scratch_shapes.append(pltpu.SemaphoreType.DMA((count_in + len(fetch),)))
+        scratch_shapes.append(pltpu.SemaphoreType.DMA((arrive + len(fetch),)))
     if sends:
         scratch_shapes.append(pltpu.SemaphoreType.DMA((sends,)))
     shapes = {"V": jax.ShapeDtypeStruct, "R": pltpu.VMEM, "H": pltpu.HBM, "B": pltpu.HBM, "D": pltpu.HBM}
@@ -634,7 +640,7 @@
     )
 
     def run(*operands):
-        placed = {"M": pltpu.SMEM, "H": pltpu.HBM, "R": pltpu.VMEM, "P": pltpu.HBM}
+        placed = {"C": pltpu.HBM, "T": pltpu.HBM, "F": pltpu.HBM, "M": pltpu.SMEM, "H": pltpu.HBM, "R": pltpu.VMEM, "P": pltpu.HBM}
         return invoke(
             *[
                 pltpu.with_memory_space_constraint(operand, placed[kind]) if kind in placed else operand
@@ -681,29 +687,31 @@
             2 * work,
         )(mats, state, grads, rate)[0]
 
-    weight_faces, rate_faces, sent = call(
+    weight_faces, rate_faces, sent, table, mats = call(
         functools.partial(pack_kernel, geo),
-        [scalar, far(stored_shape), far(block), far(rate_block)],
-        [far(faces_shape), ("R", geo.rate_faces), ("B", both)],
+        [scalar] * 2
+        + [("T", owner.shape), ("T", neighbours.shape), ("T", orientation.shape), ("F", flux_mats.shape)]
+        + [far(stored_shape), ("C", block), far(rate_block)],
+        [far(faces_shape), ("R", geo.rate_faces), ("B", both), ("I", (7 + 7 * count,)), ("M", (3 * nvars * nvars,))],
         [faces_shape],
         few,
-    )(part, checkpoint[0], grads, rate)
+    )(part, place, owner, neighbours, orientation, flux_mats, checkpoint[0], grads, rate)
+    fixed = (table, mats)
     kept, sent = lax.optimization_barrier((checkpoint[0], sent))
     arrived = swap(sent)
     state = lax.all_gather(kept, "ckpt", axis=0)
     arrived, state = lax.optimization_barrier((arrived, state))
-    (leaving,) = call(functools.partial(route_first_kernel, geo), [scalar] * 3 + [near], [("B", both)], [], few)(
-        part, owner, neighbours, arrived
+    (leaving,) = call(functools.partial(route_first_kernel, geo), [kept_scalar, near], [("B", both)], [], few)(
+        table, arrived
     )
     first_ghosts = swap(leaving)
-    inner, faces, kept_faces, table, mats = call(
-        functools.partial(first_inner_kernel, geo),
-        [scalar, far(state.shape), far(rate_block)] + [scalar] * 4,
-        [("R", block), ("R", faces_shape), ("D", faces_shape), ("I", (6 + 7 * count,)), ("M", (3 * nvars * nvars,))],
+    inner, faces, kept_faces = call(
+        functools.partial(step_inner_kernel, geo),
+        [kept_scalar, far(state.shape), far(rate_block)],
+        [("R", block), ("R", faces_shape), ("D", faces_shape)],
         [geo.tall],
         work,
-    )(flux_mats, state, rate, place, owner, neighbours, orientation)
-    fixed = (table, mats)
+    )(mats, state, rate)
     first_ghosts, inner, faces = lax.optimization_barrier((first_ghosts, inner, faces))
     gathered = lax.all_gather(first_ghosts[:, :some], "ckpt", axis=0)
     next_state, next_faces, kept_next_faces, sent, ghosts = call(

time: 101 us -> 100 us (0.990)
  waiting for transfers between devices: 19.1 us -> 20.7 us
    all_to_all x6, waiting for transfers between devices: 19.1 us -> 20.7 us  [swap(): return lax.all_to_all(buffer, 'space', 0, 0, tiled=True)]
  transfers between devices with their start and end apart: 6 -> 6, of which waited for: 6 -> 6; matrix products, arithmetic and copies ran while one was open for 0% -> 0% of each run, Pallas kernels for 26% -> 25%
where the time goes in v12:
time: 100 us; the launch traced here: 99.4 us
  Pallas kernels  36.5 us (36%)
  starting transfers between devices  26.2 us (26%)
  waiting for transfers between devices  20.7 us (21%)
  blocking collectives  15.2 us (15%)
    pallas_call x12, Pallas kernels, run(): invoke(*[pltpu.with_memory_space_constraint(operand, placed[kind]) if kin...  36.5 us
    all_to_all x6, starting transfers between devices, swap(): return lax.all_to_all(buffer, 'space', 0, 0, tiled=True)  26.2 us
    all_to_all x6, waiting for transfers between devices, swap(): return lax.all_to_all(buffer, 'space', 0, 0, tiled=True)  20.7 us
    all_gather x1, blocking collectives, on_device(): state = lax.all_gather(kept, 'ckpt', axis=0)  9.05 us
    all_gather x1, blocking collectives, on_device(): gathered = lax.all_gather(first_ghosts[:, :some], 'ckpt', axis=0)  6.15 us
  transfers between devices with their start and end apart: 6, of which 6 were waited for; matrix products, arithmetic and copies ran while one was open for 0% of the time, Pallas kernels for 25%

profile of v12, /device:TPU:0, one launch (start us, length us, event | category | flops | bytes accessed | tf_op | source)
XLA Modules:
  0.0 99.4 jit_solution(16970769396982212286)
XLA Ops:
  0.6 3.3 %shard_map.86 = (f32[6,96,128]{2,1,0:T(8,128)}, f32[6,16,128]{2,1,0:T(8,128)S(1)}, f32[8,80,128]{2,1,0:T(8,128)}, s32[63]{0:T(128)S(4)}, f32[108]{0:T(128)S(4)}) custom-call(s32[1]{0:T(128)} %bitcast.refs_0_, s32[1]{0:T(128)} %bitcast.1.refs_1_, s32[8]{0:T(128)} %refs_2_.1, s32[8,6]{1,0:T(8,128)} %refs_3_.1, s32[8,6]{1,0:T(8,128)} %refs_4_.1, ...), custom_call_target="tpu_custom_call" | custom-call | flops 884736 | bytes 3145728 | tf_op jit(solution)/shard_map/pallas_call | solution.py:644
  3.9 0.0 copy-start
  4.0 7.4 %all-to-all-start = ((f32[8,80,128]{2,1,0:T(8,128)}), f32[8,80,128]{2,1,0:T(8,128)S(1)}, u32[]{:S(2)}, u32[]{:S(2)}) async-start(f32[8,80,128]{2,1,0:T(8,128)} %get-tuple-element.51), calls=%async_computation | async-start | bytes 655360 | tf_op jit(solution)/shard_map/all_to_all | solution.py:674
  11.4 0.0 copy-done
  11.4 9.0 %all-gather = f32[24,4,16,128]{3,2,1,0:T(8,128)} all-gather(f32[6,4,16,128]{3,2,1,0:T(8,128)S(1)} %bitcast.21), channel_id=2, replica_groups=mesh['ckpt'=4,'space'=8] {'ckpt'}, dimensions={0}, use_global_device_ids=true | all-gather | bytes 983040 | tf_op jit(solution)/shard_map/all_gather | solution.py:702
  20.4 1.3 %all-to-all-done.refs_1_ = f32[8,80,128]{2,1,0:T(8,128)S(1)} async-done(((f32[8,80,128]{2,1,0:T(8,128)}), f32[8,80,128]{2,1,0:T(8,128)S(1)}, u32[]{:S(2)}, u32[]{:S(2)}) %all-to-all-start) | async-done | bytes 327712 | tf_op jit(solution)/shard_map/all_to_all | solution.py:674
  21.7 0.9 shard_map.87
  22.6 4.7 %all-to-all-start.1 = ((f32[8,80,128]{2,1,0:T(8,128)}), f32[8,80,128]{2,1,0:T(8,128)S(1)}, u32[]{:S(2)}, u32[]{:S(2)}) async-start(f32[8,80,128]{2,1,0:T(8,128)} %shard_map.87), calls=%async_computation.1 | async-start | bytes 655360 | tf_op jit(solution)/shard_map/all_to_all | solution.py:674
  27.4 5.6 %shard_map.88 = (f32[6,16,16,128]{3,2,1,0:T(8,128)S(1)}, f32[6,96,128]{2,1,0:T(8,128)S(1)}, f32[6,96,128]{2,1,0:T(8,128)}) custom-call(f32[108]{0:T(128)S(4)} %get-tuple-element.49.refs_0_.refs_1_, f32[4,6,4,16,128]{4,3,2,1,0:T(8,128)} %bitcast.10, f32[16,16,128]{2,1,0:T(8,128)} %bitcast.13), custom_call_target="tpu_custom_call" | custom-call | flops 14155776 | bytes 3145728 | tf_op jit(solution)/shard_map/pallas_call | solution.py:644
  33.0 5.2 %all-to-all-done.1.refs_4_ = f32[8,80,128]{2,1,0:T(8,128)S(1)} async-done(((f32[8,80,128]{2,1,0:T(8,128)}), f32[8,80,128]{2,1,0:T(8,128)S(1)}, u32[]{:S(2)}, u32[]{:S(2)}) %all-to-all-start.1) | async-done | bytes 327712 | tf_op jit(solution)/shard_map/all_to_all | solution.py:674
  38.2 6.1 %all-gather.1 = f32[32,24,128]{2,1,0:T(8,128)S(1)} all-gather(f32[8,24,128]{2,1,0:T(8,128)S(1)} %slice.3), channel_id=3, replica_groups=mesh['ckpt'=4,'space'=8] {'ckpt'}, dimensions={0}, use_global_device_ids=true | all-gather | bytes 491520 | tf_op jit(solution)/shard_map/all_gather | solution.py:716
  44.3 2.2 %shard_map.89 = (f32[6,16,16,128]{3,2,1,0:T(8,128)S(1)}, f32[6,96,128]{2,1,0:T(8,128)S(1)}, f32[6,96,128]{2,1,0:T(8,128)}, f32[8,56,128]{2,1,0:T(8,128)}, f32[6,96,128]{2,1,0:T(8,128)}) custom-call(s32[63]{0:T(128)S(4)} %get-tuple-element.48.refs_0_.refs_3_, f32[108]{0:T(128)S(4)} %get-tuple-element.49.refs_0_.refs_1_, ...), custom_call_target="tpu_custom_call", output_to_operand_aliasing={{0}: (2, {})} | custom-call | flops 884736 | bytes 3145728 | tf_op jit(solution)/shard_map/pallas_call | solution.py:644
  46.6 3.8 %all-to-all-start.2 = ((f32[8,56,128]{2,1,0:T(8,128)}), f32[8,56,128]{2,1,0:T(8,128)S(1)}, u32[]{:S(2)}, u32[]{:S(2)}) async-start(f32[8,56,128]{2,1,0:T(8,128)} %get-tuple-element.61), calls=%async_computation.2 | async-start | bytes 458752 | tf_op jit(solution)/shard_map/all_to_all | solution.py:674
  50.3 5.5 %shard_map.90.refs_2_ = f32[6,16,16,128]{3,2,1,0:T(8,128)S(1)} custom-call(f32[108]{0:T(128)S(4)} %get-tuple-element.49.refs_0_.refs_1_, f32[6,16,16,128]{3,2,1,0:T(8,128)S(1)} %get-tuple-element.67.refs_1_, f32[6,16,16,128]{3,2,1,0:T(8,128)} %bitcast.18, f32[16,16,128]{2,1,0:T(8,128)} %bitcast.14), custom_call_target="tpu_custom_call" | custom-call | flops 28311552 | bytes 3145728 | tf_op jit(solution)/shard_map/pallas_call | solution.py:644
  55.8 3.5 %all-to-all-done.2.refs_1_ = f32[8,56,128]{2,1,0:T(8,128)S(1)} async-done(((f32[8,56,128]{2,1,0:T(8,128)}), f32[8,56,128]{2,1,0:T(8,128)S(1)}, u32[]{:S(2)}, u32[]{:S(2)}) %all-to-all-start.2) | async-done | bytes 229408 | tf_op jit(solution)/shard_map/all_to_all | solution.py:674
  59.3 0.8 shard_map.91
  60.0 3.4 %all-to-all-start.3 = ((f32[8,56,128]{2,1,0:T(8,128)}), f32[8,56,128]{2,1,0:T(8,128)S(1)}, u32[]{:S(2)}, u32[]{:S(2)}) async-start(f32[8,56,128]{2,1,0:T(8,128)} %shard_map.91), calls=%async_computation.3 | async-start | bytes 458752 | tf_op jit(solution)/shard_map/all_to_all | solution.py:674
  63.4 5.3 %shard_map.92 = (f32[6,16,16,128]{3,2,1,0:T(8,128)}, f32[6,96,128]{2,1,0:T(8,128)S(1)}, f32[6,96,128]{2,1,0:T(8,128)S(1)}) custom-call(f32[108]{0:T(128)S(4)} %get-tuple-element.49.refs_0_.refs_1_, f32[6,16,16,128]{3,2,1,0:T(8,128)S(1)} %get-tuple-element.67.refs_1_, f32[16,16,128]{2,1,0:T(8,128)} %bitcast.15, s32[63]{0:T(128)S(4)} %get-tuple-element.48.refs_0_.refs_3_, ...), custom_call_target="tpu_custom_call" | custom-call | flops 14155776 | bytes 3145728 | tf_op jit(solution)/shard_map/pallas_call | solution.py:644
  68.7 3.1 %all-to-all-done.3.refs_6_ = f32[8,56,128]{2,1,0:T(8,128)S(1)} async-done(((f32[8,56,128]{2,1,0:T(8,128)}), f32[8,56,128]{2,1,0:T(8,128)S(1)}, u32[]{:S(2)}, u32[]{:S(2)}) %all-to-all-start.3) | async-done | bytes 229408 | tf_op jit(solution)/shard_map/all_to_all | solution.py:674
  71.8 2.3 %shard_map.93 = (f32[6,16,16,128]{3,2,1,0:T(8,128)S(1)}, f32[6,96,128]{2,1,0:T(8,128)S(1)}, f32[8,56,128]{2,1,0:T(8,128)}, f32[6,96,128]{2,1,0:T(8,128)}) custom-call(s32[63]{0:T(128)S(4)} %get-tuple-element.48.refs_0_.refs_3_, f32[108]{0:T(128)S(4)} %get-tuple-element.49.refs_0_.refs_1_, ...), custom_call_target="tpu_custom_call", output_to_operand_aliasing={{0}: (2, {})} | custom-call | flops 884736 | bytes 3145728 | tf_op jit(solution)/shard_map/pallas_call | solution.py:644
  74.2 3.4 %all-to-all-start.4 = ((f32[8,56,128]{2,1,0:T(8,128)}), f32[8,56,128]{2,1,0:T(8,128)S(1)}, u32[]{:S(2)}, u32[]{:S(2)}) async-start(f32[8,56,128]{2,1,0:T(8,128)} %get-tuple-element.75), calls=%async_computation.4 | async-start | bytes 458752 | tf_op jit(solution)/shard_map/all_to_all | solution.py:674
  77.6 5.5 %shard_map.94.refs_2_ = f32[6,16,16,128]{3,2,1,0:T(8,128)S(1)} custom-call(f32[108]{0:T(128)S(4)} %get-tuple-element.49.refs_0_.refs_1_, f32[4,6,4,16,128]{4,3,2,1,0:T(8,128)} %bitcast.11, f32[6,16,16,128]{3,2,1,0:T(8,128)S(1)} %get-tuple-element.76.refs_2_, f32[16,16,128]{2,1,0:T(8,128)} %bitcast.16), custom_call_target="tpu_custom_call" | custom-call | flops 28311552 | bytes 3145728 | tf_op jit(solution)/shard_map/pallas_call | solution.py:644
  83.1 2.6 %all-to-all-done.4.refs_1_ = f32[8,56,128]{2,1,0:T(8,128)S(1)} async-done(((f32[8,56,128]{2,1,0:T(8,128)}), f32[8,56,128]{2,1,0:T(8,128)S(1)}, u32[]{:S(2)}, u32[]{:S(2)}) %all-to-all-start.4) | async-done | bytes 229408 | tf_op jit(solution)/shard_map/all_to_all | solution.py:674
  85.7 0.8 shard_map.95
  86.5 3.5 %all-to-all-start.5 = ((f32[8,56,128]{2,1,0:T(8,128)}), f32[8,56,128]{2,1,0:T(8,128)S(1)}, u32[]{:S(2)}, u32[]{:S(2)}) async-start(f32[8,56,128]{2,1,0:T(8,128)} %shard_map.95), calls=%async_computation.5 | async-start | bytes 458752 | tf_op jit(solution)/shard_map/all_to_all | solution.py:674
  89.9 2.8 %shard_map.96 = (f32[6,16,16,128]{3,2,1,0:T(8,128)}, f32[6,96,128]{2,1,0:T(8,128)S(1)}, f32[6,96,128]{2,1,0:T(8,128)S(1)}) custom-call(s32[63]{0:T(128)S(4)} %get-tuple-element.48.refs_0_.refs_3_, f32[108]{0:T(128)S(4)} %get-tuple-element.49.refs_0_.refs_1_, f32[6,16,16,128]{3,2,1,0:T(8,128)} %get-tuple-element.81.refs_2_, ...), custom_call_target="tpu_custom_call" | custom-call | flops 14155776 | bytes 3145728 | tf_op jit(solution)/shard_map/pallas_call | solution.py:644
  92.8 5.2 %all-to-all-done.5.refs_6_ = f32[8,56,128]{2,1,0:T(8,128)S(1)} async-done(((f32[8,56,128]{2,1,0:T(8,128)}), f32[8,56,128]{2,1,0:T(8,128)S(1)}, u32[]{:S(2)}, u32[]{:S(2)}) %all-to-all-start.5) | async-done | bytes 229408 | tf_op jit(solution)/shard_map/all_to_all | solution.py:674
  97.9 1.5 %shard_map.97 = f32[6,16,16,128]{3,2,1,0:T(8,128)} custom-call(s32[63]{0:T(128)S(4)} %get-tuple-element.48.refs_0_.refs_3_, f32[108]{0:T(128)S(4)} %get-tuple-element.49.refs_0_.refs_1_, f32[6,16,16,128]{3,2,1,0:T(8,128)S(1)} %shard_map.94.refs_2_, f32[6,96,128]{2,1,0:T(8,128)S(1)} %get-tuple-element.89.refs_3_, ...), custom_call_target="tpu_custom_call" | custom-call | flops 884736 | bytes 3145728 | tf_op jit(solution)/shard_map/pallas_call | solution.py:644
  (1 shorter events, 0.0 us)
Async XLA Ops:
  3.9 7.4 %copy-start = (f32[1,6,4,16,128]{4,3,2,1,0:T(8,128)S(1)}, f32[1,6,4,16,128]{4,3,2,1,0:T(8,128)}, u32[]{:S(2)}) copy-start(f32[1,6,4,16,128]{4,3,2,1,0:T(8,128)} %param.7) | copy-start | bytes 589828
  4.0 17.7 %all-to-all-start = ((f32[8,80,128]{2,1,0:T(8,128)}), f32[8,80,128]{2,1,0:T(8,128)S(1)}, u32[]{:S(2)}, u32[]{:S(2)}) async-start(f32[8,80,128]{2,1,0:T(8,128)} %get-tuple-element.51), calls=%async_computation | async-start | bytes 655360 | tf_op jit(solution)/shard_map/all_to_all | solution.py:674
  22.6 15.5 %all-to-all-start.1 = ((f32[8,80,128]{2,1,0:T(8,128)}), f32[8,80,128]{2,1,0:T(8,128)S(1)}, u32[]{:S(2)}, u32[]{:S(2)}) async-start(f32[8,80,128]{2,1,0:T(8,128)} %shard_map.87), calls=%async_computation.1 | async-start | bytes 655360 | tf_op jit(solution)/shard_map/all_to_all | solution.py:674
  46.6 12.7 %all-to-all-start.2 = ((f32[8,56,128]{2,1,0:T(8,128)}), f32[8,56,128]{2,1,0:T(8,128)S(1)}, u32[]{:S(2)}, u32[]{:S(2)}) async-start(f32[8,56,128]{2,1,0:T(8,128)} %get-tuple-element.61), calls=%async_computation.2 | async-start | bytes 458752 | tf_op jit(solution)/shard_map/all_to_all | solution.py:674
  60.0 11.8 %all-to-all-start.3 = ((f32[8,56,128]{2,1,0:T(8,128)}), f32[8,56,128]{2,1,0:T(8,128)S(1)}, u32[]{:S(2)}, u32[]{:S(2)}) async-start(f32[8,56,128]{2,1,0:T(8,128)} %shard_map.91), calls=%async_computation.3 | async-start | bytes 458752 | tf_op jit(solution)/shard_map/all_to_all | solution.py:674
  74.2 11.5 %all-to-all-start.4 = ((f32[8,56,128]{2,1,0:T(8,128)}), f32[8,56,128]{2,1,0:T(8,128)S(1)}, u32[]{:S(2)}, u32[]{:S(2)}) async-start(f32[8,56,128]{2,1,0:T(8,128)} %get-tuple-element.75), calls=%async_computation.4 | async-start | bytes 458752 | tf_op jit(solution)/shard_map/all_to_all | solution.py:674
  86.5 11.5 %all-to-all-start.5 = ((f32[8,56,128]{2,1,0:T(8,128)}), f32[8,56,128]{2,1,0:T(8,128)S(1)}, u32[]{:S(2)}, u32[]{:S(2)}) async-start(f32[8,56,128]{2,1,0:T(8,128)} %shard_map.95), calls=%async_computation.5 | async-start | bytes 458752 | tf_op jit(solution)/shard_map/all_to_all | solution.py:674

commit v13 on v12

--- a/solution.py
+++ b/solution.py
@@ -31,7 +31,7 @@
         self.depth = cx // parts
         self.rows = [nvars * cy] * 2 + [nvars * cx] * 2 + [cy] * 2
         self.whole = Pieces(self.rows, count)
-        self.part = Pieces([nvars * cy] + [nvars * self.depth] * 2 + [cy] * 2, count)
+        self.part = Pieces([nvars * cy] + [nvars * self.depth] * 2 + [cy], count)
         self.face_rows = -(-max(run * count for run in self.whole.runs) // 8) * 8
         self.block = (nvars, cx, cy, cz)
         self.tall = (nvars, cx, cy + 2 * PAD, cz)
@@ -142,9 +142,14 @@
             raw[side, slot * run : (slot + 1) * run] = buffer[slot, start : start + run]
 
 
-def join_parts(geo, buffer, raw, piece):
+def part_of_lane(geo, rows):
+    lane = lax.broadcasted_iota(jnp.int32, (rows, geo.z), 1)
+    return lax.rem(lane, geo.x) // geo.depth
+
+
+def join_parts(geo, buffer, raw, piece, zpiece):
     for side in range(6):
-        index = 0 if side < 2 else side - 1
+        index = 0 if side < 2 else min(side - 1, 3)
         run, start = geo.part.runs[index], geo.part.starts[index]
         if side < 2:
             part = 0 if side == 0 else geo.parts - 1
@@ -158,11 +163,19 @@
                     row = var * geo.x + part * geo.depth
                     raw[side, row : row + geo.depth] = piece[var * geo.depth : (var + 1) * geo.depth]
         else:
-            for slot in range(geo.n):
-                total = buffer[0, slot, start : start + run]
-                for part in range(1, geo.parts):
-                    total = total + buffer[part, slot, start : start + run]
-                raw[side, slot * run : (slot + 1) * run] = total
+            lanes = part_of_lane(geo, geo.y)
+            total = jnp.zeros((geo.y, geo.z), jnp.float32)
+            for part in range(geo.parts):
+                if side == 4:
+                    for slot in range(geo.n):
+                        zpiece[part, slot * run : (slot + 1) * run] = buffer[part, slot, start : start + run]
+                    rows = zpiece[part, : geo.y]
+                    after = (part + 1) % geo.parts
+                    rows = jnp.where(lanes == after, rows, 0.0)
+                    total = total + pltpu.roll(rows, geo.z - geo.depth if after else geo.x - geo.depth, 1)
+                else:
+                    total = total + jnp.where(lanes == part, zpiece[part, : geo.y], 0.0)
+            raw[side, : geo.y] = total
 
 
 def turn(geo, codes, raw, ghosts):
@@ -326,13 +339,6 @@
     weight_faces, rate_faces, buffer, table, flat, pieces = rest
     v, x, y, z = geo.block
     depth = geo.depth
-    for index in range(2, 6):
-        late.wait(index)
-    fill_table(geo, place, part, owner, neighbours, orientation, table)
-    for direction in range(3):
-        for row in range(v):
-            for column in range(v):
-                flat[(direction * v + row) * v + column] = mats[direction, row, column]
     late.wait(6)
     lane = lax.broadcasted_iota(jnp.int32, (y, z), 1)
     plane = jnp.where(part[0] == geo.parts - 1, depth - 1, 0)
@@ -347,8 +353,8 @@
             tile = pltpu.roll(stored[var, step], place_now + 1, 1)
             high = jnp.where(lane == place_now, tile, high)
             low = jnp.where(lane == place_now + 1, tile, low)
-    pieces[3, :y] = high
-    pieces[4, :y] = pltpu.roll(low, z - 1, 1)
+    shift = jnp.where(part[0] == geo.parts - 1, z - x + depth, depth)
+    pieces[3, :y] = high + pltpu.roll(low, lax.rem(shift + z - 1, z), 1)
     cut(geo, geo.part, pieces, buffer, 0)
     late.wait(8)
     rate_faces[0, :y] = rate[x - 1]
@@ -361,6 +367,13 @@
     take_weight_faces(geo, grads, rate_faces, weight_faces, functools.partial(late.wait, 7))
     late.leave(0)
     cut(geo, geo.whole, weight_faces, buffer, geo.part.total, functools.partial(late.leave, 2))
+    for index in range(2, 6):
+        late.wait(index)
+    fill_table(geo, place, part, owner, neighbours, orientation, table)
+    for direction in range(3):
+        for row in range(v):
+            for column in range(v):
+                flat[(direction * v + row) * v + column] = mats[direction, row, column]
 
 
 def take_weight_faces(geo, grads, rate_faces, faces, wait=None):
@@ -403,11 +416,16 @@
     x_side = jnp.where(links.part() == geo.parts - 1, 1, 0)
     for block in range(geo.n):
         route_whole(geo, links, block, arrived, leaving, geo.part.total)
-        for index in range(5):
-            side, far_index = (x_side, 0) if index == 0 else (index + 1, ((index + 1) ^ 1) - 1)
+        for index in range(3):
+            side, far_index = (x_side, 0) if index == 0 else (index + 1, 3 - index)
             source = links.source(block, side)
             run, start, far = geo.part.runs[index], geo.part.starts[index], geo.part.starts[far_index]
             leaving[links.target(block), start : start + run] = arrived[source, far : far + run]
+        run, start = geo.part.runs[3], geo.part.starts[3]
+        from_low = arrived[links.source(block, 4), start : start + run]
+        from_high = arrived[links.source(block, 5), start : start + run]
+        own_lanes = part_of_lane(geo, run) == links.part()
+        leaving[links.target(block), start : start + run] = jnp.where(own_lanes, from_high, from_low)
         late.leave(0, links.target(block))
 
 
@@ -498,8 +516,8 @@
 def step_edge_kernel(geo, first, late, table, mats, inner, faces, rate_faces, arrived, result, *rest):
     v, x, y, z = geo.block
     if first:
-        new_faces, sent, ghosts, raw, piece = rest
-        join_parts(geo, arrived, raw, piece)
+        new_faces, sent, ghosts, raw, piece, zpiece = rest
+        join_parts(geo, arrived, raw, piece, zpiece)
         turn(geo, Table(geo, table).codes(), raw, ghosts)
         late.leave(4)
     else:
@@ -718,7 +736,7 @@
         functools.partial(step_edge_kernel, geo, True),
         [kept_scalar] * 2 + [kept_near] * 3 + [near],
         [("R", block), ("R", faces_shape), ("D", faces_shape), ("B", whole), far(faces_shape)],
-        [faces_shape, faces_shape[1:]],
+        [faces_shape, faces_shape[1:], (parts,) + faces_shape[1:]],
         few,
         aliases={2: 0},
     )(*fixed, inner, faces, rate_faces, gathered)

time: 100 us -> 99.6 us (level)
  waiting for transfers between devices: 20.7 us -> 19.3 us
    all_to_all x6, waiting for transfers between devices: 20.7 us -> 19.3 us  [swap(): return lax.all_to_all(buffer, 'space', 0, 0, tiled=True)]
where the time goes in v13:
time: 99.6 us; the launch traced here: 98.7 us
  Pallas kernels  36.5 us (37%)
  starting transfers between devices  27 us (27%)
  waiting for transfers between devices  19.3 us (19%)
  blocking collectives  15.2 us (15%)
    pallas_call x12, Pallas kernels, run(): invoke(*[pltpu.with_memory_space_constraint(operand, placed[kind]) if kin...  36.5 us
    all_to_all x6, starting transfers between devices, swap(): return lax.all_to_all(buffer, 'space', 0, 0, tiled=True)  27 us
    all_to_all x6, waiting for transfers between devices, swap(): return lax.all_to_all(buffer, 'space', 0, 0, tiled=True)  19.3 us
    all_gather x1, blocking collectives, on_device(): state = lax.all_gather(kept, 'ckpt', axis=0)  9.05 us
    all_gather x1, blocking collectives, on_device(): gathered = lax.all_gather(first_ghosts[:, :some], 'ckpt', axis=0)  6.15 us
  transfers between devices with their start and end apart: 6, of which 6 were waited for; matrix products, arithmetic and copies ran while one was open for 0% of the time, Pallas kernels for 25%

profile of v13, /device:TPU:0, one launch (start us, length us, event | category | flops | bytes accessed | tf_op | source)
XLA Modules:
  0.0 98.7 jit_solution(9104307536030057788)
XLA Ops:
  0.6 3.3 %shard_map.86 = (f32[6,96,128]{2,1,0:T(8,128)}, f32[6,16,128]{2,1,0:T(8,128)S(1)}, f32[8,72,128]{2,1,0:T(8,128)}, s32[63]{0:T(128)S(4)}, f32[108]{0:T(128)S(4)}) custom-call(s32[1]{0:T(128)} %bitcast.refs_0_, s32[1]{0:T(128)} %bitcast.1.refs_1_, s32[8]{0:T(128)} %refs_2_.1, s32[8,6]{1,0:T(8,128)} %refs_3_.1, s32[8,6]{1,0:T(8,128)} %refs_4_.1, ...), custom_call_target="tpu_custom_call" | custom-call | flops 884736 | bytes 3145728 | tf_op jit(solution)/shard_map/pallas_call | solution.py:662
  3.9 0.0 copy-start
  3.9 7.4 %all-to-all-start = ((f32[8,72,128]{2,1,0:T(8,128)}), f32[8,72,128]{2,1,0:T(8,128)S(1)}, u32[]{:S(2)}, u32[]{:S(2)}) async-start(f32[8,72,128]{2,1,0:T(8,128)} %get-tuple-element.51), calls=%async_computation | async-start | bytes 589824 | tf_op jit(solution)/shard_map/all_to_all | solution.py:692
  11.4 0.0 copy-done
  11.4 9.0 %all-gather = f32[24,4,16,128]{3,2,1,0:T(8,128)} all-gather(f32[6,4,16,128]{3,2,1,0:T(8,128)S(1)} %bitcast.21), channel_id=2, replica_groups=mesh['ckpt'=4,'space'=8] {'ckpt'}, dimensions={0}, use_global_device_ids=true | all-gather | bytes 983040 | tf_op jit(solution)/shard_map/all_gather | solution.py:720
  20.4 0.6 all-to-all-done.refs_1_
  21.0 0.9 shard_map.87
  21.8 5.5 %all-to-all-start.1 = ((f32[8,72,128]{2,1,0:T(8,128)}), f32[8,72,128]{2,1,0:T(8,128)S(1)}, u32[]{:S(2)}, u32[]{:S(2)}) async-start(f32[8,72,128]{2,1,0:T(8,128)} %shard_map.87), calls=%async_computation.1 | async-start | bytes 589824 | tf_op jit(solution)/shard_map/all_to_all | solution.py:692
  27.4 5.6 %shard_map.88 = (f32[6,16,16,128]{3,2,1,0:T(8,128)S(1)}, f32[6,96,128]{2,1,0:T(8,128)S(1)}, f32[6,96,128]{2,1,0:T(8,128)}) custom-call(f32[108]{0:T(128)S(4)} %get-tuple-element.49.refs_0_.refs_1_, f32[4,6,4,16,128]{4,3,2,1,0:T(8,128)} %bitcast.10, f32[16,16,128]{2,1,0:T(8,128)} %bitcast.13), custom_call_target="tpu_custom_call" | custom-call | flops 14155776 | bytes 3145728 | tf_op jit(solution)/shard_map/pallas_call | solution.py:662
  33.0 4.5 %all-to-all-done.1.refs_4_ = f32[8,72,128]{2,1,0:T(8,128)S(1)} async-done(((f32[8,72,128]{2,1,0:T(8,128)}), f32[8,72,128]{2,1,0:T(8,128)S(1)}, u32[]{:S(2)}, u32[]{:S(2)}) %all-to-all-start.1) | async-done | bytes 294944 | tf_op jit(solution)/shard_map/all_to_all | solution.py:692
  37.5 6.1 %all-gather.1 = f32[32,24,128]{2,1,0:T(8,128)S(1)} all-gather(f32[8,24,128]{2,1,0:T(8,128)S(1)} %slice.3), channel_id=3, replica_groups=mesh['ckpt'=4,'space'=8] {'ckpt'}, dimensions={0}, use_global_device_ids=true | all-gather | bytes 491520 | tf_op jit(solution)/shard_map/all_gather | solution.py:734
  43.6 2.2 %shard_map.89 = (f32[6,16,16,128]{3,2,1,0:T(8,128)S(1)}, f32[6,96,128]{2,1,0:T(8,128)S(1)}, f32[6,96,128]{2,1,0:T(8,128)}, f32[8,56,128]{2,1,0:T(8,128)}, f32[6,96,128]{2,1,0:T(8,128)}) custom-call(s32[63]{0:T(128)S(4)} %get-tuple-element.48.refs_0_.refs_3_, f32[108]{0:T(128)S(4)} %get-tuple-element.49.refs_0_.refs_1_, ...), custom_call_target="tpu_custom_call", output_to_operand_aliasing={{0}: (2, {})} | custom-call | flops 884736 | bytes 3145728 | tf_op jit(solution)/shard_map/pallas_call | solution.py:662
  45.8 3.7 %all-to-all-start.2 = ((f32[8,56,128]{2,1,0:T(8,128)}), f32[8,56,128]{2,1,0:T(8,128)S(1)}, u32[]{:S(2)}, u32[]{:S(2)}) async-start(f32[8,56,128]{2,1,0:T(8,128)} %get-tuple-element.61), calls=%async_computation.2 | async-start | bytes 458752 | tf_op jit(solution)/shard_map/all_to_all | solution.py:692
  49.6 5.5 %shard_map.90.refs_2_ = f32[6,16,16,128]{3,2,1,0:T(8,128)S(1)} custom-call(f32[108]{0:T(128)S(4)} %get-tuple-element.49.refs_0_.refs_1_, f32[6,16,16,128]{3,2,1,0:T(8,128)S(1)} %get-tuple-element.67.refs_1_, f32[6,16,16,128]{3,2,1,0:T(8,128)} %bitcast.18, f32[16,16,128]{2,1,0:T(8,128)} %bitcast.14), custom_call_target="tpu_custom_call" | custom-call | flops 28311552 | bytes 3145728 | tf_op jit(solution)/shard_map/pallas_call | solution.py:662
  55.1 3.5 %all-to-all-done.2.refs_1_ = f32[8,56,128]{2,1,0:T(8,128)S(1)} async-done(((f32[8,56,128]{2,1,0:T(8,128)}), f32[8,56,128]{2,1,0:T(8,128)S(1)}, u32[]{:S(2)}, u32[]{:S(2)}) %all-to-all-start.2) | async-done | bytes 229408 | tf_op jit(solution)/shard_map/all_to_all | solution.py:692
  58.5 0.8 shard_map.91
  59.3 3.4 %all-to-all-start.3 = ((f32[8,56,128]{2,1,0:T(8,128)}), f32[8,56,128]{2,1,0:T(8,128)S(1)}, u32[]{:S(2)}, u32[]{:S(2)}) async-start(f32[8,56,128]{2,1,0:T(8,128)} %shard_map.91), calls=%async_computation.3 | async-start | bytes 458752 | tf_op jit(solution)/shard_map/all_to_all | solution.py:692
  62.7 5.3 %shard_map.92 = (f32[6,16,16,128]{3,2,1,0:T(8,128)}, f32[6,96,128]{2,1,0:T(8,128)S(1)}, f32[6,96,128]{2,1,0:T(8,128)S(1)}) custom-call(f32[108]{0:T(128)S(4)} %get-tuple-element.49.refs_0_.refs_1_, f32[6,16,16,128]{3,2,1,0:T(8,128)S(1)} %get-tuple-element.67.refs_1_, f32[16,16,128]{2,1,0:T(8,128)} %bitcast.15, s32[63]{0:T(128)S(4)} %get-tuple-element.48.refs_0_.refs_3_, ...), custom_call_target="tpu_custom_call" | custom-call | flops 14155776 | bytes 3145728 | tf_op jit(solution)/shard_map/pallas_call | solution.py:662
  68.0 3.1 %all-to-all-done.3.refs_6_ = f32[8,56,128]{2,1,0:T(8,128)S(1)} async-done(((f32[8,56,128]{2,1,0:T(8,128)}), f32[8,56,128]{2,1,0:T(8,128)S(1)}, u32[]{:S(2)}, u32[]{:S(2)}) %all-to-all-start.3) | async-done | bytes 229408 | tf_op jit(solution)/shard_map/all_to_all | solution.py:692
  71.1 2.3 %shard_map.93 = (f32[6,16,16,128]{3,2,1,0:T(8,128)S(1)}, f32[6,96,128]{2,1,0:T(8,128)S(1)}, f32[8,56,128]{2,1,0:T(8,128)}, f32[6,96,128]{2,1,0:T(8,128)}) custom-call(s32[63]{0:T(128)S(4)} %get-tuple-element.48.refs_0_.refs_3_, f32[108]{0:T(128)S(4)} %get-tuple-element.49.refs_0_.refs_1_, ...), custom_call_target="tpu_custom_call", output_to_operand_aliasing={{0}: (2, {})} | custom-call | flops 884736 | bytes 3145728 | tf_op jit(solution)/shard_map/pallas_call | solution.py:662
  73.4 3.4 %all-to-all-start.4 = ((f32[8,56,128]{2,1,0:T(8,128)}), f32[8,56,128]{2,1,0:T(8,128)S(1)}, u32[]{:S(2)}, u32[]{:S(2)}) async-start(f32[8,56,128]{2,1,0:T(8,128)} %get-tuple-element.75), calls=%async_computation.4 | async-start | bytes 458752 | tf_op jit(solution)/shard_map/all_to_all | solution.py:692
  76.9 5.5 %shard_map.94.refs_2_ = f32[6,16,16,128]{3,2,1,0:T(8,128)S(1)} custom-call(f32[108]{0:T(128)S(4)} %get-tuple-element.49.refs_0_.refs_1_, f32[4,6,4,16,128]{4,3,2,1,0:T(8,128)} %bitcast.11, f32[6,16,16,128]{3,2,1,0:T(8,128)S(1)} %get-tuple-element.76.refs_2_, f32[16,16,128]{2,1,0:T(8,128)} %bitcast.16), custom_call_target="tpu_custom_call" | custom-call | flops 28311552 | bytes 3145728 | tf_op jit(solution)/shard_map/pallas_call | solution.py:662
  82.4 2.6 %all-to-all-done.4.refs_1_ = f32[8,56,128]{2,1,0:T(8,128)S(1)} async-done(((f32[8,56,128]{2,1,0:T(8,128)}), f32[8,56,128]{2,1,0:T(8,128)S(1)}, u32[]{:S(2)}, u32[]{:S(2)}) %all-to-all-start.4) | async-done | bytes 229408 | tf_op jit(solution)/shard_map/all_to_all | solution.py:692
  85.0 0.8 shard_map.95
  85.7 3.5 %all-to-all-start.5 = ((f32[8,56,128]{2,1,0:T(8,128)}), f32[8,56,128]{2,1,0:T(8,128)S(1)}, u32[]{:S(2)}, u32[]{:S(2)}) async-start(f32[8,56,128]{2,1,0:T(8,128)} %shard_map.95), calls=%async_computation.5 | async-start | bytes 458752 | tf_op jit(solution)/shard_map/all_to_all | solution.py:692
  89.2 2.8 %shard_map.96 = (f32[6,16,16,128]{3,2,1,0:T(8,128)}, f32[6,96,128]{2,1,0:T(8,128)S(1)}, f32[6,96,128]{2,1,0:T(8,128)S(1)}) custom-call(s32[63]{0:T(128)S(4)} %get-tuple-element.48.refs_0_.refs_3_, f32[108]{0:T(128)S(4)} %get-tuple-element.49.refs_0_.refs_1_, f32[6,16,16,128]{3,2,1,0:T(8,128)} %get-tuple-element.81.refs_2_, ...), custom_call_target="tpu_custom_call" | custom-call | flops 14155776 | bytes 3145728 | tf_op jit(solution)/shard_map/pallas_call | solution.py:662
  92.1 5.2 %all-to-all-done.5.refs_6_ = f32[8,56,128]{2,1,0:T(8,128)S(1)} async-done(((f32[8,56,128]{2,1,0:T(8,128)}), f32[8,56,128]{2,1,0:T(8,128)S(1)}, u32[]{:S(2)}, u32[]{:S(2)}) %all-to-all-start.5) | async-done | bytes 229408 | tf_op jit(solution)/shard_map/all_to_all | solution.py:692
  97.2 1.5 %shard_map.97 = f32[6,16,16,128]{3,2,1,0:T(8,128)} custom-call(s32[63]{0:T(128)S(4)} %get-tuple-element.48.refs_0_.refs_3_, f32[108]{0:T(128)S(4)} %get-tuple-element.49.refs_0_.refs_1_, f32[6,16,16,128]{3,2,1,0:T(8,128)S(1)} %shard_map.94.refs_2_, f32[6,96,128]{2,1,0:T(8,128)S(1)} %get-tuple-element.89.refs_3_, ...), custom_call_target="tpu_custom_call" | custom-call | flops 884736 | bytes 3145728 | tf_op jit(solution)/shard_map/pallas_call | solution.py:662
  (1 shorter events, 0.0 us)
Async XLA Ops:
  3.9 7.4 %copy-start = (f32[1,6,4,16,128]{4,3,2,1,0:T(8,128)S(1)}, f32[1,6,4,16,128]{4,3,2,1,0:T(8,128)}, u32[]{:S(2)}) copy-start(f32[1,6,4,16,128]{4,3,2,1,0:T(8,128)} %param.7) | copy-start | bytes 589828
  3.9 17.0 %all-to-all-start = ((f32[8,72,128]{2,1,0:T(8,128)}), f32[8,72,128]{2,1,0:T(8,128)S(1)}, u32[]{:S(2)}, u32[]{:S(2)}) async-start(f32[8,72,128]{2,1,0:T(8,128)} %get-tuple-element.51), calls=%async_computation | async-start | bytes 589824 | tf_op jit(solution)/shard_map/all_to_all | solution.py:692
  21.8 15.6 %all-to-all-start.1 = ((f32[8,72,128]{2,1,0:T(8,128)}), f32[8,72,128]{2,1,0:T(8,128)S(1)}, u32[]{:S(2)}, u32[]{:S(2)}) async-start(f32[8,72,128]{2,1,0:T(8,128)} %shard_map.87), calls=%async_computation.1 | async-start | bytes 589824 | tf_op jit(solution)/shard_map/all_to_all | solution.py:692
  45.8 12.7 %all-to-all-start.2 = ((f32[8,56,128]{2,1,0:T(8,128)}), f32[8,56,128]{2,1,0:T(8,128)S(1)}, u32[]{:S(2)}, u32[]{:S(2)}) async-start(f32[8,56,128]{2,1,0:T(8,128)} %get-tuple-element.61), calls=%async_computation.2 | async-start | bytes 458752 | tf_op jit(solution)/shard_map/all_to_all | solution.py:692
  59.3 11.8 %all-to-all-start.3 = ((f32[8,56,128]{2,1,0:T(8,128)}), f32[8,56,128]{2,1,0:T(8,128)S(1)}, u32[]{:S(2)}, u32[]{:S(2)}) async-start(f32[8,56,128]{2,1,0:T(8,128)} %shard_map.91), calls=%async_computation.3 | async-start | bytes 458752 | tf_op jit(solution)/shard_map/all_to_all | solution.py:692
  73.4 11.5 %all-to-all-start.4 = ((f32[8,56,128]{2,1,0:T(8,128)}), f32[8,56,128]{2,1,0:T(8,128)S(1)}, u32[]{:S(2)}, u32[]{:S(2)}) async-start(f32[8,56,128]{2,1,0:T(8,128)} %get-tuple-element.75), calls=%async_computation.4 | async-start | bytes 458752 | tf_op jit(solution)/shard_map/all_to_all | solution.py:692
  85.7 11.5 %all-to-all-start.5 = ((f32[8,56,128]{2,1,0:T(8,128)}), f32[8,56,128]{2,1,0:T(8,128)S(1)}, u32[]{:S(2)}, u32[]{:S(2)}) async-start(f32[8,56,128]{2,1,0:T(8,128)} %shard_map.95), calls=%async_computation.5 | async-start | bytes 458752 | tf_op jit(solution)/shard_map/all_to_all | solution.py:692

commit v14 on v13

--- a/solution.py
+++ b/solution.py
@@ -81,32 +81,24 @@
 
 
 class Table:
-    def __init__(self, geo, ref):
-        self.ref, self.n = ref, geo.n
+    def __init__(self, geo, refs):
+        self.n = geo.n
+        self.places, self.owner, self.neighbours, self.orientation = refs
 
     def codes(self):
-        return [self.ref[side] for side in range(6)]
+        own = jnp.int32(0)
+        for block in range(self.n):
+            own = jnp.where(self.owner[block] == self.places[0], block, own)
+        return [self.orientation[own, side] for side in range(6)]
 
     def part(self):
-        return self.ref[6]
+        return self.places[1]
 
     def target(self, block):
-        return self.ref[7 + block]
+        return self.owner[block]
 
     def source(self, block, side):
-        return self.ref[7 + self.n + block * 6 + side]
-
-
-def fill_table(geo, place, part, owner, neighbours, orientation, table):
-    own = jnp.int32(0)
-    table[6] = part[0]
-    for block in range(geo.n):
-        own = jnp.where(owner[block] == place[0], block, own)
-        table[7 + block] = owner[block]
-        for side in range(6):
-            table[7 + geo.n + block * 6 + side] = owner[neighbours[block, side]]
-    for side in range(6):
-        table[side] = orientation[own, side]
+        return self.owner[self.neighbours[block, side]]
 
 
 def flip_rows(values, flag, length):
@@ -230,7 +222,7 @@
 
 
 def flux_entry(geo, mats, direction, row, column):
-    return mats[(direction * geo.v + row) * geo.v + column]
+    return mats[direction, row, column]
 
 
 def step_plane(geo, mats, cells, low, high, rate):
@@ -335,11 +327,13 @@
     return out
 
 
-def pack_kernel(geo, late, part, place, owner, neighbours, orientation, mats, stored, grads, rate, *rest):
-    weight_faces, rate_faces, buffer, table, flat, pieces = rest
+def pack_kernel(geo, late, part, place, stored, grads, rate, *rest):
+    weight_faces, rate_faces, buffer, places, pieces = rest
+    places[0] = place[0]
+    places[1] = part[0]
     v, x, y, z = geo.block
     depth = geo.depth
-    late.wait(6)
+    late.wait(2)
     lane = lax.broadcasted_iota(jnp.int32, (y, z), 1)
     plane = jnp.where(part[0] == geo.parts - 1, depth - 1, 0)
     high = jnp.zeros((y, z), jnp.float32)
@@ -356,7 +350,7 @@
     shift = jnp.where(part[0] == geo.parts - 1, z - x + depth, depth)
     pieces[3, :y] = high + pltpu.roll(low, lax.rem(shift + z - 1, z), 1)
     cut(geo, geo.part, pieces, buffer, 0)
-    late.wait(8)
+    late.wait(4)
     rate_faces[0, :y] = rate[x - 1]
     rate_faces[1, :y] = rate[0]
     rate_faces[2, :x] = rate[:, y - 1, :]
@@ -364,16 +358,9 @@
     high, low = take_z_faces(geo, lambda var, plane: rate[plane], 1)
     rate_faces[4, :y] = repeat_lanes(geo, high)
     rate_faces[5, :y] = repeat_lanes(geo, low)
-    take_weight_faces(geo, grads, rate_faces, weight_faces, functools.partial(late.wait, 7))
+    take_weight_faces(geo, grads, rate_faces, weight_faces, functools.partial(late.wait, 3))
     late.leave(0)
     cut(geo, geo.whole, weight_faces, buffer, geo.part.total, functools.partial(late.leave, 2))
-    for index in range(2, 6):
-        late.wait(index)
-    fill_table(geo, place, part, owner, neighbours, orientation, table)
-    for direction in range(3):
-        for row in range(v):
-            for column in range(v):
-                flat[(direction * v + row) * v + column] = mats[direction, row, column]
 
 
 def take_weight_faces(geo, grads, rate_faces, faces, wait=None):
@@ -522,9 +509,9 @@
         late.leave(4)
     else:
         ghosts = arrived
-        late.wait(2)
         late.wait(5)
-    late.wait(3)
+        late.wait(8)
+    late.wait(6)
     values = []
     for side in range(6):
         depth = y if side < 2 or side > 3 else x
@@ -622,9 +609,17 @@
         late = Late(arrivals, departures, sems_out)
         hidden_in = {source for source, _ in fetch}
         hidden_out = {target for _, target in fetch}
+        operands, group = [], []
+        for index, ref in enumerate(given):
+            if ins[index][0] == "G":
+                group.append(ref)
+                if len(group) == 1:
+                    operands.append(group)
+            elif index not in hidden_in:
+                operands.append(ref)
         kernel(
             late,
-            *[ref for index, ref in enumerate(given) if index not in hidden_in],
+            *operands,
             *[ref for index, ref in enumerate(made) if index not in hidden_out and outs[index][0] != "D"],
             *own,
         )
@@ -633,7 +628,7 @@
             copy.wait()
 
     hbm = pl.BlockSpec(memory_space=pltpu.HBM)
-    specs = {"C": hbm, "T": hbm, "F": hbm, "S": SMEM, "V": VMEM, "R": VMEM, "H": hbm, "B": hbm, "D": hbm, "P": hbm, "M": SMEM, "I": SMEM}
+    specs = {"G": SMEM, "C": hbm, "T": hbm, "F": hbm, "S": SMEM, "V": VMEM, "R": VMEM, "H": hbm, "B": hbm, "D": hbm, "P": hbm, "M": SMEM, "I": SMEM}
     scratch_shapes = [pltpu.VMEM(shape, jnp.float32) for shape in scratch]
     stages = {"T": (pltpu.SMEM, jnp.int32), "F": (pltpu.SMEM, jnp.float32)}
     for _, kind, shape in late_in:
@@ -658,7 +653,7 @@
     )
 
     def run(*operands):
-        placed = {"C": pltpu.HBM, "T": pltpu.HBM, "F": pltpu.HBM, "M": pltpu.SMEM, "H": pltpu.HBM, "R": pltpu.VMEM, "P": pltpu.HBM}
+        placed = {"G": pltpu.SMEM, "C": pltpu.HBM, "T": pltpu.HBM, "F": pltpu.HBM, "M": pltpu.SMEM, "H": pltpu.HBM, "R": pltpu.VMEM, "P": pltpu.HBM}
         return invoke(
             *[
                 pltpu.with_memory_space_constraint(operand, placed[kind]) if kind in placed else operand
@@ -685,6 +680,8 @@
     rate_block = cell_rate.shape[1:]
     scalar, near, kept_near, kept_scalar = ("S", None), ("V", None), ("R", None), ("M", None)
 
+    grouped = [("G", None)] * 4
+
     def far(shape):
         return ("H", shape)
 
@@ -692,8 +689,8 @@
         return lax.all_to_all(buffer, "space", 0, 0, tiled=True)
 
     def route(arrived):
-        return call(functools.partial(route_kernel, geo), [kept_scalar, near], [("B", whole)], [], few)(
-            table, arrived
+        return call(functools.partial(route_kernel, geo), grouped + [near], [("B", whole)], [], few)(
+            *table, arrived
         )[0]
 
     def adjoint_inner(state, state_kind, grads, grads_kind):
@@ -705,22 +702,24 @@
             2 * work,
         )(mats, state, grads, rate)[0]
 
-    weight_faces, rate_faces, sent, table, mats = call(
+    links = (owner, neighbours, orientation)
+    weight_faces, rate_faces, sent, *table, mats = call(
         functools.partial(pack_kernel, geo),
-        [scalar] * 2
-        + [("T", owner.shape), ("T", neighbours.shape), ("T", orientation.shape), ("F", flux_mats.shape)]
-        + [far(stored_shape), ("C", block), far(rate_block)],
-        [far(faces_shape), ("R", geo.rate_faces), ("B", both), ("I", (7 + 7 * count,)), ("M", (3 * nvars * nvars,))],
+        [scalar] * 2 + [far(stored_shape), ("C", block), far(rate_block)] + [("P", None)] * 4,
+        [far(faces_shape), ("R", geo.rate_faces), ("B", both), ("I", (2,))]
+        + [("I", link.shape) for link in links]
+        + [("M", flux_mats.shape)],
         [faces_shape],
         few,
-    )(part, place, owner, neighbours, orientation, flux_mats, checkpoint[0], grads, rate)
-    fixed = (table, mats)
+        fetch=((5, 4), (6, 5), (7, 6), (8, 7)),
+    )(part, place, checkpoint[0], grads, rate, *links, flux_mats)
+    fixed = (*table, mats)
     kept, sent = lax.optimization_barrier((checkpoint[0], sent))
     arrived = swap(sent)
     state = lax.all_gather(kept, "ckpt", axis=0)
     arrived, state = lax.optimization_barrier((arrived, state))
-    (leaving,) = call(functools.partial(route_first_kernel, geo), [kept_scalar, near], [("B", both)], [], few)(
-        table, arrived
+    (leaving,) = call(functools.partial(route_first_kernel, geo), grouped + [near], [("B", both)], [], few)(
+        *table, arrived
     )
     first_ghosts = swap(leaving)
     inner, faces, kept_faces = call(
@@ -734,11 +733,11 @@
     gathered = lax.all_gather(first_ghosts[:, :some], "ckpt", axis=0)
     next_state, next_faces, kept_next_faces, sent, ghosts = call(
         functools.partial(step_edge_kernel, geo, True),
-        [kept_scalar] * 2 + [kept_near] * 3 + [near],
+        grouped + [kept_scalar] + [kept_near] * 3 + [near],
         [("R", block), ("R", faces_shape), ("D", faces_shape), ("B", whole), far(faces_shape)],
         [faces_shape, faces_shape[1:], (parts,) + faces_shape[1:]],
         few,
-        aliases={2: 0},
+        aliases={5: 0},
     )(*fixed, inner, faces, rate_faces, gathered)
 
     arrived = swap(sent)
@@ -749,22 +748,22 @@
     next_ghosts = swap(leaving)
     final_inner, weight_ghosts, weight_faces = call(
         functools.partial(turn_weights_kernel, geo),
-        [kept_scalar, kept_near, far(rate_block), kept_scalar, near, ("P", None)],
+        [kept_scalar, kept_near, far(rate_block)] + grouped + [near, ("P", None)],
         [far(block), ("R", faces_shape), ("R", faces_shape)],
         [geo.tall, faces_shape],
         work,
-        fetch=((5, 2),),
-    )(mats, later_state, rate, table, first_ghosts, weight_faces)
+        fetch=((8, 2),),
+    )(mats, later_state, rate, *table, first_ghosts, weight_faces)
     next_ghosts, final_inner, weight_ghosts, weight_faces = lax.optimization_barrier(
         (next_ghosts, final_inner, weight_ghosts, weight_faces)
     )
     grads_now, next_weight_faces, sent, turned = call(
         functools.partial(adjoint_edge_kernel, geo, False),
-        [kept_scalar] * 2 + [kept_near] * 4 + [near, kept_near],
+        grouped + [kept_scalar] + [kept_near] * 4 + [near, kept_near],
         [("R", block), ("R", faces_shape), ("B", whole), far(faces_shape)],
         [faces_shape],
         few,
-        aliases={2: 0},
+        aliases={5: 0},
     )(*fixed, inner, next_faces, weight_faces, rate_faces, next_ghosts, weight_ghosts)
 
     arrived = swap(sent)
@@ -775,16 +774,16 @@
     last_ghosts = swap(leaving)
     final, faces, ghosts = call(
         functools.partial(step_edge_kernel, geo, False),
-        [kept_scalar] * 2 + [far(block), far(faces_shape), kept_near, far(faces_shape), ("P", None), ("P", None)],
+        grouped + [kept_scalar] + [far(block), far(faces_shape), kept_near, far(faces_shape), ("P", None), ("P", None)],
         [("V", block), ("R", faces_shape), ("R", faces_shape)],
         [],
         work,
-        fetch=((6, 1), (7, 2)),
+        fetch=((9, 1), (10, 2)),
     )(*fixed, final_inner, kept_next_faces, rate_faces, turned, kept_faces, ghosts)
     last_ghosts, final, faces, ghosts = lax.optimization_barrier((last_ghosts, final, faces, ghosts))
     (adjoint,) = call(
         functools.partial(adjoint_edge_kernel, geo, True),
-        [kept_scalar] * 2 + [kept_near] * 4 + [near],
+        grouped + [kept_scalar] + [kept_near] * 4 + [near],
         [("B", block)],
         [faces_shape] * 2,
         few,

time: 99.6 us -> 99.6 us (level)
  no operation moved by 1% of the time
where the time goes in v14:
time: 99.6 us; the launch traced here: 98.7 us
  Pallas kernels  36.5 us (37%)
  starting transfers between devices  26.9 us (27%)
  waiting for transfers between devices  19.3 us (19%)
  blocking collectives  15.2 us (15%)
    pallas_call x12, Pallas kernels, run(): invoke(*[pltpu.with_memory_space_constraint(operand, placed[kind]) if kin...  36.5 us
    all_to_all x6, starting transfers between devices, swap(): return lax.all_to_all(buffer, 'space', 0, 0, tiled=True)  26.9 us
    all_to_all x6, waiting for transfers between devices, swap(): return lax.all_to_all(buffer, 'space', 0, 0, tiled=True)  19.3 us
    all_gather x1, blocking collectives, on_device(): state = lax.all_gather(kept, 'ckpt', axis=0)  9.05 us
    all_gather x1, blocking collectives, on_device(): gathered = lax.all_gather(first_ghosts[:, :some], 'ckpt', axis=0)  6.15 us
  transfers between devices with their start and end apart: 6, of which 6 were waited for; matrix products, arithmetic and copies ran while one was open for 0% of the time, Pallas kernels for 25%

profile of v14, /device:TPU:0, one launch (start us, length us, event | category | flops | bytes accessed | tf_op | source)
XLA Modules:
  0.0 98.7 jit_solution(46135624970969617)
XLA Ops:
  0.6 3.3 %shard_map.86 = (f32[6,96,128]{2,1,0:T(8,128)}, f32[6,16,128]{2,1,0:T(8,128)S(1)}, f32[8,72,128]{2,1,0:T(8,128)}, s32[2]{0:T(128)S(4)}, s32[8]{0:T(128)S(4)}, /*...) custom-call(s32[1]{0:T(128)} %bitcast.refs_0_, s32[1]{0:T(128)} %bitcast.1.refs_1_, ...), custom_call_target="tpu_custom_call" | custom-call | flops 884736 | bytes 3145728 | tf_op jit(solution)/shard_map/pallas_call | solution.py:657
  3.9 0.0 copy-start
  3.9 7.4 %all-to-all-start = ((f32[8,72,128]{2,1,0:T(8,128)}), f32[8,72,128]{2,1,0:T(8,128)S(1)}, u32[]{:S(2)}, u32[]{:S(2)}) async-start(f32[8,72,128]{2,1,0:T(8,128)} %get-tuple-element.57), calls=%async_computation | async-start | bytes 589824 | tf_op jit(solution)/shard_map/all_to_all | solution.py:689
  11.4 0.0 copy-done
  11.4 9.0 %all-gather = f32[24,4,16,128]{3,2,1,0:T(8,128)} all-gather(f32[6,4,16,128]{3,2,1,0:T(8,128)S(1)} %bitcast.21), channel_id=2, replica_groups=mesh['ckpt'=4,'space'=8] {'ckpt'}, dimensions={0}, use_global_device_ids=true | all-gather | bytes 983040 | tf_op jit(solution)/shard_map/all_gather | solution.py:719
  20.4 0.6 all-to-all-done.refs_4_
  21.0 1.0 shard_map.87
  21.9 5.4 %all-to-all-start.1 = ((f32[8,72,128]{2,1,0:T(8,128)}), f32[8,72,128]{2,1,0:T(8,128)S(1)}, u32[]{:S(2)}, u32[]{:S(2)}) async-start(f32[8,72,128]{2,1,0:T(8,128)} %shard_map.87), calls=%async_computation.1 | async-start | bytes 589824 | tf_op jit(solution)/shard_map/all_to_all | solution.py:689
  27.4 5.6 %shard_map.88 = (f32[6,16,16,128]{3,2,1,0:T(8,128)S(1)}, f32[6,96,128]{2,1,0:T(8,128)S(1)}, f32[6,96,128]{2,1,0:T(8,128)}) custom-call(f32[3,6,6]{2,1,0:T(8,128)S(4)} %get-tuple-element.55.refs_0_.refs_4_, f32[4,6,4,16,128]{4,3,2,1,0:T(8,128)} %bitcast.10, f32[16,16,128]{2,1,0:T(8,128)} %bitcast.13), custom_call_target="tpu_custom_call" | custom-call | flops 14155776 | bytes 3145728 | tf_op jit(solution)/shard_map/pallas_call | solution.py:657
  33.0 4.5 %all-to-all-done.1.refs_7_ = f32[8,72,128]{2,1,0:T(8,128)S(1)} async-done(((f32[8,72,128]{2,1,0:T(8,128)}), f32[8,72,128]{2,1,0:T(8,128)S(1)}, u32[]{:S(2)}, u32[]{:S(2)}) %all-to-all-start.1) | async-done | bytes 294944 | tf_op jit(solution)/shard_map/all_to_all | solution.py:689
  37.5 6.1 %all-gather.1 = f32[32,24,128]{2,1,0:T(8,128)S(1)} all-gather(f32[8,24,128]{2,1,0:T(8,128)S(1)} %slice.3), channel_id=3, replica_groups=mesh['ckpt'=4,'space'=8] {'ckpt'}, dimensions={0}, use_global_device_ids=true | all-gather | bytes 491520 | tf_op jit(solution)/shard_map/all_gather | solution.py:733
  43.6 2.3 %shard_map.89 = (f32[6,16,16,128]{3,2,1,0:T(8,128)S(1)}, f32[6,96,128]{2,1,0:T(8,128)S(1)}, f32[6,96,128]{2,1,0:T(8,128)}, f32[8,56,128]{2,1,0:T(8,128)}, f32[6,96,128]{2,1,0:T(8,128)}) custom-call(s32[2]{0:T(128)S(4)} %get-tuple-element.51.refs_0_.refs_3_, s32[8]{0:T(128)S(4)} %get-tuple-element.52.refs_1_.refs_4_, ...), custom_call_target="tpu_custom_call", output_to_operand_aliasing={{0}: (5, {})} | custom-call | flops 884736 | bytes 3145728 | tf_op jit(solution)/shard_map/pallas_call | solution.py:657
  45.9 3.7 %all-to-all-start.2 = ((f32[8,56,128]{2,1,0:T(8,128)}), f32[8,56,128]{2,1,0:T(8,128)S(1)}, u32[]{:S(2)}, u32[]{:S(2)}) async-start(f32[8,56,128]{2,1,0:T(8,128)} %get-tuple-element.67), calls=%async_computation.2 | async-start | bytes 458752 | tf_op jit(solution)/shard_map/all_to_all | solution.py:689
  49.7 5.5 %shard_map.90.refs_5_ = f32[6,16,16,128]{3,2,1,0:T(8,128)S(1)} custom-call(f32[3,6,6]{2,1,0:T(8,128)S(4)} %get-tuple-element.55.refs_0_.refs_4_, f32[6,16,16,128]{3,2,1,0:T(8,128)S(1)} %get-tuple-element.73.refs_1_, f32[6,16,16,128]{3,2,1,0:T(8,128)} %bitcast.18, f32[16,16,128]{2,1,0:T(8,128)} %bitcast.14), custom_call_target="tpu_custom_call" | custom-call | flops 28311552 | bytes 3145728 | tf_op jit(solution)/shard_map/pallas_call | solution.py:657
  55.2 3.5 %all-to-all-done.2.refs_4_ = f32[8,56,128]{2,1,0:T(8,128)S(1)} async-done(((f32[8,56,128]{2,1,0:T(8,128)}), f32[8,56,128]{2,1,0:T(8,128)S(1)}, u32[]{:S(2)}, u32[]{:S(2)}) %all-to-all-start.2) | async-done | bytes 229408 | tf_op jit(solution)/shard_map/all_to_all | solution.py:689
  58.6 0.8 shard_map.91
  59.4 3.4 %all-to-all-start.3 = ((f32[8,56,128]{2,1,0:T(8,128)}), f32[8,56,128]{2,1,0:T(8,128)S(1)}, u32[]{:S(2)}, u32[]{:S(2)}) async-start(f32[8,56,128]{2,1,0:T(8,128)} %shard_map.91), calls=%async_computation.3 | async-start | bytes 458752 | tf_op jit(solution)/shard_map/all_to_all | solution.py:689
  62.8 5.3 %shard_map.92 = (f32[6,16,16,128]{3,2,1,0:T(8,128)}, f32[6,96,128]{2,1,0:T(8,128)S(1)}, f32[6,96,128]{2,1,0:T(8,128)S(1)}) custom-call(f32[3,6,6]{2,1,0:T(8,128)S(4)} %get-tuple-element.55.refs_0_.refs_4_, f32[6,16,16,128]{3,2,1,0:T(8,128)S(1)} %get-tuple-element.73.refs_1_, f32[16,16,128]{2,1,0:T(8,128)} %bitcast.15, ...), custom_call_target="tpu_custom_call" | custom-call | flops 14155776 | bytes 3145728 | tf_op jit(solution)/shard_map/pallas_call | solution.py:657
  68.1 3.1 %all-to-all-done.3.refs_9_ = f32[8,56,128]{2,1,0:T(8,128)S(1)} async-done(((f32[8,56,128]{2,1,0:T(8,128)}), f32[8,56,128]{2,1,0:T(8,128)S(1)}, u32[]{:S(2)}, u32[]{:S(2)}) %all-to-all-start.3) | async-done | bytes 229408 | tf_op jit(solution)/shard_map/all_to_all | solution.py:689
  71.2 2.3 %shard_map.93 = (f32[6,16,16,128]{3,2,1,0:T(8,128)S(1)}, f32[6,96,128]{2,1,0:T(8,128)S(1)}, f32[8,56,128]{2,1,0:T(8,128)}, f32[6,96,128]{2,1,0:T(8,128)}) custom-call(s32[2]{0:T(128)S(4)} %get-tuple-element.51.refs_0_.refs_3_, s32[8]{0:T(128)S(4)} %get-tuple-element.52.refs_1_.refs_4_, ...), custom_call_target="tpu_custom_call", output_to_operand_aliasing={{0}: (5, {})} | custom-call | flops 884736 | bytes 3145728 | tf_op jit(solution)/shard_map/pallas_call | solution.py:657
  73.5 3.4 %all-to-all-start.4 = ((f32[8,56,128]{2,1,0:T(8,128)}), f32[8,56,128]{2,1,0:T(8,128)S(1)}, u32[]{:S(2)}, u32[]{:S(2)}) async-start(f32[8,56,128]{2,1,0:T(8,128)} %get-tuple-element.81), calls=%async_computation.4 | async-start | bytes 458752 | tf_op jit(solution)/shard_map/all_to_all | solution.py:689
  76.9 5.5 %shard_map.94.refs_5_ = f32[6,16,16,128]{3,2,1,0:T(8,128)S(1)} custom-call(f32[3,6,6]{2,1,0:T(8,128)S(4)} %get-tuple-element.55.refs_0_.refs_4_, f32[4,6,4,16,128]{4,3,2,1,0:T(8,128)} %bitcast.11, f32[6,16,16,128]{3,2,1,0:T(8,128)S(1)} %get-tuple-element.82.refs_2_, f32[16,16,128]{2,1,0:T(8,128)} %bitcast.16), custom_call_target="tpu_custom_call" | custom-call | flops 28311552 | bytes 3145728 | tf_op jit(solution)/shard_map/pallas_call | solution.py:657
  82.4 2.6 %all-to-all-done.4.refs_4_ = f32[8,56,128]{2,1,0:T(8,128)S(1)} async-done(((f32[8,56,128]{2,1,0:T(8,128)}), f32[8,56,128]{2,1,0:T(8,128)S(1)}, u32[]{:S(2)}, u32[]{:S(2)}) %all-to-all-start.4) | async-done | bytes 229408 | tf_op jit(solution)/shard_map/all_to_all | solution.py:689
  85.0 0.8 shard_map.95
  85.8 3.5 %all-to-all-start.5 = ((f32[8,56,128]{2,1,0:T(8,128)}), f32[8,56,128]{2,1,0:T(8,128)S(1)}, u32[]{:S(2)}, u32[]{:S(2)}) async-start(f32[8,56,128]{2,1,0:T(8,128)} %shard_map.95), calls=%async_computation.5 | async-start | bytes 458752 | tf_op jit(solution)/shard_map/all_to_all | solution.py:689
  89.2 2.8 %shard_map.96 = (f32[6,16,16,128]{3,2,1,0:T(8,128)}, f32[6,96,128]{2,1,0:T(8,128)S(1)}, f32[6,96,128]{2,1,0:T(8,128)S(1)}) custom-call(s32[2]{0:T(128)S(4)} %get-tuple-element.51.refs_0_.refs_3_, s32[8]{0:T(128)S(4)} %get-tuple-element.52.refs_1_.refs_4_, s32[8,6]{1,0:T(8,128)S(4)} %get-tuple-element.53.refs_2_.refs_5_, ...), custom_call_target="tpu_custom_call" | custom-call | flops 14155776 | bytes 3145728 | tf_op jit(solution)/shard_map/pallas_call | solution.py:657
  92.1 5.2 %all-to-all-done.5.refs_9_ = f32[8,56,128]{2,1,0:T(8,128)S(1)} async-done(((f32[8,56,128]{2,1,0:T(8,128)}), f32[8,56,128]{2,1,0:T(8,128)S(1)}, u32[]{:S(2)}, u32[]{:S(2)}) %all-to-all-start.5) | async-done | bytes 229408 | tf_op jit(solution)/shard_map/all_to_all | solution.py:689
  97.2 1.5 %shard_map.97 = f32[6,16,16,128]{3,2,1,0:T(8,128)} custom-call(s32[2]{0:T(128)S(4)} %get-tuple-element.51.refs_0_.refs_3_, s32[8]{0:T(128)S(4)} %get-tuple-element.52.refs_1_.refs_4_, s32[8,6]{1,0:T(8,128)S(4)} %get-tuple-element.53.refs_2_.refs_5_, s32[8,6]{1,0:T(8,128)S(4)} %get-tuple-element.54.refs_3_.refs_6_, ...), custom_call_target="tpu_custom_call" | custom-call | flops 884736 | bytes 3145728 | tf_op jit(solution)/shard_map/pallas_call | solution.py:657
  (1 shorter events, 0.0 us)
Async XLA Ops:
  3.9 7.4 %copy-start = (f32[1,6,4,16,128]{4,3,2,1,0:T(8,128)S(1)}, f32[1,6,4,16,128]{4,3,2,1,0:T(8,128)}, u32[]{:S(2)}) copy-start(f32[1,6,4,16,128]{4,3,2,1,0:T(8,128)} %param.7) | copy-start | bytes 589828
  3.9 17.0 %all-to-all-start = ((f32[8,72,128]{2,1,0:T(8,128)}), f32[8,72,128]{2,1,0:T(8,128)S(1)}, u32[]{:S(2)}, u32[]{:S(2)}) async-start(f32[8,72,128]{2,1,0:T(8,128)} %get-tuple-element.57), calls=%async_computation | async-start | bytes 589824 | tf_op jit(solution)/shard_map/all_to_all | solution.py:689
  21.9 15.5 %all-to-all-start.1 = ((f32[8,72,128]{2,1,0:T(8,128)}), f32[8,72,128]{2,1,0:T(8,128)S(1)}, u32[]{:S(2)}, u32[]{:S(2)}) async-start(f32[8,72,128]{2,1,0:T(8,128)} %shard_map.87), calls=%async_computation.1 | async-start | bytes 589824 | tf_op jit(solution)/shard_map/all_to_all | solution.py:689
  45.9 12.7 %all-to-all-start.2 = ((f32[8,56,128]{2,1,0:T(8,128)}), f32[8,56,128]{2,1,0:T(8,128)S(1)}, u32[]{:S(2)}, u32[]{:S(2)}) async-start(f32[8,56,128]{2,1,0:T(8,128)} %get-tuple-element.67), calls=%async_computation.2 | async-start | bytes 458752 | tf_op jit(solution)/shard_map/all_to_all | solution.py:689
  59.4 11.8 %all-to-all-start.3 = ((f32[8,56,128]{2,1,0:T(8,128)}), f32[8,56,128]{2,1,0:T(8,128)S(1)}, u32[]{:S(2)}, u32[]{:S(2)}) async-start(f32[8,56,128]{2,1,0:T(8,128)} %shard_map.91), calls=%async_computation.3 | async-start | bytes 458752 | tf_op jit(solution)/shard_map/all_to_all | solution.py:689
  73.5 11.5 %all-to-all-start.4 = ((f32[8,56,128]{2,1,0:T(8,128)}), f32[8,56,128]{2,1,0:T(8,128)S(1)}, u32[]{:S(2)}, u32[]{:S(2)}) async-start(f32[8,56,128]{2,1,0:T(8,128)} %get-tuple-element.81), calls=%async_computation.4 | async-start | bytes 458752 | tf_op jit(solution)/shard_map/all_to_all | solution.py:689
  85.8 11.5 %all-to-all-start.5 = ((f32[8,56,128]{2,1,0:T(8,128)}), f32[8,56,128]{2,1,0:T(8,128)S(1)}, u32[]{:S(2)}, u32[]{:S(2)}) async-start(f32[8,56,128]{2,1,0:T(8,128)} %shard_map.95), calls=%async_computation.5 | async-start | bytes 458752 | tf_op jit(solution)/shard_map/all_to_all | solution.py:689

commit v15 on v14

--- a/solution.py
+++ b/solution.py
@@ -350,6 +350,7 @@
     shift = jnp.where(part[0] == geo.parts - 1, z - x + depth, depth)
     pieces[3, :y] = high + pltpu.roll(low, lax.rem(shift + z - 1, z), 1)
     cut(geo, geo.part, pieces, buffer, 0)
+    late.wait(3)
     late.wait(4)
     rate_faces[0, :y] = rate[x - 1]
     rate_faces[1, :y] = rate[0]
@@ -358,19 +359,17 @@
     high, low = take_z_faces(geo, lambda var, plane: rate[plane], 1)
     rate_faces[4, :y] = repeat_lanes(geo, high)
     rate_faces[5, :y] = repeat_lanes(geo, low)
-    take_weight_faces(geo, grads, rate_faces, weight_faces, functools.partial(late.wait, 3))
+    take_weight_faces(geo, grads, rate_faces, weight_faces)
     late.leave(0)
     cut(geo, geo.whole, weight_faces, buffer, geo.part.total, functools.partial(late.leave, 2))
 
 
-def take_weight_faces(geo, grads, rate_faces, faces, wait=None):
+def take_weight_faces(geo, grads, rate_faces, faces):
     v, x, y, z = geo.block
     lane = lax.broadcasted_iota(jnp.int32, (y, z), 1)
     high = jnp.zeros((y, z), jnp.float32)
     low = jnp.zeros((y, z), jnp.float32)
     for var in range(v):
-        if wait:
-            wait(var)
         faces[0, var * y : (var + 1) * y] = grads[var, x - 1] * rate_faces[0, :y]
         faces[1, var * y : (var + 1) * y] = grads[var, 0] * rate_faces[1, :y]
         faces[2, var * x : (var + 1) * x] = grads[var, :, y - 1, :] * rate_faces[2, :x]
@@ -553,9 +552,9 @@
     def __init__(self, arrivals, departures, sems):
         self.arrivals, self.departures, self.sems, self.started = arrivals, departures, sems, []
 
-    def wait(self, index, slot=0):
+    def wait(self, index):
         if index in self.arrivals:
-            self.arrivals[index][slot].wait()
+            self.arrivals[index].wait()
 
     def leave(self, index, slot=None):
         if index in self.departures:
@@ -568,8 +567,7 @@
 
 
 def call(kernel, ins, outs, scratch, flops, fetch=(), aliases=None):
-    late_in = [(index, kind, shape) for index, (kind, shape) in enumerate(ins) if kind in "HCTF"]
-    arrive = sum(shape[0] if kind == "C" else 1 for _, kind, shape in late_in)
+    late_in = [(index, shape) for index, (kind, shape) in enumerate(ins) if kind == "H"]
     late_out = [(index, shape) for index, (kind, shape) in enumerate(outs) if kind in "HB"]
     count_in, count_out = len(late_in), len(late_out)
     sends = sum(shape[0] if kind == "B" else 1 for kind, shape in outs if kind in "HBD")
@@ -583,17 +581,10 @@
         sems_in = rest[len(scratch) + count_in + count_out] if count_in or fetch else None
         sems_out = rest[-1] if sends else None
         arrivals, departures = {}, {}
-        used = 0
-        for slot, (index, kind, shape) in enumerate(late_in):
-            pairs = [(given[index], stage[slot])]
-            if kind == "C":
-                pairs = [(given[index].at[chunk], stage[slot].at[chunk]) for chunk in range(shape[0])]
-            arrivals[index] = []
-            for source, target in pairs:
-                copy = pltpu.make_async_copy(source, target, sems_in.at[used])
-                copy.start()
-                arrivals[index].append(copy)
-                used += 1
+        for slot, (index, _) in enumerate(late_in):
+            copy = pltpu.make_async_copy(given[index], stage[slot], sems_in.at[slot])
+            copy.start()
+            arrivals[index] = copy
             given[index] = stage[slot]
         for slot, (index, _) in enumerate(late_out):
             departures[index] = (stage[count_in + slot], made[index])
@@ -603,7 +594,7 @@
                 departures[index] = (made[index - 1], made[index])
         fetched = []
         for slot, (source, target) in enumerate(fetch):
-            copy = pltpu.make_async_copy(given[source], made[target], sems_in.at[arrive + slot])
+            copy = pltpu.make_async_copy(given[source], made[target], sems_in.at[count_in + slot])
             copy.start()
             fetched.append(copy)
         late = Late(arrivals, departures, sems_out)
@@ -628,15 +619,11 @@
             copy.wait()
 
     hbm = pl.BlockSpec(memory_space=pltpu.HBM)
-    specs = {"G": SMEM, "C": hbm, "T": hbm, "F": hbm, "S": SMEM, "V": VMEM, "R": VMEM, "H": hbm, "B": hbm, "D": hbm, "P": hbm, "M": SMEM, "I": SMEM}
+    specs = {"G": SMEM, "S": SMEM, "V": VMEM, "R": VMEM, "H": hbm, "B": hbm, "D": hbm, "P": hbm, "M": SMEM, "I": SMEM}
     scratch_shapes = [pltpu.VMEM(shape, jnp.float32) for shape in scratch]
-    stages = {"T": (pltpu.SMEM, jnp.int32), "F": (pltpu.SMEM, jnp.float32)}
-    for _, kind, shape in late_in:
-        memory, dtype = stages.get(kind, (pltpu.VMEM, jnp.float32))
-        scratch_shapes.append(memory(shape, dtype))
-    scratch_shapes += [pltpu.VMEM(shape, jnp.float32) for _, shape in late_out]
+    scratch_shapes += [pltpu.VMEM(shape, jnp.float32) for _, shape in late_in + late_out]
     if count_in or fetch:
-        scratch_shapes.append(pltpu.SemaphoreType.DMA((arrive + len(fetch),)))
+        scratch_shapes.append(pltpu.SemaphoreType.DMA((count_in + len(fetch),)))
     if sends:
         scratch_shapes.append(pltpu.SemaphoreType.DMA((sends,)))
     shapes = {"V": jax.ShapeDtypeStruct, "R": pltpu.VMEM, "H": pltpu.HBM, "B": pltpu.HBM, "D": pltpu.HBM}
@@ -653,7 +640,7 @@
     )
 
     def run(*operands):
-        placed = {"G": pltpu.SMEM, "C": pltpu.HBM, "T": pltpu.HBM, "F": pltpu.HBM, "M": pltpu.SMEM, "H": pltpu.HBM, "R": pltpu.VMEM, "P": pltpu.HBM}
+        placed = {"G": pltpu.SMEM, "M": pltpu.SMEM, "H": pltpu.HBM, "R": pltpu.VMEM, "P": pltpu.HBM}
         return invoke(
             *[
                 pltpu.with_memory_space_constraint(operand, placed[kind]) if kind in placed else operand
@@ -705,7 +692,7 @@
     links = (owner, neighbours, orientation)
     weight_faces, rate_faces, sent, *table, mats = call(
         functools.partial(pack_kernel, geo),
-        [scalar] * 2 + [far(stored_shape), ("C", block), far(rate_block)] + [("P", None)] * 4,
+        [scalar] * 2 + [far(stored_shape), far(block), far(rate_block)] + [("P", None)] * 4,
         [far(faces_shape), ("R", geo.rate_faces), ("B", both), ("I", (2,))]
         + [("I", link.shape) for link in links]
         + [("M", flux_mats.shape)],

time: 99.6 us -> 99 us (level)
  no operation moved by 1% of the time
where the time goes in v15:
time: 99 us; the launch traced here: 98.1 us
  Pallas kernels  35.9 us (36%)
  starting transfers between devices  26.9 us (27%)
  waiting for transfers between devices  19.3 us (19%)
  blocking collectives  15.2 us (15%)
    pallas_call x12, Pallas kernels, run(): invoke(*[pltpu.with_memory_space_constraint(operand, placed[kind]) if kin...  35.9 us
    all_to_all x6, starting transfers between devices, swap(): return lax.all_to_all(buffer, 'space', 0, 0, tiled=True)  26.9 us
    all_to_all x6, waiting for transfers between devices, swap(): return lax.all_to_all(buffer, 'space', 0, 0, tiled=True)  19.3 us
    all_gather x1, blocking collectives, on_device(): state = lax.all_gather(kept, 'ckpt', axis=0)  9.05 us
    all_gather x1, blocking collectives, on_device(): gathered = lax.all_gather(first_ghosts[:, :some], 'ckpt', axis=0)  6.15 us
  transfers between devices with their start and end apart: 6, of which 6 were waited for; matrix products, arithmetic and copies ran while one was open for 0% of the time, Pallas kernels for 25%

profile of v15, /device:TPU:0, one launch (start us, length us, event | category | flops | bytes accessed | tf_op | source)
XLA Modules:
  0.0 98.1 jit_solution(12700035796846989689)
XLA Ops:
  0.6 2.6 %shard_map.86 = (f32[6,96,128]{2,1,0:T(8,128)}, f32[6,16,128]{2,1,0:T(8,128)S(1)}, f32[8,72,128]{2,1,0:T(8,128)}, s32[2]{0:T(128)S(4)}, s32[8]{0:T(128)S(4)}, /*...) custom-call(s32[1]{0:T(128)} %bitcast.refs_0_, s32[1]{0:T(128)} %bitcast.1.refs_1_, ...), custom_call_target="tpu_custom_call" | custom-call | flops 884736 | bytes 3145728 | tf_op jit(solution)/shard_map/pallas_call | solution.py:644
  3.3 0.0 copy-start
  3.3 7.4 %all-to-all-start = ((f32[8,72,128]{2,1,0:T(8,128)}), f32[8,72,128]{2,1,0:T(8,128)S(1)}, u32[]{:S(2)}, u32[]{:S(2)}) async-start(f32[8,72,128]{2,1,0:T(8,128)} %get-tuple-element.57), calls=%async_computation | async-start | bytes 589824 | tf_op jit(solution)/shard_map/all_to_all | solution.py:676
  10.7 0.0 copy-done
  10.7 9.0 %all-gather = f32[24,4,16,128]{3,2,1,0:T(8,128)} all-gather(f32[6,4,16,128]{3,2,1,0:T(8,128)S(1)} %bitcast.21), channel_id=2, replica_groups=mesh['ckpt'=4,'space'=8] {'ckpt'}, dimensions={0}, use_global_device_ids=true | all-gather | bytes 983040 | tf_op jit(solution)/shard_map/all_gather | solution.py:706
  19.8 0.6 all-to-all-done.refs_4_
  20.3 1.0 shard_map.87
  21.3 5.4 %all-to-all-start.1 = ((f32[8,72,128]{2,1,0:T(8,128)}), f32[8,72,128]{2,1,0:T(8,128)S(1)}, u32[]{:S(2)}, u32[]{:S(2)}) async-start(f32[8,72,128]{2,1,0:T(8,128)} %shard_map.87), calls=%async_computation.1 | async-start | bytes 589824 | tf_op jit(solution)/shard_map/all_to_all | solution.py:676
  26.7 5.6 %shard_map.88 = (f32[6,16,16,128]{3,2,1,0:T(8,128)S(1)}, f32[6,96,128]{2,1,0:T(8,128)S(1)}, f32[6,96,128]{2,1,0:T(8,128)}) custom-call(f32[3,6,6]{2,1,0:T(8,128)S(4)} %get-tuple-element.55.refs_0_.refs_4_, f32[4,6,4,16,128]{4,3,2,1,0:T(8,128)} %bitcast.10, f32[16,16,128]{2,1,0:T(8,128)} %bitcast.13), custom_call_target="tpu_custom_call" | custom-call | flops 14155776 | bytes 3145728 | tf_op jit(solution)/shard_map/pallas_call | solution.py:644
  32.4 4.5 %all-to-all-done.1.refs_7_ = f32[8,72,128]{2,1,0:T(8,128)S(1)} async-done(((f32[8,72,128]{2,1,0:T(8,128)}), f32[8,72,128]{2,1,0:T(8,128)S(1)}, u32[]{:S(2)}, u32[]{:S(2)}) %all-to-all-start.1) | async-done | bytes 294944 | tf_op jit(solution)/shard_map/all_to_all | solution.py:676
  36.8 6.1 %all-gather.1 = f32[32,24,128]{2,1,0:T(8,128)S(1)} all-gather(f32[8,24,128]{2,1,0:T(8,128)S(1)} %slice.3), channel_id=3, replica_groups=mesh['ckpt'=4,'space'=8] {'ckpt'}, dimensions={0}, use_global_device_ids=true | all-gather | bytes 491520 | tf_op jit(solution)/shard_map/all_gather | solution.py:720
  43.0 2.3 %shard_map.89 = (f32[6,16,16,128]{3,2,1,0:T(8,128)S(1)}, f32[6,96,128]{2,1,0:T(8,128)S(1)}, f32[6,96,128]{2,1,0:T(8,128)}, f32[8,56,128]{2,1,0:T(8,128)}, f32[6,96,128]{2,1,0:T(8,128)}) custom-call(s32[2]{0:T(128)S(4)} %get-tuple-element.51.refs_0_.refs_3_, s32[8]{0:T(128)S(4)} %get-tuple-element.52.refs_1_.refs_4_, ...), custom_call_target="tpu_custom_call", output_to_operand_aliasing={{0}: (5, {})} | custom-call | flops 884736 | bytes 3145728 | tf_op jit(solution)/shard_map/pallas_call | solution.py:644
  45.3 3.7 %all-to-all-start.2 = ((f32[8,56,128]{2,1,0:T(8,128)}), f32[8,56,128]{2,1,0:T(8,128)S(1)}, u32[]{:S(2)}, u32[]{:S(2)}) async-start(f32[8,56,128]{2,1,0:T(8,128)} %get-tuple-element.67), calls=%async_computation.2 | async-start | bytes 458752 | tf_op jit(solution)/shard_map/all_to_all | solution.py:676
  49.0 5.5 %shard_map.90.refs_5_ = f32[6,16,16,128]{3,2,1,0:T(8,128)S(1)} custom-call(f32[3,6,6]{2,1,0:T(8,128)S(4)} %get-tuple-element.55.refs_0_.refs_4_, f32[6,16,16,128]{3,2,1,0:T(8,128)S(1)} %get-tuple-element.73.refs_1_, f32[6,16,16,128]{3,2,1,0:T(8,128)} %bitcast.18, f32[16,16,128]{2,1,0:T(8,128)} %bitcast.14), custom_call_target="tpu_custom_call" | custom-call | flops 28311552 | bytes 3145728 | tf_op jit(solution)/shard_map/pallas_call | solution.py:644
  54.5 3.5 %all-to-all-done.2.refs_4_ = f32[8,56,128]{2,1,0:T(8,128)S(1)} async-done(((f32[8,56,128]{2,1,0:T(8,128)}), f32[8,56,128]{2,1,0:T(8,128)S(1)}, u32[]{:S(2)}, u32[]{:S(2)}) %all-to-all-start.2) | async-done | bytes 229408 | tf_op jit(solution)/shard_map/all_to_all | solution.py:676
  58.0 0.8 shard_map.91
  58.7 3.4 %all-to-all-start.3 = ((f32[8,56,128]{2,1,0:T(8,128)}), f32[8,56,128]{2,1,0:T(8,128)S(1)}, u32[]{:S(2)}, u32[]{:S(2)}) async-start(f32[8,56,128]{2,1,0:T(8,128)} %shard_map.91), calls=%async_computation.3 | async-start | bytes 458752 | tf_op jit(solution)/shard_map/all_to_all | solution.py:676
  62.2 5.3 %shard_map.92 = (f32[6,16,16,128]{3,2,1,0:T(8,128)}, f32[6,96,128]{2,1,0:T(8,128)S(1)}, f32[6,96,128]{2,1,0:T(8,128)S(1)}) custom-call(f32[3,6,6]{2,1,0:T(8,128)S(4)} %get-tuple-element.55.refs_0_.refs_4_, f32[6,16,16,128]{3,2,1,0:T(8,128)S(1)} %get-tuple-element.73.refs_1_, f32[16,16,128]{2,1,0:T(8,128)} %bitcast.15, ...), custom_call_target="tpu_custom_call" | custom-call | flops 14155776 | bytes 3145728 | tf_op jit(solution)/shard_map/pallas_call | solution.py:644
  67.4 3.1 %all-to-all-done.3.refs_9_ = f32[8,56,128]{2,1,0:T(8,128)S(1)} async-done(((f32[8,56,128]{2,1,0:T(8,128)}), f32[8,56,128]{2,1,0:T(8,128)S(1)}, u32[]{:S(2)}, u32[]{:S(2)}) %all-to-all-start.3) | async-done | bytes 229408 | tf_op jit(solution)/shard_map/all_to_all | solution.py:676
  70.6 2.3 %shard_map.93 = (f32[6,16,16,128]{3,2,1,0:T(8,128)S(1)}, f32[6,96,128]{2,1,0:T(8,128)S(1)}, f32[8,56,128]{2,1,0:T(8,128)}, f32[6,96,128]{2,1,0:T(8,128)}) custom-call(s32[2]{0:T(128)S(4)} %get-tuple-element.51.refs_0_.refs_3_, s32[8]{0:T(128)S(4)} %get-tuple-element.52.refs_1_.refs_4_, ...), custom_call_target="tpu_custom_call", output_to_operand_aliasing={{0}: (5, {})} | custom-call | flops 884736 | bytes 3145728 | tf_op jit(solution)/shard_map/pallas_call | solution.py:644
  72.8 3.4 %all-to-all-start.4 = ((f32[8,56,128]{2,1,0:T(8,128)}), f32[8,56,128]{2,1,0:T(8,128)S(1)}, u32[]{:S(2)}, u32[]{:S(2)}) async-start(f32[8,56,128]{2,1,0:T(8,128)} %get-tuple-element.81), calls=%async_computation.4 | async-start | bytes 458752 | tf_op jit(solution)/shard_map/all_to_all | solution.py:676
  76.3 5.5 %shard_map.94.refs_5_ = f32[6,16,16,128]{3,2,1,0:T(8,128)S(1)} custom-call(f32[3,6,6]{2,1,0:T(8,128)S(4)} %get-tuple-element.55.refs_0_.refs_4_, f32[4,6,4,16,128]{4,3,2,1,0:T(8,128)} %bitcast.11, f32[6,16,16,128]{3,2,1,0:T(8,128)S(1)} %get-tuple-element.82.refs_2_, f32[16,16,128]{2,1,0:T(8,128)} %bitcast.16), custom_call_target="tpu_custom_call" | custom-call | flops 28311552 | bytes 3145728 | tf_op jit(solution)/shard_map/pallas_call | solution.py:644
  81.8 2.6 %all-to-all-done.4.refs_4_ = f32[8,56,128]{2,1,0:T(8,128)S(1)} async-done(((f32[8,56,128]{2,1,0:T(8,128)}), f32[8,56,128]{2,1,0:T(8,128)S(1)}, u32[]{:S(2)}, u32[]{:S(2)}) %all-to-all-start.4) | async-done | bytes 229408 | tf_op jit(solution)/shard_map/all_to_all | solution.py:676
  84.3 0.8 shard_map.95
  85.1 3.5 %all-to-all-start.5 = ((f32[8,56,128]{2,1,0:T(8,128)}), f32[8,56,128]{2,1,0:T(8,128)S(1)}, u32[]{:S(2)}, u32[]{:S(2)}) async-start(f32[8,56,128]{2,1,0:T(8,128)} %shard_map.95), calls=%async_computation.5 | async-start | bytes 458752 | tf_op jit(solution)/shard_map/all_to_all | solution.py:676
  88.6 2.8 %shard_map.96 = (f32[6,16,16,128]{3,2,1,0:T(8,128)}, f32[6,96,128]{2,1,0:T(8,128)S(1)}, f32[6,96,128]{2,1,0:T(8,128)S(1)}) custom-call(s32[2]{0:T(128)S(4)} %get-tuple-element.51.refs_0_.refs_3_, s32[8]{0:T(128)S(4)} %get-tuple-element.52.refs_1_.refs_4_, s32[8,6]{1,0:T(8,128)S(4)} %get-tuple-element.53.refs_2_.refs_5_, ...), custom_call_target="tpu_custom_call" | custom-call | flops 14155776 | bytes 3145728 | tf_op jit(solution)/shard_map/pallas_call | solution.py:644
  91.4 5.2 %all-to-all-done.5.refs_9_ = f32[8,56,128]{2,1,0:T(8,128)S(1)} async-done(((f32[8,56,128]{2,1,0:T(8,128)}), f32[8,56,128]{2,1,0:T(8,128)S(1)}, u32[]{:S(2)}, u32[]{:S(2)}) %all-to-all-start.5) | async-done | bytes 229408 | tf_op jit(solution)/shard_map/all_to_all | solution.py:676
  96.6 1.5 %shard_map.97 = f32[6,16,16,128]{3,2,1,0:T(8,128)} custom-call(s32[2]{0:T(128)S(4)} %get-tuple-element.51.refs_0_.refs_3_, s32[8]{0:T(128)S(4)} %get-tuple-element.52.refs_1_.refs_4_, s32[8,6]{1,0:T(8,128)S(4)} %get-tuple-element.53.refs_2_.refs_5_, s32[8,6]{1,0:T(8,128)S(4)} %get-tuple-element.54.refs_3_.refs_6_, ...), custom_call_target="tpu_custom_call" | custom-call | flops 884736 | bytes 3145728 | tf_op jit(solution)/shard_map/pallas_call | solution.py:644
  (1 shorter events, 0.0 us)
Async XLA Ops:
  3.3 7.4 %copy-start = (f32[1,6,4,16,128]{4,3,2,1,0:T(8,128)S(1)}, f32[1,6,4,16,128]{4,3,2,1,0:T(8,128)}, u32[]{:S(2)}) copy-start(f32[1,6,4,16,128]{4,3,2,1,0:T(8,128)} %param.7) | copy-start | bytes 589828
  3.3 17.0 %all-to-all-start = ((f32[8,72,128]{2,1,0:T(8,128)}), f32[8,72,128]{2,1,0:T(8,128)S(1)}, u32[]{:S(2)}, u32[]{:S(2)}) async-start(f32[8,72,128]{2,1,0:T(8,128)} %get-tuple-element.57), calls=%async_computation | async-start | bytes 589824 | tf_op jit(solution)/shard_map/all_to_all | solution.py:676
  21.3 15.5 %all-to-all-start.1 = ((f32[8,72,128]{2,1,0:T(8,128)}), f32[8,72,128]{2,1,0:T(8,128)S(1)}, u32[]{:S(2)}, u32[]{:S(2)}) async-start(f32[8,72,128]{2,1,0:T(8,128)} %shard_map.87), calls=%async_computation.1 | async-start | bytes 589824 | tf_op jit(solution)/shard_map/all_to_all | solution.py:676
  45.3 12.7 %all-to-all-start.2 = ((f32[8,56,128]{2,1,0:T(8,128)}), f32[8,56,128]{2,1,0:T(8,128)S(1)}, u32[]{:S(2)}, u32[]{:S(2)}) async-start(f32[8,56,128]{2,1,0:T(8,128)} %get-tuple-element.67), calls=%async_computation.2 | async-start | bytes 458752 | tf_op jit(solution)/shard_map/all_to_all | solution.py:676
  58.7 11.8 %all-to-all-start.3 = ((f32[8,56,128]{2,1,0:T(8,128)}), f32[8,56,128]{2,1,0:T(8,128)S(1)}, u32[]{:S(2)}, u32[]{:S(2)}) async-start(f32[8,56,128]{2,1,0:T(8,128)} %shard_map.91), calls=%async_computation.3 | async-start | bytes 458752 | tf_op jit(solution)/shard_map/all_to_all | solution.py:676
  72.8 11.5 %all-to-all-start.4 = ((f32[8,56,128]{2,1,0:T(8,128)}), f32[8,56,128]{2,1,0:T(8,128)S(1)}, u32[]{:S(2)}, u32[]{:S(2)}) async-start(f32[8,56,128]{2,1,0:T(8,128)} %get-tuple-element.81), calls=%async_computation.4 | async-start | bytes 458752 | tf_op jit(solution)/shard_map/all_to_all | solution.py:676
  85.1 11.5 %all-to-all-start.5 = ((f32[8,56,128]{2,1,0:T(8,128)}), f32[8,56,128]{2,1,0:T(8,128)S(1)}, u32[]{:S(2)}, u32[]{:S(2)}) async-start(f32[8,56,128]{2,1,0:T(8,128)} %shard_map.95), calls=%async_computation.5 | async-start | bytes 458752 | tf_op jit(solution)/shard_map/all_to_all | solution.py:676

commit v16 on v15

--- a/solution.py
+++ b/solution.py
@@ -94,11 +94,15 @@
     def part(self):
         return self.places[1]
 
+    def slot(self, place):
+        half = place >> 1
+        return jnp.where((place & 1) == 1, self.n - 1 - half, half)
+
     def target(self, block):
-        return self.owner[block]
+        return self.slot(self.owner[block])
 
     def source(self, block, side):
-        return self.owner[self.neighbours[block, side]]
+        return self.slot(self.owner[self.neighbours[block, side]])
 
 
 def flip_rows(values, flag, length):
@@ -673,7 +677,8 @@
         return ("H", shape)
 
     def swap(buffer):
-        return lax.all_to_all(buffer, "space", 0, 0, tiled=True)
+        ring = list(range(0, count, 2)) + list(range(count - 1, 0, -2))
+        return lax.all_to_all(buffer, "space", 0, 0, axis_index_groups=[ring], tiled=True)
 
     def route(arrived):
         return call(functools.partial(route_kernel, geo), grouped + [near], [("B", whole)], [], few)(

time: 99 us -> 100 us (1.010)
  waiting for transfers between devices: 19.3 us -> 20.6 us
    all_to_all x6, waiting for transfers between devices: 19.3 us -> 20.6 us  [swap(): lax.all_to_all(buffer, 'space', 0, 0, axis_index_groups=[ring], tiled=True)]
where the time goes in v16:
time: 100 us; the launch traced here: 99.1 us
  Pallas kernels  36.2 us (36%)
  starting transfers between devices  26.3 us (26%)
  waiting for transfers between devices  20.6 us (21%)
  blocking collectives  15.2 us (15%)
    pallas_call x12, Pallas kernels, run(): invoke(*[pltpu.with_memory_space_constraint(operand, placed[kind]) if kin...  36.2 us
    all_to_all x6, starting transfers between devices, swap(): lax.all_to_all(buffer, 'space', 0, 0, axis_index_groups=[ring], tiled=True)  26.3 us
    all_to_all x6, waiting for transfers between devices, swap(): lax.all_to_all(buffer, 'space', 0, 0, axis_index_groups=[ring], tiled=True)  20.6 us
    all_gather x1, blocking collectives, on_device(): state = lax.all_gather(kept, 'ckpt', axis=0)  9.05 us
    all_gather x1, blocking collectives, on_device(): gathered = lax.all_gather(first_ghosts[:, :some], 'ckpt', axis=0)  6.15 us
  transfers between devices with their start and end apart: 6, of which 6 were waited for; matrix products, arithmetic and copies ran while one was open for 0% of the time, Pallas kernels for 25%

profile of v16, /device:TPU:0, one launch (start us, length us, event | category | flops | bytes accessed | tf_op | source)
XLA Modules:
  0.0 99.1 jit_solution(15112665826616962974)
XLA Ops:
  0.6 2.6 %shard_map.86 = (f32[6,96,128]{2,1,0:T(8,128)}, f32[6,16,128]{2,1,0:T(8,128)S(1)}, f32[8,72,128]{2,1,0:T(8,128)}, s32[2]{0:T(128)S(4)}, s32[8]{0:T(128)S(4)}, /*...) custom-call(s32[1]{0:T(128)} %bitcast.refs_0_, s32[1]{0:T(128)} %bitcast.1.refs_1_, ...), custom_call_target="tpu_custom_call" | custom-call | flops 884736 | bytes 3145728 | tf_op jit(solution)/shard_map/pallas_call | solution.py:648
  3.3 0.0 copy-start
  3.3 7.4 %all-to-all-start = ((f32[8,72,128]{2,1,0:T(8,128)}), f32[8,72,128]{2,1,0:T(8,128)S(1)}, u32[]{:S(2)}, u32[]{:S(2)}) async-start(f32[8,72,128]{2,1,0:T(8,128)} %get-tuple-element.57), calls=%async_computation | async-start | bytes 589824 | tf_op jit(solution)/shard_map/all_to_all | solution.py:681
  10.7 0.0 copy-done
  10.7 9.0 %all-gather = f32[24,4,16,128]{3,2,1,0:T(8,128)} all-gather(f32[6,4,16,128]{3,2,1,0:T(8,128)S(1)} %bitcast.21), channel_id=2, replica_groups=mesh['ckpt'=4,'space'=8] {'ckpt'}, dimensions={0}, use_global_device_ids=true | all-gather | bytes 983040 | tf_op jit(solution)/shard_map/all_gather | solution.py:711
  19.8 0.8 all-to-all-done.refs_4_
  20.5 1.1 %shard_map.87 = f32[8,72,128]{2,1,0:T(8,128)} custom-call(s32[2]{0:T(128)S(4)} %get-tuple-element.51.refs_0_.refs_3_, s32[8]{0:T(128)S(4)} %get-tuple-element.52.refs_1_.refs_4_, s32[8,6]{1,0:T(8,128)S(4)} %get-tuple-element.53.refs_2_.refs_5_, s32[8,6]{1,0:T(8,128)S(4)} %get-tuple-element.54.refs_3_.refs_6_, f32[8,72,128]{2,1,0:T(8,128)S(1)} %all-to-all-done.refs_4_), custom_call_target="tpu_custom_call" | custom-call | flops 884736 | bytes 3145728 | tf_op jit(solution)/shard_map/pallas_call | solution.py:648
  21.7 5.2 %all-to-all-start.1 = ((f32[8,72,128]{2,1,0:T(8,128)}), f32[8,72,128]{2,1,0:T(8,128)S(1)}, u32[]{:S(2)}, u32[]{:S(2)}) async-start(f32[8,72,128]{2,1,0:T(8,128)} %shard_map.87), calls=%async_computation.1 | async-start | bytes 589824 | tf_op jit(solution)/shard_map/all_to_all | solution.py:681
  26.9 5.6 %shard_map.88 = (f32[6,16,16,128]{3,2,1,0:T(8,128)S(1)}, f32[6,96,128]{2,1,0:T(8,128)S(1)}, f32[6,96,128]{2,1,0:T(8,128)}) custom-call(f32[3,6,6]{2,1,0:T(8,128)S(4)} %get-tuple-element.55.refs_0_.refs_4_, f32[4,6,4,16,128]{4,3,2,1,0:T(8,128)} %bitcast.10, f32[16,16,128]{2,1,0:T(8,128)} %bitcast.13), custom_call_target="tpu_custom_call" | custom-call | flops 14155776 | bytes 3145728 | tf_op jit(solution)/shard_map/pallas_call | solution.py:648
  32.5 4.7 %all-to-all-done.1.refs_7_ = f32[8,72,128]{2,1,0:T(8,128)S(1)} async-done(((f32[8,72,128]{2,1,0:T(8,128)}), f32[8,72,128]{2,1,0:T(8,128)S(1)}, u32[]{:S(2)}, u32[]{:S(2)}) %all-to-all-start.1) | async-done | bytes 294944 | tf_op jit(solution)/shard_map/all_to_all | solution.py:681
  37.3 6.1 %all-gather.1 = f32[32,24,128]{2,1,0:T(8,128)S(1)} all-gather(f32[8,24,128]{2,1,0:T(8,128)S(1)} %slice.3), channel_id=3, replica_groups=mesh['ckpt'=4,'space'=8] {'ckpt'}, dimensions={0}, use_global_device_ids=true | all-gather | bytes 491520 | tf_op jit(solution)/shard_map/all_gather | solution.py:725
  43.4 2.3 %shard_map.89 = (f32[6,16,16,128]{3,2,1,0:T(8,128)S(1)}, f32[6,96,128]{2,1,0:T(8,128)S(1)}, f32[6,96,128]{2,1,0:T(8,128)}, f32[8,56,128]{2,1,0:T(8,128)}, f32[6,96,128]{2,1,0:T(8,128)}) custom-call(s32[2]{0:T(128)S(4)} %get-tuple-element.51.refs_0_.refs_3_, s32[8]{0:T(128)S(4)} %get-tuple-element.52.refs_1_.refs_4_, ...), custom_call_target="tpu_custom_call", output_to_operand_aliasing={{0}: (5, {})} | custom-call | flops 884736 | bytes 3145728 | tf_op jit(solution)/shard_map/pallas_call | solution.py:648
  45.7 3.4 %all-to-all-start.2 = ((f32[8,56,128]{2,1,0:T(8,128)}), f32[8,56,128]{2,1,0:T(8,128)S(1)}, u32[]{:S(2)}, u32[]{:S(2)}) async-start(f32[8,56,128]{2,1,0:T(8,128)} %get-tuple-element.67), calls=%async_computation.2 | async-start | bytes 458752 | tf_op jit(solution)/shard_map/all_to_all | solution.py:681
  49.1 5.5 %shard_map.90.refs_5_ = f32[6,16,16,128]{3,2,1,0:T(8,128)S(1)} custom-call(f32[3,6,6]{2,1,0:T(8,128)S(4)} %get-tuple-element.55.refs_0_.refs_4_, f32[6,16,16,128]{3,2,1,0:T(8,128)S(1)} %get-tuple-element.73.refs_1_, f32[6,16,16,128]{3,2,1,0:T(8,128)} %bitcast.18, f32[16,16,128]{2,1,0:T(8,128)} %bitcast.14), custom_call_target="tpu_custom_call" | custom-call | flops 28311552 | bytes 3145728 | tf_op jit(solution)/shard_map/pallas_call | solution.py:648
  54.6 4.0 %all-to-all-done.2.refs_4_ = f32[8,56,128]{2,1,0:T(8,128)S(1)} async-done(((f32[8,56,128]{2,1,0:T(8,128)}), f32[8,56,128]{2,1,0:T(8,128)S(1)}, u32[]{:S(2)}, u32[]{:S(2)}) %all-to-all-start.2) | async-done | bytes 229408 | tf_op jit(solution)/shard_map/all_to_all | solution.py:681
  58.6 0.8 shard_map.91
  59.5 3.4 %all-to-all-start.3 = ((f32[8,56,128]{2,1,0:T(8,128)}), f32[8,56,128]{2,1,0:T(8,128)S(1)}, u32[]{:S(2)}, u32[]{:S(2)}) async-start(f32[8,56,128]{2,1,0:T(8,128)} %shard_map.91), calls=%async_computation.3 | async-start | bytes 458752 | tf_op jit(solution)/shard_map/all_to_all | solution.py:681
  62.9 5.3 %shard_map.92 = (f32[6,16,16,128]{3,2,1,0:T(8,128)}, f32[6,96,128]{2,1,0:T(8,128)S(1)}, f32[6,96,128]{2,1,0:T(8,128)S(1)}) custom-call(f32[3,6,6]{2,1,0:T(8,128)S(4)} %get-tuple-element.55.refs_0_.refs_4_, f32[6,16,16,128]{3,2,1,0:T(8,128)S(1)} %get-tuple-element.73.refs_1_, f32[16,16,128]{2,1,0:T(8,128)} %bitcast.15, ...), custom_call_target="tpu_custom_call" | custom-call | flops 14155776 | bytes 3145728 | tf_op jit(solution)/shard_map/pallas_call | solution.py:648
  68.2 3.1 %all-to-all-done.3.refs_9_ = f32[8,56,128]{2,1,0:T(8,128)S(1)} async-done(((f32[8,56,128]{2,1,0:T(8,128)}), f32[8,56,128]{2,1,0:T(8,128)S(1)}, u32[]{:S(2)}, u32[]{:S(2)}) %all-to-all-start.3) | async-done | bytes 229408 | tf_op jit(solution)/shard_map/all_to_all | solution.py:681
  71.2 2.3 %shard_map.93 = (f32[6,16,16,128]{3,2,1,0:T(8,128)S(1)}, f32[6,96,128]{2,1,0:T(8,128)S(1)}, f32[8,56,128]{2,1,0:T(8,128)}, f32[6,96,128]{2,1,0:T(8,128)}) custom-call(s32[2]{0:T(128)S(4)} %get-tuple-element.51.refs_0_.refs_3_, s32[8]{0:T(128)S(4)} %get-tuple-element.52.refs_1_.refs_4_, ...), custom_call_target="tpu_custom_call", output_to_operand_aliasing={{0}: (5, {})} | custom-call | flops 884736 | bytes 3145728 | tf_op jit(solution)/shard_map/pallas_call | solution.py:648
  73.5 3.4 %all-to-all-start.4 = ((f32[8,56,128]{2,1,0:T(8,128)}), f32[8,56,128]{2,1,0:T(8,128)S(1)}, u32[]{:S(2)}, u32[]{:S(2)}) async-start(f32[8,56,128]{2,1,0:T(8,128)} %get-tuple-element.81), calls=%async_computation.4 | async-start | bytes 458752 | tf_op jit(solution)/shard_map/all_to_all | solution.py:681
  76.9 5.5 %shard_map.94.refs_5_ = f32[6,16,16,128]{3,2,1,0:T(8,128)S(1)} custom-call(f32[3,6,6]{2,1,0:T(8,128)S(4)} %get-tuple-element.55.refs_0_.refs_4_, f32[4,6,4,16,128]{4,3,2,1,0:T(8,128)} %bitcast.11, f32[6,16,16,128]{3,2,1,0:T(8,128)S(1)} %get-tuple-element.82.refs_2_, f32[16,16,128]{2,1,0:T(8,128)} %bitcast.16), custom_call_target="tpu_custom_call" | custom-call | flops 28311552 | bytes 3145728 | tf_op jit(solution)/shard_map/pallas_call | solution.py:648
  82.5 2.7 %all-to-all-done.4.refs_4_ = f32[8,56,128]{2,1,0:T(8,128)S(1)} async-done(((f32[8,56,128]{2,1,0:T(8,128)}), f32[8,56,128]{2,1,0:T(8,128)S(1)}, u32[]{:S(2)}, u32[]{:S(2)}) %all-to-all-start.4) | async-done | bytes 229408 | tf_op jit(solution)/shard_map/all_to_all | solution.py:681
  85.2 0.8 shard_map.95
  86.0 3.4 %all-to-all-start.5 = ((f32[8,56,128]{2,1,0:T(8,128)}), f32[8,56,128]{2,1,0:T(8,128)S(1)}, u32[]{:S(2)}, u32[]{:S(2)}) async-start(f32[8,56,128]{2,1,0:T(8,128)} %shard_map.95), calls=%async_computation.5 | async-start | bytes 458752 | tf_op jit(solution)/shard_map/all_to_all | solution.py:681
  89.4 2.9 %shard_map.96 = (f32[6,16,16,128]{3,2,1,0:T(8,128)}, f32[6,96,128]{2,1,0:T(8,128)S(1)}, f32[6,96,128]{2,1,0:T(8,128)S(1)}) custom-call(s32[2]{0:T(128)S(4)} %get-tuple-element.51.refs_0_.refs_3_, s32[8]{0:T(128)S(4)} %get-tuple-element.52.refs_1_.refs_4_, s32[8,6]{1,0:T(8,128)S(4)} %get-tuple-element.53.refs_2_.refs_5_, ...), custom_call_target="tpu_custom_call" | custom-call | flops 14155776 | bytes 3145728 | tf_op jit(solution)/shard_map/pallas_call | solution.py:648
  92.3 5.4 %all-to-all-done.5.refs_9_ = f32[8,56,128]{2,1,0:T(8,128)S(1)} async-done(((f32[8,56,128]{2,1,0:T(8,128)}), f32[8,56,128]{2,1,0:T(8,128)S(1)}, u32[]{:S(2)}, u32[]{:S(2)}) %all-to-all-start.5) | async-done | bytes 229408 | tf_op jit(solution)/shard_map/all_to_all | solution.py:681
  97.7 1.5 %shard_map.97 = f32[6,16,16,128]{3,2,1,0:T(8,128)} custom-call(s32[2]{0:T(128)S(4)} %get-tuple-element.51.refs_0_.refs_3_, s32[8]{0:T(128)S(4)} %get-tuple-element.52.refs_1_.refs_4_, s32[8,6]{1,0:T(8,128)S(4)} %get-tuple-element.53.refs_2_.refs_5_, s32[8,6]{1,0:T(8,128)S(4)} %get-tuple-element.54.refs_3_.refs_6_, ...), custom_call_target="tpu_custom_call" | custom-call | flops 884736 | bytes 3145728 | tf_op jit(solution)/shard_map/pallas_call | solution.py:648
  (1 shorter events, 0.0 us)
Async XLA Ops:
  3.3 7.4 %copy-start = (f32[1,6,4,16,128]{4,3,2,1,0:T(8,128)S(1)}, f32[1,6,4,16,128]{4,3,2,1,0:T(8,128)}, u32[]{:S(2)}) copy-start(f32[1,6,4,16,128]{4,3,2,1,0:T(8,128)} %param.7) | copy-start | bytes 589828
  3.3 17.3 %all-to-all-start = ((f32[8,72,128]{2,1,0:T(8,128)}), f32[8,72,128]{2,1,0:T(8,128)S(1)}, u32[]{:S(2)}, u32[]{:S(2)}) async-start(f32[8,72,128]{2,1,0:T(8,128)} %get-tuple-element.57), calls=%async_computation | async-start | bytes 589824 | tf_op jit(solution)/shard_map/all_to_all | solution.py:681
  21.7 15.6 %all-to-all-start.1 = ((f32[8,72,128]{2,1,0:T(8,128)}), f32[8,72,128]{2,1,0:T(8,128)S(1)}, u32[]{:S(2)}, u32[]{:S(2)}) async-start(f32[8,72,128]{2,1,0:T(8,128)} %shard_map.87), calls=%async_computation.1 | async-start | bytes 589824 | tf_op jit(solution)/shard_map/all_to_all | solution.py:681
  45.7 12.9 %all-to-all-start.2 = ((f32[8,56,128]{2,1,0:T(8,128)}), f32[8,56,128]{2,1,0:T(8,128)S(1)}, u32[]{:S(2)}, u32[]{:S(2)}) async-start(f32[8,56,128]{2,1,0:T(8,128)} %get-tuple-element.67), calls=%async_computation.2 | async-start | bytes 458752 | tf_op jit(solution)/shard_map/all_to_all | solution.py:681
  59.5 11.8 %all-to-all-start.3 = ((f32[8,56,128]{2,1,0:T(8,128)}), f32[8,56,128]{2,1,0:T(8,128)S(1)}, u32[]{:S(2)}, u32[]{:S(2)}) async-start(f32[8,56,128]{2,1,0:T(8,128)} %shard_map.91), calls=%async_computation.3 | async-start | bytes 458752 | tf_op jit(solution)/shard_map/all_to_all | solution.py:681
  73.5 11.6 %all-to-all-start.4 = ((f32[8,56,128]{2,1,0:T(8,128)}), f32[8,56,128]{2,1,0:T(8,128)S(1)}, u32[]{:S(2)}, u32[]{:S(2)}) async-start(f32[8,56,128]{2,1,0:T(8,128)} %get-tuple-element.81), calls=%async_computation.4 | async-start | bytes 458752 | tf_op jit(solution)/shard_map/all_to_all | solution.py:681
  86.0 11.7 %all-to-all-start.5 = ((f32[8,56,128]{2,1,0:T(8,128)}), f32[8,56,128]{2,1,0:T(8,128)S(1)}, u32[]{:S(2)}, u32[]{:S(2)}) async-start(f32[8,56,128]{2,1,0:T(8,128)} %shard_map.95), calls=%async_computation.5 | async-start | bytes 458752 | tf_op jit(solution)/shard_map/all_to_all | solution.py:681

commit v17 on v15

--- a/solution.py
+++ b/solution.py
@@ -522,8 +522,8 @@
         high, low = take_z_faces(geo, lambda var, plane: result[var, plane])
         new_faces[4, :y] = high
         new_faces[5, :y] = low
+        cut(geo, geo.whole, new_faces, sent, 0, functools.partial(late.leave, 3))
         late.leave(2)
-        cut(geo, geo.whole, new_faces, sent, 0, functools.partial(late.leave, 3))
 
 
 def adjoint_edge_kernel(geo, last, late, table, mats, inner, faces, weight_faces, *rest):

time: 99 us -> 99 us (level)
  no operation moved by 1% of the time
where the time goes in v17:
time: 99 us; the launch traced here: 98.1 us
  Pallas kernels  35.9 us (36%)
  starting transfers between devices  26.9 us (27%)
  waiting for transfers between devices  19.3 us (19%)
  blocking collectives  15.2 us (15%)
    pallas_call x12, Pallas kernels, run(): invoke(*[pltpu.with_memory_space_constraint(operand, placed[kind]) if kin...  35.9 us
    all_to_all x6, starting transfers between devices, swap(): return lax.all_to_all(buffer, 'space', 0, 0, tiled=True)  26.9 us
    all_to_all x6, waiting for transfers between devices, swap(): return lax.all_to_all(buffer, 'space', 0, 0, tiled=True)  19.3 us
    all_gather x1, blocking collectives, on_device(): state = lax.all_gather(kept, 'ckpt', axis=0)  9.05 us
    all_gather x1, blocking collectives, on_device(): gathered = lax.all_gather(first_ghosts[:, :some], 'ckpt', axis=0)  6.15 us
  transfers between devices with their start and end apart: 6, of which 6 were waited for; matrix products, arithmetic and copies ran while one was open for 0% of the time, Pallas kernels for 25%

profile of v17, /device:TPU:0, one launch (start us, length us, event | category | flops | bytes accessed | tf_op | source)
XLA Modules:
  0.0 98.1 jit_solution(2122588557064931425)
XLA Ops:
  0.6 2.6 %shard_map.86 = (f32[6,96,128]{2,1,0:T(8,128)}, f32[6,16,128]{2,1,0:T(8,128)S(1)}, f32[8,72,128]{2,1,0:T(8,128)}, s32[2]{0:T(128)S(4)}, s32[8]{0:T(128)S(4)}, /*...) custom-call(s32[1]{0:T(128)} %bitcast.refs_0_, s32[1]{0:T(128)} %bitcast.1.refs_1_, ...), custom_call_target="tpu_custom_call" | custom-call | flops 884736 | bytes 3145728 | tf_op jit(solution)/shard_map/pallas_call | solution.py:644
  3.3 0.0 copy-start
  3.3 7.4 %all-to-all-start = ((f32[8,72,128]{2,1,0:T(8,128)}), f32[8,72,128]{2,1,0:T(8,128)S(1)}, u32[]{:S(2)}, u32[]{:S(2)}) async-start(f32[8,72,128]{2,1,0:T(8,128)} %get-tuple-element.57), calls=%async_computation | async-start | bytes 589824 | tf_op jit(solution)/shard_map/all_to_all | solution.py:676
  10.7 0.0 copy-done
  10.7 9.0 %all-gather = f32[24,4,16,128]{3,2,1,0:T(8,128)} all-gather(f32[6,4,16,128]{3,2,1,0:T(8,128)S(1)} %bitcast.21), channel_id=2, replica_groups=mesh['ckpt'=4,'space'=8] {'ckpt'}, dimensions={0}, use_global_device_ids=true | all-gather | bytes 983040 | tf_op jit(solution)/shard_map/all_gather | solution.py:706
  19.8 0.6 all-to-all-done.refs_4_
  20.3 1.0 shard_map.87
  21.3 5.4 %all-to-all-start.1 = ((f32[8,72,128]{2,1,0:T(8,128)}), f32[8,72,128]{2,1,0:T(8,128)S(1)}, u32[]{:S(2)}, u32[]{:S(2)}) async-start(f32[8,72,128]{2,1,0:T(8,128)} %shard_map.87), calls=%async_computation.1 | async-start | bytes 589824 | tf_op jit(solution)/shard_map/all_to_all | solution.py:676
  26.7 5.6 %shard_map.88 = (f32[6,16,16,128]{3,2,1,0:T(8,128)S(1)}, f32[6,96,128]{2,1,0:T(8,128)S(1)}, f32[6,96,128]{2,1,0:T(8,128)}) custom-call(f32[3,6,6]{2,1,0:T(8,128)S(4)} %get-tuple-element.55.refs_0_.refs_4_, f32[4,6,4,16,128]{4,3,2,1,0:T(8,128)} %bitcast.10, f32[16,16,128]{2,1,0:T(8,128)} %bitcast.13), custom_call_target="tpu_custom_call" | custom-call | flops 14155776 | bytes 3145728 | tf_op jit(solution)/shard_map/pallas_call | solution.py:644
  32.4 4.5 %all-to-all-done.1.refs_7_ = f32[8,72,128]{2,1,0:T(8,128)S(1)} async-done(((f32[8,72,128]{2,1,0:T(8,128)}), f32[8,72,128]{2,1,0:T(8,128)S(1)}, u32[]{:S(2)}, u32[]{:S(2)}) %all-to-all-start.1) | async-done | bytes 294944 | tf_op jit(solution)/shard_map/all_to_all | solution.py:676
  36.8 6.1 %all-gather.1 = f32[32,24,128]{2,1,0:T(8,128)S(1)} all-gather(f32[8,24,128]{2,1,0:T(8,128)S(1)} %slice.3), channel_id=3, replica_groups=mesh['ckpt'=4,'space'=8] {'ckpt'}, dimensions={0}, use_global_device_ids=true | all-gather | bytes 491520 | tf_op jit(solution)/shard_map/all_gather | solution.py:720
  43.0 2.3 %shard_map.89 = (f32[6,16,16,128]{3,2,1,0:T(8,128)S(1)}, f32[6,96,128]{2,1,0:T(8,128)S(1)}, f32[6,96,128]{2,1,0:T(8,128)}, f32[8,56,128]{2,1,0:T(8,128)}, f32[6,96,128]{2,1,0:T(8,128)}) custom-call(s32[2]{0:T(128)S(4)} %get-tuple-element.51.refs_0_.refs_3_, s32[8]{0:T(128)S(4)} %get-tuple-element.52.refs_1_.refs_4_, ...), custom_call_target="tpu_custom_call", output_to_operand_aliasing={{0}: (5, {})} | custom-call | flops 884736 | bytes 3145728 | tf_op jit(solution)/shard_map/pallas_call | solution.py:644
  45.3 3.7 %all-to-all-start.2 = ((f32[8,56,128]{2,1,0:T(8,128)}), f32[8,56,128]{2,1,0:T(8,128)S(1)}, u32[]{:S(2)}, u32[]{:S(2)}) async-start(f32[8,56,128]{2,1,0:T(8,128)} %get-tuple-element.67), calls=%async_computation.2 | async-start | bytes 458752 | tf_op jit(solution)/shard_map/all_to_all | solution.py:676
  49.0 5.5 %shard_map.90.refs_5_ = f32[6,16,16,128]{3,2,1,0:T(8,128)S(1)} custom-call(f32[3,6,6]{2,1,0:T(8,128)S(4)} %get-tuple-element.55.refs_0_.refs_4_, f32[6,16,16,128]{3,2,1,0:T(8,128)S(1)} %get-tuple-element.73.refs_1_, f32[6,16,16,128]{3,2,1,0:T(8,128)} %bitcast.18, f32[16,16,128]{2,1,0:T(8,128)} %bitcast.14), custom_call_target="tpu_custom_call" | custom-call | flops 28311552 | bytes 3145728 | tf_op jit(solution)/shard_map/pallas_call | solution.py:644
  54.5 3.5 %all-to-all-done.2.refs_4_ = f32[8,56,128]{2,1,0:T(8,128)S(1)} async-done(((f32[8,56,128]{2,1,0:T(8,128)}), f32[8,56,128]{2,1,0:T(8,128)S(1)}, u32[]{:S(2)}, u32[]{:S(2)}) %all-to-all-start.2) | async-done | bytes 229408 | tf_op jit(solution)/shard_map/all_to_all | solution.py:676
  58.0 0.8 shard_map.91
  58.8 3.4 %all-to-all-start.3 = ((f32[8,56,128]{2,1,0:T(8,128)}), f32[8,56,128]{2,1,0:T(8,128)S(1)}, u32[]{:S(2)}, u32[]{:S(2)}) async-start(f32[8,56,128]{2,1,0:T(8,128)} %shard_map.91), calls=%async_computation.3 | async-start | bytes 458752 | tf_op jit(solution)/shard_map/all_to_all | solution.py:676
  62.2 5.3 %shard_map.92 = (f32[6,16,16,128]{3,2,1,0:T(8,128)}, f32[6,96,128]{2,1,0:T(8,128)S(1)}, f32[6,96,128]{2,1,0:T(8,128)S(1)}) custom-call(f32[3,6,6]{2,1,0:T(8,128)S(4)} %get-tuple-element.55.refs_0_.refs_4_, f32[6,16,16,128]{3,2,1,0:T(8,128)S(1)} %get-tuple-element.73.refs_1_, f32[16,16,128]{2,1,0:T(8,128)} %bitcast.15, ...), custom_call_target="tpu_custom_call" | custom-call | flops 14155776 | bytes 3145728 | tf_op jit(solution)/shard_map/pallas_call | solution.py:644
  67.5 3.1 %all-to-all-done.3.refs_9_ = f32[8,56,128]{2,1,0:T(8,128)S(1)} async-done(((f32[8,56,128]{2,1,0:T(8,128)}), f32[8,56,128]{2,1,0:T(8,128)S(1)}, u32[]{:S(2)}, u32[]{:S(2)}) %all-to-all-start.3) | async-done | bytes 229408 | tf_op jit(solution)/shard_map/all_to_all | solution.py:676
  70.6 2.3 %shard_map.93 = (f32[6,16,16,128]{3,2,1,0:T(8,128)S(1)}, f32[6,96,128]{2,1,0:T(8,128)S(1)}, f32[8,56,128]{2,1,0:T(8,128)}, f32[6,96,128]{2,1,0:T(8,128)}) custom-call(s32[2]{0:T(128)S(4)} %get-tuple-element.51.refs_0_.refs_3_, s32[8]{0:T(128)S(4)} %get-tuple-element.52.refs_1_.refs_4_, ...), custom_call_target="tpu_custom_call", output_to_operand_aliasing={{0}: (5, {})} | custom-call | flops 884736 | bytes 3145728 | tf_op jit(solution)/shard_map/pallas_call | solution.py:644
  72.9 3.4 %all-to-all-start.4 = ((f32[8,56,128]{2,1,0:T(8,128)}), f32[8,56,128]{2,1,0:T(8,128)S(1)}, u32[]{:S(2)}, u32[]{:S(2)}) async-start(f32[8,56,128]{2,1,0:T(8,128)} %get-tuple-element.81), calls=%async_computation.4 | async-start | bytes 458752 | tf_op jit(solution)/shard_map/all_to_all | solution.py:676
  76.3 5.5 %shard_map.94.refs_5_ = f32[6,16,16,128]{3,2,1,0:T(8,128)S(1)} custom-call(f32[3,6,6]{2,1,0:T(8,128)S(4)} %get-tuple-element.55.refs_0_.refs_4_, f32[4,6,4,16,128]{4,3,2,1,0:T(8,128)} %bitcast.11, f32[6,16,16,128]{3,2,1,0:T(8,128)S(1)} %get-tuple-element.82.refs_2_, f32[16,16,128]{2,1,0:T(8,128)} %bitcast.16), custom_call_target="tpu_custom_call" | custom-call | flops 28311552 | bytes 3145728 | tf_op jit(solution)/shard_map/pallas_call | solution.py:644
  81.8 2.6 %all-to-all-done.4.refs_4_ = f32[8,56,128]{2,1,0:T(8,128)S(1)} async-done(((f32[8,56,128]{2,1,0:T(8,128)}), f32[8,56,128]{2,1,0:T(8,128)S(1)}, u32[]{:S(2)}, u32[]{:S(2)}) %all-to-all-start.4) | async-done | bytes 229408 | tf_op jit(solution)/shard_map/all_to_all | solution.py:676
  84.4 0.8 shard_map.95
  85.2 3.5 %all-to-all-start.5 = ((f32[8,56,128]{2,1,0:T(8,128)}), f32[8,56,128]{2,1,0:T(8,128)S(1)}, u32[]{:S(2)}, u32[]{:S(2)}) async-start(f32[8,56,128]{2,1,0:T(8,128)} %shard_map.95), calls=%async_computation.5 | async-start | bytes 458752 | tf_op jit(solution)/shard_map/all_to_all | solution.py:676
  88.6 2.8 %shard_map.96 = (f32[6,16,16,128]{3,2,1,0:T(8,128)}, f32[6,96,128]{2,1,0:T(8,128)S(1)}, f32[6,96,128]{2,1,0:T(8,128)S(1)}) custom-call(s32[2]{0:T(128)S(4)} %get-tuple-element.51.refs_0_.refs_3_, s32[8]{0:T(128)S(4)} %get-tuple-element.52.refs_1_.refs_4_, s32[8,6]{1,0:T(8,128)S(4)} %get-tuple-element.53.refs_2_.refs_5_, ...), custom_call_target="tpu_custom_call" | custom-call | flops 14155776 | bytes 3145728 | tf_op jit(solution)/shard_map/pallas_call | solution.py:644
  91.5 5.2 %all-to-all-done.5.refs_9_ = f32[8,56,128]{2,1,0:T(8,128)S(1)} async-done(((f32[8,56,128]{2,1,0:T(8,128)}), f32[8,56,128]{2,1,0:T(8,128)S(1)}, u32[]{:S(2)}, u32[]{:S(2)}) %all-to-all-start.5) | async-done | bytes 229408 | tf_op jit(solution)/shard_map/all_to_all | solution.py:676
  96.6 1.5 %shard_map.97 = f32[6,16,16,128]{3,2,1,0:T(8,128)} custom-call(s32[2]{0:T(128)S(4)} %get-tuple-element.51.refs_0_.refs_3_, s32[8]{0:T(128)S(4)} %get-tuple-element.52.refs_1_.refs_4_, s32[8,6]{1,0:T(8,128)S(4)} %get-tuple-element.53.refs_2_.refs_5_, s32[8,6]{1,0:T(8,128)S(4)} %get-tuple-element.54.refs_3_.refs_6_, ...), custom_call_target="tpu_custom_call" | custom-call | flops 884736 | bytes 3145728 | tf_op jit(solution)/shard_map/pallas_call | solution.py:644
  (1 shorter events, 0.0 us)
Async XLA Ops:
  3.3 7.4 %copy-start = (f32[1,6,4,16,128]{4,3,2,1,0:T(8,128)S(1)}, f32[1,6,4,16,128]{4,3,2,1,0:T(8,128)}, u32[]{:S(2)}) copy-start(f32[1,6,4,16,128]{4,3,2,1,0:T(8,128)} %param.7) | copy-start | bytes 589828
  3.3 17.0 %all-to-all-start = ((f32[8,72,128]{2,1,0:T(8,128)}), f32[8,72,128]{2,1,0:T(8,128)S(1)}, u32[]{:S(2)}, u32[]{:S(2)}) async-start(f32[8,72,128]{2,1,0:T(8,128)} %get-tuple-element.57), calls=%async_computation | async-start | bytes 589824 | tf_op jit(solution)/shard_map/all_to_all | solution.py:676
  21.3 15.5 %all-to-all-start.1 = ((f32[8,72,128]{2,1,0:T(8,128)}), f32[8,72,128]{2,1,0:T(8,128)S(1)}, u32[]{:S(2)}, u32[]{:S(2)}) async-start(f32[8,72,128]{2,1,0:T(8,128)} %shard_map.87), calls=%async_computation.1 | async-start | bytes 589824 | tf_op jit(solution)/shard_map/all_to_all | solution.py:676
  45.3 12.7 %all-to-all-start.2 = ((f32[8,56,128]{2,1,0:T(8,128)}), f32[8,56,128]{2,1,0:T(8,128)S(1)}, u32[]{:S(2)}, u32[]{:S(2)}) async-start(f32[8,56,128]{2,1,0:T(8,128)} %get-tuple-element.67), calls=%async_computation.2 | async-start | bytes 458752 | tf_op jit(solution)/shard_map/all_to_all | solution.py:676
  58.8 11.8 %all-to-all-start.3 = ((f32[8,56,128]{2,1,0:T(8,128)}), f32[8,56,128]{2,1,0:T(8,128)S(1)}, u32[]{:S(2)}, u32[]{:S(2)}) async-start(f32[8,56,128]{2,1,0:T(8,128)} %shard_map.91), calls=%async_computation.3 | async-start | bytes 458752 | tf_op jit(solution)/shard_map/all_to_all | solution.py:676
  72.9 11.5 %all-to-all-start.4 = ((f32[8,56,128]{2,1,0:T(8,128)}), f32[8,56,128]{2,1,0:T(8,128)S(1)}, u32[]{:S(2)}, u32[]{:S(2)}) async-start(f32[8,56,128]{2,1,0:T(8,128)} %get-tuple-element.81), calls=%async_computation.4 | async-start | bytes 458752 | tf_op jit(solution)/shard_map/all_to_all | solution.py:676
  85.2 11.5 %all-to-all-start.5 = ((f32[8,56,128]{2,1,0:T(8,128)}), f32[8,56,128]{2,1,0:T(8,128)S(1)}, u32[]{:S(2)}, u32[]{:S(2)}) async-start(f32[8,56,128]{2,1,0:T(8,128)} %shard_map.95), calls=%async_computation.5 | async-start | bytes 458752 | tf_op jit(solution)/shard_map/all_to_all | solution.py:676
